TPU v7x, 32 devices: a whole 2x2x4 slice. The times are simulated.
32 devices in a mesh: occi: 4 (over y, x), occj: 2 (over core), virt: 4 (over z).
Axes of the slice: x: 2, y: 2, z: 4, core: 2. Of those that a mesh axis runs over, the one named last changes fastest.
Arguments:
- amplitudes: bfloat16 [8, 8, 128, 128], P('occi', 'occj'), may hold values from -6 to 6
- vectors: bfloat16 [32, 128, 128], P('virt'), may hold values from -0.15625 to 0.15625
- tile_mask: int32 [8, 8, 2, 2], P('occi', 'occj'), may hold values 0 or 1
- pair_mask: int32 [8, 8], P('occi', 'occj'), may hold values 0 or 1
Outputs:
- ladder: bfloat16 [8, 8, 128, 128], P('occi', 'occj', 'virt')
All inputs are finite; a program needn't handle non-finite values. No bound on the sum of `tile_mask` or of `pair_mask` on one device may be relied on, other than what follows from the above.
Results may differ from a plain program's by a relative error of at most 0.0059.
Values may be sent and summed in bfloat16 or wider, within the bound.
No kernel may reach another device: no remote copies, remote signals or barrier semaphores. Data moves between devices by JAX's collectives and lax.ppermute only.
A program may use at most 64 MiB of HBM per device.

v0:
```python
import jax
import jax.numpy as jnp
from jax import lax
from jax.sharding import PartitionSpec as P

TILE = 64
SLAB_TILES = 2


def masked_tiles(amplitudes, tile_mask):
    first, second = (amplitudes.shape[0], amplitudes.shape[1])
    tiled = amplitudes.reshape(first, second, SLAB_TILES, TILE, SLAB_TILES, TILE)
    keep_tiles = tile_mask.astype(jnp.bfloat16)[:, :, :, None, :, None]
    return (tiled * keep_tiles).reshape(amplitudes.shape)


def shards(amplitudes, vectors, tile_mask, pair_mask):
    kept = masked_tiles(amplitudes, tile_mask)
    slab_total = kept.shape[2]
    row_count = slab_total // lax.axis_size("virt")
    first_row = lax.axis_index("virt") * row_count
    pair_rows, pair_cols = (kept.shape[0], kept.shape[1])

    def advance(partial_sum, vector):
        contracted = jnp.einsum(
            "ac,ipcd->aipd", vector, kept, preferred_element_type=jnp.float32
        ).astype(jnp.bfloat16)
        return (
            partial_sum
            + jnp.einsum("aipd,bd->aipb", contracted, vector, preferred_element_type=jnp.float32),
            None,
        )

    initial = jnp.zeros(
        (lax.axis_size("virt") * row_count, pair_rows, pair_cols, slab_total), jnp.float32
    )
    summed, _ = lax.scan(advance, initial, vectors)
    reduced = lax.psum_scatter(summed, "virt", scatter_dimension=0, tiled=True)
    total = jnp.transpose(reduced, (1, 2, 0, 3))
    half = total.astype(jnp.bfloat16)
    full_rows = lax.all_gather(half, "virt", axis=2, tiled=True)
    swapped = lax.all_to_all(
        lax.all_to_all(full_rows, "occi", split_axis=1, concat_axis=1, tiled=True),
        "occj",
        split_axis=0,
        concat_axis=0,
        tiled=True,
    )
    columns = lax.dynamic_slice_in_dim(swapped, first_row, row_count, 3)
    summed = half.astype(jnp.float32) + jnp.swapaxes(columns, 2, 3).astype(jnp.float32)
    return (pair_mask.astype(jnp.float32)[:, :, None, None] * summed).astype(jnp.bfloat16)


def solution(mesh):
    placed = (
        P("occi", "occj", None, None),
        P("virt", None, None),
        P("occi", "occj", None, None),
        P("occi", "occj"),
    )
    return jax.shard_map(
        shards,
        mesh=mesh,
        in_specs=placed,
        out_specs=P("occi", "occj", "virt", None),
        check_vma=False,
    )
```

profile of v0, /device:TPU:0, one launch (start us, length us, event | category | flops | bytes accessed | tf_op | source)
XLA Modules:
  0.0 75.8 jit_solution(5871530727843587421)
XLA Ops:
  0.0 0.7 copy-done.1
  0.8 0.3 mul.23
  1.2 0.2 mul.24
  1.4 0.7 copy-done
  2.2 10.5 %while.11 = (s32[]{:T(128)}, f32[128,2,4,128]{3,0,2,1:T(8,128)S(1)}, bf16[8,128,128]{2,1,0:T(8,128)(2,1)}, bf16[2,4,128,128]{3,2,1,0:T(8,128)(2,1)S(1)}, s32[]{:T(128)}, /*index=5*/s32[]{:T(128)}) while((s32[]{:T(128)}, f32[128,2,4,128]{3,0,2,1:T(8,128)S(1)}, bf16[8,128,128]{2,1,0:T(8,128)(2,1)}, ...), condition=%wide.region_1.2_spmd.clone, body=%wide.region_0.1_spmd.clone.sunk | while | flops 67502080 | bytes 1377359 | solution.py:37
  2.2 1.3 %convolution_add_fusion.2 = f32[128,2,4,128]{3,0,2,1:T(8,128)S(1)} fusion(bf16[2,4,128,128]{3,2,1,0:T(8,128)(2,1)S(1)} %get-tuple-element.91, f32[128,2,4,128]{3,0,2,1:T(8,128)S(1)} %get-tuple-element.83, pred[]{:T(512)S(6)} %compare.3, bf16[8,128,128]{2,1,0:T(8,128)(2,1)} %get-tuple-element.90, s32[]{:T(128)} %get-tuple-element.82), kind=kOutput, calls=%fused_computation.clone.1 | convolution fusion | flops 67502080 | bytes 1377281 | tf_op jit(solution)/shard_map/while/body/eval_jaxpr/aipd,bd->aipb/dot_general | solution.py:30
  3.5 1.3 %convolution_add_fusion.2 = f32[128,2,4,128]{3,0,2,1:T(8,128)S(1)} fusion(bf16[2,4,128,128]{3,2,1,0:T(8,128)(2,1)S(1)} %get-tuple-element.91, f32[128,2,4,128]{3,0,2,1:T(8,128)S(1)} %get-tuple-element.83, pred[]{:T(512)S(6)} %compare.3, bf16[8,128,128]{2,1,0:T(8,128)(2,1)} %get-tuple-element.90, s32[]{:T(128)} %get-tuple-element.82), kind=kOutput, calls=%fused_computation.clone.1 | convolution fusion | flops 67502080 | bytes 1377281 | tf_op jit(solution)/shard_map/while/body/eval_jaxpr/aipd,bd->aipb/dot_general | solution.py:30
  4.8 1.3 %convolution_add_fusion.2 = f32[128,2,4,128]{3,0,2,1:T(8,128)S(1)} fusion(bf16[2,4,128,128]{3,2,1,0:T(8,128)(2,1)S(1)} %get-tuple-element.91, f32[128,2,4,128]{3,0,2,1:T(8,128)S(1)} %get-tuple-element.83, pred[]{:T(512)S(6)} %compare.3, bf16[8,128,128]{2,1,0:T(8,128)(2,1)} %get-tuple-element.90, s32[]{:T(128)} %get-tuple-element.82), kind=kOutput, calls=%fused_computation.clone.1 | convolution fusion | flops 67502080 | bytes 1377281 | tf_op jit(solution)/shard_map/while/body/eval_jaxpr/aipd,bd->aipb/dot_general | solution.py:30
  6.1 1.3 %convolution_add_fusion.2 = f32[128,2,4,128]{3,0,2,1:T(8,128)S(1)} fusion(bf16[2,4,128,128]{3,2,1,0:T(8,128)(2,1)S(1)} %get-tuple-element.91, f32[128,2,4,128]{3,0,2,1:T(8,128)S(1)} %get-tuple-element.83, pred[]{:T(512)S(6)} %compare.3, bf16[8,128,128]{2,1,0:T(8,128)(2,1)} %get-tuple-element.90, s32[]{:T(128)} %get-tuple-element.82), kind=kOutput, calls=%fused_computation.clone.1 | convolution fusion | flops 67502080 | bytes 1377281 | tf_op jit(solution)/shard_map/while/body/eval_jaxpr/aipd,bd->aipb/dot_general | solution.py:30
  7.5 1.3 %convolution_add_fusion.2 = f32[128,2,4,128]{3,0,2,1:T(8,128)S(1)} fusion(bf16[2,4,128,128]{3,2,1,0:T(8,128)(2,1)S(1)} %get-tuple-element.91, f32[128,2,4,128]{3,0,2,1:T(8,128)S(1)} %get-tuple-element.83, pred[]{:T(512)S(6)} %compare.3, bf16[8,128,128]{2,1,0:T(8,128)(2,1)} %get-tuple-element.90, s32[]{:T(128)} %get-tuple-element.82), kind=kOutput, calls=%fused_computation.clone.1 | convolution fusion | flops 67502080 | bytes 1377281 | tf_op jit(solution)/shard_map/while/body/eval_jaxpr/aipd,bd->aipb/dot_general | solution.py:30
  8.8 1.3 %convolution_add_fusion.2 = f32[128,2,4,128]{3,0,2,1:T(8,128)S(1)} fusion(bf16[2,4,128,128]{3,2,1,0:T(8,128)(2,1)S(1)} %get-tuple-element.91, f32[128,2,4,128]{3,0,2,1:T(8,128)S(1)} %get-tuple-element.83, pred[]{:T(512)S(6)} %compare.3, bf16[8,128,128]{2,1,0:T(8,128)(2,1)} %get-tuple-element.90, s32[]{:T(128)} %get-tuple-element.82), kind=kOutput, calls=%fused_computation.clone.1 | convolution fusion | flops 67502080 | bytes 1377281 | tf_op jit(solution)/shard_map/while/body/eval_jaxpr/aipd,bd->aipb/dot_general | solution.py:30
  10.1 1.3 %convolution_add_fusion.2 = f32[128,2,4,128]{3,0,2,1:T(8,128)S(1)} fusion(bf16[2,4,128,128]{3,2,1,0:T(8,128)(2,1)S(1)} %get-tuple-element.91, f32[128,2,4,128]{3,0,2,1:T(8,128)S(1)} %get-tuple-element.83, pred[]{:T(512)S(6)} %compare.3, bf16[8,128,128]{2,1,0:T(8,128)(2,1)} %get-tuple-element.90, s32[]{:T(128)} %get-tuple-element.82), kind=kOutput, calls=%fused_computation.clone.1 | convolution fusion | flops 67502080 | bytes 1377281 | tf_op jit(solution)/shard_map/while/body/eval_jaxpr/aipd,bd->aipb/dot_general | solution.py:30
  11.4 1.3 %convolution_add_fusion.2 = f32[128,2,4,128]{3,0,2,1:T(8,128)S(1)} fusion(bf16[2,4,128,128]{3,2,1,0:T(8,128)(2,1)S(1)} %get-tuple-element.91, f32[128,2,4,128]{3,0,2,1:T(8,128)S(1)} %get-tuple-element.83, pred[]{:T(512)S(6)} %compare.3, bf16[8,128,128]{2,1,0:T(8,128)(2,1)} %get-tuple-element.90, s32[]{:T(128)} %get-tuple-element.82), kind=kOutput, calls=%fused_computation.clone.1 | convolution fusion | flops 67502080 | bytes 1377281 | tf_op jit(solution)/shard_map/while/body/eval_jaxpr/aipd,bd->aipb/dot_general | solution.py:30
  12.7 0.3 copy.14
  13.0 32.1 %all-reduce.2 = bf16[128,2,4,128]{3,2,1,0:T(4,128)(2,1)S(1)} all-reduce(f32[128,2,4,128]{3,2,1,0:T(4,128)S(1)} %copy.14), channel_id=2, replica_groups=mesh['occi'=4,'occj'=2,'virt'=4] {'virt'}, use_global_device_ids=true, to_apply=%region_2.3.clone | all-reduce | flops 131072 | bytes 786432
  45.2 0.6 copy-done.3
  45.8 0.6 dynamic-slice
  47.1 13.8 %all_gather.3 = bf16[2,4,128,128]{3,1,0,2:T(4,128)(2,1)S(1)} all-gather(bf16[2,4,32,128]{3,1,0,2:T(4,128)(2,1)S(1)} %fusion.8), channel_id=1, replica_groups=mesh['occi'=4,'occj'=2,'virt'=4] {'virt'}, dimensions={2}, use_global_device_ids=true | all-gather | bytes 327680 | tf_op jit(solution)/shard_map/all_gather | solution.py:41
  60.9 0.9 %copy.15 = bf16[2,4,128,128]{2,3,0,1:T(8,128)(2,1)} copy(bf16[2,4,128,128]{3,1,0,2:T(4,128)(2,1)S(1)} %all_gather.3) | data formatting | bytes 524288 | tf_op jit(solution)/shard_map/all_gather | solution.py:41
  61.8 3.7 %all-to-all-start = ((bf16[2,4,128,128]{2,3,0,1:T(8,128)(2,1)}), bf16[2,4,128,128]{2,3,0,1:T(8,128)(2,1)S(1)}, u32[]{:S(2)}, u32[]{:S(2)}) async-start(bf16[2,4,128,128]{2,3,0,1:T(8,128)(2,1)} %copy.15), calls=%async_computation | async-start | bytes 524288 | tf_op jit(solution)/shard_map/all_to_all | solution.py:43
  65.5 0.7 copy-done.2
  66.2 4.7 %all-to-all-done = bf16[2,4,128,128]{2,3,0,1:T(8,128)(2,1)S(1)} async-done(((bf16[2,4,128,128]{2,3,0,1:T(8,128)(2,1)}), bf16[2,4,128,128]{2,3,0,1:T(8,128)(2,1)S(1)}, u32[]{:S(2)}, u32[]{:S(2)}) %all-to-all-start) | async-done | bytes 262176 | tf_op jit(solution)/shard_map/all_to_all | solution.py:43
  71.1 3.9 %all_to_all.10 = bf16[2,4,128,128]{2,1,3,0:T(4,128)(2,1)S(1)} all-to-all(bf16[2,4,128,128]{2,1,3,0:T(4,128)(2,1)S(1)} %copy.16), channel_id=1, replica_groups=mesh['occi'=4,'occj'=2,'virt'=4] {'occj'}, dimensions={0} | all-to-all | bytes 524288 | tf_op jit(solution)/shard_map/all_to_all | solution.py:42
  75.1 0.6 copy.18
  (12 shorter events, 0.5 us)
Async XLA Ops:
  0.0 0.7 copy-start.1
  1.2 1.0 %copy-start = (bf16[2,4,128,128]{3,2,1,0:T(8,128)(2,1)S(1)}, bf16[2,4,128,128]{3,2,1,0:T(8,128)(2,1)}, u32[]{:S(2)}) copy-start(bf16[2,4,128,128]{3,2,1,0:T(8,128)(2,1)} %param.6) | copy-start | bytes 786436
  45.2 0.7 copy-start.3
  61.8 9.1 %all-to-all-start = ((bf16[2,4,128,128]{2,3,0,1:T(8,128)(2,1)}), bf16[2,4,128,128]{2,3,0,1:T(8,128)(2,1)S(1)}, u32[]{:S(2)}, u32[]{:S(2)}) async-start(bf16[2,4,128,128]{2,3,0,1:T(8,128)(2,1)} %copy.15), calls=%async_computation | async-start | bytes 524288 | tf_op jit(solution)/shard_map/all_to_all | solution.py:43
  65.5 0.7 copy-start.2
where the time goes:
time: 76.7 us; the launch traced here: 75.8 us
  blocking collectives  49.9 us (65%)
  matrix products  10.3 us (13%)
  local copies, waits for them, and re-layouts  6.1 us (8%)
  waiting for transfers between devices  4.69 us (6%)
  starting transfers between devices  3.71 us (5%)
    unnamed x1, blocking collectives  32.1 us
    all_gather x1, blocking collectives, shards(): full_rows = lax.all_gather(half, 'virt', axis=2, tiled=True)  13.8 us
    dot_general x8, matrix products, advance(): jnp.einsum('aipd,bd->aipb', contracted, vector, preferred_element_type=jn...  10.3 us
    all_to_all x1, waiting for transfers between devices, shards(): lax.all_to_all(full_rows, 'occi', split_axis=1, concat_axis=1, tiled=True)  4.69 us
    all_to_all x1, blocking collectives, shards(): lax.all_to_all(lax.all_to_all(full_rows, 'occi', split_axis=1, concat_axi...  3.94 us
    all_to_all x1, starting transfers between devices, shards(): lax.all_to_all(full_rows, 'occi', split_axis=1, concat_axis=1, tiled=True)  3.71 us
    unnamed x9, local copies, waits for them, and re-layouts  3.29 us
  transfers between devices with their start and end apart: 1, of which 1 were waited for; matrix products, arithmetic and copies ran while one was open for 0% of the time, Pallas kernels for 0%

commit v1 on v0

v1 whole, which is shorter than its diff:
```python
import functools

import jax
import jax.numpy as jnp
from jax import lax
from jax.experimental import pallas as pl
from jax.experimental.pallas import tpu as pltpu
from jax.sharding import PartitionSpec as P

TILE = 64
SLAB_TILES = 2
PAIR_GROUP = 8


def mask_kernel(mask_ref, amp_ref, kept_ref):
    firsts, seconds, slab, _ = amp_ref.shape
    row = lax.broadcasted_iota(jnp.int32, (slab, slab), 0) // TILE
    col = lax.broadcasted_iota(jnp.int32, (slab, slab), 1) // TILE
    tile = row * SLAB_TILES + col

    def one(block, _):
        first, second = block // seconds, block % seconds
        keep = jnp.zeros((slab, slab), jnp.float32)
        for t in range(SLAB_TILES * SLAB_TILES):
            keep = jnp.where(tile == t, mask_ref[block, t].astype(jnp.float32), keep)
        wide = amp_ref[first, second].astype(jnp.float32) * keep
        kept_ref[block] = wide.astype(kept_ref.dtype)
        return 0

    lax.fori_loop(0, firsts * seconds, one, 0, unroll=firsts * seconds <= 8)


def ladder_kernel(kept_ref, partner_ref, vec_ref, half_ref):
    pairs, slab, _ = kept_ref.shape
    vectors = vec_ref.shape[0]
    chunks, _, rows, _ = half_ref.shape
    flat = vec_ref[...].reshape(vectors * slab, slab)
    turned = jnp.concatenate(
        [vec_ref[q].astype(jnp.float32).T.astype(jnp.bfloat16) for q in range(vectors)], axis=0
    )

    def step(base):
        for j in range(0, min(PAIR_GROUP, pairs), 2):
            both = []
            for k in (j, j + 1):
                wide = kept_ref[base + k].astype(jnp.float32) + partner_ref[base + k].astype(jnp.float32).T
                both.append(wide.astype(jnp.bfloat16))
            inner = jnp.dot(flat, jnp.concatenate(both, axis=1), preferred_element_type=jnp.float32)
            inner = inner.astype(jnp.bfloat16).reshape(vectors, slab, 2 * slab)
            stacked = jnp.concatenate(
                [
                    jnp.concatenate([inner[q, :, n * slab : (n + 1) * slab] for q in range(vectors)], axis=1)
                    for n in range(2)
                ],
                axis=0,
            )
            half = jnp.dot(stacked, turned, preferred_element_type=jnp.float32)
            for n, k in enumerate((j, j + 1)):
                for chunk in range(chunks):
                    start = n * slab + chunk * rows
                    half_ref[chunk, base + k] = half[start : start + rows].astype(half_ref.dtype)

    if pairs <= PAIR_GROUP:
        step(0)
    else:
        lax.fori_loop(0, pairs // PAIR_GROUP, lambda g, c: (step(g * PAIR_GROUP), c)[1], 0)


def vmem_specs(count):
    return [pl.BlockSpec(memory_space=pltpu.VMEM)] * count


def shards(amplitudes, vectors, tile_mask, pair_mask):
    firsts, seconds, slab, _ = amplitudes.shape
    pairs = firsts * seconds
    virt = lax.axis_size("virt")
    rows = slab // virt
    params = pltpu.CompilerParams(vmem_limit_bytes=24 * 1024 * 1024)
    kept = pl.pallas_call(
        mask_kernel,
        out_shape=jax.ShapeDtypeStruct((pairs, slab, slab), jnp.bfloat16),
        in_specs=[pl.BlockSpec(memory_space=pltpu.SMEM)] + vmem_specs(1),
        out_specs=vmem_specs(1)[0],
        compiler_params=params,
    )(tile_mask.reshape(pairs, SLAB_TILES * SLAB_TILES), amplitudes)
    partner = lax.all_to_all(kept, ("occj", "occi"), split_axis=0, concat_axis=0, tiled=True)
    half = pl.pallas_call(
        ladder_kernel,
        out_shape=jax.ShapeDtypeStruct((virt, pairs, rows, slab), jnp.bfloat16),
        in_specs=vmem_specs(3),
        out_specs=vmem_specs(1)[0],
        compiler_params=params,
    )(kept, partner, vectors)
    terms = lax.all_to_all(half, "virt", split_axis=0, concat_axis=0, tiled=True)
    summed = jnp.sum(terms.astype(jnp.float32), axis=0).reshape(firsts, seconds, rows, slab)
    return (pair_mask.astype(jnp.float32)[:, :, None, None] * summed).astype(jnp.bfloat16)


def solution(mesh):
    placed = (
        P("occi", "occj", None, None),
        P("virt", None, None),
        P("occi", "occj", None, None),
        P("occi", "occj"),
    )
    return jax.shard_map(
        shards,
        mesh=mesh,
        in_specs=placed,
        out_specs=P("occi", "occj", "virt", None),
        check_vma=False,
    )
```

time: 76.7 us -> 31.8 us (0.41)
  blocking collectives: 49.9 us -> 11.7 us
  matrix products: 10.3 us -> 0 us
  waiting for transfers between devices: 4.69 us -> 9.25 us
  local copies, waits for them, and re-layouts: 6.1 us -> 1.82 us
  Pallas kernels: 0 us -> 2.94 us
  starting transfers between devices: 3.71 us -> 5 us
    unnamed x1 -> x0, blocking collectives: 32.1 us -> none
    all_gather x1 -> x0, blocking collectives: 13.8 us -> none  [shards(): full_rows = lax.all_gather(half, 'virt', axis=2, tiled=True)]
    dot_general x8 -> x0, matrix products: 10.3 us -> none  [advance(): jnp.einsum('aipd,bd->aipb', contracted, vector, preferred_element_type=jn...]
    all_to_all x1, blocking collectives: 3.94 us -> 11.7 us  [shards(): lax.all_to_all(kept, ('occj', 'occi'), split_axis=0, concat_axis=0, tiled...]
    all_to_all x1, waiting for transfers between devices: 4.69 us -> 9.25 us  [shards(): lax.all_to_all(half, 'virt', split_axis=0, concat_axis=0, tiled=True)]
    pallas_call x0 -> x2, Pallas kernels: none -> 2.94 us  [the longest x1 2.16 us: shards(): pl.pallas_call(ladder_kernel, out_shape=jax.ShapeDtypeStruct((virt, pairs...]
    unnamed x9 -> x7, local copies, waits for them, and re-layouts: 3.29 us -> 1.65 us
    all_to_all x1, starting transfers between devices: 3.71 us -> 5 us  [shards(): lax.all_to_all(half, 'virt', split_axis=0, concat_axis=0, tiled=True)]
where the time goes in v1:
time: 31.8 us; the launch traced here: 31.5 us
  blocking collectives  11.7 us (37%)
  waiting for transfers between devices  9.25 us (29%)
  starting transfers between devices  5 us (16%)
  Pallas kernels  2.94 us (9%)
  local copies, waits for them, and re-layouts  1.82 us (6%)
  other arithmetic  0.75 us (2%)
    all_to_all x1, blocking collectives, shards(): lax.all_to_all(kept, ('occj', 'occi'), split_axis=0, concat_axis=0, tiled...  11.7 us
    all_to_all x1, waiting for transfers between devices, shards(): lax.all_to_all(half, 'virt', split_axis=0, concat_axis=0, tiled=True)  9.25 us
    all_to_all x1, starting transfers between devices, shards(): lax.all_to_all(half, 'virt', split_axis=0, concat_axis=0, tiled=True)  5 us
    pallas_call x1, Pallas kernels, shards(): pl.pallas_call(ladder_kernel, out_shape=jax.ShapeDtypeStruct((virt, pairs...  2.16 us
    unnamed x7, local copies, waits for them, and re-layouts  1.65 us
    pallas_call x1, Pallas kernels, shards(): pl.pallas_call(mask_kernel, out_shape=jax.ShapeDtypeStruct((pairs, slab,...  0.78 us
    convert_element_type x1, other arithmetic, shards(): (pair_mask.astype(jnp.float32)[:, :, None, None] * summed).astype(jnp.bfl...  0.71 us
  transfers between devices with their start and end apart: 1, of which 1 were waited for; matrix products, arithmetic and copies ran while one was open for 0% of the time, Pallas kernels for 0%

profile of v1, /device:TPU:0, one launch (start us, length us, event | category | flops | bytes accessed | tf_op | source)
XLA Modules:
  0.0 31.5 jit_solution(2968188488471919435)
XLA Ops:
  0.0 0.7 %copy.5 = s32[2,4,2,2]{1,0,3,2:T(2,128)S(1)} copy(s32[2,4,2,2]{1,3,2,0:T(2,128)} %param.6) | data formatting | bytes 256 | tf_op args[2]
  0.7 0.1 reshape.7
  0.8 0.1 copy.6.mask_ref
  0.9 0.0 copy-start
  0.9 0.9 %copy-done = bf16[2,4,128,128]{3,2,1,0:T(8,128)(2,1)S(1)} copy-done((bf16[2,4,128,128]{3,2,1,0:T(8,128)(2,1)S(1)}, bf16[2,4,128,128]{3,2,1,0:T(8,128)(2,1)}, u32[]{:S(2)}) %copy-start) | copy-done | bytes 262168
  1.8 0.8 %shard_map.46.kept_ref = bf16[8,128,128]{2,1,0:T(8,128)(2,1)S(1)} custom-call(s32[8,4]{1,0:T(8,128)S(1)} %copy.6.mask_ref, bf16[2,4,128,128]{3,2,1,0:T(8,128)(2,1)S(1)} %copy-done), custom_call_target="tpu_custom_call" | custom-call | tf_op jit(solution)/shard_map/pallas_call | solution.py:79
  2.6 0.0 copy-start.1
  2.6 11.7 %all_to_all.10.partner_ref = bf16[8,128,128]{2,1,0:T(8,128)(2,1)S(1)} all-to-all(bf16[8,128,128]{2,1,0:T(8,128)(2,1)S(1)} %shard_map.46.kept_ref), channel_id=1, replica_groups=mesh['occi'=4,'occj'=2,'virt'=4] {'occj','occi'}, dimensions={0} | all-to-all | bytes 524288 | tf_op jit(solution)/shard_map/all_to_all | solution.py:86
  14.3 0.0 copy-done.1
  14.3 2.2 %shard_map.47 = bf16[4,8,32,128]{3,2,1,0:T(8,128)(2,1)} custom-call(bf16[8,128,128]{2,1,0:T(8,128)(2,1)S(1)} %shard_map.46.kept_ref, bf16[8,128,128]{2,1,0:T(8,128)(2,1)S(1)} %all_to_all.10.partner_ref, bf16[8,128,128]{2,1,0:T(8,128)(2,1)S(1)} %copy-done.1), custom_call_target="tpu_custom_call" | custom-call | tf_op jit(solution)/shard_map/pallas_call | solution.py:87
  16.5 0.0 copy-start.2
  16.5 5.0 %all-to-all-start.1 = ((bf16[4,8,32,128]{3,2,1,0:T(8,128)(2,1)}), bf16[4,8,32,128]{3,2,1,0:T(8,128)(2,1)S(1)}, u32[]{:S(2)}, u32[]{:S(2)}) async-start(bf16[4,8,32,128]{3,2,1,0:T(8,128)(2,1)} %shard_map.47), calls=%async_computation.1 | async-start | bytes 524288 | tf_op jit(solution)/shard_map/all_to_all | solution.py:94
  21.5 0.0 copy-done.2
  21.5 9.2 %all-to-all-done.1 = bf16[4,8,32,128]{3,2,1,0:T(8,128)(2,1)S(1)} async-done(((bf16[4,8,32,128]{3,2,1,0:T(8,128)(2,1)}), bf16[4,8,32,128]{3,2,1,0:T(8,128)(2,1)S(1)}, u32[]{:S(2)}, u32[]{:S(2)}) %all-to-all-start.1) | async-done | bytes 262176 | tf_op jit(solution)/shard_map/all_to_all | solution.py:94
  30.8 0.7 %multiply_convert_fusion = bf16[2,4,32,128]{3,2,1,0:T(8,128)(2,1)} fusion(f32[2,4,32,128]{3,2,1,0:T(8,128)S(1)} %bitcast.3, f32[2,4]{1,0:T(2,128)S(1)} %convert_element_type.9), kind=kLoop, calls=%fused_computation.1 | loop fusion | flops 65536 | bytes 196640 | tf_op jit(solution)/shard_map/convert_element_type | solution.py:96
  (2 shorter events, 0.0 us)
Async XLA Ops:
  0.9 0.9 %copy-start = (bf16[2,4,128,128]{3,2,1,0:T(8,128)(2,1)S(1)}, bf16[2,4,128,128]{3,2,1,0:T(8,128)(2,1)}, u32[]{:S(2)}) copy-start(bf16[2,4,128,128]{3,2,1,0:T(8,128)(2,1)} %amp_ref.1) | copy-start | bytes 786436
  2.6 11.7 %copy-start.1 = (bf16[8,128,128]{2,1,0:T(8,128)(2,1)S(1)}, bf16[8,128,128]{2,1,0:T(8,128)(2,1)}, u32[]{:S(2)}) copy-start(bf16[8,128,128]{2,1,0:T(8,128)(2,1)} %vec_ref.1) | copy-start | bytes 786436
  16.5 5.0 %copy-start.2 = (s32[2,4]{1,0:T(2,128)S(1)}, s32[2,4]{1,0:T(2,128)}, u32[]{:S(2)}) copy-start(s32[2,4]{1,0:T(2,128)} %param.7) | copy-start | bytes 100
  16.5 14.3 %all-to-all-start.1 = ((bf16[4,8,32,128]{3,2,1,0:T(8,128)(2,1)}), bf16[4,8,32,128]{3,2,1,0:T(8,128)(2,1)S(1)}, u32[]{:S(2)}, u32[]{:S(2)}) async-start(bf16[4,8,32,128]{3,2,1,0:T(8,128)(2,1)} %shard_map.47), calls=%async_computation.1 | async-start | bytes 524288 | tf_op jit(solution)/shard_map/all_to_all | solution.py:94

commit v2 on v1

v2 whole, which is shorter than its diff:
```python
import functools

import jax
import jax.numpy as jnp
from jax import lax
from jax.experimental import pallas as pl
from jax.experimental.pallas import tpu as pltpu
from jax.sharding import PartitionSpec as P

TILE = 64
SLAB_TILES = 2
PAIR_GROUP = 8
PLANE = ("occj", "occi")


def plane_index():
    return lax.axis_index("occj") * lax.axis_size("occi") + lax.axis_index("occi")


def mask_kernel(mask_ref, amp_ref, *kept_refs):
    _, seconds, slab, _ = amp_ref.shape
    row = lax.broadcasted_iota(jnp.int32, (slab, slab), 0) // TILE
    col = lax.broadcasted_iota(jnp.int32, (slab, slab), 1) // TILE

    def masked(block):
        first, second = block // seconds, block % seconds
        keep = jnp.zeros((slab, slab), jnp.float32)
        for r in range(SLAB_TILES):
            for c in range(SLAB_TILES):
                here = mask_ref[first, r, c, second].astype(jnp.float32)
                keep = jnp.where((row == r) & (col == c), here, keep)
        return (amp_ref[first, second].astype(jnp.float32) * keep).astype(jnp.bfloat16)

    if len(kept_refs) == 1:

        def one(block, carry):
            kept_refs[0][block] = masked(block)
            return carry

        lax.fori_loop(0, kept_refs[0].shape[0], one, 0)
    else:
        mine = plane_index()
        for step, kept_ref in enumerate(kept_refs):
            kept_ref[...] = masked(mine ^ step)


def ladder_kernel(steps, chunks, *refs):
    vec_ref, half_refs, refs = refs[0], refs[-chunks:], refs[1:-chunks]
    kept_refs, partner_refs = refs[:steps], refs[steps:]
    vectors, slab, _ = vec_ref.shape
    pairs, rows, _ = half_refs[0].shape
    me = lax.axis_index("virt")
    flat = jnp.concatenate(
        [
            vec_ref[q, pl.ds(pl.multiple_of((me ^ chunk) * rows, rows), rows), :]
            for q in range(vectors)
            for chunk in range(chunks)
        ],
        axis=0,
    )
    turned = jnp.concatenate(
        [vec_ref[q].astype(jnp.float32).T.astype(jnp.bfloat16) for q in range(vectors)], axis=0
    )

    def work(blocks):
        both = [
            (kept.astype(jnp.float32) + partner.astype(jnp.float32).T).astype(jnp.bfloat16)
            for _, kept, partner in blocks
        ]
        inner = jnp.dot(flat, jnp.concatenate(both, axis=1), preferred_element_type=jnp.float32)
        inner = inner.astype(jnp.bfloat16).reshape(vectors, slab, len(blocks) * slab)
        stacked = jnp.concatenate(
            [
                jnp.concatenate([inner[q, :, n * slab : (n + 1) * slab] for q in range(vectors)], axis=1)
                for n in range(len(blocks))
            ],
            axis=0,
        )
        half = jnp.dot(stacked, turned, preferred_element_type=jnp.float32)
        for n, (pair, _, _) in enumerate(blocks):
            for chunk in range(chunks):
                start = n * slab + chunk * rows
                half_refs[chunk][pair] = half[start : start + rows].astype(jnp.bfloat16)

    if steps == 1:

        def two(g, carry):
            work([(2 * g + n, kept_refs[0][2 * g + n], partner_refs[0][2 * g + n]) for n in range(2)])
            return carry

        lax.fori_loop(0, pairs // 2, two, 0)
    else:
        mine = plane_index()
        for step in range(0, steps, 2):
            blocks = []
            for s in (step, step + 1):
                partner_ref = partner_refs[s - 1] if s else kept_refs[0]
                blocks.append((mine ^ s, kept_refs[s][...], partner_ref[...]))
            work(blocks)


def vmem_specs(count):
    return [pl.BlockSpec(memory_space=pltpu.VMEM)] * count


def swap_virt(array, step):
    return lax.ppermute(array, "virt", [(d, d ^ step) for d in range(lax.axis_size("virt"))])


def swap_plane(array, step):
    size, across = lax.axis_size("occi"), lax.axis_size("occj")
    turn_j, turn_i = step // size, step % size
    moves = [(i * across + j, (i ^ turn_i) * across + (j ^ turn_j)) for i in range(size) for j in range(across)]
    return lax.ppermute(array, ("occi", "occj"), moves)


def shards(amplitudes, vectors, tile_mask, pair_mask):
    firsts, seconds, slab, _ = amplitudes.shape
    pairs = firsts * seconds
    virt = lax.axis_size("virt")
    rows = slab // virt
    plane = lax.axis_size("occi") * lax.axis_size("occj")
    params = pltpu.CompilerParams(vmem_limit_bytes=24 * 1024 * 1024)
    steps = plane if plane == pairs and plane <= PAIR_GROUP else 1
    block_shape = (slab, slab) if steps > 1 else (pairs, slab, slab)
    kept = pl.pallas_call(
        mask_kernel,
        out_shape=[jax.ShapeDtypeStruct(block_shape, jnp.bfloat16)] * steps,
        in_specs=[pl.BlockSpec(memory_space=pltpu.SMEM)] + vmem_specs(1),
        out_specs=vmem_specs(steps),
        compiler_params=params,
    )(jnp.transpose(tile_mask, (0, 2, 3, 1)), amplitudes)
    if steps > 1:
        partner = [swap_plane(kept[step], step) for step in range(1, steps)]
    else:
        partner = [lax.all_to_all(kept[0], PLANE, split_axis=0, concat_axis=0, tiled=True)]
    half = pl.pallas_call(
        functools.partial(ladder_kernel, steps, virt),
        out_shape=[jax.ShapeDtypeStruct((pairs, rows, slab), jnp.bfloat16)] * virt,
        in_specs=vmem_specs(1 + len(kept) + len(partner)),
        out_specs=vmem_specs(virt),
        compiler_params=params,
    )(vectors, *kept, *partner)
    summed = half[0].astype(jnp.float32)
    for step in range(1, virt):
        summed = summed + swap_virt(half[step], step).astype(jnp.float32)
    summed = summed.reshape(firsts, seconds, rows, slab)
    return (pair_mask.astype(jnp.float32)[:, :, None, None] * summed).astype(jnp.bfloat16)


def solution(mesh):
    placed = (
        P("occi", "occj", None, None),
        P("virt", None, None),
        P("occi", "occj", None, None),
        P("occi", "occj"),
    )
    return jax.shard_map(
        shards,
        mesh=mesh,
        in_specs=placed,
        out_specs=P("occi", "occj", "virt", None),
        check_vma=False,
    )
```

time: 31.8 us -> 27.2 us (0.86)
  blocking collectives: 11.7 us -> 0 us
  starting transfers between devices: 5 us -> 12.8 us
  Pallas kernels: 2.94 us -> 2.2 us
    ppermute x0 -> x10, starting transfers between devices: none -> 12.8 us  [the longest x7 8.32 us: swap_plane(): return lax.ppermute(array, ('occi', 'occj'), moves)]
    all_to_all x1 -> x0, blocking collectives: 11.7 us -> none  [shards(): lax.all_to_all(kept, ('occj', 'occi'), split_axis=0, concat_axis=0, tiled...]
    ppermute x0 -> x10, waiting for transfers between devices: none -> 9.56 us  [the longest x3 5.89 us: swap_virt(): lax.ppermute(array, 'virt', [(d, d ^ step) for d in range(lax.axis_size('...]
    all_to_all x1 -> x0, waiting for transfers between devices: 9.25 us -> none  [shards(): lax.all_to_all(half, 'virt', split_axis=0, concat_axis=0, tiled=True)]
    all_to_all x1 -> x0, starting transfers between devices: 5 us -> none  [shards(): lax.all_to_all(half, 'virt', split_axis=0, concat_axis=0, tiled=True)]
    pallas_call x2, Pallas kernels: 2.94 us -> 2.2 us  [the longest x1 1.47 us: shards(): pl.pallas_call(functools.partial(ladder_kernel, steps, virt), out_shape=[...]
    unnamed x7 -> x8, local copies, waits for them, and re-layouts: 1.65 us -> 1.69 us
  transfers between devices with their start and end apart: 1 -> 10, of which waited for: 1 -> 6; matrix products, arithmetic and copies ran while one was open for 0% -> 0% of each run, Pallas kernels for 0% -> 0%
where the time goes in v2:
time: 27.2 us; the launch traced here: 27 us
  starting transfers between devices  12.8 us (47%)
  waiting for transfers between devices  9.56 us (35%)
  Pallas kernels  2.2 us (8%)
  local copies, waits for them, and re-layouts  1.69 us (6%)
  other arithmetic  0.75 us (3%)
    ppermute x7, starting transfers between devices, swap_plane(): return lax.ppermute(array, ('occi', 'occj'), moves)  8.32 us
    ppermute x3, waiting for transfers between devices, swap_virt(): lax.ppermute(array, 'virt', [(d, d ^ step) for d in range(lax.axis_size('...  5.89 us
    ppermute x3, starting transfers between devices, swap_virt(): lax.ppermute(array, 'virt', [(d, d ^ step) for d in range(lax.axis_size('...  4.45 us
    ppermute x7, waiting for transfers between devices, swap_plane(): return lax.ppermute(array, ('occi', 'occj'), moves)  3.66 us
    unnamed x8, local copies, waits for them, and re-layouts  1.69 us
    pallas_call x1, Pallas kernels, shards(): pl.pallas_call(functools.partial(ladder_kernel, steps, virt), out_shape=[...  1.47 us
    pallas_call x1, Pallas kernels, shards(): pl.pallas_call(mask_kernel, out_shape=[jax.ShapeDtypeStruct(block_shape,...  0.73 us
    convert_element_type x1, other arithmetic, shards(): (pair_mask.astype(jnp.float32)[:, :, None, None] * summed).astype(jnp.bfl...  0.71 us
  transfers between devices with their start and end apart: 10, of which 6 were waited for; matrix products, arithmetic and copies ran while one was open for 0% of the time, Pallas kernels for 0%

profile of v2, /device:TPU:0, one launch (start us, length us, event | category | flops | bytes accessed | tf_op | source)
XLA Modules:
  0.0 27.0 jit_solution(2057051515755815306)
XLA Ops:
  0.0 1.0 %copy-done.1 = bf16[2,4,128,128]{3,2,1,0:T(8,128)(2,1)S(1)} copy-done((bf16[2,4,128,128]{3,2,1,0:T(8,128)(2,1)S(1)}, bf16[2,4,128,128]{3,2,1,0:T(8,128)(2,1)}, u32[]{:S(2)}) %copy-start.1) | copy-done | bytes 262168
  1.0 0.7 %copy-done.2 = s32[2,4,2,2]{1,3,2,0:T(2,128)S(1)} copy-done((s32[2,4,2,2]{1,3,2,0:T(2,128)S(1)}, s32[2,4,2,2]{1,3,2,0:T(2,128)}, u32[]{:S(2)}) %copy-start.2) | copy-done | bytes 152
  1.7 0.7 %shard_map.46 = (bf16[128,128]{1,0:T(8,128)(2,1)S(1)}, bf16[128,128]{1,0:T(8,128)(2,1)S(1)}, bf16[128,128]{1,0:T(8,128)(2,1)S(1)}, bf16[128,128]{1,0:T(8,128)(2,...) custom-call(s32[2,2,2,4]{3,2,1,0:T(2,128)S(1)} %bitcast.2, ...), custom_call_target="tpu_custom_call" | custom-call | tf_op jit(solution)/shard_map/pallas_call | solution.py:126
  2.4 3.0 %collective-permute-start = (bf16[128,128]{1,0:T(8,128)(2,1)S(1)}, bf16[128,128]{1,0:T(8,128)(2,1)S(1)}, u32[]{:S(2)}, u32[]{:S(2)}) collective-permute-start(bf16[128,128]{1,0:T(8,128)(2,1)S(1)} %get-tuple-element.18.refs_2_), channel_id=1, source_target_pairs={{0,8},{4,12},{8,0},{12,4},{16,24},{20,28},{24,16},{28,20},{1,9},{5... | collective-permute-start | bytes 98312 | tf_op jit(solution)/shard_map/ppermute | solution.py:114
  5.4 1.5 %collective-permute-start.1 = (bf16[128,128]{1,0:T(8,128)(2,1)S(1)}, bf16[128,128]{1,0:T(8,128)(2,1)S(1)}, u32[]{:S(2)}, u32[]{:S(2)}) collective-permute-start(bf16[128,128]{1,0:T(8,128)(2,1)S(1)} %get-tuple-element.19.refs_3_), channel_id=1, source_target_pairs={{0,16},{4,20},{8,24},{12,28},{16,0},{20,4},{24,8},{28,12},{1,17},{... | collective-permute-start | bytes 98312 | tf_op jit(solution)/shard_map/ppermute | solution.py:114
  6.9 0.0 collective-permute-start.2
  7.0 0.0 collective-permute-start.3
  7.0 2.1 %collective-permute-start.4 = (bf16[128,128]{1,0:T(8,128)(2,1)S(1)}, bf16[128,128]{1,0:T(8,128)(2,1)S(1)}, u32[]{:S(2)}, u32[]{:S(2)}) collective-permute-start(bf16[128,128]{1,0:T(8,128)(2,1)S(1)} %get-tuple-element.22.refs_6_), channel_id=1, source_target_pairs={{0,12},{4,8},{8,4},{12,0},{16,28},{20,24},{24,20},{28,16},{1,13},{... | collective-permute-start | bytes 98312 | tf_op jit(solution)/shard_map/ppermute | solution.py:114
  9.0 0.0 collective-permute-done.refs_9_
  9.0 1.1 %collective-permute-start.5 = (bf16[128,128]{1,0:T(8,128)(2,1)S(1)}, bf16[128,128]{1,0:T(8,128)(2,1)S(1)}, u32[]{:S(2)}, u32[]{:S(2)}) collective-permute-start(bf16[128,128]{1,0:T(8,128)(2,1)S(1)} %get-tuple-element.23.refs_7_), channel_id=1, source_target_pairs={{0,20},{4,16},{8,28},{12,24},{16,4},{20,0},{24,12},{28,8},{1,21},{... | collective-permute-start | bytes 98312 | tf_op jit(solution)/shard_map/ppermute | solution.py:114
  10.2 0.0 collective-permute-done.1.refs_10_
  10.2 0.6 %collective-permute-start.6 = (bf16[128,128]{1,0:T(8,128)(2,1)S(1)}, bf16[128,128]{1,0:T(8,128)(2,1)S(1)}, u32[]{:S(2)}, u32[]{:S(2)}) collective-permute-start(bf16[128,128]{1,0:T(8,128)(2,1)S(1)} %get-tuple-element.24.refs_8_), channel_id=1, source_target_pairs={{0,28},{4,24},{8,20},{12,16},{16,12},{20,8},{24,4},{28,0},{1,29},{... | collective-permute-start | bytes 98312 | tf_op jit(solution)/shard_map/ppermute | solution.py:114
  10.7 1.4 %collective-permute-done.2.refs_11_ = bf16[128,128]{1,0:T(8,128)(2,1)S(1)} collective-permute-done((bf16[128,128]{1,0:T(8,128)(2,1)S(1)}, bf16[128,128]{1,0:T(8,128)(2,1)S(1)}, u32[]{:S(2)}, u32[]{:S(2)}) %collective-permute-start.2) | collective-permute-done | bytes 32800 | tf_op jit(solution)/shard_map/ppermute | solution.py:114
  12.2 0.0 collective-permute-done.3.refs_12_
  12.2 0.4 %collective-permute-done.5.refs_14_ = bf16[128,128]{1,0:T(8,128)(2,1)S(1)} collective-permute-done((bf16[128,128]{1,0:T(8,128)(2,1)S(1)}, bf16[128,128]{1,0:T(8,128)(2,1)S(1)}, u32[]{:S(2)}, u32[]{:S(2)}) %collective-permute-start.5) | collective-permute-done | bytes 32800 | tf_op jit(solution)/shard_map/ppermute | solution.py:114
  12.6 1.8 %collective-permute-done.6.refs_15_ = bf16[128,128]{1,0:T(8,128)(2,1)S(1)} collective-permute-done((bf16[128,128]{1,0:T(8,128)(2,1)S(1)}, bf16[128,128]{1,0:T(8,128)(2,1)S(1)}, u32[]{:S(2)}, u32[]{:S(2)}) %collective-permute-start.6) | collective-permute-done | bytes 32800 | tf_op jit(solution)/shard_map/ppermute | solution.py:114
  14.4 1.5 %shard_map.47 = (bf16[8,32,128]{2,1,0:T(8,128)(2,1)S(1)}, bf16[8,32,128]{2,1,0:T(8,128)(2,1)S(1)}, bf16[8,32,128]{2,1,0:T(8,128)(2,1)S(1)}, bf16[8,32,128]{2,1,0:T(8,128)(2,1)S(1)}) custom-call(bf16[8,128,128]{2,1,0:T(8,128)(2,1)S(1)} %copy-done, bf16[128,128]{1,0:T(8,128)(2,1)S(1)} %get-tuple-element.17.refs_1_, ...), custom_call_target="tpu_custom_call" | custom-call | tf_op jit(solution)/shard_map/pallas_call | solution.py:137
  15.9 1.6 %collective-permute-start.7 = (bf16[8,32,128]{2,1,0:T(8,128)(2,1)S(1)}, bf16[8,32,128]{2,1,0:T(8,128)(2,1)S(1)}, u32[]{:S(2)}, u32[]{:S(2)}) collective-permute-start(bf16[8,32,128]{2,1,0:T(8,128)(2,1)S(1)} %get-tuple-element.26), channel_id=1, source_target_pairs={{0,1},{1,0},{2,3},{3,2},{4,5},{5,4},{6,7},{7,6},{8,9},{9,8},{10,11... | collective-permute-start | bytes 196616 | tf_op jit(solution)/shard_map/ppermute | solution.py:107
  17.5 2.6 %collective-permute-start.8 = (bf16[8,32,128]{2,1,0:T(8,128)(2,1)S(1)}, bf16[8,32,128]{2,1,0:T(8,128)(2,1)S(1)}, u32[]{:S(2)}, u32[]{:S(2)}) collective-permute-start(bf16[8,32,128]{2,1,0:T(8,128)(2,1)S(1)} %get-tuple-element.27), channel_id=1, source_target_pairs={{0,2},{1,3},{2,0},{3,1},{4,6},{5,7},{6,4},{7,5},{8,10},{9,11},{10,... | collective-permute-start | bytes 196616 | tf_op jit(solution)/shard_map/ppermute | solution.py:107
  20.1 0.2 collective-permute-start.9
  20.3 0.1 collective-permute-done.7
  20.5 4.0 %collective-permute-done.8 = bf16[8,32,128]{2,1,0:T(8,128)(2,1)S(1)} collective-permute-done((bf16[8,32,128]{2,1,0:T(8,128)(2,1)S(1)}, bf16[8,32,128]{2,1,0:T(8,128)(2,1)S(1)}, u32[]{:S(2)}, u32[]{:S(2)}) %collective-permute-start.8) | collective-permute-done | bytes 65568 | tf_op jit(solution)/shard_map/ppermute | solution.py:107
  24.5 1.8 %collective-permute-done.9 = bf16[8,32,128]{2,1,0:T(8,128)(2,1)S(1)} collective-permute-done((bf16[8,32,128]{2,1,0:T(8,128)(2,1)S(1)}, bf16[8,32,128]{2,1,0:T(8,128)(2,1)S(1)}, u32[]{:S(2)}, u32[]{:S(2)}) %collective-permute-start.9) | collective-permute-done | bytes 65568 | tf_op jit(solution)/shard_map/ppermute | solution.py:107
  26.3 0.7 %multiply_convert_fusion = bf16[2,4,32,128]{3,2,1,0:T(8,128)(2,1)} fusion(f32[2,4,32,128]{3,2,1,0:T(8,128)S(1)} %bitcast.3, f32[2,4]{1,0:T(2,128)S(1)} %convert_element_type.18), kind=kLoop, calls=%fused_computation | loop fusion | flops 65536 | bytes 196640 | tf_op jit(solution)/shard_map/convert_element_type | solution.py:148
  (9 shorter events, 0.0 us)
Async XLA Ops:
  0.0 14.4 %copy-start = (bf16[8,128,128]{2,1,0:T(8,128)(2,1)S(1)}, bf16[8,128,128]{2,1,0:T(8,128)(2,1)}, u32[]{:S(2)}) copy-start(bf16[8,128,128]{2,1,0:T(8,128)(2,1)} %refs_0_.1) | copy-start | bytes 786436
  0.0 1.0 %copy-start.1 = (bf16[2,4,128,128]{3,2,1,0:T(8,128)(2,1)S(1)}, bf16[2,4,128,128]{3,2,1,0:T(8,128)(2,1)}, u32[]{:S(2)}) copy-start(bf16[2,4,128,128]{3,2,1,0:T(8,128)(2,1)} %amp_ref.1) | copy-start | bytes 786436
  1.0 0.7 %copy-start.2 = (s32[2,4,2,2]{1,3,2,0:T(2,128)S(1)}, s32[2,4,2,2]{1,3,2,0:T(2,128)}, u32[]{:S(2)}) copy-start(s32[2,4,2,2]{1,3,2,0:T(2,128)} %param.6) | copy-start | bytes 388
  2.4 6.6 %collective-permute-start = (bf16[128,128]{1,0:T(8,128)(2,1)S(1)}, bf16[128,128]{1,0:T(8,128)(2,1)S(1)}, u32[]{:S(2)}, u32[]{:S(2)}) collective-permute-start(bf16[128,128]{1,0:T(8,128)(2,1)S(1)} %get-tuple-element.18.refs_2_), channel_id=1, source_target_pairs={{0,8},{4,12},{8,0},{12,4},{16,24},{20,28},{24,16},{28,20},{1,9},{5... | collective-permute-start | bytes 98312 | tf_op jit(solution)/shard_map/ppermute | solution.py:114
  5.4 4.7 %collective-permute-start.1 = (bf16[128,128]{1,0:T(8,128)(2,1)S(1)}, bf16[128,128]{1,0:T(8,128)(2,1)S(1)}, u32[]{:S(2)}, u32[]{:S(2)}) collective-permute-start(bf16[128,128]{1,0:T(8,128)(2,1)S(1)} %get-tuple-element.19.refs_3_), channel_id=1, source_target_pairs={{0,16},{4,20},{8,24},{12,28},{16,0},{20,4},{24,8},{28,12},{1,17},{... | collective-permute-start | bytes 98312 | tf_op jit(solution)/shard_map/ppermute | solution.py:114
  6.9 5.2 %collective-permute-start.2 = (bf16[128,128]{1,0:T(8,128)(2,1)S(1)}, bf16[128,128]{1,0:T(8,128)(2,1)S(1)}, u32[]{:S(2)}, u32[]{:S(2)}) collective-permute-start(bf16[128,128]{1,0:T(8,128)(2,1)S(1)} %get-tuple-element.20.refs_4_), channel_id=1, source_target_pairs={{0,24},{4,28},{8,16},{12,20},{16,8},{20,12},{24,0},{28,4},{1,25},{... | collective-permute-start | bytes 98312 | tf_op jit(solution)/shard_map/ppermute | solution.py:114
  7.0 5.2 %collective-permute-start.3 = (bf16[128,128]{1,0:T(8,128)(2,1)S(1)}, bf16[128,128]{1,0:T(8,128)(2,1)S(1)}, u32[]{:S(2)}, u32[]{:S(2)}) collective-permute-start(bf16[128,128]{1,0:T(8,128)(2,1)S(1)} %get-tuple-element.21.refs_5_), channel_id=1, source_target_pairs={{0,4},{4,0},{8,12},{12,8},{16,20},{20,16},{24,28},{28,24},{1,5},{5... | collective-permute-start | bytes 98312 | tf_op jit(solution)/shard_map/ppermute | solution.py:114
  7.0 5.2 %collective-permute-start.4 = (bf16[128,128]{1,0:T(8,128)(2,1)S(1)}, bf16[128,128]{1,0:T(8,128)(2,1)S(1)}, u32[]{:S(2)}, u32[]{:S(2)}) collective-permute-start(bf16[128,128]{1,0:T(8,128)(2,1)S(1)} %get-tuple-element.22.refs_6_), channel_id=1, source_target_pairs={{0,12},{4,8},{8,4},{12,0},{16,28},{20,24},{24,20},{28,16},{1,13},{... | collective-permute-start | bytes 98312 | tf_op jit(solution)/shard_map/ppermute | solution.py:114
  9.0 3.6 %collective-permute-start.5 = (bf16[128,128]{1,0:T(8,128)(2,1)S(1)}, bf16[128,128]{1,0:T(8,128)(2,1)S(1)}, u32[]{:S(2)}, u32[]{:S(2)}) collective-permute-start(bf16[128,128]{1,0:T(8,128)(2,1)S(1)} %get-tuple-element.23.refs_7_), channel_id=1, source_target_pairs={{0,20},{4,16},{8,28},{12,24},{16,4},{20,0},{24,12},{28,8},{1,21},{... | collective-permute-start | bytes 98312 | tf_op jit(solution)/shard_map/ppermute | solution.py:114
  10.2 4.2 %collective-permute-start.6 = (bf16[128,128]{1,0:T(8,128)(2,1)S(1)}, bf16[128,128]{1,0:T(8,128)(2,1)S(1)}, u32[]{:S(2)}, u32[]{:S(2)}) collective-permute-start(bf16[128,128]{1,0:T(8,128)(2,1)S(1)} %get-tuple-element.24.refs_8_), channel_id=1, source_target_pairs={{0,28},{4,24},{8,20},{12,16},{16,12},{20,8},{24,4},{28,0},{1,29},{... | collective-permute-start | bytes 98312 | tf_op jit(solution)/shard_map/ppermute | solution.py:114
  15.9 4.6 %collective-permute-start.7 = (bf16[8,32,128]{2,1,0:T(8,128)(2,1)S(1)}, bf16[8,32,128]{2,1,0:T(8,128)(2,1)S(1)}, u32[]{:S(2)}, u32[]{:S(2)}) collective-permute-start(bf16[8,32,128]{2,1,0:T(8,128)(2,1)S(1)} %get-tuple-element.26), channel_id=1, source_target_pairs={{0,1},{1,0},{2,3},{3,2},{4,5},{5,4},{6,7},{7,6},{8,9},{9,8},{10,11... | collective-permute-start | bytes 196616 | tf_op jit(solution)/shard_map/ppermute | solution.py:107
  17.5 2.8 %copy-start.3 = (s32[2,4]{1,0:T(2,128)S(1)}, s32[2,4]{1,0:T(2,128)}, u32[]{:S(2)}) copy-start(s32[2,4]{1,0:T(2,128)} %param.7) | copy-start | bytes 100
  17.5 6.9 %collective-permute-start.8 = (bf16[8,32,128]{2,1,0:T(8,128)(2,1)S(1)}, bf16[8,32,128]{2,1,0:T(8,128)(2,1)S(1)}, u32[]{:S(2)}, u32[]{:S(2)}) collective-permute-start(bf16[8,32,128]{2,1,0:T(8,128)(2,1)S(1)} %get-tuple-element.27), channel_id=1, source_target_pairs={{0,2},{1,3},{2,0},{3,1},{4,6},{5,7},{6,4},{7,5},{8,10},{9,11},{10,... | collective-permute-start | bytes 196616 | tf_op jit(solution)/shard_map/ppermute | solution.py:107
  20.1 6.1 %collective-permute-start.9 = (bf16[8,32,128]{2,1,0:T(8,128)(2,1)S(1)}, bf16[8,32,128]{2,1,0:T(8,128)(2,1)S(1)}, u32[]{:S(2)}, u32[]{:S(2)}) collective-permute-start(bf16[8,32,128]{2,1,0:T(8,128)(2,1)S(1)} %get-tuple-element.28), channel_id=1, source_target_pairs={{0,3},{1,2},{2,1},{3,0},{4,7},{5,6},{6,5},{7,4},{8,11},{9,10},{10,... | collective-permute-start | bytes 196616 | tf_op jit(solution)/shard_map/ppermute | solution.py:107

commit v3 on v0

v3 whole, which is shorter than its diff:
```python
import functools

import jax
import jax.numpy as jnp
from jax import lax
from jax.experimental import pallas as pl
from jax.experimental.pallas import tpu as pltpu
from jax.sharding import PartitionSpec as P

TILE = 64
SLAB_TILES = 2
CHIPS = 4
BF16 = jnp.bfloat16
F32 = jnp.float32


def swap_virt(array, step):
    return lax.ppermute(array, "virt", [(d, d ^ step) for d in range(lax.axis_size("virt"))])


def swap_core(array):
    return lax.ppermute(array, "occj", [(0, 1), (1, 0)])


def swap_chip(array, step):
    return lax.ppermute(array, "occi", [(d, d ^ step) for d in range(lax.axis_size("occi"))])


def slot(kind, step):
    first = lax.axis_index("occj") if kind == 0 else 1 - lax.axis_index("occj")
    return first, lax.axis_index("occi") ^ step


def masked(mask_ref, amp_ref, first, second):
    slab = amp_ref.shape[-1]
    row = lax.broadcasted_iota(jnp.int32, (slab, slab), 0) // TILE
    col = lax.broadcasted_iota(jnp.int32, (slab, slab), 1) // TILE
    keep = jnp.zeros((slab, slab), F32)
    for r in range(SLAB_TILES):
        for c in range(SLAB_TILES):
            keep = jnp.where((row == r) & (col == c), mask_ref[first, r, c, second].astype(F32), keep)
    return (amp_ref[first, second].astype(F32) * keep).astype(BF16)


def mask_split_kernel(mask_ref, pair_ref, amp_ref, same_ref, cross_ref, gate_ref):
    for kind, kept_ref in ((1, cross_ref), (0, same_ref)):
        for step in range(CHIPS):
            first, second = slot(kind, step)
            kept_ref[step] = masked(mask_ref, amp_ref, first, second)
            gate_ref[kind * CHIPS + step] = jnp.full(gate_ref.shape[1:], pair_ref[first, second].astype(F32))


def mask_whole_kernel(mask_ref, pair_ref, amp_ref, kept_ref, gate_ref):
    seconds = amp_ref.shape[1]

    def one(block, carry):
        first, second = block // seconds, block % seconds
        kept_ref[block] = masked(mask_ref, amp_ref, first, second)
        gate_ref[block] = jnp.full(gate_ref.shape[1:], pair_ref[first, second].astype(F32))
        return carry

    lax.fori_loop(0, kept_ref.shape[0], one, 0)


def pack_kernel(same_ref, other_ref, *send_refs):
    for step, send_ref in enumerate(send_refs, 1):
        send_ref[0] = same_ref[step]
        send_ref[1] = other_ref[step]


def turn(vec_refs, turned_ref):
    slab = vec_refs[0].shape[-1]
    at = 0
    for vec_ref in vec_refs:
        for q in range(vec_ref.shape[0]):
            turned_ref[at : at + slab] = vec_ref[q].astype(F32).T.astype(BF16)
            at += slab


def left_rows(vec_refs, rows, chunks):
    me = lax.axis_index("virt")
    return jnp.concatenate(
        [
            vec_ref[q, pl.ds(pl.multiple_of((me ^ (2 * chunk)) * rows, rows), rows), :]
            for vec_ref in vec_refs
            for q in range(vec_ref.shape[0])
            for chunk in range(chunks)
        ],
        axis=0,
    )


def products(flat, turned_ref, inner_ref, sources, outs):
    slab = turned_ref.shape[1]
    vectors = turned_ref.shape[0] // slab
    height = flat.shape[0] // vectors
    rows = height // len(outs[0])
    for base in range(0, len(sources), 2):
        both = [
            ((kept.astype(F32) + partner.astype(F32).T) * gate[:1]).astype(BF16)
            for kept, partner, gate in sources[base : base + 2]
        ]
        inner = jnp.dot(flat, jnp.concatenate(both, axis=1), preferred_element_type=F32).astype(BF16)
        for n in range(len(both)):
            for q in range(vectors):
                inner_ref[(base + n) * height : (base + n + 1) * height, q * slab : (q + 1) * slab] = inner[
                    q * height : (q + 1) * height, n * slab : (n + 1) * slab
                ]
    half = jnp.dot(inner_ref[...], turned_ref[...], preferred_element_type=F32)
    for n, targets in enumerate(outs):
        for chunk, (ref, index) in enumerate(targets):
            start = n * height + chunk * rows
            ref[index] = half[start : start + rows].astype(ref.dtype)


def early_kernel(chunks, own_ref, near_ref, gate_ref, same_ref, cross_ref, other_ref, *refs):
    got_refs, refs = refs[: CHIPS - 2], refs[CHIPS - 2 :]
    part_refs, turned_ref, inner_ref = refs[:chunks], refs[chunks], refs[chunks + 1]
    turn((own_ref, near_ref), turned_ref)
    flat = left_rows((own_ref, near_ref), part_refs[0].shape[1], chunks)
    sources = [
        (same_ref[0], same_ref[0], gate_ref[0]),
        (cross_ref[0], other_ref[0], gate_ref[CHIPS]),
    ]
    for step, got_ref in enumerate(got_refs, 1):
        sources.append((same_ref[step], got_ref[0], gate_ref[step]))
        sources.append((cross_ref[step], got_ref[1], gate_ref[CHIPS + step]))
    outs = [[(ref, n) for ref in part_refs] for n in range(len(sources))]
    products(flat, turned_ref, inner_ref, sources, outs)


def late_kernel(chunks, own_ref, near_ref, gate_ref, same_ref, cross_ref, turned_ref, got_ref, *refs):
    part_refs, inner_ref = refs[:chunks], refs[chunks]
    flat = left_rows((own_ref, near_ref), part_refs[0].shape[1], chunks)
    step = CHIPS - 1
    sources = [
        (same_ref[step], got_ref[0], gate_ref[step]),
        (cross_ref[step], got_ref[1], gate_ref[CHIPS + step]),
    ]
    outs = [[(ref, n) for ref in part_refs] for n in range(len(sources))]
    products(flat, turned_ref, inner_ref, sources, outs)


def whole_kernel(chunks, own_ref, near_ref, gate_ref, kept_ref, partner_ref, *refs):
    part_refs, turned_ref, inner_ref = refs[:chunks], refs[chunks], refs[chunks + 1]
    turn((own_ref, near_ref), turned_ref)

    def two(g, carry):
        flat = left_rows((own_ref, near_ref), part_refs[0].shape[1], chunks)
        pairs = [2 * g, 2 * g + 1]
        sources = [(kept_ref[k], partner_ref[k], gate_ref[k]) for k in pairs]
        products(flat, turned_ref, inner_ref, sources, [[(ref, k) for ref in part_refs] for k in pairs])
        return carry

    lax.fori_loop(0, kept_ref.shape[0] // 2, two, 0)


def finish_kernel(counts, chunks, *refs):
    out_ref = refs[-1]
    at = 0
    for group, count in enumerate(counts):
        terms = refs[group * chunks : (group + 1) * chunks]
        for n in range(count):
            total = terms[0][n]
            for term in terms[1:]:
                total = total + term[n].astype(F32)
            first, second = slot((at + n) % 2, (at + n) // 2)
            out_ref[first, second] = total.astype(BF16)
        at += count


def vmem_specs(count):
    return [pl.BlockSpec(memory_space=pltpu.VMEM)] * count


def shaped(dtype, *shape):
    return jax.ShapeDtypeStruct(shape, dtype)


def kernel(body, outs, operands, scalars=0, scratch=()):
    return pl.pallas_call(
        body,
        out_shape=outs,
        in_specs=[pl.BlockSpec(memory_space=pltpu.SMEM)] * scalars + vmem_specs(len(operands) - scalars),
        out_specs=vmem_specs(len(outs)),
        scratch_shapes=list(scratch),
        compiler_params=pltpu.CompilerParams(vmem_limit_bytes=24 * 1024 * 1024),
    )(*operands)


def shards(amplitudes, vectors, tile_mask, pair_mask):
    firsts, seconds, slab, _ = amplitudes.shape
    pairs = firsts * seconds
    virt, chips, cores = lax.axis_size("virt"), lax.axis_size("occi"), lax.axis_size("occj")
    rows = slab // virt
    chunks = virt // 2
    depth = 2 * vectors.shape[0] * slab
    masks = (jnp.transpose(tile_mask, (0, 2, 3, 1)), pair_mask, amplitudes)
    gate = shaped(F32, pairs, 8, slab)

    def parts(count):
        return [shaped(F32 if chunk == 0 else BF16, count, rows, slab) for chunk in range(chunks)]

    def inner(count):
        return pltpu.VMEM((count * chunks * rows, depth), BF16)

    def sent(part):
        return [part[0]] + [swap_virt(part[chunk], 2 * chunk) for chunk in range(1, chunks)]

    near = swap_virt(vectors, 1)
    turned = shaped(BF16, depth, slab)
    if (firsts, seconds, chips, cores) == (2, CHIPS, CHIPS, 2):
        half_blocks = shaped(BF16, CHIPS, slab, slab)
        same, cross, gates = kernel(mask_split_kernel, [half_blocks, half_blocks, gate], masks, 2)
        other = swap_core(cross)
        packed = kernel(pack_kernel, [shaped(BF16, 2, slab, slab)] * (CHIPS - 1), (same, other))
        got = [swap_chip(block, step) for step, block in enumerate(packed, 1)]
        count = 2 * (CHIPS - 1)
        *early, turned = kernel(
            functools.partial(early_kernel, chunks),
            parts(count) + [turned],
            (vectors, near, gates, same, cross, other, *got[:-1]),
            scratch=[inner(count)],
        )
        early = sent(early)
        late = kernel(
            functools.partial(late_kernel, chunks),
            parts(2),
            (vectors, near, gates, same, cross, turned, got[-1]),
            scratch=[inner(2)],
        )
        late = sent(late)
        (out,) = kernel(
            functools.partial(finish_kernel, (count, 2), chunks),
            [shaped(BF16, firsts, seconds, rows, slab)],
            (*early, *late),
        )
        return out
    kept, gates = kernel(mask_whole_kernel, [shaped(BF16, pairs, slab, slab), gate], masks, 2)
    partner = lax.all_to_all(kept, ("occj", "occi"), split_axis=0, concat_axis=0, tiled=True)
    *part, _ = kernel(
        functools.partial(whole_kernel, chunks),
        parts(pairs) + [turned],
        (vectors, near, gates, kept, partner),
        scratch=[inner(2)],
    )
    part = sent(part)
    summed = part[0]
    for term in part[1:]:
        summed = summed + term.astype(F32)
    return summed.reshape(firsts, seconds, rows, slab).astype(BF16)


def solution(mesh):
    placed = (
        P("occi", "occj", None, None),
        P("virt", None, None),
        P("occi", "occj", None, None),
        P("occi", "occj"),
    )
    return jax.shard_map(
        shards,
        mesh=mesh,
        in_specs=placed,
        out_specs=P("occi", "occj", "virt", None),
        check_vma=False,
    )
```

time: 76.7 us -> 23.3 us (0.30)
  blocking collectives: 49.9 us -> 0 us
  matrix products: 10.3 us -> 0 us
  starting transfers between devices: 3.71 us -> 9.98 us
  local copies, waits for them, and re-layouts: 6.1 us -> 1.64 us
  Pallas kernels: 0 us -> 3.77 us
  waiting for transfers between devices: 4.69 us -> 7.65 us
    unnamed x1 -> x0, blocking collectives: 32.1 us -> none
    all_gather x1 -> x0, blocking collectives: 13.8 us -> none  [shards(): full_rows = lax.all_gather(half, 'virt', axis=2, tiled=True)]
    dot_general x8 -> x0, matrix products: 10.3 us -> none  [advance(): jnp.einsum('aipd,bd->aipb', contracted, vector, preferred_element_type=jn...]
    ppermute x0 -> x7, starting transfers between devices: none -> 9.98 us  [the longest x3 6.36 us: swap_virt(): lax.ppermute(array, 'virt', [(d, d ^ step) for d in range(lax.axis_size('...]
    ppermute x0 -> x7, waiting for transfers between devices: none -> 7.65 us  [the longest x3 4.04 us: swap_virt(): lax.ppermute(array, 'virt', [(d, d ^ step) for d in range(lax.axis_size('...]
    all_to_all x1 -> x0, waiting for transfers between devices: 4.69 us -> none  [shards(): lax.all_to_all(full_rows, 'occi', split_axis=1, concat_axis=1, tiled=True)]
    all_to_all x1 -> x0, blocking collectives: 3.94 us -> none  [shards(): lax.all_to_all(lax.all_to_all(full_rows, 'occi', split_axis=1, concat_axi...]
    pallas_call x0 -> x5, Pallas kernels: none -> 3.77 us  [kernel(): pl.pallas_call(body, out_shape=outs, in_specs=[pl.BlockSpec(memory_space=...]
  transfers between devices with their start and end apart: 1 -> 7, of which waited for: 1 -> 4; matrix products, arithmetic and copies ran while one was open for 0% -> 0% of each run, Pallas kernels for 0% -> 14%
where the time goes in v3:
time: 23.3 us; the launch traced here: 23.1 us
  starting transfers between devices  9.98 us (43%)
  waiting for transfers between devices  7.65 us (33%)
  Pallas kernels  3.77 us (16%)
  local copies, waits for them, and re-layouts  1.64 us (7%)
    ppermute x3, starting transfers between devices, swap_virt(): lax.ppermute(array, 'virt', [(d, d ^ step) for d in range(lax.axis_size('...  6.36 us
    ppermute x3, waiting for transfers between devices, swap_virt(): lax.ppermute(array, 'virt', [(d, d ^ step) for d in range(lax.axis_size('...  4.04 us
    pallas_call x5, Pallas kernels, kernel(): pl.pallas_call(body, out_shape=outs, in_specs=[pl.BlockSpec(memory_space=...  3.77 us
    ppermute x3, starting transfers between devices, swap_chip(): lax.ppermute(array, 'occi', [(d, d ^ step) for d in range(lax.axis_size('...  3.55 us
    ppermute x3, waiting for transfers between devices, swap_chip(): lax.ppermute(array, 'occi', [(d, d ^ step) for d in range(lax.axis_size('...  2.27 us
    unnamed x8, local copies, waits for them, and re-layouts  1.64 us
    ppermute x1, waiting for transfers between devices, swap_core(): return lax.ppermute(array, 'occj', [(0, 1), (1, 0)])  1.33 us
  transfers between devices with their start and end apart: 7, of which 4 were waited for; matrix products, arithmetic and copies ran while one was open for 0% of the time, Pallas kernels for 14%

profile of v3, /device:TPU:0, one launch (start us, length us, event | category | flops | bytes accessed | tf_op | source)
XLA Modules:
  0.0 23.1 jit_solution(11768332903242345812)
XLA Ops:
  0.0 0.0 copy-start.3
  0.0 3.0 %collective-permute-start = (bf16[8,128,128]{2,1,0:T(8,128)(2,1)}, bf16[8,128,128]{2,1,0:T(8,128)(2,1)S(1)}, u32[]{:S(2)}, u32[]{:S(2)}) collective-permute-start(bf16[8,128,128]{2,1,0:T(8,128)(2,1)} %own_ref.3), channel_id=1, source_target_pairs={{0,1},{1,0},{2,3},{3,2},{4,5},{5,4},{6,7},{7,6},{8,9},{9,8},{10,11... | collective-permute-start | bytes 786440 | tf_op jit(solution)/shard_map/ppermute | solution.py:18
  3.0 0.0 copy-done.3
  3.0 0.0 copy-start.1
  3.0 0.9 %copy-done.1 = bf16[2,4,128,128]{3,2,1,0:T(8,128)(2,1)S(1)} copy-done((bf16[2,4,128,128]{3,2,1,0:T(8,128)(2,1)S(1)}, bf16[2,4,128,128]{3,2,1,0:T(8,128)(2,1)}, u32[]{:S(2)}) %copy-start.1) | copy-done | bytes 262168
  4.0 0.7 %copy-done.2 = s32[2,4,2,2]{1,3,2,0:T(2,128)S(1)} copy-done((s32[2,4,2,2]{1,3,2,0:T(2,128)S(1)}, s32[2,4,2,2]{1,3,2,0:T(2,128)}, u32[]{:S(2)}) %copy-start.2) | copy-done | bytes 152
  4.7 0.7 %shard_map.46 = (bf16[4,128,128]{2,1,0:T(8,128)(2,1)S(1)}, bf16[4,128,128]{2,1,0:T(8,128)(2,1)S(1)}, f32[8,8,128]{2,1,0:T(8,128)S(1)}) custom-call(s32[2,2,2,4]{3,2,1,0:T(2,128)S(1)} %bitcast.1, s32[2,4]{1,0:T(2,128)S(1)} %copy-done.3, bf16[2,4,128,128]{3,2,1,0:T(8,128)(2,1)S(1)} %copy-done.1), custom_call_target="tpu_custom_call" | custom-call | tf_op jit(solution)/shard_map/pallas_call | solution.py:181
  5.4 0.1 collective-permute-start.1
  5.5 1.3 %collective-permute-done.1.other_ref = bf16[4,128,128]{2,1,0:T(8,128)(2,1)S(1)} collective-permute-done((bf16[4,128,128]{2,1,0:T(8,128)(2,1)S(1)}, bf16[4,128,128]{2,1,0:T(8,128)(2,1)S(1)}, u32[]{:S(2)}, u32[]{:S(2)}) %collective-permute-start.1) | collective-permute-done | bytes 131104 | tf_op jit(solution)/shard_map/ppermute | solution.py:22
  6.8 1.6 %collective-permute-start.2 = (bf16[2,128,128]{2,1,0:T(8,128)(2,1)S(1)}, bf16[2,128,128]{2,1,0:T(8,128)(2,1)S(1)}, u32[]{:S(2)}, u32[]{:S(2)}) collective-permute-start(bf16[2,128,128]{2,1,0:T(8,128)(2,1)S(1)} %get-tuple-element.19), channel_id=1, source_target_pairs={{0,8},{8,0},{16,24},{24,16},{1,9},{9,1},{17,25},{25,17},{2,10},{10... | collective-permute-start | bytes 196616 | tf_op jit(solution)/shard_map/ppermute | solution.py:26
  8.4 1.5 %collective-permute-start.3 = (bf16[2,128,128]{2,1,0:T(8,128)(2,1)S(1)}, bf16[2,128,128]{2,1,0:T(8,128)(2,1)S(1)}, u32[]{:S(2)}, u32[]{:S(2)}) collective-permute-start(bf16[2,128,128]{2,1,0:T(8,128)(2,1)S(1)} %get-tuple-element.20), channel_id=1, source_target_pairs={{0,16},{8,24},{16,0},{24,8},{1,17},{9,25},{17,1},{25,9},{2,18},{10... | collective-permute-start | bytes 196616 | tf_op jit(solution)/shard_map/ppermute | solution.py:26
  9.9 0.5 %collective-permute-start.5 = (bf16[2,128,128]{2,1,0:T(8,128)(2,1)S(1)}, bf16[2,128,128]{2,1,0:T(8,128)(2,1)S(1)}, u32[]{:S(2)}, u32[]{:S(2)}) collective-permute-start(bf16[2,128,128]{2,1,0:T(8,128)(2,1)S(1)} %get-tuple-element.24), channel_id=1, source_target_pairs={{0,24},{8,16},{16,8},{24,0},{1,25},{9,17},{17,9},{25,1},{2,26},{10... | collective-permute-start | bytes 196616 | tf_op jit(solution)/shard_map/ppermute | solution.py:26
  10.4 0.8 %collective-permute-done.2.refs_0_ = bf16[2,128,128]{2,1,0:T(8,128)(2,1)S(1)} collective-permute-done((bf16[2,128,128]{2,1,0:T(8,128)(2,1)S(1)}, bf16[2,128,128]{2,1,0:T(8,128)(2,1)S(1)}, u32[]{:S(2)}, u32[]{:S(2)}) %collective-permute-start.2) | collective-permute-done | bytes 65568 | tf_op jit(solution)/shard_map/ppermute | solution.py:26
  11.1 1.5 %collective-permute-done.3.refs_1_ = bf16[2,128,128]{2,1,0:T(8,128)(2,1)S(1)} collective-permute-done((bf16[2,128,128]{2,1,0:T(8,128)(2,1)S(1)}, bf16[2,128,128]{2,1,0:T(8,128)(2,1)S(1)}, u32[]{:S(2)}, u32[]{:S(2)}) %collective-permute-start.3) | collective-permute-done | bytes 65568 | tf_op jit(solution)/shard_map/ppermute | solution.py:26
  12.6 0.0 collective-permute-done.near_ref
  12.6 0.0 copy-done
  12.6 1.7 %shard_map.48 = (f32[6,32,128]{2,1,0:T(8,128)S(1)}, bf16[6,32,128]{2,1,0:T(8,128)(2,1)S(1)}, bf16[2048,128]{1,0:T(8,128)(2,1)S(1)}) custom-call(bf16[8,128,128]{2,1,0:T(8,128)(2,1)S(1)} %copy-done, bf16[8,128,128]{2,1,0:T(8,128)(2,1)S(1)} %collective-permute-done.near_ref, f32[8,8,128]{2,1,0:T(8,128)S(1)} %get-tuple-element.16.gate_ref, ...), custom_call_target="tpu_custom_call" | custom-call | tf_op jit(solution)/shard_map/pallas_call | solution.py:181
  14.4 2.7 %collective-permute-start.4 = (bf16[6,32,128]{2,1,0:T(8,128)(2,1)S(1)}, bf16[6,32,128]{2,1,0:T(8,128)(2,1)S(1)}, u32[]{:S(2)}, u32[]{:S(2)}) collective-permute-start(bf16[6,32,128]{2,1,0:T(8,128)(2,1)S(1)} %get-tuple-element.22), channel_id=1, source_target_pairs={{0,2},{1,3},{2,0},{3,1},{4,6},{5,7},{6,4},{7,5},{8,10},{9,11},{10,... | collective-permute-start | bytes 147464 | tf_op jit(solution)/shard_map/ppermute | solution.py:18
  17.0 0.0 collective-permute-done.5.got_ref
  17.0 0.7 %shard_map.49 = (f32[2,32,128]{2,1,0:T(8,128)S(1)}, bf16[2,32,128]{2,1,0:T(8,128)(2,1)S(1)}) custom-call(bf16[8,128,128]{2,1,0:T(8,128)(2,1)S(1)} %copy-done, bf16[8,128,128]{2,1,0:T(8,128)(2,1)S(1)} %collective-permute-done.near_ref, f32[8,8,128]{2,1,0:T(8,128)S(1)} %get-tuple-element.16.gate_ref, bf16[4,128,128]{2,1,0:T(8,128)(2,1)S(1)} %get-tuple-element.17.same_ref, ...), custom_call_target="tpu_custom_call" | custom-call | tf_op jit(solution)/shard_map/pallas_call | solution.py:181
  17.7 0.7 %collective-permute-start.6 = (bf16[2,32,128]{2,1,0:T(8,128)(2,1)S(1)}, bf16[2,32,128]{2,1,0:T(8,128)(2,1)S(1)}, u32[]{:S(2)}, u32[]{:S(2)}) collective-permute-start(bf16[2,32,128]{2,1,0:T(8,128)(2,1)S(1)} %get-tuple-element.26), channel_id=1, source_target_pairs={{0,2},{1,3},{2,0},{3,1},{4,6},{5,7},{6,4},{7,5},{8,10},{9,11},{10,... | collective-permute-start | bytes 49160 | tf_op jit(solution)/shard_map/ppermute | solution.py:18
  18.4 4.0 %collective-permute-done.6.refs_3_ = bf16[2,32,128]{2,1,0:T(8,128)(2,1)S(1)} collective-permute-done((bf16[2,32,128]{2,1,0:T(8,128)(2,1)S(1)}, bf16[2,32,128]{2,1,0:T(8,128)(2,1)S(1)}, u32[]{:S(2)}, u32[]{:S(2)}) %collective-permute-start.6) | collective-permute-done | bytes 16416 | tf_op jit(solution)/shard_map/ppermute | solution.py:18
  22.4 0.0 collective-permute-done.4.refs_1_
  22.4 0.6 %shard_map.50 = bf16[2,4,32,128]{3,2,1,0:T(8,128)(2,1)} custom-call(f32[6,32,128]{2,1,0:T(8,128)S(1)} %get-tuple-element.21.refs_0_, bf16[6,32,128]{2,1,0:T(8,128)(2,1)S(1)} %collective-permute-done.4.refs_1_, f32[2,32,128]{2,1,0:T(8,128)S(1)} %get-tuple-element.25.refs_2_, bf16[2,32,128]{2,1,0:T(8,128)(2,1)S(1)} %collective-permute-done.6.refs_3_), custom_call_target="tpu_custom_call" | custom-call | tf_op jit(solution)/shard_map/pallas_call | solution.py:181
  (3 shorter events, 0.0 us)
Async XLA Ops:
  0.0 3.0 %copy-start.3 = (s32[2,4]{1,0:T(2,128)S(1)}, s32[2,4]{1,0:T(2,128)}, u32[]{:S(2)}) copy-start(s32[2,4]{1,0:T(2,128)} %pair_ref.1) | copy-start | bytes 100
  0.0 12.6 %collective-permute-start = (bf16[8,128,128]{2,1,0:T(8,128)(2,1)}, bf16[8,128,128]{2,1,0:T(8,128)(2,1)S(1)}, u32[]{:S(2)}, u32[]{:S(2)}) collective-permute-start(bf16[8,128,128]{2,1,0:T(8,128)(2,1)} %own_ref.3), channel_id=1, source_target_pairs={{0,1},{1,0},{2,3},{3,2},{4,5},{5,4},{6,7},{7,6},{8,9},{9,8},{10,11... | collective-permute-start | bytes 786440 | tf_op jit(solution)/shard_map/ppermute | solution.py:18
  3.0 1.0 %copy-start.1 = (bf16[2,4,128,128]{3,2,1,0:T(8,128)(2,1)S(1)}, bf16[2,4,128,128]{3,2,1,0:T(8,128)(2,1)}, u32[]{:S(2)}) copy-start(bf16[2,4,128,128]{3,2,1,0:T(8,128)(2,1)} %amp_ref.1) | copy-start | bytes 786436
  4.0 0.7 %copy-start.2 = (s32[2,4,2,2]{1,3,2,0:T(2,128)S(1)}, s32[2,4,2,2]{1,3,2,0:T(2,128)}, u32[]{:S(2)}) copy-start(s32[2,4,2,2]{1,3,2,0:T(2,128)} %param.6) | copy-start | bytes 388
  4.7 8.0 %copy-start = (bf16[8,128,128]{2,1,0:T(8,128)(2,1)S(1)}, bf16[8,128,128]{2,1,0:T(8,128)(2,1)}, u32[]{:S(2)}) copy-start(bf16[8,128,128]{2,1,0:T(8,128)(2,1)} %own_ref.3) | copy-start | bytes 786436
  5.4 1.4 %collective-permute-start.1 = (bf16[4,128,128]{2,1,0:T(8,128)(2,1)S(1)}, bf16[4,128,128]{2,1,0:T(8,128)(2,1)S(1)}, u32[]{:S(2)}, u32[]{:S(2)}) collective-permute-start(bf16[4,128,128]{2,1,0:T(8,128)(2,1)S(1)} %get-tuple-element.18.cross_ref), channel_id=1, source_target_pairs={{0,4},{4,0},{1,5},{5,1},{2,6},{6,2},{3,7},{7,3},{8,12},{12,8},{9,1... | collective-permute-start | bytes 393224 | tf_op jit(solution)/shard_map/ppermute | solution.py:22
  6.8 4.3 %collective-permute-start.2 = (bf16[2,128,128]{2,1,0:T(8,128)(2,1)S(1)}, bf16[2,128,128]{2,1,0:T(8,128)(2,1)S(1)}, u32[]{:S(2)}, u32[]{:S(2)}) collective-permute-start(bf16[2,128,128]{2,1,0:T(8,128)(2,1)S(1)} %get-tuple-element.19), channel_id=1, source_target_pairs={{0,8},{8,0},{16,24},{24,16},{1,9},{9,1},{17,25},{25,17},{2,10},{10... | collective-permute-start | bytes 196616 | tf_op jit(solution)/shard_map/ppermute | solution.py:26
  8.4 4.3 %collective-permute-start.3 = (bf16[2,128,128]{2,1,0:T(8,128)(2,1)S(1)}, bf16[2,128,128]{2,1,0:T(8,128)(2,1)S(1)}, u32[]{:S(2)}, u32[]{:S(2)}) collective-permute-start(bf16[2,128,128]{2,1,0:T(8,128)(2,1)S(1)} %get-tuple-element.20), channel_id=1, source_target_pairs={{0,16},{8,24},{16,0},{24,8},{1,17},{9,25},{17,1},{25,9},{2,18},{10... | collective-permute-start | bytes 196616 | tf_op jit(solution)/shard_map/ppermute | solution.py:26
  9.9 7.1 %collective-permute-start.5 = (bf16[2,128,128]{2,1,0:T(8,128)(2,1)S(1)}, bf16[2,128,128]{2,1,0:T(8,128)(2,1)S(1)}, u32[]{:S(2)}, u32[]{:S(2)}) collective-permute-start(bf16[2,128,128]{2,1,0:T(8,128)(2,1)S(1)} %get-tuple-element.24), channel_id=1, source_target_pairs={{0,24},{8,16},{16,8},{24,0},{1,25},{9,17},{17,9},{25,1},{2,26},{10... | collective-permute-start | bytes 196616 | tf_op jit(solution)/shard_map/ppermute | solution.py:26
  14.4 8.1 %collective-permute-start.4 = (bf16[6,32,128]{2,1,0:T(8,128)(2,1)S(1)}, bf16[6,32,128]{2,1,0:T(8,128)(2,1)S(1)}, u32[]{:S(2)}, u32[]{:S(2)}) collective-permute-start(bf16[6,32,128]{2,1,0:T(8,128)(2,1)S(1)} %get-tuple-element.22), channel_id=1, source_target_pairs={{0,2},{1,3},{2,0},{3,1},{4,6},{5,7},{6,4},{7,5},{8,10},{9,11},{10,... | collective-permute-start | bytes 147464 | tf_op jit(solution)/shard_map/ppermute | solution.py:18
  17.7 4.7 %collective-permute-start.6 = (bf16[2,32,128]{2,1,0:T(8,128)(2,1)S(1)}, bf16[2,32,128]{2,1,0:T(8,128)(2,1)S(1)}, u32[]{:S(2)}, u32[]{:S(2)}) collective-permute-start(bf16[2,32,128]{2,1,0:T(8,128)(2,1)S(1)} %get-tuple-element.26), channel_id=1, source_target_pairs={{0,2},{1,3},{2,0},{3,1},{4,6},{5,7},{6,4},{7,5},{8,10},{9,11},{10,... | collective-permute-start | bytes 49160 | tf_op jit(solution)/shard_map/ppermute | solution.py:18

commit v4 on v3

v4 whole, which is shorter than its diff:
```python
import functools

import jax
import jax.numpy as jnp
from jax import lax
from jax.experimental import pallas as pl
from jax.experimental.pallas import tpu as pltpu
from jax.sharding import PartitionSpec as P

TILE = 64
SLAB_TILES = 2
CHIPS = 4
STEPS = (3, 1, 2)
GROUPS = ((0, 3), (1, 2))
BF16 = jnp.bfloat16
F32 = jnp.float32


def swap_virt(array, step):
    return lax.ppermute(array, "virt", [(d, d ^ step) for d in range(lax.axis_size("virt"))])


def swap_core(array):
    return lax.ppermute(array, "occj", [(0, 1), (1, 0)])


def swap_chip(array, step):
    return lax.ppermute(array, "occi", [(d, d ^ step) for d in range(lax.axis_size("occi"))])


def slot(kind, step):
    first = lax.axis_index("occj") if kind == 0 else 1 - lax.axis_index("occj")
    return first, lax.axis_index("occi") ^ step


def keep_rows(mask_ref, first, second, half):
    lane = lax.broadcasted_iota(jnp.int32, (1, SLAB_TILES * TILE), 1) // TILE
    keep = jnp.zeros(lane.shape, F32)
    for tile in range(SLAB_TILES):
        keep = jnp.where(lane == tile, mask_ref[first, half, tile, second].astype(F32), keep)
    return jnp.broadcast_to(keep, (TILE, SLAB_TILES * TILE)).astype(BF16)


def mask_split_kernel(mask_hbm, pair_hbm, amp_hbm, same_ref, cross_ref, gate_ref, mask_ref, pair_ref, sems):
    copies = [
        pltpu.make_async_copy(mask_hbm, mask_ref, sems.at[0]),
        pltpu.make_async_copy(pair_hbm, pair_ref, sems.at[1]),
    ]
    blocks = []
    for kind, kept_ref in ((1, cross_ref), (0, same_ref)):
        for step in range(CHIPS):
            first, second = slot(kind, step)
            copies.append(
                pltpu.make_async_copy(amp_hbm.at[first, second], kept_ref.at[step], sems.at[len(copies)])
            )
            blocks.append((first, second, kept_ref, step, kind * CHIPS + step, copies[-1]))
    for copy in copies:
        copy.start()
    copies[0].wait()
    copies[1].wait()
    for first, second, kept_ref, step, gate, copy in blocks:
        gate_ref[gate] = jnp.full(gate_ref.shape[1:], pair_ref[first, second].astype(F32))
        keeps = [keep_rows(mask_ref, first, second, half) for half in range(SLAB_TILES)]
        copy.wait()
        for half, keep in enumerate(keeps):
            part = slice(half * TILE, (half + 1) * TILE)
            kept_ref[step, part] = kept_ref[step, part] * keep


def mask_whole_kernel(mask_ref, pair_ref, amp_ref, kept_ref, gate_ref):
    seconds = amp_ref.shape[1]

    def one(block, carry):
        first, second = block // seconds, block % seconds
        for half in range(SLAB_TILES):
            part = slice(half * TILE, (half + 1) * TILE)
            kept_ref[block, part] = amp_ref[first, second, part] * keep_rows(mask_ref, first, second, half)
        gate_ref[block] = jnp.full(gate_ref.shape[1:], pair_ref[first, second].astype(F32))
        return carry

    lax.fori_loop(0, kept_ref.shape[0], one, 0)


def pack_kernel(same_ref, other_ref, *send_refs):
    for step, send_ref in zip(STEPS, send_refs):
        send_ref[0] = same_ref[step]
        send_ref[1] = other_ref[step]


def turn_kernel(chunks, vec_ref, turned_ref, left_ref):
    vectors, slab, _ = vec_ref.shape
    rows = left_ref.shape[0] // (vectors * chunks)
    me = lax.axis_index("virt")
    for q in range(vectors):
        turned_ref[q * slab : (q + 1) * slab] = vec_ref[q].astype(F32).T.astype(BF16)
        for chunk in range(chunks):
            start = pl.multiple_of((me ^ (2 * chunk)) * rows, rows)
            low = (q * chunks + chunk) * rows
            left_ref[low : low + rows] = vec_ref[q, pl.ds(start, rows), :]


def products(ready, inner_ref, sources, outs):
    turned_refs, left_refs = ready[::2], ready[1::2]
    slab = turned_refs[0].shape[1]
    depth = turned_refs[0].shape[0]
    vectors = depth // slab
    height = left_refs[0].shape[0] // vectors
    rows = height // len(outs[0])
    for base in range(0, len(sources), 2):
        both = [
            ((kept.astype(F32) + partner.astype(F32).T) * gate[:1]).astype(BF16)
            for kept, partner, gate in sources[base : base + 2]
        ]
        right = jnp.concatenate(both, axis=1)
        for side, left_ref in enumerate(left_refs):
            inner = jnp.dot(left_ref[...], right, preferred_element_type=F32).astype(BF16)
            for n in range(len(both)):
                for q in range(vectors):
                    at = side * depth + q * slab
                    inner_ref[(base + n) * height : (base + n + 1) * height, at : at + slab] = inner[
                        q * height : (q + 1) * height, n * slab : (n + 1) * slab
                    ]
    half = sum(
        jnp.dot(inner_ref[:, side * depth : (side + 1) * depth], turned_ref[...], preferred_element_type=F32)
        for side, turned_ref in enumerate(turned_refs)
    )
    for n, targets in enumerate(outs):
        for chunk, (ref, index) in enumerate(targets):
            start = n * height + chunk * rows
            ref[index] = half[start : start + rows].astype(ref.dtype)


def group_kernel(chunks, steps, *refs):
    ready, (gate_ref, same_ref, cross_ref), refs = refs[:4], refs[4:7], refs[7:]
    got_refs, part_refs, inner_ref = refs[: len(steps)], refs[len(steps) : -1], refs[-1]
    sources = []
    for step, got_ref in zip(steps, got_refs):
        if step:
            partners = got_ref[0], got_ref[1]
        else:
            partners = same_ref[0], got_ref[0]
        sources.append((same_ref[step], partners[0], gate_ref[step]))
        sources.append((cross_ref[step], partners[1], gate_ref[CHIPS + step]))
    outs = [[(ref, n) for ref in part_refs] for n in range(len(sources))]
    products(ready, inner_ref, sources, outs)


def whole_kernel(*refs):
    ready, (gate_ref, kept_ref, partner_ref), part_refs, inner_ref = refs[:4], refs[4:7], refs[7:-1], refs[-1]

    def two(g, carry):
        pairs = [2 * g, 2 * g + 1]
        sources = [(kept_ref[k], partner_ref[k], gate_ref[k]) for k in pairs]
        products(ready, inner_ref, sources, [[(ref, k) for ref in part_refs] for k in pairs])
        return carry

    lax.fori_loop(0, kept_ref.shape[0] // 2, two, 0)


def finish_kernel(groups, chunks, *refs):
    out_ref = refs[-1]
    for group, steps in enumerate(groups):
        terms = refs[group * chunks : (group + 1) * chunks]
        for n in range(2 * len(steps)):
            total = terms[0][n]
            for term in terms[1:]:
                total = total + term[n].astype(F32)
            first, second = slot(n % 2, steps[n // 2])
            out_ref[first, second] = total.astype(BF16)


def vmem_specs(count):
    return [pl.BlockSpec(memory_space=pltpu.VMEM)] * count


def shaped(dtype, *shape):
    return jax.ShapeDtypeStruct(shape, dtype)


def kernel(body, outs, operands, spaces=(), scratch=(), flops=0):
    spaces = list(spaces) + [pltpu.VMEM] * (len(operands) - len(spaces))
    return pl.pallas_call(
        body,
        out_shape=outs,
        in_specs=[pl.BlockSpec(memory_space=space) for space in spaces],
        out_specs=vmem_specs(len(outs)),
        scratch_shapes=list(scratch),
        compiler_params=pltpu.CompilerParams(vmem_limit_bytes=24 * 1024 * 1024),
        cost_estimate=pl.CostEstimate(flops=flops, bytes_accessed=1 << 20, transcendentals=0),
    )(*operands)


def shards(amplitudes, vectors, tile_mask, pair_mask):
    firsts, seconds, slab, _ = amplitudes.shape
    pairs = firsts * seconds
    virt, chips, cores = lax.axis_size("virt"), lax.axis_size("occi"), lax.axis_size("occj")
    rows = slab // virt
    chunks = virt // 2
    depth = 2 * vectors.shape[0] * slab
    turned_mask = jnp.transpose(tile_mask, (0, 2, 3, 1))
    gate = shaped(F32, pairs, 8, slab)
    arranged = [shaped(BF16, depth // 2, slab), shaped(BF16, depth // 4, slab)]
    turn = functools.partial(turn_kernel, chunks)

    def parts(count):
        return [shaped(F32 if chunk == 0 else BF16, count, rows, slab) for chunk in range(chunks)]

    def inner(count):
        return pltpu.VMEM((count * chunks * rows, depth), BF16)

    def sent(part):
        return [part[0]] + [swap_virt(part[chunk], 2 * chunk) for chunk in range(1, chunks)]

    def work(count):
        return 2 * count * depth * slab * slab

    near = swap_virt(vectors, 1)
    if (firsts, seconds, chips, cores) == (2, CHIPS, CHIPS, 2):
        half_blocks = shaped(BF16, CHIPS, slab, slab)
        same, cross, gates = kernel(
            mask_split_kernel,
            [half_blocks, half_blocks, gate],
            [
                pltpu.with_memory_space_constraint(array, pltpu.HBM)
                for array in (turned_mask, pair_mask, amplitudes)
            ],
            spaces=[pltpu.HBM] * 3,
            scratch=[
                pltpu.SMEM(turned_mask.shape, jnp.int32),
                pltpu.SMEM(pair_mask.shape, jnp.int32),
                pltpu.SemaphoreType.DMA((pairs + 2,)),
            ],
        )
        other = swap_core(cross)
        packed = kernel(pack_kernel, [shaped(BF16, 2, slab, slab)] * (CHIPS - 1), (same, other))
        got = {step: swap_chip(block, step) for step, block in zip(STEPS, packed)}
        got[0] = other
        ready = kernel(turn, arranged, (vectors,)) + kernel(turn, arranged, (near,))
        finished = []
        for steps in GROUPS:
            part = kernel(
                functools.partial(group_kernel, chunks, steps),
                parts(2 * len(steps)),
                (*ready, gates, same, cross, *[got[step] for step in steps]),
                scratch=[inner(2 * len(steps))],
                flops=work(2 * len(steps)),
            )
            finished += sent(part)
        (out,) = kernel(
            functools.partial(finish_kernel, GROUPS, chunks),
            [shaped(BF16, firsts, seconds, rows, slab)],
            finished,
        )
        return out
    kept, gates = kernel(
        mask_whole_kernel,
        [shaped(BF16, pairs, slab, slab), gate],
        (turned_mask, pair_mask, amplitudes),
        spaces=[pltpu.SMEM] * 2,
    )
    partner = lax.all_to_all(kept, ("occj", "occi"), split_axis=0, concat_axis=0, tiled=True)
    ready = kernel(turn, arranged, (vectors,)) + kernel(turn, arranged, (near,))
    part = sent(
        kernel(whole_kernel, parts(pairs), (*ready, gates, kept, partner), scratch=[inner(2)], flops=work(pairs))
    )
    summed = part[0]
    for term in part[1:]:
        summed = summed + term.astype(F32)
    return summed.reshape(firsts, seconds, rows, slab).astype(BF16)


def solution(mesh):
    placed = (
        P("occi", "occj", None, None),
        P("virt", None, None),
        P("occi", "occj", None, None),
        P("occi", "occj"),
    )
    return jax.shard_map(
        shards,
        mesh=mesh,
        in_specs=placed,
        out_specs=P("occi", "occj", "virt", None),
        check_vma=False,
    )
```

time: 23.3 us -> 21.5 us (0.923)
  local copies, waits for them, and re-layouts: 1.64 us -> 0.01 us
    unnamed x8 -> x2, local copies, waits for them, and re-layouts: 1.64 us -> 0.01 us
    ppermute x3, waiting for transfers between devices: 2.27 us -> 1.52 us  [swap_chip(): lax.ppermute(array, 'occi', [(d, d ^ step) for d in range(lax.axis_size('...]
    ppermute x3, waiting for transfers between devices: 4.04 us -> 4.58 us  [swap_virt(): lax.ppermute(array, 'virt', [(d, d ^ step) for d in range(lax.axis_size('...]
    pallas_call x5 -> x7, Pallas kernels: 3.77 us -> 3.72 us  [kernel(): pl.pallas_call(body, out_shape=outs, in_specs=[pl.BlockSpec(memory_space=...]
  transfers between devices with their start and end apart: 7 -> 7, of which waited for: 4 -> 5; matrix products, arithmetic and copies ran while one was open for 0% -> 0% of each run, Pallas kernels for 14% -> 14%
where the time goes in v4:
time: 21.5 us; the launch traced here: 21.3 us
  starting transfers between devices  10.1 us (47%)
  waiting for transfers between devices  7.43 us (35%)
  Pallas kernels  3.72 us (17%)
    ppermute x3, starting transfers between devices, swap_virt(): lax.ppermute(array, 'virt', [(d, d ^ step) for d in range(lax.axis_size('...  6.49 us
    ppermute x3, waiting for transfers between devices, swap_virt(): lax.ppermute(array, 'virt', [(d, d ^ step) for d in range(lax.axis_size('...  4.58 us
    pallas_call x7, Pallas kernels, kernel(): pl.pallas_call(body, out_shape=outs, in_specs=[pl.BlockSpec(memory_space=...  3.72 us
    ppermute x3, starting transfers between devices, swap_chip(): lax.ppermute(array, 'occi', [(d, d ^ step) for d in range(lax.axis_size('...  3.55 us
    ppermute x3, waiting for transfers between devices, swap_chip(): lax.ppermute(array, 'occi', [(d, d ^ step) for d in range(lax.axis_size('...  1.52 us
    ppermute x1, waiting for transfers between devices, swap_core(): return lax.ppermute(array, 'occj', [(0, 1), (1, 0)])  1.33 us
  transfers between devices with their start and end apart: 7, of which 5 were waited for; matrix products, arithmetic and copies ran while one was open for 0% of the time, Pallas kernels for 14%

profile of v4, /device:TPU:0, one launch (start us, length us, event | category | flops | bytes accessed | tf_op | source)
XLA Modules:
  0.0 21.3 jit_solution(647065535121444204)
XLA Ops:
  0.0 3.0 %collective-permute-start = (bf16[8,128,128]{2,1,0:T(8,128)(2,1)}, bf16[8,128,128]{2,1,0:T(8,128)(2,1)S(1)}, u32[]{:S(2)}, u32[]{:S(2)}) collective-permute-start(bf16[8,128,128]{2,1,0:T(8,128)(2,1)} %vec_ref.1), channel_id=1, source_target_pairs={{0,1},{1,0},{2,3},{3,2},{4,5},{5,4},{6,7},{7,6},{8,9},{9,8},{10,11... | collective-permute-start | bytes 786440 | tf_op jit(solution)/shard_map/ppermute | solution.py:20
  3.0 0.0 copy-start
  3.0 1.1 %shard_map.48 = (bf16[4,128,128]{2,1,0:T(8,128)(2,1)S(1)}, bf16[4,128,128]{2,1,0:T(8,128)(2,1)S(1)}, f32[8,8,128]{2,1,0:T(8,128)S(1)}) custom-call(s32[2,2,2,4]{3,2,1,0:T(2,128)} %bitcast.1, s32[2,4]{1,0:T(2,128)} %pair_hbm.1, bf16[2,4,128,128]{3,2,1,0:T(8,128)(2,1)} %amp_hbm.1), custom_call_target="tpu_custom_call" | custom-call | bytes 1048576 | tf_op jit(solution)/shard_map/pallas_call | solution.py:182
  4.1 0.1 collective-permute-start.1
  4.2 1.3 %collective-permute-done.1.other_ref.refs_7_ = bf16[4,128,128]{2,1,0:T(8,128)(2,1)S(1)} collective-permute-done((bf16[4,128,128]{2,1,0:T(8,128)(2,1)S(1)}, bf16[4,128,128]{2,1,0:T(8,128)(2,1)S(1)}, u32[]{:S(2)}, u32[]{:S(2)}) %collective-permute-start.1) | collective-permute-done | bytes 131104 | tf_op jit(solution)/shard_map/ppermute | solution.py:24
  5.6 2.5 %collective-permute-start.2 = (bf16[2,128,128]{2,1,0:T(8,128)(2,1)S(1)}, bf16[2,128,128]{2,1,0:T(8,128)(2,1)S(1)}, u32[]{:S(2)}, u32[]{:S(2)}) collective-permute-start(bf16[2,128,128]{2,1,0:T(8,128)(2,1)S(1)} %get-tuple-element.26), channel_id=1, source_target_pairs={{0,24},{8,16},{16,8},{24,0},{1,25},{9,17},{17,9},{25,1},{2,26},{10... | collective-permute-start | bytes 196616 | tf_op jit(solution)/shard_map/ppermute | solution.py:28
  8.1 0.5 %collective-permute-start.4 = (bf16[2,128,128]{2,1,0:T(8,128)(2,1)S(1)}, bf16[2,128,128]{2,1,0:T(8,128)(2,1)S(1)}, u32[]{:S(2)}, u32[]{:S(2)}) collective-permute-start(bf16[2,128,128]{2,1,0:T(8,128)(2,1)S(1)} %get-tuple-element.29), channel_id=1, source_target_pairs={{0,8},{8,0},{16,24},{24,16},{1,9},{9,1},{17,25},{25,17},{2,10},{10... | collective-permute-start | bytes 196616 | tf_op jit(solution)/shard_map/ppermute | solution.py:28
  8.6 0.5 %collective-permute-start.5 = (bf16[2,128,128]{2,1,0:T(8,128)(2,1)S(1)}, bf16[2,128,128]{2,1,0:T(8,128)(2,1)S(1)}, u32[]{:S(2)}, u32[]{:S(2)}) collective-permute-start(bf16[2,128,128]{2,1,0:T(8,128)(2,1)S(1)} %get-tuple-element.30), channel_id=1, source_target_pairs={{0,16},{8,24},{16,0},{24,8},{1,17},{9,25},{17,1},{25,9},{2,18},{10... | collective-permute-start | bytes 196616 | tf_op jit(solution)/shard_map/ppermute | solution.py:28
  9.1 0.0 copy-done
  9.1 0.1 shard_map.46
  9.3 0.3 %collective-permute-done.vec_ref = bf16[8,128,128]{2,1,0:T(8,128)(2,1)S(1)} collective-permute-done((bf16[8,128,128]{2,1,0:T(8,128)(2,1)}, bf16[8,128,128]{2,1,0:T(8,128)(2,1)S(1)}, u32[]{:S(2)}, u32[]{:S(2)}) %collective-permute-start) | collective-permute-done | bytes 262176 | tf_op jit(solution)/shard_map/ppermute | solution.py:20
  9.5 0.1 shard_map.47
  9.7 1.5 %collective-permute-done.2.refs_8_ = bf16[2,128,128]{2,1,0:T(8,128)(2,1)S(1)} collective-permute-done((bf16[2,128,128]{2,1,0:T(8,128)(2,1)S(1)}, bf16[2,128,128]{2,1,0:T(8,128)(2,1)S(1)}, u32[]{:S(2)}, u32[]{:S(2)}) %collective-permute-start.2) | collective-permute-done | bytes 65568 | tf_op jit(solution)/shard_map/ppermute | solution.py:28
  11.2 0.8 %shard_map.50 = (f32[4,32,128]{2,1,0:T(8,128)S(1)}, bf16[4,32,128]{2,1,0:T(8,128)(2,1)S(1)}) custom-call(bf16[1024,128]{1,0:T(8,128)(2,1)S(1)} %get-tuple-element.19.refs_0_, bf16[512,128]{1,0:T(8,128)(2,1)S(1)} %get-tuple-element.20.refs_1_, bf16[1024,128]{1,0:T(8,128)(2,1)S(1)} %get-tuple-element.21.refs_2_, ...), custom_call_target="tpu_custom_call" | custom-call | flops 268435456 | bytes 1048576 | tf_op jit(solution)/shard_map/pallas_call | solution.py:182
  12.0 2.7 %collective-permute-start.3 = (bf16[4,32,128]{2,1,0:T(8,128)(2,1)S(1)}, bf16[4,32,128]{2,1,0:T(8,128)(2,1)S(1)}, u32[]{:S(2)}, u32[]{:S(2)}) collective-permute-start(bf16[4,32,128]{2,1,0:T(8,128)(2,1)S(1)} %get-tuple-element.28), channel_id=1, source_target_pairs={{0,2},{1,3},{2,0},{3,1},{4,6},{5,7},{6,4},{7,5},{8,10},{9,11},{10,... | collective-permute-start | bytes 98312 | tf_op jit(solution)/shard_map/ppermute | solution.py:20
  14.7 0.0 collective-permute-done.4.refs_7_
  14.7 0.0 collective-permute-done.5.refs_8_
  14.7 0.9 %shard_map.51 = (f32[4,32,128]{2,1,0:T(8,128)S(1)}, bf16[4,32,128]{2,1,0:T(8,128)(2,1)S(1)}) custom-call(bf16[1024,128]{1,0:T(8,128)(2,1)S(1)} %get-tuple-element.19.refs_0_, bf16[512,128]{1,0:T(8,128)(2,1)S(1)} %get-tuple-element.20.refs_1_, bf16[1024,128]{1,0:T(8,128)(2,1)S(1)} %get-tuple-element.21.refs_2_, ...), custom_call_target="tpu_custom_call" | custom-call | flops 268435456 | bytes 1048576 | tf_op jit(solution)/shard_map/pallas_call | solution.py:182
  15.6 0.8 %collective-permute-start.6 = (bf16[4,32,128]{2,1,0:T(8,128)(2,1)S(1)}, bf16[4,32,128]{2,1,0:T(8,128)(2,1)S(1)}, u32[]{:S(2)}, u32[]{:S(2)}) collective-permute-start(bf16[4,32,128]{2,1,0:T(8,128)(2,1)S(1)} %get-tuple-element.32), channel_id=1, source_target_pairs={{0,2},{1,3},{2,0},{3,1},{4,6},{5,7},{6,4},{7,5},{8,10},{9,11},{10,... | collective-permute-start | bytes 98312 | tf_op jit(solution)/shard_map/ppermute | solution.py:20
  16.4 0.6 %collective-permute-done.3.refs_1_ = bf16[4,32,128]{2,1,0:T(8,128)(2,1)S(1)} collective-permute-done((bf16[4,32,128]{2,1,0:T(8,128)(2,1)S(1)}, bf16[4,32,128]{2,1,0:T(8,128)(2,1)S(1)}, u32[]{:S(2)}, u32[]{:S(2)}) %collective-permute-start.3) | collective-permute-done | bytes 32800 | tf_op jit(solution)/shard_map/ppermute | solution.py:20
  17.0 3.7 %collective-permute-done.6.refs_3_ = bf16[4,32,128]{2,1,0:T(8,128)(2,1)S(1)} collective-permute-done((bf16[4,32,128]{2,1,0:T(8,128)(2,1)S(1)}, bf16[4,32,128]{2,1,0:T(8,128)(2,1)S(1)}, u32[]{:S(2)}, u32[]{:S(2)}) %collective-permute-start.6) | collective-permute-done | bytes 32800 | tf_op jit(solution)/shard_map/ppermute | solution.py:20
  20.7 0.6 %shard_map.52 = bf16[2,4,32,128]{3,2,1,0:T(8,128)(2,1)} custom-call(f32[4,32,128]{2,1,0:T(8,128)S(1)} %get-tuple-element.27.refs_0_, bf16[4,32,128]{2,1,0:T(8,128)(2,1)S(1)} %collective-permute-done.3.refs_1_, f32[4,32,128]{2,1,0:T(8,128)S(1)} %get-tuple-element.31.refs_2_, bf16[4,32,128]{2,1,0:T(8,128)(2,1)S(1)} %collective-permute-done.6.refs_3_), custom_call_target="tpu_custom_call" | custom-call | bytes 1048576 | tf_op jit(solution)/shard_map/pallas_call | solution.py:182
  (1 shorter events, 0.0 us)
Async XLA Ops:
  0.0 9.5 %collective-permute-start = (bf16[8,128,128]{2,1,0:T(8,128)(2,1)}, bf16[8,128,128]{2,1,0:T(8,128)(2,1)S(1)}, u32[]{:S(2)}, u32[]{:S(2)}) collective-permute-start(bf16[8,128,128]{2,1,0:T(8,128)(2,1)} %vec_ref.1), channel_id=1, source_target_pairs={{0,1},{1,0},{2,3},{3,2},{4,5},{5,4},{6,7},{7,6},{8,9},{9,8},{10,11... | collective-permute-start | bytes 786440 | tf_op jit(solution)/shard_map/ppermute | solution.py:20
  3.0 6.1 %copy-start = (bf16[8,128,128]{2,1,0:T(8,128)(2,1)S(1)}, bf16[8,128,128]{2,1,0:T(8,128)(2,1)}, u32[]{:S(2)}) copy-start(bf16[8,128,128]{2,1,0:T(8,128)(2,1)} %vec_ref.1) | copy-start | bytes 786436
  4.1 1.4 %collective-permute-start.1 = (bf16[4,128,128]{2,1,0:T(8,128)(2,1)S(1)}, bf16[4,128,128]{2,1,0:T(8,128)(2,1)S(1)}, u32[]{:S(2)}, u32[]{:S(2)}) collective-permute-start(bf16[4,128,128]{2,1,0:T(8,128)(2,1)S(1)} %get-tuple-element.25.refs_6_), channel_id=1, source_target_pairs={{0,4},{4,0},{1,5},{5,1},{2,6},{6,2},{3,7},{7,3},{8,12},{12,8},{9,1... | collective-permute-start | bytes 393224 | tf_op jit(solution)/shard_map/ppermute | solution.py:24
  5.6 5.6 %collective-permute-start.2 = (bf16[2,128,128]{2,1,0:T(8,128)(2,1)S(1)}, bf16[2,128,128]{2,1,0:T(8,128)(2,1)S(1)}, u32[]{:S(2)}, u32[]{:S(2)}) collective-permute-start(bf16[2,128,128]{2,1,0:T(8,128)(2,1)S(1)} %get-tuple-element.26), channel_id=1, source_target_pairs={{0,24},{8,16},{16,8},{24,0},{1,25},{9,17},{17,9},{25,1},{2,26},{10... | collective-permute-start | bytes 196616 | tf_op jit(solution)/shard_map/ppermute | solution.py:28
  8.1 6.6 %collective-permute-start.4 = (bf16[2,128,128]{2,1,0:T(8,128)(2,1)S(1)}, bf16[2,128,128]{2,1,0:T(8,128)(2,1)S(1)}, u32[]{:S(2)}, u32[]{:S(2)}) collective-permute-start(bf16[2,128,128]{2,1,0:T(8,128)(2,1)S(1)} %get-tuple-element.29), channel_id=1, source_target_pairs={{0,8},{8,0},{16,24},{24,16},{1,9},{9,1},{17,25},{25,17},{2,10},{10... | collective-permute-start | bytes 196616 | tf_op jit(solution)/shard_map/ppermute | solution.py:28
  8.6 6.1 %collective-permute-start.5 = (bf16[2,128,128]{2,1,0:T(8,128)(2,1)S(1)}, bf16[2,128,128]{2,1,0:T(8,128)(2,1)S(1)}, u32[]{:S(2)}, u32[]{:S(2)}) collective-permute-start(bf16[2,128,128]{2,1,0:T(8,128)(2,1)S(1)} %get-tuple-element.30), channel_id=1, source_target_pairs={{0,16},{8,24},{16,0},{24,8},{1,17},{9,25},{17,1},{25,9},{2,18},{10... | collective-permute-start | bytes 196616 | tf_op jit(solution)/shard_map/ppermute | solution.py:28
  12.0 4.9 %collective-permute-start.3 = (bf16[4,32,128]{2,1,0:T(8,128)(2,1)S(1)}, bf16[4,32,128]{2,1,0:T(8,128)(2,1)S(1)}, u32[]{:S(2)}, u32[]{:S(2)}) collective-permute-start(bf16[4,32,128]{2,1,0:T(8,128)(2,1)S(1)} %get-tuple-element.28), channel_id=1, source_target_pairs={{0,2},{1,3},{2,0},{3,1},{4,6},{5,7},{6,4},{7,5},{8,10},{9,11},{10,... | collective-permute-start | bytes 98312 | tf_op jit(solution)/shard_map/ppermute | solution.py:20
  15.6 5.1 %collective-permute-start.6 = (bf16[4,32,128]{2,1,0:T(8,128)(2,1)S(1)}, bf16[4,32,128]{2,1,0:T(8,128)(2,1)S(1)}, u32[]{:S(2)}, u32[]{:S(2)}) collective-permute-start(bf16[4,32,128]{2,1,0:T(8,128)(2,1)S(1)} %get-tuple-element.32), channel_id=1, source_target_pairs={{0,2},{1,3},{2,0},{3,1},{4,6},{5,7},{6,4},{7,5},{8,10},{9,11},{10,... | collective-permute-start | bytes 98312 | tf_op jit(solution)/shard_map/ppermute | solution.py:20

commit v5 on v4

--- a/solution.py
+++ b/solution.py
@@ -11,7 +11,6 @@
 SLAB_TILES = 2
 CHIPS = 4
 STEPS = (3, 1, 2)
-GROUPS = ((0, 3), (1, 2))
 BF16 = jnp.bfloat16
 F32 = jnp.float32
 
@@ -41,30 +40,34 @@
     return jnp.broadcast_to(keep, (TILE, SLAB_TILES * TILE)).astype(BF16)
 
 
-def mask_split_kernel(mask_hbm, pair_hbm, amp_hbm, same_ref, cross_ref, gate_ref, mask_ref, pair_ref, sems):
+def mask_split_kernel(mask_hbm, pair_hbm, amp_hbm, vec_hbm, *refs):
+    kept_refs, (gate_ref, part_ref, mask_ref, pair_ref, sems) = refs[:CHIPS], refs[CHIPS:]
+    count = part_ref.shape[0]
+    mine = vec_hbm.at[pl.ds(lax.axis_index("occj") * count, count)]
     copies = [
         pltpu.make_async_copy(mask_hbm, mask_ref, sems.at[0]),
         pltpu.make_async_copy(pair_hbm, pair_ref, sems.at[1]),
+        pltpu.make_async_copy(mine, part_ref, sems.at[2]),
     ]
     blocks = []
-    for kind, kept_ref in ((1, cross_ref), (0, same_ref)):
-        for step in range(CHIPS):
+    for step in STEPS + (0,):
+        for kind in range(2):
             first, second = slot(kind, step)
-            copies.append(
-                pltpu.make_async_copy(amp_hbm.at[first, second], kept_ref.at[step], sems.at[len(copies)])
-            )
-            blocks.append((first, second, kept_ref, step, kind * CHIPS + step, copies[-1]))
+            target = kept_refs[step].at[kind]
+            copies.append(pltpu.make_async_copy(amp_hbm.at[first, second], target, sems.at[len(copies)]))
+            blocks.append((first, second, target, kind * CHIPS + step, copies[-1]))
     for copy in copies:
         copy.start()
     copies[0].wait()
     copies[1].wait()
-    for first, second, kept_ref, step, gate, copy in blocks:
+    for first, second, target, gate, copy in blocks:
         gate_ref[gate] = jnp.full(gate_ref.shape[1:], pair_ref[first, second].astype(F32))
         keeps = [keep_rows(mask_ref, first, second, half) for half in range(SLAB_TILES)]
         copy.wait()
         for half, keep in enumerate(keeps):
             part = slice(half * TILE, (half + 1) * TILE)
-            kept_ref[step, part] = kept_ref[step, part] * keep
+            target[part] = target[part] * keep
+    copies[2].wait()
 
 
 def mask_whole_kernel(mask_ref, pair_ref, amp_ref, kept_ref, gate_ref):
@@ -81,22 +84,25 @@
     lax.fori_loop(0, kept_ref.shape[0], one, 0)
 
 
-def pack_kernel(same_ref, other_ref, *send_refs):
-    for step, send_ref in zip(STEPS, send_refs):
-        send_ref[0] = same_ref[step]
-        send_ref[1] = other_ref[step]
-
-
-def turn_kernel(chunks, vec_ref, turned_ref, left_ref):
-    vectors, slab, _ = vec_ref.shape
-    rows = left_ref.shape[0] // (vectors * chunks)
+def pack_kernel(*refs):
+    for step in range(CHIPS):
+        refs[-1][step] = refs[step][1]
+
+
+def turn_kernel(chunks, *refs):
+    vec_refs, turned_ref, left_ref = refs[:-2], refs[-2], refs[-1]
+    slab = turned_ref.shape[1]
+    rows = slab * left_ref.shape[0] // (turned_ref.shape[0] * chunks)
     me = lax.axis_index("virt")
-    for q in range(vectors):
-        turned_ref[q * slab : (q + 1) * slab] = vec_ref[q].astype(F32).T.astype(BF16)
-        for chunk in range(chunks):
-            start = pl.multiple_of((me ^ (2 * chunk)) * rows, rows)
-            low = (q * chunks + chunk) * rows
-            left_ref[low : low + rows] = vec_ref[q, pl.ds(start, rows), :]
+    at, low = 0, 0
+    for vec_ref in vec_refs:
+        for q in range(vec_ref.shape[0]):
+            turned_ref[at : at + slab] = vec_ref[q].astype(F32).T.astype(BF16)
+            at += slab
+            for chunk in range(chunks):
+                start = pl.multiple_of((me ^ (2 * chunk)) * rows, rows)
+                left_ref[low : low + rows] = vec_ref[q, pl.ds(start, rows), :]
+                low += rows
 
 
 def products(ready, inner_ref, sources, outs):
@@ -130,19 +136,18 @@
             ref[index] = half[start : start + rows].astype(ref.dtype)
 
 
-def group_kernel(chunks, steps, *refs):
-    ready, (gate_ref, same_ref, cross_ref), refs = refs[:4], refs[4:7], refs[7:]
-    got_refs, part_refs, inner_ref = refs[: len(steps)], refs[len(steps) : -1], refs[-1]
-    sources = []
-    for step, got_ref in zip(steps, got_refs):
-        if step:
-            partners = got_ref[0], got_ref[1]
-        else:
-            partners = same_ref[0], got_ref[0]
-        sources.append((same_ref[step], partners[0], gate_ref[step]))
-        sources.append((cross_ref[step], partners[1], gate_ref[CHIPS + step]))
-    outs = [[(ref, n) for ref in part_refs] for n in range(len(sources))]
-    products(ready, inner_ref, sources, outs)
+def same_kernel(chunks, *refs):
+    ready, gate_ref, kept_refs, refs = refs[:4], refs[4], refs[5 : 5 + CHIPS], refs[5 + CHIPS :]
+    got_refs, part_refs, inner_ref = (kept_refs[0],) + refs[: CHIPS - 1], refs[CHIPS - 1 : -1], refs[-1]
+    sources = [(kept_refs[step][0], got_refs[step][0], gate_ref[step]) for step in range(CHIPS)]
+    products(ready, inner_ref, sources, [[(ref, n) for ref in part_refs] for n in range(CHIPS)])
+
+
+def cross_kernel(chunks, *refs):
+    ready, gate_ref, kept_refs, other_ref, refs = refs[:4], refs[4], refs[5 : 5 + CHIPS], refs[5 + CHIPS], refs[6 + CHIPS :]
+    part_refs, inner_ref = refs[:-1], refs[-1]
+    sources = [(kept_refs[step][1], other_ref[step], gate_ref[CHIPS + step]) for step in range(CHIPS)]
+    products(ready, inner_ref, sources, [[(ref, n) for ref in part_refs] for n in range(CHIPS)])
 
 
 def whole_kernel(*refs):
@@ -157,15 +162,15 @@
     lax.fori_loop(0, kept_ref.shape[0] // 2, two, 0)
 
 
-def finish_kernel(groups, chunks, *refs):
+def finish_kernel(chunks, *refs):
     out_ref = refs[-1]
-    for group, steps in enumerate(groups):
-        terms = refs[group * chunks : (group + 1) * chunks]
-        for n in range(2 * len(steps)):
-            total = terms[0][n]
+    for kind in range(2):
+        terms = refs[kind * chunks : (kind + 1) * chunks]
+        for step in range(CHIPS):
+            total = terms[0][step]
             for term in terms[1:]:
-                total = total + term[n].astype(F32)
-            first, second = slot(n % 2, steps[n // 2])
+                total = total + term[step].astype(F32)
+            first, second = slot(kind, step)
             out_ref[first, second] = total.astype(BF16)
 
 
@@ -214,42 +219,41 @@
     def work(count):
         return 2 * count * depth * slab * slab
 
-    near = swap_virt(vectors, 1)
     if (firsts, seconds, chips, cores) == (2, CHIPS, CHIPS, 2):
-        half_blocks = shaped(BF16, CHIPS, slab, slab)
-        same, cross, gates = kernel(
+        half_vectors = shaped(vectors.dtype, vectors.shape[0] // 2, slab, slab)
+        *kept, gates, mine = kernel(
             mask_split_kernel,
-            [half_blocks, half_blocks, gate],
+            [shaped(BF16, 2, slab, slab)] * CHIPS + [gate, half_vectors],
             [
                 pltpu.with_memory_space_constraint(array, pltpu.HBM)
-                for array in (turned_mask, pair_mask, amplitudes)
+                for array in (turned_mask, pair_mask, amplitudes, vectors)
             ],
-            spaces=[pltpu.HBM] * 3,
+            spaces=[pltpu.HBM] * 4,
             scratch=[
                 pltpu.SMEM(turned_mask.shape, jnp.int32),
                 pltpu.SMEM(pair_mask.shape, jnp.int32),
-                pltpu.SemaphoreType.DMA((pairs + 2,)),
+                pltpu.SemaphoreType.DMA((pairs + 3,)),
             ],
         )
-        other = swap_core(cross)
-        packed = kernel(pack_kernel, [shaped(BF16, 2, slab, slab)] * (CHIPS - 1), (same, other))
-        got = {step: swap_chip(block, step) for step, block in zip(STEPS, packed)}
-        got[0] = other
-        ready = kernel(turn, arranged, (vectors,)) + kernel(turn, arranged, (near,))
+        near = swap_virt(mine, 1)
+        swapped = {step: swap_chip(kept[step], step) for step in STEPS}
+        got = [swapped[step] for step in range(1, CHIPS)]
+        beside = swap_core(near)
+        (packed,) = kernel(pack_kernel, [shaped(BF16, CHIPS, slab, slab)], (kept[0], *got))
+        other = swap_core(packed)
+        ready = kernel(turn, arranged, (vectors,)) + kernel(turn, arranged, (near, beside))
         finished = []
-        for steps in GROUPS:
+        for body, partners in ((same_kernel, got), (cross_kernel, [other])):
             part = kernel(
-                functools.partial(group_kernel, chunks, steps),
-                parts(2 * len(steps)),
-                (*ready, gates, same, cross, *[got[step] for step in steps]),
-                scratch=[inner(2 * len(steps))],
-                flops=work(2 * len(steps)),
+                functools.partial(body, chunks),
+                parts(CHIPS),
+                (*ready, gates, *kept, *partners),
+                scratch=[inner(CHIPS)],
+                flops=work(CHIPS),
             )
             finished += sent(part)
         (out,) = kernel(
-            functools.partial(finish_kernel, GROUPS, chunks),
-            [shaped(BF16, firsts, seconds, rows, slab)],
-            finished,
+            functools.partial(finish_kernel, chunks), [shaped(BF16, firsts, seconds, rows, slab)], finished
         )
         return out
     kept, gates = kernel(
@@ -259,7 +263,7 @@
         spaces=[pltpu.SMEM] * 2,
     )
     partner = lax.all_to_all(kept, ("occj", "occi"), split_axis=0, concat_axis=0, tiled=True)
-    ready = kernel(turn, arranged, (vectors,)) + kernel(turn, arranged, (near,))
+    ready = kernel(turn, arranged, (vectors,)) + kernel(turn, arranged, (swap_virt(vectors, 1),))
     part = sent(
         kernel(whole_kernel, parts(pairs), (*ready, gates, kept, partner), scratch=[inner(2)], flops=work(pairs))
     )

time: 21.5 us -> 23 us (1.070)
  waiting for transfers between devices: 7.43 us -> 9.4 us
  starting transfers between devices: 10.1 us -> 9.71 us
    ppermute x3, waiting for transfers between devices: 1.52 us -> 4.68 us  [swap_chip(): lax.ppermute(array, 'occi', [(d, d ^ step) for d in range(lax.axis_size('...]
    ppermute x1 -> x2, waiting for transfers between devices: 1.33 us -> 0.01 us  [swap_core(): return lax.ppermute(array, 'occj', [(0, 1), (1, 0)])]
    ppermute x3, starting transfers between devices: 6.49 us -> 6.15 us  [swap_virt(): lax.ppermute(array, 'virt', [(d, d ^ step) for d in range(lax.axis_size('...]
  transfers between devices with their start and end apart: 7 -> 8, of which waited for: 5 -> 5; matrix products, arithmetic and copies ran while one was open for 0% -> 0% of each run, Pallas kernels for 14% -> 9%
where the time goes in v5:
time: 23 us; the launch traced here: 22.9 us
  starting transfers between devices  9.71 us (42%)
  waiting for transfers between devices  9.4 us (41%)
  Pallas kernels  3.66 us (16%)
    ppermute x3, starting transfers between devices, swap_virt(): lax.ppermute(array, 'virt', [(d, d ^ step) for d in range(lax.axis_size('...  6.15 us
    ppermute x3, waiting for transfers between devices, swap_virt(): lax.ppermute(array, 'virt', [(d, d ^ step) for d in range(lax.axis_size('...  4.72 us
    ppermute x3, waiting for transfers between devices, swap_chip(): lax.ppermute(array, 'occi', [(d, d ^ step) for d in range(lax.axis_size('...  4.68 us
    pallas_call x7, Pallas kernels, kernel(): pl.pallas_call(body, out_shape=outs, in_specs=[pl.BlockSpec(memory_space=...  3.66 us
    ppermute x3, starting transfers between devices, swap_chip(): lax.ppermute(array, 'occi', [(d, d ^ step) for d in range(lax.axis_size('...  3.49 us
  transfers between devices with their start and end apart: 8, of which 5 were waited for; matrix products, arithmetic and copies ran while one was open for 0% of the time, Pallas kernels for 9%

profile of v5, /device:TPU:0, one launch (start us, length us, event | category | flops | bytes accessed | tf_op | source)
XLA Modules:
  0.0 22.9 jit_solution(5686438576875824700)
XLA Ops:
  0.0 1.0 %shard_map.47 = (bf16[2,128,128]{2,1,0:T(8,128)(2,1)S(1)}, bf16[2,128,128]{2,1,0:T(8,128)(2,1)S(1)}, bf16[2,128,128]{2,1,0:T(8,128)(2,1)S(1)}, bf16[2,128,128]{2...) custom-call(s32[2,2,2,4]{3,2,1,0:T(2,128)} %bitcast.1, s32[2,4]{1,0:T(2,128)} %pair_hbm.1, ...), custom_call_target="tpu_custom_call" | custom-call | bytes 1048576 | tf_op jit(solution)/shard_map/pallas_call | solution.py:187
  1.0 0.0 copy-start
  1.1 3.1 %collective-permute-start = (bf16[4,128,128]{2,1,0:T(8,128)(2,1)S(1)}, bf16[4,128,128]{2,1,0:T(8,128)(2,1)S(1)}, u32[]{:S(2)}, u32[]{:S(2)}) collective-permute-start(bf16[4,128,128]{2,1,0:T(8,128)(2,1)S(1)} %get-tuple-element.21), channel_id=1, source_target_pairs={{0,1},{1,0},{2,3},{3,2},{4,5},{5,4},{6,7},{7,6},{8,9},{9,8},{10,11... | collective-permute-start | bytes 393224 | tf_op jit(solution)/shard_map/ppermute | solution.py:19
  4.1 1.5 %collective-permute-start.2 = (bf16[2,128,128]{2,1,0:T(8,128)(2,1)S(1)}, bf16[2,128,128]{2,1,0:T(8,128)(2,1)S(1)}, u32[]{:S(2)}, u32[]{:S(2)}) collective-permute-start(bf16[2,128,128]{2,1,0:T(8,128)(2,1)S(1)} %get-tuple-element.26.refs_6_), channel_id=1, source_target_pairs={{0,8},{8,0},{16,24},{24,16},{1,9},{9,1},{17,25},{25,17},{2,10},{10... | collective-permute-start | bytes 196616 | tf_op jit(solution)/shard_map/ppermute | solution.py:27
  5.6 1.5 %collective-permute-start.3 = (bf16[2,128,128]{2,1,0:T(8,128)(2,1)S(1)}, bf16[2,128,128]{2,1,0:T(8,128)(2,1)S(1)}, u32[]{:S(2)}, u32[]{:S(2)}) collective-permute-start(bf16[2,128,128]{2,1,0:T(8,128)(2,1)S(1)} %get-tuple-element.27.refs_7_), channel_id=1, source_target_pairs={{0,16},{8,24},{16,0},{24,8},{1,17},{9,25},{17,1},{25,9},{2,18},{10... | collective-permute-start | bytes 196616 | tf_op jit(solution)/shard_map/ppermute | solution.py:27
  7.2 0.5 %collective-permute-start.4 = (bf16[2,128,128]{2,1,0:T(8,128)(2,1)S(1)}, bf16[2,128,128]{2,1,0:T(8,128)(2,1)S(1)}, u32[]{:S(2)}, u32[]{:S(2)}) collective-permute-start(bf16[2,128,128]{2,1,0:T(8,128)(2,1)S(1)} %get-tuple-element.28.refs_8_), channel_id=1, source_target_pairs={{0,24},{8,16},{16,8},{24,0},{1,25},{9,17},{17,9},{25,1},{2,26},{10... | collective-permute-start | bytes 196616 | tf_op jit(solution)/shard_map/ppermute | solution.py:27
  7.6 0.0 collective-permute-done.refs_0_
  7.6 0.0 collective-permute-start.1
  7.6 0.8 %collective-permute-done.2.refs_9_.refs_1_ = bf16[2,128,128]{2,1,0:T(8,128)(2,1)S(1)} collective-permute-done((bf16[2,128,128]{2,1,0:T(8,128)(2,1)S(1)}, bf16[2,128,128]{2,1,0:T(8,128)(2,1)S(1)}, u32[]{:S(2)}, u32[]{:S(2)}) %collective-permute-start.2) | collective-permute-done | bytes 65568 | tf_op jit(solution)/shard_map/ppermute | solution.py:27
  8.4 2.2 %collective-permute-done.3.refs_10_.refs_2_ = bf16[2,128,128]{2,1,0:T(8,128)(2,1)S(1)} collective-permute-done((bf16[2,128,128]{2,1,0:T(8,128)(2,1)S(1)}, bf16[2,128,128]{2,1,0:T(8,128)(2,1)S(1)}, u32[]{:S(2)}, u32[]{:S(2)}) %collective-permute-start.3) | collective-permute-done | bytes 65568 | tf_op jit(solution)/shard_map/ppermute | solution.py:27
  10.6 1.7 %collective-permute-done.4.refs_11_.refs_3_ = bf16[2,128,128]{2,1,0:T(8,128)(2,1)S(1)} collective-permute-done((bf16[2,128,128]{2,1,0:T(8,128)(2,1)S(1)}, bf16[2,128,128]{2,1,0:T(8,128)(2,1)S(1)}, u32[]{:S(2)}, u32[]{:S(2)}) %collective-permute-start.4) | collective-permute-done | bytes 65568 | tf_op jit(solution)/shard_map/ppermute | solution.py:27
  12.3 0.1 collective-permute-start.6
  12.4 0.0 copy-done
  12.4 0.1 shard_map.46
  12.6 0.0 collective-permute-done.1.refs_1_
  12.6 0.1 shard_map.48
  12.7 0.8 %shard_map.49 = (f32[4,32,128]{2,1,0:T(8,128)S(1)}, bf16[4,32,128]{2,1,0:T(8,128)(2,1)S(1)}) custom-call(bf16[1024,128]{1,0:T(8,128)(2,1)S(1)} %get-tuple-element.19.refs_0_, bf16[512,128]{1,0:T(8,128)(2,1)S(1)} %get-tuple-element.20.refs_1_, bf16[1024,128]{1,0:T(8,128)(2,1)S(1)} %get-tuple-element.22.refs_2_, ...), custom_call_target="tpu_custom_call" | custom-call | flops 268435456 | bytes 1048576 | tf_op jit(solution)/shard_map/pallas_call | solution.py:187
  13.6 2.7 %collective-permute-start.5 = (bf16[4,32,128]{2,1,0:T(8,128)(2,1)S(1)}, bf16[4,32,128]{2,1,0:T(8,128)(2,1)S(1)}, u32[]{:S(2)}, u32[]{:S(2)}) collective-permute-start(bf16[4,32,128]{2,1,0:T(8,128)(2,1)S(1)} %get-tuple-element.30), channel_id=1, source_target_pairs={{0,2},{1,3},{2,0},{3,1},{4,6},{5,7},{6,4},{7,5},{8,10},{9,11},{10,... | collective-permute-start | bytes 98312 | tf_op jit(solution)/shard_map/ppermute | solution.py:19
  16.2 0.0 collective-permute-done.6.refs_9_
  16.2 0.8 %shard_map.51 = (f32[4,32,128]{2,1,0:T(8,128)S(1)}, bf16[4,32,128]{2,1,0:T(8,128)(2,1)S(1)}) custom-call(bf16[1024,128]{1,0:T(8,128)(2,1)S(1)} %get-tuple-element.19.refs_0_, bf16[512,128]{1,0:T(8,128)(2,1)S(1)} %get-tuple-element.20.refs_1_, bf16[1024,128]{1,0:T(8,128)(2,1)S(1)} %get-tuple-element.22.refs_2_, ...), custom_call_target="tpu_custom_call" | custom-call | flops 268435456 | bytes 1048576 | tf_op jit(solution)/shard_map/pallas_call | solution.py:187
  17.1 0.4 %collective-permute-start.7 = (bf16[4,32,128]{2,1,0:T(8,128)(2,1)S(1)}, bf16[4,32,128]{2,1,0:T(8,128)(2,1)S(1)}, u32[]{:S(2)}, u32[]{:S(2)}) collective-permute-start(bf16[4,32,128]{2,1,0:T(8,128)(2,1)S(1)} %get-tuple-element.32), channel_id=1, source_target_pairs={{0,2},{1,3},{2,0},{3,1},{4,6},{5,7},{6,4},{7,5},{8,10},{9,11},{10,... | collective-permute-start | bytes 98312 | tf_op jit(solution)/shard_map/ppermute | solution.py:19
  17.5 1.4 %collective-permute-done.5.refs_1_ = bf16[4,32,128]{2,1,0:T(8,128)(2,1)S(1)} collective-permute-done((bf16[4,32,128]{2,1,0:T(8,128)(2,1)S(1)}, bf16[4,32,128]{2,1,0:T(8,128)(2,1)S(1)}, u32[]{:S(2)}, u32[]{:S(2)}) %collective-permute-start.5) | collective-permute-done | bytes 32800 | tf_op jit(solution)/shard_map/ppermute | solution.py:19
  18.9 3.3 %collective-permute-done.7.refs_3_ = bf16[4,32,128]{2,1,0:T(8,128)(2,1)S(1)} collective-permute-done((bf16[4,32,128]{2,1,0:T(8,128)(2,1)S(1)}, bf16[4,32,128]{2,1,0:T(8,128)(2,1)S(1)}, u32[]{:S(2)}, u32[]{:S(2)}) %collective-permute-start.7) | collective-permute-done | bytes 32800 | tf_op jit(solution)/shard_map/ppermute | solution.py:19
  22.2 0.6 %shard_map.52 = bf16[2,4,32,128]{3,2,1,0:T(8,128)(2,1)} custom-call(f32[4,32,128]{2,1,0:T(8,128)S(1)} %get-tuple-element.29.refs_0_, bf16[4,32,128]{2,1,0:T(8,128)(2,1)S(1)} %collective-permute-done.5.refs_1_, f32[4,32,128]{2,1,0:T(8,128)S(1)} %get-tuple-element.31.refs_2_, bf16[4,32,128]{2,1,0:T(8,128)(2,1)S(1)} %collective-permute-done.7.refs_3_), custom_call_target="tpu_custom_call" | custom-call | bytes 1048576 | tf_op jit(solution)/shard_map/pallas_call | solution.py:187
  (1 shorter events, 0.0 us)
Async XLA Ops:
  1.0 11.4 %copy-start = (bf16[8,128,128]{2,1,0:T(8,128)(2,1)S(1)}, bf16[8,128,128]{2,1,0:T(8,128)(2,1)}, u32[]{:S(2)}) copy-start(bf16[8,128,128]{2,1,0:T(8,128)(2,1)} %vec_hbm.1) | copy-start | bytes 786436
  1.1 6.6 %collective-permute-start = (bf16[4,128,128]{2,1,0:T(8,128)(2,1)S(1)}, bf16[4,128,128]{2,1,0:T(8,128)(2,1)S(1)}, u32[]{:S(2)}, u32[]{:S(2)}) collective-permute-start(bf16[4,128,128]{2,1,0:T(8,128)(2,1)S(1)} %get-tuple-element.21), channel_id=1, source_target_pairs={{0,1},{1,0},{2,3},{3,2},{4,5},{5,4},{6,7},{7,6},{8,9},{9,8},{10,11... | collective-permute-start | bytes 393224 | tf_op jit(solution)/shard_map/ppermute | solution.py:19
  4.1 4.3 %collective-permute-start.2 = (bf16[2,128,128]{2,1,0:T(8,128)(2,1)S(1)}, bf16[2,128,128]{2,1,0:T(8,128)(2,1)S(1)}, u32[]{:S(2)}, u32[]{:S(2)}) collective-permute-start(bf16[2,128,128]{2,1,0:T(8,128)(2,1)S(1)} %get-tuple-element.26.refs_6_), channel_id=1, source_target_pairs={{0,8},{8,0},{16,24},{24,16},{1,9},{9,1},{17,25},{25,17},{2,10},{10... | collective-permute-start | bytes 196616 | tf_op jit(solution)/shard_map/ppermute | solution.py:27
  5.6 5.0 %collective-permute-start.3 = (bf16[2,128,128]{2,1,0:T(8,128)(2,1)S(1)}, bf16[2,128,128]{2,1,0:T(8,128)(2,1)S(1)}, u32[]{:S(2)}, u32[]{:S(2)}) collective-permute-start(bf16[2,128,128]{2,1,0:T(8,128)(2,1)S(1)} %get-tuple-element.27.refs_7_), channel_id=1, source_target_pairs={{0,16},{8,24},{16,0},{24,8},{1,17},{9,25},{17,1},{25,9},{2,18},{10... | collective-permute-start | bytes 196616 | tf_op jit(solution)/shard_map/ppermute | solution.py:27
  7.2 5.2 %collective-permute-start.4 = (bf16[2,128,128]{2,1,0:T(8,128)(2,1)S(1)}, bf16[2,128,128]{2,1,0:T(8,128)(2,1)S(1)}, u32[]{:S(2)}, u32[]{:S(2)}) collective-permute-start(bf16[2,128,128]{2,1,0:T(8,128)(2,1)S(1)} %get-tuple-element.28.refs_8_), channel_id=1, source_target_pairs={{0,24},{8,16},{16,8},{24,0},{1,25},{9,17},{17,9},{25,1},{2,26},{10... | collective-permute-start | bytes 196616 | tf_op jit(solution)/shard_map/ppermute | solution.py:27
  7.6 4.9 %collective-permute-start.1 = (bf16[4,128,128]{2,1,0:T(8,128)(2,1)S(1)}, bf16[4,128,128]{2,1,0:T(8,128)(2,1)S(1)}, u32[]{:S(2)}, u32[]{:S(2)}) collective-permute-start(bf16[4,128,128]{2,1,0:T(8,128)(2,1)S(1)} %collective-permute-done.refs_0_), channel_id=1, source_target_pairs={{0,4},{4,0},{1,5},{5,1},{2,6},{6,2},{3,7},{7,3},{8,12},{12,8},{9,1... | collective-permute-start | bytes 393224 | tf_op jit(solution)/shard_map/ppermute | solution.py:23
  12.3 3.9 %collective-permute-start.6 = (bf16[4,128,128]{2,1,0:T(8,128)(2,1)S(1)}, bf16[4,128,128]{2,1,0:T(8,128)(2,1)S(1)}, u32[]{:S(2)}, u32[]{:S(2)}) collective-permute-start(bf16[4,128,128]{2,1,0:T(8,128)(2,1)S(1)} %shard_map.50), channel_id=1, source_target_pairs={{0,4},{4,0},{1,5},{5,1},{2,6},{6,2},{3,7},{7,3},{8,12},{12,8},{9,1... | collective-permute-start | bytes 393224 | tf_op jit(solution)/shard_map/ppermute | solution.py:23
  13.6 5.3 %collective-permute-start.5 = (bf16[4,32,128]{2,1,0:T(8,128)(2,1)S(1)}, bf16[4,32,128]{2,1,0:T(8,128)(2,1)S(1)}, u32[]{:S(2)}, u32[]{:S(2)}) collective-permute-start(bf16[4,32,128]{2,1,0:T(8,128)(2,1)S(1)} %get-tuple-element.30), channel_id=1, source_target_pairs={{0,2},{1,3},{2,0},{3,1},{4,6},{5,7},{6,4},{7,5},{8,10},{9,11},{10,... | collective-permute-start | bytes 98312 | tf_op jit(solution)/shard_map/ppermute | solution.py:19
  17.1 5.1 %collective-permute-start.7 = (bf16[4,32,128]{2,1,0:T(8,128)(2,1)S(1)}, bf16[4,32,128]{2,1,0:T(8,128)(2,1)S(1)}, u32[]{:S(2)}, u32[]{:S(2)}) collective-permute-start(bf16[4,32,128]{2,1,0:T(8,128)(2,1)S(1)} %get-tuple-element.32), channel_id=1, source_target_pairs={{0,2},{1,3},{2,0},{3,1},{4,6},{5,7},{6,4},{7,5},{8,10},{9,11},{10,... | collective-permute-start | bytes 98312 | tf_op jit(solution)/shard_map/ppermute | solution.py:19

commit v6 on v4

--- a/solution.py
+++ b/solution.py
@@ -18,6 +18,12 @@
 
 def swap_virt(array, step):
     return lax.ppermute(array, "virt", [(d, d ^ step) for d in range(lax.axis_size("virt"))])
+
+
+def move_virt(array, step, up):
+    size = lax.axis_size("virt")
+    low = [d for d in range(size) if not d & step]
+    return lax.ppermute(array, "virt", [(d, d + step) if up else (d + step, d) for d in low])
 
 
 def swap_core(array):
@@ -132,7 +138,9 @@
 
 def group_kernel(chunks, steps, *refs):
     ready, (gate_ref, same_ref, cross_ref), refs = refs[:4], refs[4:7], refs[7:]
-    got_refs, part_refs, inner_ref = refs[: len(steps)], refs[len(steps) : -1], refs[-1]
+    got_refs, refs = refs[: len(steps)], refs[len(steps) :]
+    joined = len(refs) > chunks + 1
+    part_refs, inner_ref = refs[joined : joined + chunks], refs[-1]
     sources = []
     for step, got_ref in zip(steps, got_refs):
         if step:
@@ -143,6 +151,9 @@
         sources.append((cross_ref[step], partners[1], gate_ref[CHIPS + step]))
     outs = [[(ref, n) for ref in part_refs] for n in range(len(sources))]
     products(ready, inner_ref, sources, outs)
+    if joined:
+        refs[-3][...] = refs[0][...]
+        refs[-2][...] = part_refs[1][...]
 
 
 def whole_kernel(*refs):
@@ -157,16 +168,16 @@
     lax.fori_loop(0, kept_ref.shape[0] // 2, two, 0)
 
 
-def finish_kernel(groups, chunks, *refs):
-    out_ref = refs[-1]
-    for group, steps in enumerate(groups):
-        terms = refs[group * chunks : (group + 1) * chunks]
+def add_kernel(own_ref, down_ref, *refs):
+    refs[-1][...] = own_ref[...] + down_ref[...].astype(F32)
+
+
+def finish_kernel(*refs):
+    total_refs, up_refs, out_ref = refs[: len(GROUPS)], refs[len(GROUPS) : -1], refs[-1]
+    for steps, total_ref, up_ref in zip(GROUPS, total_refs, up_refs):
         for n in range(2 * len(steps)):
-            total = terms[0][n]
-            for term in terms[1:]:
-                total = total + term[n].astype(F32)
             first, second = slot(n % 2, steps[n // 2])
-            out_ref[first, second] = total.astype(BF16)
+            out_ref[first, second] = (total_ref[n] + up_ref[n].astype(F32)).astype(BF16)
 
 
 def vmem_specs(count):
@@ -215,7 +226,7 @@
         return 2 * count * depth * slab * slab
 
     near = swap_virt(vectors, 1)
-    if (firsts, seconds, chips, cores) == (2, CHIPS, CHIPS, 2):
+    if (firsts, seconds, chips, cores, virt) == (2, CHIPS, CHIPS, 2, 4):
         half_blocks = shaped(BF16, CHIPS, slab, slab)
         same, cross, gates = kernel(
             mask_split_kernel,
@@ -236,21 +247,30 @@
         got = {step: swap_chip(block, step) for step, block in zip(STEPS, packed)}
         got[0] = other
         ready = kernel(turn, arranged, (vectors,)) + kernel(turn, arranged, (near,))
-        finished = []
+        owned, down, leaving = [], [], []
         for steps in GROUPS:
-            part = kernel(
+            count = 2 * len(steps)
+            own, sending, *leaving = kernel(
                 functools.partial(group_kernel, chunks, steps),
-                parts(2 * len(steps)),
-                (*ready, gates, same, cross, *[got[step] for step in steps]),
-                scratch=[inner(2 * len(steps))],
-                flops=work(2 * len(steps)),
+                parts(count) + [shaped(BF16, count, rows, slab)] * (2 * len(leaving)),
+                (*ready, gates, same, cross, *[got[step] for step in steps], *leaving),
+                scratch=[inner(count)],
+                flops=work(count),
             )
-            finished += sent(part)
-        (out,) = kernel(
-            functools.partial(finish_kernel, GROUPS, chunks),
-            [shaped(BF16, firsts, seconds, rows, slab)],
-            finished,
-        )
+            owned.append(own)
+            down.append(move_virt(sending, 2, False))
+            leaving = leaving or [sending]
+        up = [move_virt(sending, 2, True) for sending in leaving]
+        totals = []
+        for own, arrived in zip(owned, down):
+            totals += kernel(
+                add_kernel,
+                [shaped(F32, *own.shape)],
+                (own, arrived, *totals),
+                spaces=[pltpu.VMEM] * 2 + [pl.ANY] * len(totals),
+                flops=work(pairs),
+            )
+        (out,) = kernel(finish_kernel, [shaped(BF16, firsts, seconds, rows, slab)], (*totals, *up))
         return out
     kept, gates = kernel(
         mask_whole_kernel,

time: 21.5 us -> 24.7 us (1.15)
  starting transfers between devices: 10.1 us -> 16 us
  waiting for transfers between devices: 7.43 us -> 4.66 us
    ppermute x0 -> x4, starting transfers between devices: none -> 9.32 us  [move_virt(): lax.ppermute(array, 'virt', [(d, d + step) if up else (d + step, d) for d...]
    ppermute x3 -> x1, waiting for transfers between devices: 4.58 us -> 0.28 us  [swap_virt(): lax.ppermute(array, 'virt', [(d, d ^ step) for d in range(lax.axis_size('...]
    ppermute x3 -> x1, starting transfers between devices: 6.49 us -> 3.02 us  [swap_virt(): lax.ppermute(array, 'virt', [(d, d ^ step) for d in range(lax.axis_size('...]
    ppermute x0 -> x4, waiting for transfers between devices: none -> 1.53 us  [move_virt(): lax.ppermute(array, 'virt', [(d, d + step) if up else (d + step, d) for d...]
    pallas_call x7 -> x9, Pallas kernels: 3.72 us -> 3.75 us  [kernel(): pl.pallas_call(body, out_shape=outs, in_specs=[pl.BlockSpec(memory_space=...]
  transfers between devices with their start and end apart: 7 -> 9, of which waited for: 5 -> 5; matrix products, arithmetic and copies ran while one was open for 0% -> 0% of each run, Pallas kernels for 14% -> 13%
where the time goes in v6:
time: 24.7 us; the launch traced here: 24.5 us
  starting transfers between devices  16 us (65%)
  waiting for transfers between devices  4.66 us (19%)
  Pallas kernels  3.75 us (15%)
    ppermute x4, starting transfers between devices, move_virt(): lax.ppermute(array, 'virt', [(d, d + step) if up else (d + step, d) for d...  9.32 us
    pallas_call x9, Pallas kernels, kernel(): pl.pallas_call(body, out_shape=outs, in_specs=[pl.BlockSpec(memory_space=...  3.75 us
    ppermute x3, starting transfers between devices, swap_chip(): lax.ppermute(array, 'occi', [(d, d ^ step) for d in range(lax.axis_size('...  3.55 us
    ppermute x1, starting transfers between devices, swap_virt(): lax.ppermute(array, 'virt', [(d, d ^ step) for d in range(lax.axis_size('...  3.02 us
    ppermute x4, waiting for transfers between devices, move_virt(): lax.ppermute(array, 'virt', [(d, d + step) if up else (d + step, d) for d...  1.53 us
    ppermute x3, waiting for transfers between devices, swap_chip(): lax.ppermute(array, 'occi', [(d, d ^ step) for d in range(lax.axis_size('...  1.52 us
    ppermute x1, waiting for transfers between devices, swap_core(): return lax.ppermute(array, 'occj', [(0, 1), (1, 0)])  1.33 us
  transfers between devices with their start and end apart: 9, of which 5 were waited for; matrix products, arithmetic and copies ran while one was open for 0% of the time, Pallas kernels for 13%

profile of v6, /device:TPU:0, one launch (start us, length us, event | category | flops | bytes accessed | tf_op | source)
XLA Modules:
  0.0 24.5 jit_solution(10106508838843943690)
XLA Ops:
  0.0 3.0 %collective-permute-start = (bf16[8,128,128]{2,1,0:T(8,128)(2,1)}, bf16[8,128,128]{2,1,0:T(8,128)(2,1)S(1)}, u32[]{:S(2)}, u32[]{:S(2)}) collective-permute-start(bf16[8,128,128]{2,1,0:T(8,128)(2,1)} %vec_ref.1), channel_id=1, source_target_pairs={{0,1},{1,0},{2,3},{3,2},{4,5},{5,4},{6,7},{7,6},{8,9},{9,8},{10,11... | collective-permute-start | bytes 786440 | tf_op jit(solution)/shard_map/ppermute | solution.py:20
  3.0 1.1 %shard_map.48 = (bf16[4,128,128]{2,1,0:T(8,128)(2,1)S(1)}, bf16[4,128,128]{2,1,0:T(8,128)(2,1)S(1)}, f32[8,8,128]{2,1,0:T(8,128)S(1)}) custom-call(s32[2,2,2,4]{3,2,1,0:T(2,128)} %bitcast.1, s32[2,4]{1,0:T(2,128)} %pair_hbm.1, bf16[2,4,128,128]{3,2,1,0:T(8,128)(2,1)} %amp_hbm.1), custom_call_target="tpu_custom_call" | custom-call | bytes 1048576 | tf_op jit(solution)/shard_map/pallas_call | solution.py:193
  4.1 0.1 collective-permute-start.1
  4.2 1.3 %collective-permute-done.1.other_ref.refs_7_ = bf16[4,128,128]{2,1,0:T(8,128)(2,1)S(1)} collective-permute-done((bf16[4,128,128]{2,1,0:T(8,128)(2,1)S(1)}, bf16[4,128,128]{2,1,0:T(8,128)(2,1)S(1)}, u32[]{:S(2)}, u32[]{:S(2)}) %collective-permute-start.1) | collective-permute-done | bytes 131104 | tf_op jit(solution)/shard_map/ppermute | solution.py:30
  5.6 2.5 %collective-permute-start.2 = (bf16[2,128,128]{2,1,0:T(8,128)(2,1)S(1)}, bf16[2,128,128]{2,1,0:T(8,128)(2,1)S(1)}, u32[]{:S(2)}, u32[]{:S(2)}) collective-permute-start(bf16[2,128,128]{2,1,0:T(8,128)(2,1)S(1)} %get-tuple-element.28), channel_id=1, source_target_pairs={{0,24},{8,16},{16,8},{24,0},{1,25},{9,17},{17,9},{25,1},{2,26},{10... | collective-permute-start | bytes 196616 | tf_op jit(solution)/shard_map/ppermute | solution.py:34
  8.1 0.5 %collective-permute-start.4 = (bf16[2,128,128]{2,1,0:T(8,128)(2,1)S(1)}, bf16[2,128,128]{2,1,0:T(8,128)(2,1)S(1)}, u32[]{:S(2)}, u32[]{:S(2)}) collective-permute-start(bf16[2,128,128]{2,1,0:T(8,128)(2,1)S(1)} %get-tuple-element.31), channel_id=1, source_target_pairs={{0,8},{8,0},{16,24},{24,16},{1,9},{9,1},{17,25},{25,17},{2,10},{10... | collective-permute-start | bytes 196616 | tf_op jit(solution)/shard_map/ppermute | solution.py:34
  8.6 0.5 %collective-permute-start.5 = (bf16[2,128,128]{2,1,0:T(8,128)(2,1)S(1)}, bf16[2,128,128]{2,1,0:T(8,128)(2,1)S(1)}, u32[]{:S(2)}, u32[]{:S(2)}) collective-permute-start(bf16[2,128,128]{2,1,0:T(8,128)(2,1)S(1)} %get-tuple-element.32), channel_id=1, source_target_pairs={{0,16},{8,24},{16,0},{24,8},{1,17},{9,25},{17,1},{25,9},{2,18},{10... | collective-permute-start | bytes 196616 | tf_op jit(solution)/shard_map/ppermute | solution.py:34
  9.1 0.1 shard_map.46
  9.3 0.3 %collective-permute-done.vec_ref = bf16[8,128,128]{2,1,0:T(8,128)(2,1)S(1)} collective-permute-done((bf16[8,128,128]{2,1,0:T(8,128)(2,1)}, bf16[8,128,128]{2,1,0:T(8,128)(2,1)S(1)}, u32[]{:S(2)}, u32[]{:S(2)}) %collective-permute-start) | collective-permute-done | bytes 262176 | tf_op jit(solution)/shard_map/ppermute | solution.py:20
  9.5 0.1 shard_map.47
  9.7 1.5 %collective-permute-done.2.refs_8_ = bf16[2,128,128]{2,1,0:T(8,128)(2,1)S(1)} collective-permute-done((bf16[2,128,128]{2,1,0:T(8,128)(2,1)S(1)}, bf16[2,128,128]{2,1,0:T(8,128)(2,1)S(1)}, u32[]{:S(2)}, u32[]{:S(2)}) %collective-permute-start.2) | collective-permute-done | bytes 65568 | tf_op jit(solution)/shard_map/ppermute | solution.py:34
  11.2 0.8 %shard_map.50 = (f32[4,32,128]{2,1,0:T(8,128)S(1)}, bf16[4,32,128]{2,1,0:T(8,128)(2,1)S(1)}) custom-call(bf16[1024,128]{1,0:T(8,128)(2,1)S(1)} %get-tuple-element.21.refs_0_, bf16[512,128]{1,0:T(8,128)(2,1)S(1)} %get-tuple-element.22.refs_1_, bf16[1024,128]{1,0:T(8,128)(2,1)S(1)} %get-tuple-element.23.refs_2_, ...), custom_call_target="tpu_custom_call" | custom-call | flops 268435456 | bytes 1048576 | tf_op jit(solution)/shard_map/pallas_call | solution.py:193
  12.0 1.3 %collective-permute-start.3 = (bf16[4,32,128]{2,1,0:T(8,128)(2,1)S(1)}, bf16[4,32,128]{2,1,0:T(8,128)(2,1)S(1)}, u32[]{:S(2)}, u32[]{:S(2)}) collective-permute-start(bf16[4,32,128]{2,1,0:T(8,128)(2,1)S(1)} %get-tuple-element.30.refs_9_), channel_id=1, source_target_pairs={{2,0},{3,1},{6,4},{7,5},{10,8},{11,9},{14,12},{15,13},{18,16},{19,... | collective-permute-start | bytes 98312 | tf_op jit(solution)/shard_map/ppermute | solution.py:26
  13.3 0.0 collective-permute-done.4.refs_7_
  13.4 0.0 collective-permute-done.5.refs_8_
  13.4 0.9 %shard_map.52 = (f32[4,32,128]{2,1,0:T(8,128)S(1)}, bf16[4,32,128]{2,1,0:T(8,128)(2,1)S(1)}, bf16[4,32,128]{2,1,0:T(8,128)(2,1)S(1)}, bf16[4,32,128]{2,1,0:T(8,128)(2,1)S(1)}) custom-call(bf16[1024,128]{1,0:T(8,128)(2,1)S(1)} %get-tuple-element.21.refs_0_, bf16[512,128]{1,0:T(8,128)(2,1)S(1)} %get-tuple-element.22.refs_1_, ...), custom_call_target="tpu_custom_call" | custom-call | flops 268435456 | bytes 1048576 | tf_op jit(solution)/shard_map/pallas_call | solution.py:193
  14.2 1.3 %collective-permute-start.6 = (bf16[4,32,128]{2,1,0:T(8,128)(2,1)S(1)}, bf16[4,32,128]{2,1,0:T(8,128)(2,1)S(1)}, u32[]{:S(2)}, u32[]{:S(2)}) collective-permute-start(bf16[4,32,128]{2,1,0:T(8,128)(2,1)S(1)} %get-tuple-element.34), channel_id=1, source_target_pairs={{2,0},{3,1},{6,4},{7,5},{10,8},{11,9},{14,12},{15,13},{18,16},{19,... | collective-permute-start | bytes 98312 | tf_op jit(solution)/shard_map/ppermute | solution.py:26
  15.5 5.4 %collective-permute-start.7 = (bf16[4,32,128]{2,1,0:T(8,128)(2,1)S(1)}, bf16[4,32,128]{2,1,0:T(8,128)(2,1)S(1)}, u32[]{:S(2)}, u32[]{:S(2)}) collective-permute-start(bf16[4,32,128]{2,1,0:T(8,128)(2,1)S(1)} %get-tuple-element.35), channel_id=1, source_target_pairs={{0,2},{1,3},{4,6},{5,7},{8,10},{9,11},{12,14},{13,15},{16,18},{17,... | collective-permute-start | bytes 98312 | tf_op jit(solution)/shard_map/ppermute | solution.py:26
  21.0 1.3 %collective-permute-start.8 = (bf16[4,32,128]{2,1,0:T(8,128)(2,1)S(1)}, bf16[4,32,128]{2,1,0:T(8,128)(2,1)S(1)}, u32[]{:S(2)}, u32[]{:S(2)}) collective-permute-start(bf16[4,32,128]{2,1,0:T(8,128)(2,1)S(1)} %get-tuple-element.36), channel_id=1, source_target_pairs={{0,2},{1,3},{4,6},{5,7},{8,10},{9,11},{12,14},{13,15},{16,18},{17,... | collective-permute-start | bytes 98312 | tf_op jit(solution)/shard_map/ppermute | solution.py:26
  22.3 0.0 collective-permute-done.3.down_ref
  22.3 0.0 collective-permute-done.6.down_ref
  22.3 0.2 collective-permute-done.7.refs_2_
  22.6 1.3 %collective-permute-done.8.refs_3_ = bf16[4,32,128]{2,1,0:T(8,128)(2,1)S(1)} collective-permute-done((bf16[4,32,128]{2,1,0:T(8,128)(2,1)S(1)}, bf16[4,32,128]{2,1,0:T(8,128)(2,1)S(1)}, u32[]{:S(2)}, u32[]{:S(2)}) %collective-permute-start.8) | collective-permute-done | bytes 32800 | tf_op jit(solution)/shard_map/ppermute | solution.py:26
  23.9 0.6 %shard_map.54 = bf16[2,4,32,128]{3,2,1,0:T(8,128)(2,1)} custom-call(f32[4,32,128]{2,1,0:T(8,128)S(1)} %shard_map.51.refs_0_, f32[4,32,128]{2,1,0:T(8,128)S(1)} %shard_map.53.refs_1_, bf16[4,32,128]{2,1,0:T(8,128)(2,1)S(1)} %collective-permute-done.7.refs_2_, bf16[4,32,128]{2,1,0:T(8,128)(2,1)S(1)} %collective-permute-done.8.refs_3_), custom_call_target="tpu_custom_call" | custom-call | bytes 1048576 | tf_op jit(solution)/shard_map/pallas_call | solution.py:193
  (5 shorter events, 0.0 us)
Async XLA Ops:
  0.0 9.5 %collective-permute-start = (bf16[8,128,128]{2,1,0:T(8,128)(2,1)}, bf16[8,128,128]{2,1,0:T(8,128)(2,1)S(1)}, u32[]{:S(2)}, u32[]{:S(2)}) collective-permute-start(bf16[8,128,128]{2,1,0:T(8,128)(2,1)} %vec_ref.1), channel_id=1, source_target_pairs={{0,1},{1,0},{2,3},{3,2},{4,5},{5,4},{6,7},{7,6},{8,9},{9,8},{10,11... | collective-permute-start | bytes 786440 | tf_op jit(solution)/shard_map/ppermute | solution.py:20
  3.0 6.1 %copy-start = (bf16[8,128,128]{2,1,0:T(8,128)(2,1)S(1)}, bf16[8,128,128]{2,1,0:T(8,128)(2,1)}, u32[]{:S(2)}) copy-start(bf16[8,128,128]{2,1,0:T(8,128)(2,1)} %vec_ref.1) | copy-start | bytes 786436
  4.1 1.4 %collective-permute-start.1 = (bf16[4,128,128]{2,1,0:T(8,128)(2,1)S(1)}, bf16[4,128,128]{2,1,0:T(8,128)(2,1)S(1)}, u32[]{:S(2)}, u32[]{:S(2)}) collective-permute-start(bf16[4,128,128]{2,1,0:T(8,128)(2,1)S(1)} %get-tuple-element.27.refs_6_), channel_id=1, source_target_pairs={{0,4},{4,0},{1,5},{5,1},{2,6},{6,2},{3,7},{7,3},{8,12},{12,8},{9,1... | collective-permute-start | bytes 393224 | tf_op jit(solution)/shard_map/ppermute | solution.py:30
  5.6 5.6 %collective-permute-start.2 = (bf16[2,128,128]{2,1,0:T(8,128)(2,1)S(1)}, bf16[2,128,128]{2,1,0:T(8,128)(2,1)S(1)}, u32[]{:S(2)}, u32[]{:S(2)}) collective-permute-start(bf16[2,128,128]{2,1,0:T(8,128)(2,1)S(1)} %get-tuple-element.28), channel_id=1, source_target_pairs={{0,24},{8,16},{16,8},{24,0},{1,25},{9,17},{17,9},{25,1},{2,26},{10... | collective-permute-start | bytes 196616 | tf_op jit(solution)/shard_map/ppermute | solution.py:34
  8.1 5.3 %collective-permute-start.4 = (bf16[2,128,128]{2,1,0:T(8,128)(2,1)S(1)}, bf16[2,128,128]{2,1,0:T(8,128)(2,1)S(1)}, u32[]{:S(2)}, u32[]{:S(2)}) collective-permute-start(bf16[2,128,128]{2,1,0:T(8,128)(2,1)S(1)} %get-tuple-element.31), channel_id=1, source_target_pairs={{0,8},{8,0},{16,24},{24,16},{1,9},{9,1},{17,25},{25,17},{2,10},{10... | collective-permute-start | bytes 196616 | tf_op jit(solution)/shard_map/ppermute | solution.py:34
  8.6 4.8 %collective-permute-start.5 = (bf16[2,128,128]{2,1,0:T(8,128)(2,1)S(1)}, bf16[2,128,128]{2,1,0:T(8,128)(2,1)S(1)}, u32[]{:S(2)}, u32[]{:S(2)}) collective-permute-start(bf16[2,128,128]{2,1,0:T(8,128)(2,1)S(1)} %get-tuple-element.32), channel_id=1, source_target_pairs={{0,16},{8,24},{16,0},{24,8},{1,17},{9,25},{17,1},{25,9},{2,18},{10... | collective-permute-start | bytes 196616 | tf_op jit(solution)/shard_map/ppermute | solution.py:34
  12.0 10.2 %collective-permute-start.3 = (bf16[4,32,128]{2,1,0:T(8,128)(2,1)S(1)}, bf16[4,32,128]{2,1,0:T(8,128)(2,1)S(1)}, u32[]{:S(2)}, u32[]{:S(2)}) collective-permute-start(bf16[4,32,128]{2,1,0:T(8,128)(2,1)S(1)} %get-tuple-element.30.refs_9_), channel_id=1, source_target_pairs={{2,0},{3,1},{6,4},{7,5},{10,8},{11,9},{14,12},{15,13},{18,16},{19,... | collective-permute-start | bytes 98312 | tf_op jit(solution)/shard_map/ppermute | solution.py:26
  14.2 8.1 %collective-permute-start.6 = (bf16[4,32,128]{2,1,0:T(8,128)(2,1)S(1)}, bf16[4,32,128]{2,1,0:T(8,128)(2,1)S(1)}, u32[]{:S(2)}, u32[]{:S(2)}) collective-permute-start(bf16[4,32,128]{2,1,0:T(8,128)(2,1)S(1)} %get-tuple-element.34), channel_id=1, source_target_pairs={{2,0},{3,1},{6,4},{7,5},{10,8},{11,9},{14,12},{15,13},{18,16},{19,... | collective-permute-start | bytes 98312 | tf_op jit(solution)/shard_map/ppermute | solution.py:26
  15.5 7.0 %collective-permute-start.7 = (bf16[4,32,128]{2,1,0:T(8,128)(2,1)S(1)}, bf16[4,32,128]{2,1,0:T(8,128)(2,1)S(1)}, u32[]{:S(2)}, u32[]{:S(2)}) collective-permute-start(bf16[4,32,128]{2,1,0:T(8,128)(2,1)S(1)} %get-tuple-element.35), channel_id=1, source_target_pairs={{0,2},{1,3},{4,6},{5,7},{8,10},{9,11},{12,14},{13,15},{16,18},{17,... | collective-permute-start | bytes 98312 | tf_op jit(solution)/shard_map/ppermute | solution.py:26
  21.0 2.9 %collective-permute-start.8 = (bf16[4,32,128]{2,1,0:T(8,128)(2,1)S(1)}, bf16[4,32,128]{2,1,0:T(8,128)(2,1)S(1)}, u32[]{:S(2)}, u32[]{:S(2)}) collective-permute-start(bf16[4,32,128]{2,1,0:T(8,128)(2,1)S(1)} %get-tuple-element.36), channel_id=1, source_target_pairs={{0,2},{1,3},{4,6},{5,7},{8,10},{9,11},{12,14},{13,15},{16,18},{17,... | collective-permute-start | bytes 98312 | tf_op jit(solution)/shard_map/ppermute | solution.py:26

commit v7 on v6

--- a/solution.py
+++ b/solution.py
@@ -11,19 +11,13 @@
 SLAB_TILES = 2
 CHIPS = 4
 STEPS = (3, 1, 2)
-GROUPS = ((0, 3), (1, 2))
+GROUPS = ((0, 3, 1), (2,))
 BF16 = jnp.bfloat16
 F32 = jnp.float32
 
 
 def swap_virt(array, step):
     return lax.ppermute(array, "virt", [(d, d ^ step) for d in range(lax.axis_size("virt"))])
-
-
-def move_virt(array, step, up):
-    size = lax.axis_size("virt")
-    low = [d for d in range(size) if not d & step]
-    return lax.ppermute(array, "virt", [(d, d + step) if up else (d + step, d) for d in low])
 
 
 def swap_core(array):
@@ -152,8 +146,9 @@
     outs = [[(ref, n) for ref in part_refs] for n in range(len(sources))]
     products(ready, inner_ref, sources, outs)
     if joined:
-        refs[-3][...] = refs[0][...]
-        refs[-2][...] = part_refs[1][...]
+        count = refs[0].shape[0]
+        refs[-2][:count] = refs[0][...]
+        refs[-2][count:] = part_refs[1][...]
 
 
 def whole_kernel(*refs):
@@ -168,16 +163,14 @@
     lax.fori_loop(0, kept_ref.shape[0] // 2, two, 0)
 
 
-def add_kernel(own_ref, down_ref, *refs):
-    refs[-1][...] = own_ref[...] + down_ref[...].astype(F32)
-
-
 def finish_kernel(*refs):
-    total_refs, up_refs, out_ref = refs[: len(GROUPS)], refs[len(GROUPS) : -1], refs[-1]
-    for steps, total_ref, up_ref in zip(GROUPS, total_refs, up_refs):
+    own_refs, got_ref, out_ref = refs[: len(GROUPS)], refs[-2], refs[-1]
+    at = 0
+    for steps, own_ref in zip(GROUPS, own_refs):
         for n in range(2 * len(steps)):
             first, second = slot(n % 2, steps[n // 2])
-            out_ref[first, second] = (total_ref[n] + up_ref[n].astype(F32)).astype(BF16)
+            out_ref[first, second] = (own_ref[n] + got_ref[at].astype(F32)).astype(BF16)
+            at += 1
 
 
 def vmem_specs(count):
@@ -247,30 +240,19 @@
         got = {step: swap_chip(block, step) for step, block in zip(STEPS, packed)}
         got[0] = other
         ready = kernel(turn, arranged, (vectors,)) + kernel(turn, arranged, (near,))
-        owned, down, leaving = [], [], []
+        owned, leaving = [], []
         for steps in GROUPS:
             count = 2 * len(steps)
-            own, sending, *leaving = kernel(
+            own, *leaving = kernel(
                 functools.partial(group_kernel, chunks, steps),
-                parts(count) + [shaped(BF16, count, rows, slab)] * (2 * len(leaving)),
+                parts(count) + [shaped(BF16, pairs, rows, slab)] * len(leaving),
                 (*ready, gates, same, cross, *[got[step] for step in steps], *leaving),
                 scratch=[inner(count)],
                 flops=work(count),
             )
             owned.append(own)
-            down.append(move_virt(sending, 2, False))
-            leaving = leaving or [sending]
-        up = [move_virt(sending, 2, True) for sending in leaving]
-        totals = []
-        for own, arrived in zip(owned, down):
-            totals += kernel(
-                add_kernel,
-                [shaped(F32, *own.shape)],
-                (own, arrived, *totals),
-                spaces=[pltpu.VMEM] * 2 + [pl.ANY] * len(totals),
-                flops=work(pairs),
-            )
-        (out,) = kernel(finish_kernel, [shaped(BF16, firsts, seconds, rows, slab)], (*totals, *up))
+        operands = (*owned, swap_virt(leaving[-1], 2))
+        (out,) = kernel(finish_kernel, [shaped(BF16, firsts, seconds, rows, slab)], operands)
         return out
     kept, gates = kernel(
         mask_whole_kernel,

time: 24.7 us -> 21.9 us (0.89)
  starting transfers between devices: 16 us -> 9.24 us
  waiting for transfers between devices: 4.66 us -> 7.43 us
  Pallas kernels: 3.75 us -> 5.06 us
    ppermute x4 -> x0, starting transfers between devices: 9.32 us -> none  [move_virt(): lax.ppermute(array, 'virt', [(d, d + step) if up else (d + step, d) for d...]
    ppermute x1 -> x2, waiting for transfers between devices: 0.28 us -> 3.44 us  [swap_virt(): lax.ppermute(array, 'virt', [(d, d ^ step) for d in range(lax.axis_size('...]
    ppermute x1 -> x2, starting transfers between devices: 3.02 us -> 5.61 us  [swap_virt(): lax.ppermute(array, 'virt', [(d, d ^ step) for d in range(lax.axis_size('...]
    ppermute x4 -> x0, waiting for transfers between devices: 1.53 us -> none  [move_virt(): lax.ppermute(array, 'virt', [(d, d + step) if up else (d + step, d) for d...]
    pallas_call x9 -> x7, Pallas kernels: 3.75 us -> 5.06 us  [kernel(): pl.pallas_call(body, out_shape=outs, in_specs=[pl.BlockSpec(memory_space=...]
    ppermute x3, waiting for transfers between devices: 1.52 us -> 2.66 us  [swap_chip(): lax.ppermute(array, 'occi', [(d, d ^ step) for d in range(lax.axis_size('...]
  transfers between devices with their start and end apart: 9 -> 6, of which waited for: 5 -> 5; matrix products, arithmetic and copies ran while one was open for 0% -> 0% of each run, Pallas kernels for 13% -> 15%
where the time goes in v7:
time: 21.9 us; the launch traced here: 21.8 us
  starting transfers between devices  9.24 us (42%)
  waiting for transfers between devices  7.43 us (34%)
  Pallas kernels  5.06 us (23%)
    ppermute x2, starting transfers between devices, swap_virt(): lax.ppermute(array, 'virt', [(d, d ^ step) for d in range(lax.axis_size('...  5.61 us
    pallas_call x7, Pallas kernels, kernel(): pl.pallas_call(body, out_shape=outs, in_specs=[pl.BlockSpec(memory_space=...  5.06 us
    ppermute x3, starting transfers between devices, swap_chip(): lax.ppermute(array, 'occi', [(d, d ^ step) for d in range(lax.axis_size('...  3.55 us
    ppermute x2, waiting for transfers between devices, swap_virt(): lax.ppermute(array, 'virt', [(d, d ^ step) for d in range(lax.axis_size('...  3.44 us
    ppermute x3, waiting for transfers between devices, swap_chip(): lax.ppermute(array, 'occi', [(d, d ^ step) for d in range(lax.axis_size('...  2.66 us
    ppermute x1, waiting for transfers between devices, swap_core(): return lax.ppermute(array, 'occj', [(0, 1), (1, 0)])  1.33 us
  transfers between devices with their start and end apart: 6, of which 5 were waited for; matrix products, arithmetic and copies ran while one was open for 0% of the time, Pallas kernels for 15%

profile of v7, /device:TPU:0, one launch (start us, length us, event | category | flops | bytes accessed | tf_op | source)
XLA Modules:
  0.0 21.8 jit_solution(14858218749717850957)
XLA Ops:
  0.0 3.0 %collective-permute-start = (bf16[8,128,128]{2,1,0:T(8,128)(2,1)}, bf16[8,128,128]{2,1,0:T(8,128)(2,1)S(1)}, u32[]{:S(2)}, u32[]{:S(2)}) collective-permute-start(bf16[8,128,128]{2,1,0:T(8,128)(2,1)} %vec_ref.1), channel_id=1, source_target_pairs={{0,1},{1,0},{2,3},{3,2},{4,5},{5,4},{6,7},{7,6},{8,9},{9,8},{10,11... | collective-permute-start | bytes 786440 | tf_op jit(solution)/shard_map/ppermute | solution.py:20
  3.0 0.0 copy-start
  3.0 1.1 %shard_map.48 = (bf16[4,128,128]{2,1,0:T(8,128)(2,1)S(1)}, bf16[4,128,128]{2,1,0:T(8,128)(2,1)S(1)}, f32[8,8,128]{2,1,0:T(8,128)S(1)}) custom-call(s32[2,2,2,4]{3,2,1,0:T(2,128)} %bitcast.1, s32[2,4]{1,0:T(2,128)} %pair_hbm.1, bf16[2,4,128,128]{3,2,1,0:T(8,128)(2,1)} %amp_hbm.1), custom_call_target="tpu_custom_call" | custom-call | bytes 1048576 | tf_op jit(solution)/shard_map/pallas_call | solution.py:186
  4.1 0.1 collective-permute-start.1
  4.2 1.3 %collective-permute-done.1.other_ref.refs_7_ = bf16[4,128,128]{2,1,0:T(8,128)(2,1)S(1)} collective-permute-done((bf16[4,128,128]{2,1,0:T(8,128)(2,1)S(1)}, bf16[4,128,128]{2,1,0:T(8,128)(2,1)S(1)}, u32[]{:S(2)}, u32[]{:S(2)}) %collective-permute-start.1) | collective-permute-done | bytes 131104 | tf_op jit(solution)/shard_map/ppermute | solution.py:24
  5.6 2.5 %collective-permute-start.2 = (bf16[2,128,128]{2,1,0:T(8,128)(2,1)S(1)}, bf16[2,128,128]{2,1,0:T(8,128)(2,1)S(1)}, u32[]{:S(2)}, u32[]{:S(2)}) collective-permute-start(bf16[2,128,128]{2,1,0:T(8,128)(2,1)S(1)} %get-tuple-element.26), channel_id=1, source_target_pairs={{0,24},{8,16},{16,8},{24,0},{1,25},{9,17},{17,9},{25,1},{2,26},{10... | collective-permute-start | bytes 196616 | tf_op jit(solution)/shard_map/ppermute | solution.py:28
  8.1 0.5 %collective-permute-start.3 = (bf16[2,128,128]{2,1,0:T(8,128)(2,1)S(1)}, bf16[2,128,128]{2,1,0:T(8,128)(2,1)S(1)}, u32[]{:S(2)}, u32[]{:S(2)}) collective-permute-start(bf16[2,128,128]{2,1,0:T(8,128)(2,1)S(1)} %get-tuple-element.27), channel_id=1, source_target_pairs={{0,8},{8,0},{16,24},{24,16},{1,9},{9,1},{17,25},{25,17},{2,10},{10... | collective-permute-start | bytes 196616 | tf_op jit(solution)/shard_map/ppermute | solution.py:28
  8.6 0.5 %collective-permute-start.4 = (bf16[2,128,128]{2,1,0:T(8,128)(2,1)S(1)}, bf16[2,128,128]{2,1,0:T(8,128)(2,1)S(1)}, u32[]{:S(2)}, u32[]{:S(2)}) collective-permute-start(bf16[2,128,128]{2,1,0:T(8,128)(2,1)S(1)} %get-tuple-element.29), channel_id=1, source_target_pairs={{0,16},{8,24},{16,0},{24,8},{1,17},{9,25},{17,1},{25,9},{2,18},{10... | collective-permute-start | bytes 196616 | tf_op jit(solution)/shard_map/ppermute | solution.py:28
  9.1 0.0 copy-done
  9.1 0.1 shard_map.46
  9.3 0.3 %collective-permute-done.vec_ref = bf16[8,128,128]{2,1,0:T(8,128)(2,1)S(1)} collective-permute-done((bf16[8,128,128]{2,1,0:T(8,128)(2,1)}, bf16[8,128,128]{2,1,0:T(8,128)(2,1)S(1)}, u32[]{:S(2)}, u32[]{:S(2)}) %collective-permute-start) | collective-permute-done | bytes 262176 | tf_op jit(solution)/shard_map/ppermute | solution.py:20
  9.5 0.1 shard_map.47
  9.7 1.5 %collective-permute-done.2.refs_8_ = bf16[2,128,128]{2,1,0:T(8,128)(2,1)S(1)} collective-permute-done((bf16[2,128,128]{2,1,0:T(8,128)(2,1)S(1)}, bf16[2,128,128]{2,1,0:T(8,128)(2,1)S(1)}, u32[]{:S(2)}, u32[]{:S(2)}) %collective-permute-start.2) | collective-permute-done | bytes 65568 | tf_op jit(solution)/shard_map/ppermute | solution.py:28
  11.2 1.1 %collective-permute-done.3.refs_9_ = bf16[2,128,128]{2,1,0:T(8,128)(2,1)S(1)} collective-permute-done((bf16[2,128,128]{2,1,0:T(8,128)(2,1)S(1)}, bf16[2,128,128]{2,1,0:T(8,128)(2,1)S(1)}, u32[]{:S(2)}, u32[]{:S(2)}) %collective-permute-start.3) | collective-permute-done | bytes 65568 | tf_op jit(solution)/shard_map/ppermute | solution.py:28
  12.3 1.8 %shard_map.50 = (f32[6,32,128]{2,1,0:T(8,128)S(1)}, bf16[6,32,128]{2,1,0:T(8,128)(2,1)S(1)}) custom-call(bf16[1024,128]{1,0:T(8,128)(2,1)S(1)} %get-tuple-element.19.refs_0_, bf16[512,128]{1,0:T(8,128)(2,1)S(1)} %get-tuple-element.20.refs_1_, bf16[1024,128]{1,0:T(8,128)(2,1)S(1)} %get-tuple-element.21.refs_2_, ...), custom_call_target="tpu_custom_call" | custom-call | flops 402653184 | bytes 1048576 | tf_op jit(solution)/shard_map/pallas_call | solution.py:186
  14.1 0.0 collective-permute-done.4.refs_7_
  14.2 1.2 %shard_map.51 = (f32[2,32,128]{2,1,0:T(8,128)S(1)}, bf16[2,32,128]{2,1,0:T(8,128)(2,1)}, bf16[8,32,128]{2,1,0:T(8,128)(2,1)S(1)}) custom-call(bf16[1024,128]{1,0:T(8,128)(2,1)S(1)} %get-tuple-element.19.refs_0_, bf16[512,128]{1,0:T(8,128)(2,1)S(1)} %get-tuple-element.20.refs_1_, bf16[1024,128]{1,0:T(8,128)(2,1)S(1)} %get-tuple-element.21.refs_2_, ...), custom_call_target="tpu_custom_call" | custom-call | flops 134217728 | bytes 1048576 | tf_op jit(solution)/shard_map/pallas_call | solution.py:186
  15.4 2.6 %collective-permute-start.5 = (bf16[8,32,128]{2,1,0:T(8,128)(2,1)S(1)}, bf16[8,32,128]{2,1,0:T(8,128)(2,1)S(1)}, u32[]{:S(2)}, u32[]{:S(2)}) collective-permute-start(bf16[8,32,128]{2,1,0:T(8,128)(2,1)S(1)} %get-tuple-element.32), channel_id=1, source_target_pairs={{0,2},{1,3},{2,0},{3,1},{4,6},{5,7},{6,4},{7,5},{8,10},{9,11},{10,... | collective-permute-start | bytes 196616 | tf_op jit(solution)/shard_map/ppermute | solution.py:20
  18.0 3.2 %collective-permute-done.5.refs_2_ = bf16[8,32,128]{2,1,0:T(8,128)(2,1)S(1)} collective-permute-done((bf16[8,32,128]{2,1,0:T(8,128)(2,1)S(1)}, bf16[8,32,128]{2,1,0:T(8,128)(2,1)S(1)}, u32[]{:S(2)}, u32[]{:S(2)}) %collective-permute-start.5) | collective-permute-done | bytes 65568 | tf_op jit(solution)/shard_map/ppermute | solution.py:20
  21.1 0.6 %shard_map.52 = bf16[2,4,32,128]{3,2,1,0:T(8,128)(2,1)} custom-call(f32[6,32,128]{2,1,0:T(8,128)S(1)} %get-tuple-element.28.refs_0_, f32[2,32,128]{2,1,0:T(8,128)S(1)} %get-tuple-element.31.refs_1_, bf16[8,32,128]{2,1,0:T(8,128)(2,1)S(1)} %collective-permute-done.5.refs_2_), custom_call_target="tpu_custom_call" | custom-call | bytes 1048576 | tf_op jit(solution)/shard_map/pallas_call | solution.py:186
  (1 shorter events, 0.0 us)
Async XLA Ops:
  0.0 9.5 %collective-permute-start = (bf16[8,128,128]{2,1,0:T(8,128)(2,1)}, bf16[8,128,128]{2,1,0:T(8,128)(2,1)S(1)}, u32[]{:S(2)}, u32[]{:S(2)}) collective-permute-start(bf16[8,128,128]{2,1,0:T(8,128)(2,1)} %vec_ref.1), channel_id=1, source_target_pairs={{0,1},{1,0},{2,3},{3,2},{4,5},{5,4},{6,7},{7,6},{8,9},{9,8},{10,11... | collective-permute-start | bytes 786440 | tf_op jit(solution)/shard_map/ppermute | solution.py:20
  3.0 6.1 %copy-start = (bf16[8,128,128]{2,1,0:T(8,128)(2,1)S(1)}, bf16[8,128,128]{2,1,0:T(8,128)(2,1)}, u32[]{:S(2)}) copy-start(bf16[8,128,128]{2,1,0:T(8,128)(2,1)} %vec_ref.1) | copy-start | bytes 786436
  4.1 1.4 %collective-permute-start.1 = (bf16[4,128,128]{2,1,0:T(8,128)(2,1)S(1)}, bf16[4,128,128]{2,1,0:T(8,128)(2,1)S(1)}, u32[]{:S(2)}, u32[]{:S(2)}) collective-permute-start(bf16[4,128,128]{2,1,0:T(8,128)(2,1)S(1)} %get-tuple-element.25.refs_6_), channel_id=1, source_target_pairs={{0,4},{4,0},{1,5},{5,1},{2,6},{6,2},{3,7},{7,3},{8,12},{12,8},{9,1... | collective-permute-start | bytes 393224 | tf_op jit(solution)/shard_map/ppermute | solution.py:24
  5.6 5.6 %collective-permute-start.2 = (bf16[2,128,128]{2,1,0:T(8,128)(2,1)S(1)}, bf16[2,128,128]{2,1,0:T(8,128)(2,1)S(1)}, u32[]{:S(2)}, u32[]{:S(2)}) collective-permute-start(bf16[2,128,128]{2,1,0:T(8,128)(2,1)S(1)} %get-tuple-element.26), channel_id=1, source_target_pairs={{0,24},{8,16},{16,8},{24,0},{1,25},{9,17},{17,9},{25,1},{2,26},{10... | collective-permute-start | bytes 196616 | tf_op jit(solution)/shard_map/ppermute | solution.py:28
  8.1 4.3 %collective-permute-start.3 = (bf16[2,128,128]{2,1,0:T(8,128)(2,1)S(1)}, bf16[2,128,128]{2,1,0:T(8,128)(2,1)S(1)}, u32[]{:S(2)}, u32[]{:S(2)}) collective-permute-start(bf16[2,128,128]{2,1,0:T(8,128)(2,1)S(1)} %get-tuple-element.27), channel_id=1, source_target_pairs={{0,8},{8,0},{16,24},{24,16},{1,9},{9,1},{17,25},{25,17},{2,10},{10... | collective-permute-start | bytes 196616 | tf_op jit(solution)/shard_map/ppermute | solution.py:28
  8.6 5.5 %collective-permute-start.4 = (bf16[2,128,128]{2,1,0:T(8,128)(2,1)S(1)}, bf16[2,128,128]{2,1,0:T(8,128)(2,1)S(1)}, u32[]{:S(2)}, u32[]{:S(2)}) collective-permute-start(bf16[2,128,128]{2,1,0:T(8,128)(2,1)S(1)} %get-tuple-element.29), channel_id=1, source_target_pairs={{0,16},{8,24},{16,0},{24,8},{1,17},{9,25},{17,1},{25,9},{2,18},{10... | collective-permute-start | bytes 196616 | tf_op jit(solution)/shard_map/ppermute | solution.py:28
  15.4 5.8 %collective-permute-start.5 = (bf16[8,32,128]{2,1,0:T(8,128)(2,1)S(1)}, bf16[8,32,128]{2,1,0:T(8,128)(2,1)S(1)}, u32[]{:S(2)}, u32[]{:S(2)}) collective-permute-start(bf16[8,32,128]{2,1,0:T(8,128)(2,1)S(1)} %get-tuple-element.32), channel_id=1, source_target_pairs={{0,2},{1,3},{2,0},{3,1},{4,6},{5,7},{6,4},{7,5},{8,10},{9,11},{10,... | collective-permute-start | bytes 196616 | tf_op jit(solution)/shard_map/ppermute | solution.py:20

commit v8 on v4

--- a/solution.py
+++ b/solution.py
@@ -94,7 +94,7 @@
     for q in range(vectors):
         turned_ref[q * slab : (q + 1) * slab] = vec_ref[q].astype(F32).T.astype(BF16)
         for chunk in range(chunks):
-            start = pl.multiple_of((me ^ (2 * chunk)) * rows, rows)
+            start = pl.multiple_of((me ^ chunk) * rows, rows)
             low = (q * chunks + chunk) * rows
             left_ref[low : low + rows] = vec_ref[q, pl.ds(start, rows), :]
 
@@ -209,12 +209,12 @@
         return pltpu.VMEM((count * chunks * rows, depth), BF16)
 
     def sent(part):
-        return [part[0]] + [swap_virt(part[chunk], 2 * chunk) for chunk in range(1, chunks)]
+        return [part[0]] + [swap_virt(part[chunk], chunk) for chunk in range(1, chunks)]
 
     def work(count):
         return 2 * count * depth * slab * slab
 
-    near = swap_virt(vectors, 1)
+    near = swap_virt(vectors, chunks)
     if (firsts, seconds, chips, cores) == (2, CHIPS, CHIPS, 2):
         half_blocks = shaped(BF16, CHIPS, slab, slab)
         same, cross, gates = kernel(

time: 21.5 us -> 23.7 us (1.10)
  waiting for transfers between devices: 7.43 us -> 9.95 us
  starting transfers between devices: 10.1 us -> 9.82 us
    ppermute x3, waiting for transfers between devices: 4.58 us -> 8.61 us  [swap_virt(): lax.ppermute(array, 'virt', [(d, d ^ step) for d in range(lax.axis_size('...]
    ppermute x3, waiting for transfers between devices: 1.52 us -> 0.01 us  [swap_chip(): lax.ppermute(array, 'occi', [(d, d ^ step) for d in range(lax.axis_size('...]
    ppermute x3, starting transfers between devices: 6.49 us -> 6.19 us  [swap_virt(): lax.ppermute(array, 'virt', [(d, d ^ step) for d in range(lax.axis_size('...]
  transfers between devices with their start and end apart: 7 -> 7, of which waited for: 5 -> 4; matrix products, arithmetic and copies ran while one was open for 0% -> 0% of each run, Pallas kernels for 14% -> 13%
where the time goes in v8:
time: 23.7 us; the launch traced here: 23.6 us
  waiting for transfers between devices  9.95 us (42%)
  starting transfers between devices  9.82 us (41%)
  Pallas kernels  3.71 us (16%)
    ppermute x3, waiting for transfers between devices, swap_virt(): lax.ppermute(array, 'virt', [(d, d ^ step) for d in range(lax.axis_size('...  8.61 us
    ppermute x3, starting transfers between devices, swap_virt(): lax.ppermute(array, 'virt', [(d, d ^ step) for d in range(lax.axis_size('...  6.19 us
    pallas_call x7, Pallas kernels, kernel(): pl.pallas_call(body, out_shape=outs, in_specs=[pl.BlockSpec(memory_space=...  3.71 us
    ppermute x3, starting transfers between devices, swap_chip(): lax.ppermute(array, 'occi', [(d, d ^ step) for d in range(lax.axis_size('...  3.55 us
    ppermute x1, waiting for transfers between devices, swap_core(): return lax.ppermute(array, 'occj', [(0, 1), (1, 0)])  1.33 us
  transfers between devices with their start and end apart: 7, of which 4 were waited for; matrix products, arithmetic and copies ran while one was open for 0% of the time, Pallas kernels for 13%

profile of v8, /device:TPU:0, one launch (start us, length us, event | category | flops | bytes accessed | tf_op | source)
XLA Modules:
  0.0 23.6 jit_solution(12440564097660247656)
XLA Ops:
  0.0 4.0 %collective-permute-start = (bf16[8,128,128]{2,1,0:T(8,128)(2,1)}, bf16[8,128,128]{2,1,0:T(8,128)(2,1)S(1)}, u32[]{:S(2)}, u32[]{:S(2)}) collective-permute-start(bf16[8,128,128]{2,1,0:T(8,128)(2,1)} %vec_ref.1), channel_id=1, source_target_pairs={{0,2},{1,3},{2,0},{3,1},{4,6},{5,7},{6,4},{7,5},{8,10},{9,11},{10,... | collective-permute-start | bytes 786440 | tf_op jit(solution)/shard_map/ppermute | solution.py:20
  4.0 0.0 copy-start
  4.0 1.1 %shard_map.48 = (bf16[4,128,128]{2,1,0:T(8,128)(2,1)S(1)}, bf16[4,128,128]{2,1,0:T(8,128)(2,1)S(1)}, f32[8,8,128]{2,1,0:T(8,128)S(1)}) custom-call(s32[2,2,2,4]{3,2,1,0:T(2,128)} %bitcast.1, s32[2,4]{1,0:T(2,128)} %pair_hbm.1, bf16[2,4,128,128]{3,2,1,0:T(8,128)(2,1)} %amp_hbm.1), custom_call_target="tpu_custom_call" | custom-call | bytes 1048576 | tf_op jit(solution)/shard_map/pallas_call | solution.py:182
  5.1 0.1 collective-permute-start.1
  5.2 1.3 %collective-permute-done.1.other_ref.refs_7_ = bf16[4,128,128]{2,1,0:T(8,128)(2,1)S(1)} collective-permute-done((bf16[4,128,128]{2,1,0:T(8,128)(2,1)S(1)}, bf16[4,128,128]{2,1,0:T(8,128)(2,1)S(1)}, u32[]{:S(2)}, u32[]{:S(2)}) %collective-permute-start.1) | collective-permute-done | bytes 131104 | tf_op jit(solution)/shard_map/ppermute | solution.py:24
  6.6 2.5 %collective-permute-start.2 = (bf16[2,128,128]{2,1,0:T(8,128)(2,1)S(1)}, bf16[2,128,128]{2,1,0:T(8,128)(2,1)S(1)}, u32[]{:S(2)}, u32[]{:S(2)}) collective-permute-start(bf16[2,128,128]{2,1,0:T(8,128)(2,1)S(1)} %get-tuple-element.26), channel_id=1, source_target_pairs={{0,24},{8,16},{16,8},{24,0},{1,25},{9,17},{17,9},{25,1},{2,26},{10... | collective-permute-start | bytes 196616 | tf_op jit(solution)/shard_map/ppermute | solution.py:28
  9.1 0.5 %collective-permute-start.4 = (bf16[2,128,128]{2,1,0:T(8,128)(2,1)S(1)}, bf16[2,128,128]{2,1,0:T(8,128)(2,1)S(1)}, u32[]{:S(2)}, u32[]{:S(2)}) collective-permute-start(bf16[2,128,128]{2,1,0:T(8,128)(2,1)S(1)} %get-tuple-element.29), channel_id=1, source_target_pairs={{0,8},{8,0},{16,24},{24,16},{1,9},{9,1},{17,25},{25,17},{2,10},{10... | collective-permute-start | bytes 196616 | tf_op jit(solution)/shard_map/ppermute | solution.py:28
  9.6 0.5 %collective-permute-start.5 = (bf16[2,128,128]{2,1,0:T(8,128)(2,1)S(1)}, bf16[2,128,128]{2,1,0:T(8,128)(2,1)S(1)}, u32[]{:S(2)}, u32[]{:S(2)}) collective-permute-start(bf16[2,128,128]{2,1,0:T(8,128)(2,1)S(1)} %get-tuple-element.30), channel_id=1, source_target_pairs={{0,16},{8,24},{16,0},{24,8},{1,17},{9,25},{17,1},{25,9},{2,18},{10... | collective-permute-start | bytes 196616 | tf_op jit(solution)/shard_map/ppermute | solution.py:28
  10.1 0.0 copy-done
  10.1 0.1 shard_map.46
  10.3 5.9 %collective-permute-done.vec_ref = bf16[8,128,128]{2,1,0:T(8,128)(2,1)S(1)} collective-permute-done((bf16[8,128,128]{2,1,0:T(8,128)(2,1)}, bf16[8,128,128]{2,1,0:T(8,128)(2,1)S(1)}, u32[]{:S(2)}, u32[]{:S(2)}) %collective-permute-start) | collective-permute-done | bytes 262176 | tf_op jit(solution)/shard_map/ppermute | solution.py:20
  16.2 0.1 shard_map.47
  16.3 0.0 collective-permute-done.2.refs_8_
  16.3 0.8 %shard_map.50 = (f32[4,32,128]{2,1,0:T(8,128)S(1)}, bf16[4,32,128]{2,1,0:T(8,128)(2,1)S(1)}) custom-call(bf16[1024,128]{1,0:T(8,128)(2,1)S(1)} %get-tuple-element.19.refs_0_, bf16[512,128]{1,0:T(8,128)(2,1)S(1)} %get-tuple-element.20.refs_1_, bf16[1024,128]{1,0:T(8,128)(2,1)S(1)} %get-tuple-element.21.refs_2_, ...), custom_call_target="tpu_custom_call" | custom-call | flops 268435456 | bytes 1048576 | tf_op jit(solution)/shard_map/pallas_call | solution.py:182
  17.2 0.9 %collective-permute-start.3 = (bf16[4,32,128]{2,1,0:T(8,128)(2,1)S(1)}, bf16[4,32,128]{2,1,0:T(8,128)(2,1)S(1)}, u32[]{:S(2)}, u32[]{:S(2)}) collective-permute-start(bf16[4,32,128]{2,1,0:T(8,128)(2,1)S(1)} %get-tuple-element.28), channel_id=1, source_target_pairs={{0,1},{1,0},{2,3},{3,2},{4,5},{5,4},{6,7},{7,6},{8,9},{9,8},{10,11... | collective-permute-start | bytes 98312 | tf_op jit(solution)/shard_map/ppermute | solution.py:20
  18.1 0.0 collective-permute-done.4.refs_7_
  18.1 0.0 collective-permute-done.5.refs_8_
  18.1 0.8 %shard_map.51 = (f32[4,32,128]{2,1,0:T(8,128)S(1)}, bf16[4,32,128]{2,1,0:T(8,128)(2,1)S(1)}) custom-call(bf16[1024,128]{1,0:T(8,128)(2,1)S(1)} %get-tuple-element.19.refs_0_, bf16[512,128]{1,0:T(8,128)(2,1)S(1)} %get-tuple-element.20.refs_1_, bf16[1024,128]{1,0:T(8,128)(2,1)S(1)} %get-tuple-element.21.refs_2_, ...), custom_call_target="tpu_custom_call" | custom-call | flops 268435456 | bytes 1048576 | tf_op jit(solution)/shard_map/pallas_call | solution.py:182
  18.9 1.3 %collective-permute-start.6 = (bf16[4,32,128]{2,1,0:T(8,128)(2,1)S(1)}, bf16[4,32,128]{2,1,0:T(8,128)(2,1)S(1)}, u32[]{:S(2)}, u32[]{:S(2)}) collective-permute-start(bf16[4,32,128]{2,1,0:T(8,128)(2,1)S(1)} %get-tuple-element.32), channel_id=1, source_target_pairs={{0,1},{1,0},{2,3},{3,2},{4,5},{5,4},{6,7},{7,6},{8,9},{9,8},{10,11... | collective-permute-start | bytes 98312 | tf_op jit(solution)/shard_map/ppermute | solution.py:20
  20.2 1.0 %collective-permute-done.3.refs_1_ = bf16[4,32,128]{2,1,0:T(8,128)(2,1)S(1)} collective-permute-done((bf16[4,32,128]{2,1,0:T(8,128)(2,1)S(1)}, bf16[4,32,128]{2,1,0:T(8,128)(2,1)S(1)}, u32[]{:S(2)}, u32[]{:S(2)}) %collective-permute-start.3) | collective-permute-done | bytes 32800 | tf_op jit(solution)/shard_map/ppermute | solution.py:20
  21.2 1.8 %collective-permute-done.6.refs_3_ = bf16[4,32,128]{2,1,0:T(8,128)(2,1)S(1)} collective-permute-done((bf16[4,32,128]{2,1,0:T(8,128)(2,1)S(1)}, bf16[4,32,128]{2,1,0:T(8,128)(2,1)S(1)}, u32[]{:S(2)}, u32[]{:S(2)}) %collective-permute-start.6) | collective-permute-done | bytes 32800 | tf_op jit(solution)/shard_map/ppermute | solution.py:20
  22.9 0.6 %shard_map.52 = bf16[2,4,32,128]{3,2,1,0:T(8,128)(2,1)} custom-call(f32[4,32,128]{2,1,0:T(8,128)S(1)} %get-tuple-element.27.refs_0_, bf16[4,32,128]{2,1,0:T(8,128)(2,1)S(1)} %collective-permute-done.3.refs_1_, f32[4,32,128]{2,1,0:T(8,128)S(1)} %get-tuple-element.31.refs_2_, bf16[4,32,128]{2,1,0:T(8,128)(2,1)S(1)} %collective-permute-done.6.refs_3_), custom_call_target="tpu_custom_call" | custom-call | bytes 1048576 | tf_op jit(solution)/shard_map/pallas_call | solution.py:182
  (1 shorter events, 0.0 us)
Async XLA Ops:
  0.0 16.2 %collective-permute-start = (bf16[8,128,128]{2,1,0:T(8,128)(2,1)}, bf16[8,128,128]{2,1,0:T(8,128)(2,1)S(1)}, u32[]{:S(2)}, u32[]{:S(2)}) collective-permute-start(bf16[8,128,128]{2,1,0:T(8,128)(2,1)} %vec_ref.1), channel_id=1, source_target_pairs={{0,2},{1,3},{2,0},{3,1},{4,6},{5,7},{6,4},{7,5},{8,10},{9,11},{10,... | collective-permute-start | bytes 786440 | tf_op jit(solution)/shard_map/ppermute | solution.py:20
  4.0 6.1 %copy-start = (bf16[8,128,128]{2,1,0:T(8,128)(2,1)S(1)}, bf16[8,128,128]{2,1,0:T(8,128)(2,1)}, u32[]{:S(2)}) copy-start(bf16[8,128,128]{2,1,0:T(8,128)(2,1)} %vec_ref.1) | copy-start | bytes 786436
  5.1 1.4 %collective-permute-start.1 = (bf16[4,128,128]{2,1,0:T(8,128)(2,1)S(1)}, bf16[4,128,128]{2,1,0:T(8,128)(2,1)S(1)}, u32[]{:S(2)}, u32[]{:S(2)}) collective-permute-start(bf16[4,128,128]{2,1,0:T(8,128)(2,1)S(1)} %get-tuple-element.25.refs_6_), channel_id=1, source_target_pairs={{0,4},{4,0},{1,5},{5,1},{2,6},{6,2},{3,7},{7,3},{8,12},{12,8},{9,1... | collective-permute-start | bytes 393224 | tf_op jit(solution)/shard_map/ppermute | solution.py:24
  6.6 9.7 %collective-permute-start.2 = (bf16[2,128,128]{2,1,0:T(8,128)(2,1)S(1)}, bf16[2,128,128]{2,1,0:T(8,128)(2,1)S(1)}, u32[]{:S(2)}, u32[]{:S(2)}) collective-permute-start(bf16[2,128,128]{2,1,0:T(8,128)(2,1)S(1)} %get-tuple-element.26), channel_id=1, source_target_pairs={{0,24},{8,16},{16,8},{24,0},{1,25},{9,17},{17,9},{25,1},{2,26},{10... | collective-permute-start | bytes 196616 | tf_op jit(solution)/shard_map/ppermute | solution.py:28
  9.1 9.0 %collective-permute-start.4 = (bf16[2,128,128]{2,1,0:T(8,128)(2,1)S(1)}, bf16[2,128,128]{2,1,0:T(8,128)(2,1)S(1)}, u32[]{:S(2)}, u32[]{:S(2)}) collective-permute-start(bf16[2,128,128]{2,1,0:T(8,128)(2,1)S(1)} %get-tuple-element.29), channel_id=1, source_target_pairs={{0,8},{8,0},{16,24},{24,16},{1,9},{9,1},{17,25},{25,17},{2,10},{10... | collective-permute-start | bytes 196616 | tf_op jit(solution)/shard_map/ppermute | solution.py:28
  9.6 8.5 %collective-permute-start.5 = (bf16[2,128,128]{2,1,0:T(8,128)(2,1)S(1)}, bf16[2,128,128]{2,1,0:T(8,128)(2,1)S(1)}, u32[]{:S(2)}, u32[]{:S(2)}) collective-permute-start(bf16[2,128,128]{2,1,0:T(8,128)(2,1)S(1)} %get-tuple-element.30), channel_id=1, source_target_pairs={{0,16},{8,24},{16,0},{24,8},{1,17},{9,25},{17,1},{25,9},{2,18},{10... | collective-permute-start | bytes 196616 | tf_op jit(solution)/shard_map/ppermute | solution.py:28
  17.2 4.0 %collective-permute-start.3 = (bf16[4,32,128]{2,1,0:T(8,128)(2,1)S(1)}, bf16[4,32,128]{2,1,0:T(8,128)(2,1)S(1)}, u32[]{:S(2)}, u32[]{:S(2)}) collective-permute-start(bf16[4,32,128]{2,1,0:T(8,128)(2,1)S(1)} %get-tuple-element.28), channel_id=1, source_target_pairs={{0,1},{1,0},{2,3},{3,2},{4,5},{5,4},{6,7},{7,6},{8,9},{9,8},{10,11... | collective-permute-start | bytes 98312 | tf_op jit(solution)/shard_map/ppermute | solution.py:20
  18.9 4.0 %collective-permute-start.6 = (bf16[4,32,128]{2,1,0:T(8,128)(2,1)S(1)}, bf16[4,32,128]{2,1,0:T(8,128)(2,1)S(1)}, u32[]{:S(2)}, u32[]{:S(2)}) collective-permute-start(bf16[4,32,128]{2,1,0:T(8,128)(2,1)S(1)} %get-tuple-element.32), channel_id=1, source_target_pairs={{0,1},{1,0},{2,3},{3,2},{4,5},{5,4},{6,7},{7,6},{8,9},{9,8},{10,11... | collective-permute-start | bytes 98312 | tf_op jit(solution)/shard_map/ppermute | solution.py:20

commit v9 on v7

--- a/solution.py
+++ b/solution.py
@@ -11,13 +11,19 @@
 SLAB_TILES = 2
 CHIPS = 4
 STEPS = (3, 1, 2)
-GROUPS = ((0, 3, 1), (2,))
+ORDER = (0, 3, 1, 2)
 BF16 = jnp.bfloat16
 F32 = jnp.float32
 
 
 def swap_virt(array, step):
     return lax.ppermute(array, "virt", [(d, d ^ step) for d in range(lax.axis_size("virt"))])
+
+
+def swap_both(array, step):
+    size = lax.axis_size("virt")
+    moves = [(c * size + d, (1 - c) * size + (d ^ step)) for c in range(2) for d in range(size)]
+    return lax.ppermute(array, ("occj", "virt"), moves)
 
 
 def swap_core(array):
@@ -41,30 +47,33 @@
     return jnp.broadcast_to(keep, (TILE, SLAB_TILES * TILE)).astype(BF16)
 
 
-def mask_split_kernel(mask_hbm, pair_hbm, amp_hbm, same_ref, cross_ref, gate_ref, mask_ref, pair_ref, sems):
+def mask_split_kernel(mask_hbm, pair_hbm, amp_hbm, *refs):
+    kept_refs, (cross_ref, gate_ref, mask_ref, pair_ref, sems) = refs[:CHIPS], refs[CHIPS:]
     copies = [
         pltpu.make_async_copy(mask_hbm, mask_ref, sems.at[0]),
         pltpu.make_async_copy(pair_hbm, pair_ref, sems.at[1]),
     ]
     blocks = []
-    for kind, kept_ref in ((1, cross_ref), (0, same_ref)):
-        for step in range(CHIPS):
+    for step in STEPS + (0,):
+        for kind in range(2):
             first, second = slot(kind, step)
-            copies.append(
-                pltpu.make_async_copy(amp_hbm.at[first, second], kept_ref.at[step], sems.at[len(copies)])
-            )
-            blocks.append((first, second, kept_ref, step, kind * CHIPS + step, copies[-1]))
+            target = kept_refs[step].at[kind]
+            copies.append(pltpu.make_async_copy(amp_hbm.at[first, second], target, sems.at[len(copies)]))
+            blocks.append((first, second, target, kind, step, copies[-1]))
     for copy in copies:
         copy.start()
     copies[0].wait()
     copies[1].wait()
-    for first, second, kept_ref, step, gate, copy in blocks:
-        gate_ref[gate] = jnp.full(gate_ref.shape[1:], pair_ref[first, second].astype(F32))
+    for first, second, target, kind, step, copy in blocks:
+        gate_ref[kind * CHIPS + step] = jnp.full(gate_ref.shape[1:], pair_ref[first, second].astype(F32))
         keeps = [keep_rows(mask_ref, first, second, half) for half in range(SLAB_TILES)]
         copy.wait()
         for half, keep in enumerate(keeps):
             part = slice(half * TILE, (half + 1) * TILE)
-            kept_ref[step, part] = kept_ref[step, part] * keep
+            kept = target[part] * keep
+            target[part] = kept
+            if kind:
+                cross_ref[step, part] = kept
 
 
 def mask_whole_kernel(mask_ref, pair_ref, amp_ref, kept_ref, gate_ref):
@@ -79,12 +88,6 @@
         return carry
 
     lax.fori_loop(0, kept_ref.shape[0], one, 0)
-
-
-def pack_kernel(same_ref, other_ref, *send_refs):
-    for step, send_ref in zip(STEPS, send_refs):
-        send_ref[0] = same_ref[step]
-        send_ref[1] = other_ref[step]
 
 
 def turn_kernel(chunks, vec_ref, turned_ref, left_ref):
@@ -108,8 +111,8 @@
     rows = height // len(outs[0])
     for base in range(0, len(sources), 2):
         both = [
-            ((kept.astype(F32) + partner.astype(F32).T) * gate[:1]).astype(BF16)
-            for kept, partner, gate in sources[base : base + 2]
+            (kept.astype(F32) + partner.astype(F32).T).astype(BF16)
+            for kept, partner in sources[base : base + 2]
         ]
         right = jnp.concatenate(both, axis=1)
         for side, left_ref in enumerate(left_refs):
@@ -130,47 +133,52 @@
             ref[index] = half[start : start + rows].astype(ref.dtype)
 
 
-def group_kernel(chunks, steps, *refs):
-    ready, (gate_ref, same_ref, cross_ref), refs = refs[:4], refs[4:7], refs[7:]
-    got_refs, refs = refs[: len(steps)], refs[len(steps) :]
-    joined = len(refs) > chunks + 1
-    part_refs, inner_ref = refs[joined : joined + chunks], refs[-1]
-    sources = []
-    for step, got_ref in zip(steps, got_refs):
-        if step:
-            partners = got_ref[0], got_ref[1]
-        else:
-            partners = same_ref[0], got_ref[0]
-        sources.append((same_ref[step], partners[0], gate_ref[step]))
-        sources.append((cross_ref[step], partners[1], gate_ref[CHIPS + step]))
-    outs = [[(ref, n) for ref in part_refs] for n in range(len(sources))]
-    products(ready, inner_ref, sources, outs)
-    if joined:
-        count = refs[0].shape[0]
-        refs[-2][:count] = refs[0][...]
-        refs[-2][count:] = part_refs[1][...]
+def first_kernel(*refs):
+    ready, (kept_ref, far_ref, got_ref, beside_ref), outs = refs[:4], refs[4:8], refs[8:]
+    own_ref, lent_ref, send_ref, inner_ref = outs
+    sources = [
+        (kept_ref[0], kept_ref[0]),
+        (far_ref[0], got_ref[0]),
+        (beside_ref[0], kept_ref[1]),
+        (beside_ref[ORDER[1]], got_ref[1]),
+    ]
+    targets = [[(ref, n), (send_ref, at + n)] for at, ref in ((0, own_ref), (2, lent_ref)) for n in range(2)]
+    products(ready, inner_ref, sources, targets)
+
+
+def second_kernel(*refs):
+    ready, kept_refs, got_refs, (beside_ref, lent_in, send_in) = refs[:4], refs[4:6], refs[6:8], refs[8:11]
+    own_ref, lent_ref, same_ref, cross_ref, inner_ref = refs[11:]
+    sources = [(kept[0], got[0]) for kept, got in zip(kept_refs, got_refs)]
+    sources += [(beside_ref[step], got[1]) for step, got in zip(ORDER[2:], got_refs)]
+    targets = [[(own_ref, n), (same_ref, 2 + n)] for n in range(2)]
+    targets += [[(lent_ref, 2 + n), (cross_ref, 2 + n)] for n in range(2)]
+    lent_ref[:2] = lent_in[...]
+    same_ref[:2] = send_in[:2]
+    cross_ref[:2] = send_in[2:]
+    products(ready, inner_ref, sources, targets)
 
 
 def whole_kernel(*refs):
-    ready, (gate_ref, kept_ref, partner_ref), part_refs, inner_ref = refs[:4], refs[4:7], refs[7:-1], refs[-1]
+    ready, (kept_ref, partner_ref), part_refs, inner_ref = refs[:4], refs[4:6], refs[6:-1], refs[-1]
 
     def two(g, carry):
         pairs = [2 * g, 2 * g + 1]
-        sources = [(kept_ref[k], partner_ref[k], gate_ref[k]) for k in pairs]
+        sources = [(kept_ref[k], partner_ref[k]) for k in pairs]
         products(ready, inner_ref, sources, [[(ref, k) for ref in part_refs] for k in pairs])
         return carry
 
     lax.fori_loop(0, kept_ref.shape[0] // 2, two, 0)
 
 
-def finish_kernel(*refs):
-    own_refs, got_ref, out_ref = refs[: len(GROUPS)], refs[-2], refs[-1]
-    at = 0
-    for steps, own_ref in zip(GROUPS, own_refs):
-        for n in range(2 * len(steps)):
-            first, second = slot(n % 2, steps[n // 2])
-            out_ref[first, second] = (own_ref[n] + got_ref[at].astype(F32)).astype(BF16)
-            at += 1
+def finish_kernel(first_ref, second_ref, same_ref, cross_ref, lent_ref, gate_ref, out_ref):
+    for n, step in enumerate(ORDER):
+        own = first_ref[n] if n < 2 else second_ref[n - 2]
+        totals = own + same_ref[n].astype(F32), lent_ref[n].astype(F32) + cross_ref[n].astype(F32)
+        for kind, total in enumerate(totals):
+            first, second = slot(kind, step)
+            gate = gate_ref[kind * CHIPS + step, :1]
+            out_ref[first, second] = (total * gate).astype(BF16)
 
 
 def vmem_specs(count):
@@ -220,10 +228,9 @@
 
     near = swap_virt(vectors, 1)
     if (firsts, seconds, chips, cores, virt) == (2, CHIPS, CHIPS, 2, 4):
-        half_blocks = shaped(BF16, CHIPS, slab, slab)
-        same, cross, gates = kernel(
+        *kept, cross, gates = kernel(
             mask_split_kernel,
-            [half_blocks, half_blocks, gate],
+            [shaped(BF16, 2, slab, slab)] * CHIPS + [shaped(BF16, CHIPS, slab, slab), gate],
             [
                 pltpu.with_memory_space_constraint(array, pltpu.HBM)
                 for array in (turned_mask, pair_mask, amplitudes)
@@ -235,23 +242,25 @@
                 pltpu.SemaphoreType.DMA((pairs + 2,)),
             ],
         )
-        other = swap_core(cross)
-        packed = kernel(pack_kernel, [shaped(BF16, 2, slab, slab)] * (CHIPS - 1), (same, other))
-        got = {step: swap_chip(block, step) for step, block in zip(STEPS, packed)}
-        got[0] = other
+        got = {step: swap_chip(kept[step], step) for step in STEPS}
+        beside = swap_core(cross)
         ready = kernel(turn, arranged, (vectors,)) + kernel(turn, arranged, (near,))
-        owned, leaving = [], []
-        for steps in GROUPS:
-            count = 2 * len(steps)
-            own, *leaving = kernel(
-                functools.partial(group_kernel, chunks, steps),
-                parts(count) + [shaped(BF16, pairs, rows, slab)] * len(leaving),
-                (*ready, gates, same, cross, *[got[step] for step in steps], *leaving),
-                scratch=[inner(count)],
-                flops=work(count),
-            )
-            owned.append(own)
-        operands = (*owned, swap_virt(leaving[-1], 2))
+        _, far, *rest = ORDER
+        own_first, lent, sending = kernel(
+            first_kernel,
+            [shaped(F32, 2, rows, slab), shaped(BF16, 2, rows, slab), shaped(BF16, 4, rows, slab)],
+            (*ready, kept[0], kept[far], got[far], beside),
+            scratch=[inner(4)],
+            flops=work(4),
+        )
+        own_second, lent, same, crossing = kernel(
+            second_kernel,
+            [shaped(F32, 2, rows, slab)] + [shaped(BF16, 4, rows, slab)] * 3,
+            (*ready, *[kept[step] for step in rest], *[got[step] for step in rest], beside, lent, sending),
+            scratch=[inner(4)],
+            flops=work(4),
+        )
+        operands = (own_first, own_second, swap_virt(same, 2), swap_both(crossing, 2), swap_core(lent), gates)
         (out,) = kernel(finish_kernel, [shaped(BF16, firsts, seconds, rows, slab)], operands)
         return out
     kept, gates = kernel(
@@ -263,12 +272,12 @@
     partner = lax.all_to_all(kept, ("occj", "occi"), split_axis=0, concat_axis=0, tiled=True)
     ready = kernel(turn, arranged, (vectors,)) + kernel(turn, arranged, (near,))
     part = sent(
-        kernel(whole_kernel, parts(pairs), (*ready, gates, kept, partner), scratch=[inner(2)], flops=work(pairs))
+        kernel(whole_kernel, parts(pairs), (*ready, kept, partner), scratch=[inner(2)], flops=work(pairs))
     )
     summed = part[0]
     for term in part[1:]:
         summed = summed + term.astype(F32)
-    return summed.reshape(firsts, seconds, rows, slab).astype(BF16)
+    return (summed * gates[:, :1]).reshape(firsts, seconds, rows, slab).astype(BF16)
 
 
 def solution(mesh):

time: 21.9 us -> 20 us (0.913)
  Pallas kernels: 5.06 us -> 3.57 us
  waiting for transfers between devices: 7.43 us -> 6.39 us
  starting transfers between devices: 9.24 us -> 9.75 us
    ppermute x0 -> x1, waiting for transfers between devices: none -> 2.02 us  [swap_both(): return lax.ppermute(array, ('occj', 'virt'), moves)]
    ppermute x3, waiting for transfers between devices: 2.66 us -> 0.77 us  [swap_chip(): lax.ppermute(array, 'occi', [(d, d ^ step) for d in range(lax.axis_size('...]
    pallas_call x7 -> x6, Pallas kernels: 5.06 us -> 3.57 us  [kernel(): pl.pallas_call(body, out_shape=outs, in_specs=[pl.BlockSpec(memory_space=...]
    ppermute x1 -> x2, waiting for transfers between devices: 1.33 us -> 0.01 us  [swap_core(): return lax.ppermute(array, 'occj', [(0, 1), (1, 0)])]
    ppermute x1 -> x2, starting transfers between devices: 0.07 us -> 0.52 us  [swap_core(): return lax.ppermute(array, 'occj', [(0, 1), (1, 0)])]
  transfers between devices with their start and end apart: 6 -> 8, of which waited for: 5 -> 5; matrix products, arithmetic and copies ran while one was open for 0% -> 0% of each run, Pallas kernels for 15% -> 11%
where the time goes in v9:
time: 20 us; the launch traced here: 19.8 us
  starting transfers between devices  9.75 us (49%)
  waiting for transfers between devices  6.39 us (32%)
  Pallas kernels  3.57 us (18%)
    ppermute x2, starting transfers between devices, swap_virt(): lax.ppermute(array, 'virt', [(d, d ^ step) for d in range(lax.axis_size('...  5.68 us
    ppermute x2, waiting for transfers between devices, swap_virt(): lax.ppermute(array, 'virt', [(d, d ^ step) for d in range(lax.axis_size('...  3.6 us
    pallas_call x6, Pallas kernels, kernel(): pl.pallas_call(body, out_shape=outs, in_specs=[pl.BlockSpec(memory_space=...  3.57 us
    ppermute x3, starting transfers between devices, swap_chip(): lax.ppermute(array, 'occi', [(d, d ^ step) for d in range(lax.axis_size('...  3.55 us
    ppermute x1, waiting for transfers between devices, swap_both(): return lax.ppermute(array, ('occj', 'virt'), moves)  2.02 us
    ppermute x3, waiting for transfers between devices, swap_chip(): lax.ppermute(array, 'occi', [(d, d ^ step) for d in range(lax.axis_size('...  0.77 us
    ppermute x2, starting transfers between devices, swap_core(): return lax.ppermute(array, 'occj', [(0, 1), (1, 0)])  0.52 us
  transfers between devices with their start and end apart: 8, of which 5 were waited for; matrix products, arithmetic and copies ran while one was open for 0% of the time, Pallas kernels for 11%

profile of v9, /device:TPU:0, one launch (start us, length us, event | category | flops | bytes accessed | tf_op | source)
XLA Modules:
  0.0 19.8 jit_solution(17764682472034644910)
XLA Ops:
  0.0 0.0 copy-start
  0.0 3.0 %collective-permute-start = (bf16[8,128,128]{2,1,0:T(8,128)(2,1)}, bf16[8,128,128]{2,1,0:T(8,128)(2,1)S(1)}, u32[]{:S(2)}, u32[]{:S(2)}) collective-permute-start(bf16[8,128,128]{2,1,0:T(8,128)(2,1)} %vec_ref.1), channel_id=1, source_target_pairs={{0,1},{1,0},{2,3},{3,2},{4,5},{5,4},{6,7},{7,6},{8,9},{9,8},{10,11... | collective-permute-start | bytes 786440 | tf_op jit(solution)/shard_map/ppermute | solution.py:20
  3.0 1.0 %shard_map.48 = (bf16[2,128,128]{2,1,0:T(8,128)(2,1)S(1)}, bf16[2,128,128]{2,1,0:T(8,128)(2,1)S(1)}, bf16[2,128,128]{2,1,0:T(8,128)(2,1)S(1)}, bf16[2,128,128]{2...) custom-call(s32[2,2,2,4]{3,2,1,0:T(2,128)} %bitcast.1, s32[2,4]{1,0:T(2,128)} %pair_hbm.1, ...), custom_call_target="tpu_custom_call" | custom-call | bytes 1048576 | tf_op jit(solution)/shard_map/pallas_call | solution.py:194
  4.0 0.1 collective-permute-start.2
  4.1 2.5 %collective-permute-start.1 = (bf16[2,128,128]{2,1,0:T(8,128)(2,1)S(1)}, bf16[2,128,128]{2,1,0:T(8,128)(2,1)S(1)}, u32[]{:S(2)}, u32[]{:S(2)}) collective-permute-start(bf16[2,128,128]{2,1,0:T(8,128)(2,1)S(1)} %get-tuple-element.27.refs_5_), channel_id=1, source_target_pairs={{0,24},{8,16},{16,8},{24,0},{1,25},{9,17},{17,9},{25,1},{2,26},{10... | collective-permute-start | bytes 196616 | tf_op jit(solution)/shard_map/ppermute | solution.py:34
  6.6 0.5 %collective-permute-start.3 = (bf16[2,128,128]{2,1,0:T(8,128)(2,1)S(1)}, bf16[2,128,128]{2,1,0:T(8,128)(2,1)S(1)}, u32[]{:S(2)}, u32[]{:S(2)}) collective-permute-start(bf16[2,128,128]{2,1,0:T(8,128)(2,1)S(1)} %get-tuple-element.30.refs_4_), channel_id=1, source_target_pairs={{0,8},{8,0},{16,24},{24,16},{1,9},{9,1},{17,25},{25,17},{2,10},{10... | collective-permute-start | bytes 196616 | tf_op jit(solution)/shard_map/ppermute | solution.py:34
  7.1 0.5 %collective-permute-start.4 = (bf16[2,128,128]{2,1,0:T(8,128)(2,1)S(1)}, bf16[2,128,128]{2,1,0:T(8,128)(2,1)S(1)}, u32[]{:S(2)}, u32[]{:S(2)}) collective-permute-start(bf16[2,128,128]{2,1,0:T(8,128)(2,1)S(1)} %get-tuple-element.31.refs_5_), channel_id=1, source_target_pairs={{0,16},{8,24},{16,0},{24,8},{1,17},{9,25},{17,1},{25,9},{2,18},{10... | collective-permute-start | bytes 196616 | tf_op jit(solution)/shard_map/ppermute | solution.py:34
  7.6 0.0 copy-done
  7.6 0.1 shard_map.46
  7.8 1.8 %collective-permute-done.vec_ref = bf16[8,128,128]{2,1,0:T(8,128)(2,1)S(1)} collective-permute-done((bf16[8,128,128]{2,1,0:T(8,128)(2,1)}, bf16[8,128,128]{2,1,0:T(8,128)(2,1)S(1)}, u32[]{:S(2)}, u32[]{:S(2)}) %collective-permute-start) | collective-permute-done | bytes 262176 | tf_op jit(solution)/shard_map/ppermute | solution.py:20
  9.6 0.1 shard_map.47
  9.8 0.0 collective-permute-done.1.refs_6_
  9.8 0.0 collective-permute-done.2.refs_7_.refs_8_
  9.8 0.8 %shard_map.49 = (f32[2,32,128]{2,1,0:T(8,128)S(1)}, bf16[2,32,128]{2,1,0:T(8,128)(2,1)S(1)}, bf16[4,32,128]{2,1,0:T(8,128)(2,1)S(1)}) custom-call(bf16[1024,128]{1,0:T(8,128)(2,1)S(1)} %get-tuple-element.22.refs_0_, bf16[512,128]{1,0:T(8,128)(2,1)S(1)} %get-tuple-element.23.refs_1_, bf16[1024,128]{1,0:T(8,128)(2,1)S(1)} %get-tuple-element.24.refs_2_, ...), custom_call_target="tpu_custom_call" | custom-call | flops 268435456 | bytes 1048576 | tf_op jit(solution)/shard_map/pallas_call | solution.py:194
  10.6 0.3 %collective-permute-done.3.refs_6_ = bf16[2,128,128]{2,1,0:T(8,128)(2,1)S(1)} collective-permute-done((bf16[2,128,128]{2,1,0:T(8,128)(2,1)S(1)}, bf16[2,128,128]{2,1,0:T(8,128)(2,1)S(1)}, u32[]{:S(2)}, u32[]{:S(2)}) %collective-permute-start.3) | collective-permute-done | bytes 65568 | tf_op jit(solution)/shard_map/ppermute | solution.py:34
  10.9 0.4 %collective-permute-done.4.refs_7_ = bf16[2,128,128]{2,1,0:T(8,128)(2,1)S(1)} collective-permute-done((bf16[2,128,128]{2,1,0:T(8,128)(2,1)S(1)}, bf16[2,128,128]{2,1,0:T(8,128)(2,1)S(1)}, u32[]{:S(2)}, u32[]{:S(2)}) %collective-permute-start.4) | collective-permute-done | bytes 65568 | tf_op jit(solution)/shard_map/ppermute | solution.py:34
  11.4 0.8 %shard_map.50 = (f32[2,32,128]{2,1,0:T(8,128)S(1)}, bf16[4,32,128]{2,1,0:T(8,128)(2,1)S(1)}, bf16[4,32,128]{2,1,0:T(8,128)(2,1)S(1)}, bf16[4,32,128]{2,1,0:T(8,128)(2,1)S(1)}) custom-call(bf16[1024,128]{1,0:T(8,128)(2,1)S(1)} %get-tuple-element.22.refs_0_, bf16[512,128]{1,0:T(8,128)(2,1)S(1)} %get-tuple-element.23.refs_1_, ...), custom_call_target="tpu_custom_call" | custom-call | flops 268435456 | bytes 1048576 | tf_op jit(solution)/shard_map/pallas_call | solution.py:194
  12.2 2.7 %collective-permute-start.5 = (bf16[4,32,128]{2,1,0:T(8,128)(2,1)S(1)}, bf16[4,32,128]{2,1,0:T(8,128)(2,1)S(1)}, u32[]{:S(2)}, u32[]{:S(2)}) collective-permute-start(bf16[4,32,128]{2,1,0:T(8,128)(2,1)S(1)} %get-tuple-element.35), channel_id=1, source_target_pairs={{0,2},{1,3},{2,0},{3,1},{4,6},{5,7},{6,4},{7,5},{8,10},{9,11},{10,... | collective-permute-start | bytes 98312 | tf_op jit(solution)/shard_map/ppermute | solution.py:20
  14.9 0.0 collective-permute-start.6
  14.9 0.4 %collective-permute-start.7 = (bf16[4,32,128]{2,1,0:T(8,128)(2,1)S(1)}, bf16[4,32,128]{2,1,0:T(8,128)(2,1)S(1)}, u32[]{:S(2)}, u32[]{:S(2)}) collective-permute-start(bf16[4,32,128]{2,1,0:T(8,128)(2,1)S(1)} %get-tuple-element.37), channel_id=1, source_target_pairs={{0,4},{4,0},{1,5},{5,1},{2,6},{6,2},{3,7},{7,3},{8,12},{12,8},{9,1... | collective-permute-start | bytes 98312 | tf_op jit(solution)/shard_map/ppermute | solution.py:30
  15.3 1.8 %collective-permute-done.5.same_ref = bf16[4,32,128]{2,1,0:T(8,128)(2,1)S(1)} collective-permute-done((bf16[4,32,128]{2,1,0:T(8,128)(2,1)S(1)}, bf16[4,32,128]{2,1,0:T(8,128)(2,1)S(1)}, u32[]{:S(2)}, u32[]{:S(2)}) %collective-permute-start.5) | collective-permute-done | bytes 32800 | tf_op jit(solution)/shard_map/ppermute | solution.py:20
  17.1 2.0 %collective-permute-done.6.cross_ref = bf16[4,32,128]{2,1,0:T(8,128)(2,1)S(1)} collective-permute-done((bf16[4,32,128]{2,1,0:T(8,128)(2,1)S(1)}, bf16[4,32,128]{2,1,0:T(8,128)(2,1)S(1)}, u32[]{:S(2)}, u32[]{:S(2)}) %collective-permute-start.6) | collective-permute-done | bytes 32800 | tf_op jit(solution)/shard_map/ppermute | solution.py:26
  19.1 0.0 collective-permute-done.7.lent_ref
  19.1 0.7 %shard_map.51 = bf16[2,4,32,128]{3,2,1,0:T(8,128)(2,1)} custom-call(f32[2,32,128]{2,1,0:T(8,128)S(1)} %get-tuple-element.29.first_ref, f32[2,32,128]{2,1,0:T(8,128)S(1)} %get-tuple-element.34.second_ref, bf16[4,32,128]{2,1,0:T(8,128)(2,1)S(1)} %collective-permute-done.5.same_ref, bf16[4,32,128]{2,1,0:T(8,128)(2,1)S(1)} %collective-permute-done.6.cross_ref, ...), custom_call_target="tpu_custom_call" | custom-call | bytes 1048576 | tf_op jit(solution)/shard_map/pallas_call | solution.py:194
Async XLA Ops:
  0.0 7.6 %copy-start = (bf16[8,128,128]{2,1,0:T(8,128)(2,1)S(1)}, bf16[8,128,128]{2,1,0:T(8,128)(2,1)}, u32[]{:S(2)}) copy-start(bf16[8,128,128]{2,1,0:T(8,128)(2,1)} %vec_ref.1) | copy-start | bytes 786436
  0.0 9.6 %collective-permute-start = (bf16[8,128,128]{2,1,0:T(8,128)(2,1)}, bf16[8,128,128]{2,1,0:T(8,128)(2,1)S(1)}, u32[]{:S(2)}, u32[]{:S(2)}) collective-permute-start(bf16[8,128,128]{2,1,0:T(8,128)(2,1)} %vec_ref.1), channel_id=1, source_target_pairs={{0,1},{1,0},{2,3},{3,2},{4,5},{5,4},{6,7},{7,6},{8,9},{9,8},{10,11... | collective-permute-start | bytes 786440 | tf_op jit(solution)/shard_map/ppermute | solution.py:20
  4.0 5.8 %collective-permute-start.2 = (bf16[4,128,128]{2,1,0:T(8,128)(2,1)S(1)}, bf16[4,128,128]{2,1,0:T(8,128)(2,1)S(1)}, u32[]{:S(2)}, u32[]{:S(2)}) collective-permute-start(bf16[4,128,128]{2,1,0:T(8,128)(2,1)S(1)} %get-tuple-element.28), channel_id=1, source_target_pairs={{0,4},{4,0},{1,5},{5,1},{2,6},{6,2},{3,7},{7,3},{8,12},{12,8},{9,1... | collective-permute-start | bytes 393224 | tf_op jit(solution)/shard_map/ppermute | solution.py:30
  4.1 5.7 %collective-permute-start.1 = (bf16[2,128,128]{2,1,0:T(8,128)(2,1)S(1)}, bf16[2,128,128]{2,1,0:T(8,128)(2,1)S(1)}, u32[]{:S(2)}, u32[]{:S(2)}) collective-permute-start(bf16[2,128,128]{2,1,0:T(8,128)(2,1)S(1)} %get-tuple-element.27.refs_5_), channel_id=1, source_target_pairs={{0,24},{8,16},{16,8},{24,0},{1,25},{9,17},{17,9},{25,1},{2,26},{10... | collective-permute-start | bytes 196616 | tf_op jit(solution)/shard_map/ppermute | solution.py:34
  6.6 4.4 %collective-permute-start.3 = (bf16[2,128,128]{2,1,0:T(8,128)(2,1)S(1)}, bf16[2,128,128]{2,1,0:T(8,128)(2,1)S(1)}, u32[]{:S(2)}, u32[]{:S(2)}) collective-permute-start(bf16[2,128,128]{2,1,0:T(8,128)(2,1)S(1)} %get-tuple-element.30.refs_4_), channel_id=1, source_target_pairs={{0,8},{8,0},{16,24},{24,16},{1,9},{9,1},{17,25},{25,17},{2,10},{10... | collective-permute-start | bytes 196616 | tf_op jit(solution)/shard_map/ppermute | solution.py:34
  7.1 4.3 %collective-permute-start.4 = (bf16[2,128,128]{2,1,0:T(8,128)(2,1)S(1)}, bf16[2,128,128]{2,1,0:T(8,128)(2,1)S(1)}, u32[]{:S(2)}, u32[]{:S(2)}) collective-permute-start(bf16[2,128,128]{2,1,0:T(8,128)(2,1)S(1)} %get-tuple-element.31.refs_5_), channel_id=1, source_target_pairs={{0,16},{8,24},{16,0},{24,8},{1,17},{9,25},{17,1},{25,9},{2,18},{10... | collective-permute-start | bytes 196616 | tf_op jit(solution)/shard_map/ppermute | solution.py:34
  12.2 4.9 %collective-permute-start.5 = (bf16[4,32,128]{2,1,0:T(8,128)(2,1)S(1)}, bf16[4,32,128]{2,1,0:T(8,128)(2,1)S(1)}, u32[]{:S(2)}, u32[]{:S(2)}) collective-permute-start(bf16[4,32,128]{2,1,0:T(8,128)(2,1)S(1)} %get-tuple-element.35), channel_id=1, source_target_pairs={{0,2},{1,3},{2,0},{3,1},{4,6},{5,7},{6,4},{7,5},{8,10},{9,11},{10,... | collective-permute-start | bytes 98312 | tf_op jit(solution)/shard_map/ppermute | solution.py:20
  14.9 4.2 %collective-permute-start.6 = (bf16[4,32,128]{2,1,0:T(8,128)(2,1)S(1)}, bf16[4,32,128]{2,1,0:T(8,128)(2,1)S(1)}, u32[]{:S(2)}, u32[]{:S(2)}) collective-permute-start(bf16[4,32,128]{2,1,0:T(8,128)(2,1)S(1)} %get-tuple-element.36), channel_id=1, source_target_pairs={{0,6},{1,7},{2,4},{3,5},{4,2},{5,3},{6,0},{7,1},{8,14},{9,15},{10,... | collective-permute-start | bytes 98312 | tf_op jit(solution)/shard_map/ppermute | solution.py:26
  14.9 4.2 %collective-permute-start.7 = (bf16[4,32,128]{2,1,0:T(8,128)(2,1)S(1)}, bf16[4,32,128]{2,1,0:T(8,128)(2,1)S(1)}, u32[]{:S(2)}, u32[]{:S(2)}) collective-permute-start(bf16[4,32,128]{2,1,0:T(8,128)(2,1)S(1)} %get-tuple-element.37), channel_id=1, source_target_pairs={{0,4},{4,0},{1,5},{5,1},{2,6},{6,2},{3,7},{7,3},{8,12},{12,8},{9,1... | collective-permute-start | bytes 98312 | tf_op jit(solution)/shard_map/ppermute | solution.py:30

commit v10 on v9

--- a/solution.py
+++ b/solution.py
@@ -18,12 +18,6 @@
 
 def swap_virt(array, step):
     return lax.ppermute(array, "virt", [(d, d ^ step) for d in range(lax.axis_size("virt"))])
-
-
-def swap_both(array, step):
-    size = lax.axis_size("virt")
-    moves = [(c * size + d, (1 - c) * size + (d ^ step)) for c in range(2) for d in range(size)]
-    return lax.ppermute(array, ("occj", "virt"), moves)
 
 
 def swap_core(array):
@@ -90,16 +84,20 @@
     lax.fori_loop(0, kept_ref.shape[0], one, 0)
 
 
-def turn_kernel(chunks, vec_ref, turned_ref, left_ref):
-    vectors, slab, _ = vec_ref.shape
-    rows = left_ref.shape[0] // (vectors * chunks)
+def turn_kernel(chunks, *refs):
+    vec_refs, turned_ref, left_ref = refs[:-2], refs[-2], refs[-1]
+    slab = turned_ref.shape[1]
+    rows = slab * left_ref.shape[0] // (turned_ref.shape[0] * chunks)
     me = lax.axis_index("virt")
-    for q in range(vectors):
-        turned_ref[q * slab : (q + 1) * slab] = vec_ref[q].astype(F32).T.astype(BF16)
-        for chunk in range(chunks):
-            start = pl.multiple_of((me ^ (2 * chunk)) * rows, rows)
-            low = (q * chunks + chunk) * rows
-            left_ref[low : low + rows] = vec_ref[q, pl.ds(start, rows), :]
+    at, low = 0, 0
+    for vec_ref in vec_refs:
+        for q in range(vec_ref.shape[0]):
+            turned_ref[at : at + slab] = vec_ref[q].astype(F32).T.astype(BF16)
+            at += slab
+            for chunk in range(chunks):
+                start = pl.multiple_of((me ^ (2 * chunk)) * rows, rows)
+                left_ref[low : low + rows] = vec_ref[q, pl.ds(start, rows), :]
+                low += rows
 
 
 def products(ready, inner_ref, sources, outs):
@@ -135,28 +133,35 @@
 
 def first_kernel(*refs):
     ready, (kept_ref, far_ref, got_ref, beside_ref), outs = refs[:4], refs[4:8], refs[8:]
-    own_ref, lent_ref, send_ref, inner_ref = outs
+    own_ref, send_ref, lent_ref, inner_ref = outs
     sources = [
         (kept_ref[0], kept_ref[0]),
+        (kept_ref[1], beside_ref[0]),
         (far_ref[0], got_ref[0]),
-        (beside_ref[0], kept_ref[1]),
         (beside_ref[ORDER[1]], got_ref[1]),
     ]
-    targets = [[(ref, n), (send_ref, at + n)] for at, ref in ((0, own_ref), (2, lent_ref)) for n in range(2)]
+    targets = [[(own_ref, n), (send_ref, n)] for n in range(3)] + [[(lent_ref.at[0], 0), (lent_ref.at[1], 0)]]
     products(ready, inner_ref, sources, targets)
 
 
-def second_kernel(*refs):
-    ready, kept_refs, got_refs, (beside_ref, lent_in, send_in) = refs[:4], refs[4:6], refs[6:8], refs[8:11]
-    own_ref, lent_ref, same_ref, cross_ref, inner_ref = refs[11:]
+def cross_kernel(*refs):
+    ready, got_refs, (beside_ref, lent_in, lent_ref, inner_ref) = refs[:4], refs[4:6], refs[6:]
+    lent_ref[:, :1] = lent_in[...]
+    sources = [(beside_ref[step], got[1]) for step, got in zip(ORDER[2:], got_refs)]
+    targets = [[(lent_ref.at[0], 1 + n), (lent_ref.at[1], 1 + n)] for n in range(2)]
+    products(ready, inner_ref, sources, targets)
+
+
+def same_kernel(*refs):
+    ready, kept_refs, got_refs, (own_ref, send_ref, inner_ref) = refs[:4], refs[4:6], refs[6:8], refs[8:]
     sources = [(kept[0], got[0]) for kept, got in zip(kept_refs, got_refs)]
-    sources += [(beside_ref[step], got[1]) for step, got in zip(ORDER[2:], got_refs)]
-    targets = [[(own_ref, n), (same_ref, 2 + n)] for n in range(2)]
-    targets += [[(lent_ref, 2 + n), (cross_ref, 2 + n)] for n in range(2)]
-    lent_ref[:2] = lent_in[...]
-    same_ref[:2] = send_in[:2]
-    cross_ref[:2] = send_in[2:]
-    products(ready, inner_ref, sources, targets)
+    products(ready, inner_ref, sources, [[(own_ref, n), (send_ref, n)] for n in range(2)])
+
+
+def join_kernel(first_ref, second_ref, back_ref, out_ref):
+    out_ref[:3] = first_ref[...]
+    out_ref[3:5] = second_ref[...]
+    out_ref[5:] = back_ref[1]
 
 
 def whole_kernel(*refs):
@@ -171,14 +176,13 @@
     lax.fori_loop(0, kept_ref.shape[0] // 2, two, 0)
 
 
-def finish_kernel(first_ref, second_ref, same_ref, cross_ref, lent_ref, gate_ref, out_ref):
-    for n, step in enumerate(ORDER):
-        own = first_ref[n] if n < 2 else second_ref[n - 2]
-        totals = own + same_ref[n].astype(F32), lent_ref[n].astype(F32) + cross_ref[n].astype(F32)
-        for kind, total in enumerate(totals):
-            first, second = slot(kind, step)
-            gate = gate_ref[kind * CHIPS + step, :1]
-            out_ref[first, second] = (total * gate).astype(BF16)
+def finish_kernel(first_ref, second_ref, back_ref, got_ref, gate_ref, out_ref):
+    places = [(0, 0), (1, 0)] + [(0, step) for step in ORDER[1:]] + [(1, step) for step in ORDER[1:]]
+    for n, (kind, step) in enumerate(places):
+        own = first_ref[n] if n < 3 else second_ref[n - 3] if n < 5 else back_ref[0, n - 5].astype(F32)
+        first, second = slot(kind, step)
+        gate = gate_ref[kind * CHIPS + step, :1]
+        out_ref[first, second] = ((own + got_ref[n].astype(F32)) * gate).astype(BF16)
 
 
 def vmem_specs(count):
@@ -226,7 +230,6 @@
     def work(count):
         return 2 * count * depth * slab * slab
 
-    near = swap_virt(vectors, 1)
     if (firsts, seconds, chips, cores, virt) == (2, CHIPS, CHIPS, 2, 4):
         *kept, cross, gates = kernel(
             mask_split_kernel,
@@ -242,25 +245,36 @@
                 pltpu.SemaphoreType.DMA((pairs + 2,)),
             ],
         )
+        near = swap_virt(vectors, 1)
         got = {step: swap_chip(kept[step], step) for step in STEPS}
         beside = swap_core(cross)
         ready = kernel(turn, arranged, (vectors,)) + kernel(turn, arranged, (near,))
         _, far, *rest = ORDER
-        own_first, lent, sending = kernel(
+        arrived = [got[step] for step in rest]
+        own_first, send_first, lent = kernel(
             first_kernel,
-            [shaped(F32, 2, rows, slab), shaped(BF16, 2, rows, slab), shaped(BF16, 4, rows, slab)],
+            [shaped(F32, 3, rows, slab), shaped(BF16, 3, rows, slab), shaped(BF16, 2, 1, rows, slab)],
             (*ready, kept[0], kept[far], got[far], beside),
             scratch=[inner(4)],
             flops=work(4),
         )
-        own_second, lent, same, crossing = kernel(
-            second_kernel,
-            [shaped(F32, 2, rows, slab)] + [shaped(BF16, 4, rows, slab)] * 3,
-            (*ready, *[kept[step] for step in rest], *[got[step] for step in rest], beside, lent, sending),
-            scratch=[inner(4)],
-            flops=work(4),
+        (lent,) = kernel(
+            cross_kernel,
+            [shaped(BF16, 2, 3, rows, slab)],
+            (*ready, *arrived, beside, lent),
+            scratch=[inner(2)],
+            flops=work(2),
         )
-        operands = (own_first, own_second, swap_virt(same, 2), swap_both(crossing, 2), swap_core(lent), gates)
+        back = swap_core(lent)
+        own_second, send_second = kernel(
+            same_kernel,
+            [shaped(F32, 2, rows, slab), shaped(BF16, 2, rows, slab)],
+            (*ready, *[kept[step] for step in rest], *arrived),
+            scratch=[inner(2)],
+            flops=work(2),
+        )
+        (sending,) = kernel(join_kernel, [shaped(BF16, pairs, rows, slab)], (send_first, send_second, back))
+        operands = (own_first, own_second, back, swap_virt(sending, 2), gates)
         (out,) = kernel(finish_kernel, [shaped(BF16, firsts, seconds, rows, slab)], operands)
         return out
     kept, gates = kernel(
@@ -270,7 +284,7 @@
         spaces=[pltpu.SMEM] * 2,
     )
     partner = lax.all_to_all(kept, ("occj", "occi"), split_axis=0, concat_axis=0, tiled=True)
-    ready = kernel(turn, arranged, (vectors,)) + kernel(turn, arranged, (near,))
+    ready = kernel(turn, arranged, (vectors,)) + kernel(turn, arranged, (swap_virt(vectors, 1),))
     part = sent(
         kernel(whole_kernel, parts(pairs), (*ready, kept, partner), scratch=[inner(2)], flops=work(pairs))
     )

time: 20 us -> 20.6 us (1.030)
  waiting for transfers between devices: 6.39 us -> 7.05 us
  Pallas kernels: 3.57 us -> 4.02 us
  starting transfers between devices: 9.75 us -> 9.3 us
    ppermute x2, waiting for transfers between devices: 3.6 us -> 5.71 us  [swap_virt(): lax.ppermute(array, 'virt', [(d, d ^ step) for d in range(lax.axis_size('...]
    ppermute x1 -> x0, waiting for transfers between devices: 2.02 us -> none  [swap_both(): return lax.ppermute(array, ('occj', 'virt'), moves)]
    ppermute x2, waiting for transfers between devices: 0.01 us -> 0.58 us  [swap_core(): return lax.ppermute(array, 'occj', [(0, 1), (1, 0)])]
    pallas_call x6 -> x8, Pallas kernels: 3.57 us -> 4.02 us  [kernel(): pl.pallas_call(body, out_shape=outs, in_specs=[pl.BlockSpec(memory_space=...]
    ppermute x2, starting transfers between devices: 0.52 us -> 0.14 us  [swap_core(): return lax.ppermute(array, 'occj', [(0, 1), (1, 0)])]
  transfers between devices with their start and end apart: 8 -> 7, of which waited for: 5 -> 5; matrix products, arithmetic and copies ran while one was open for 0% -> 0% of each run, Pallas kernels for 11% -> 13%
where the time goes in v10:
time: 20.6 us; the launch traced here: 20.5 us
  starting transfers between devices  9.3 us (45%)
  waiting for transfers between devices  7.05 us (34%)
  Pallas kernels  4.02 us (20%)
    ppermute x2, waiting for transfers between devices, swap_virt(): lax.ppermute(array, 'virt', [(d, d ^ step) for d in range(lax.axis_size('...  5.71 us
    ppermute x2, starting transfers between devices, swap_virt(): lax.ppermute(array, 'virt', [(d, d ^ step) for d in range(lax.axis_size('...  5.61 us
    pallas_call x8, Pallas kernels, kernel(): pl.pallas_call(body, out_shape=outs, in_specs=[pl.BlockSpec(memory_space=...  4.02 us
    ppermute x3, starting transfers between devices, swap_chip(): lax.ppermute(array, 'occi', [(d, d ^ step) for d in range(lax.axis_size('...  3.55 us
    ppermute x3, waiting for transfers between devices, swap_chip(): lax.ppermute(array, 'occi', [(d, d ^ step) for d in range(lax.axis_size('...  0.76 us
    ppermute x2, waiting for transfers between devices, swap_core(): return lax.ppermute(array, 'occj', [(0, 1), (1, 0)])  0.58 us
  transfers between devices with their start and end apart: 7, of which 5 were waited for; matrix products, arithmetic and copies ran while one was open for 0% of the time, Pallas kernels for 13%

profile of v10, /device:TPU:0, one launch (start us, length us, event | category | flops | bytes accessed | tf_op | source)
XLA Modules:
  0.0 20.5 jit_solution(14477728706260151475)
XLA Ops:
  0.0 0.0 copy-start
  0.0 3.0 %collective-permute-start = (bf16[8,128,128]{2,1,0:T(8,128)(2,1)}, bf16[8,128,128]{2,1,0:T(8,128)(2,1)S(1)}, u32[]{:S(2)}, u32[]{:S(2)}) collective-permute-start(bf16[8,128,128]{2,1,0:T(8,128)(2,1)} %refs_0_.1), channel_id=1, source_target_pairs={{0,1},{1,0},{2,3},{3,2},{4,5},{5,4},{6,7},{7,6},{8,9},{9,8},{10,11... | collective-permute-start | bytes 786440 | tf_op jit(solution)/shard_map/ppermute | solution.py:20
  3.0 1.0 %shard_map.48 = (bf16[2,128,128]{2,1,0:T(8,128)(2,1)S(1)}, bf16[2,128,128]{2,1,0:T(8,128)(2,1)S(1)}, bf16[2,128,128]{2,1,0:T(8,128)(2,1)S(1)}, bf16[2,128,128]{2...) custom-call(s32[2,2,2,4]{3,2,1,0:T(2,128)} %bitcast.1, s32[2,4]{1,0:T(2,128)} %pair_hbm.1, ...), custom_call_target="tpu_custom_call" | custom-call | bytes 1048576 | tf_op jit(solution)/shard_map/pallas_call | solution.py:198
  4.0 0.1 collective-permute-start.2
  4.1 2.5 %collective-permute-start.1 = (bf16[2,128,128]{2,1,0:T(8,128)(2,1)S(1)}, bf16[2,128,128]{2,1,0:T(8,128)(2,1)S(1)}, u32[]{:S(2)}, u32[]{:S(2)}) collective-permute-start(bf16[2,128,128]{2,1,0:T(8,128)(2,1)S(1)} %get-tuple-element.25.refs_5_), channel_id=1, source_target_pairs={{0,24},{8,16},{16,8},{24,0},{1,25},{9,17},{17,9},{25,1},{2,26},{10... | collective-permute-start | bytes 196616 | tf_op jit(solution)/shard_map/ppermute | solution.py:28
  6.6 0.5 %collective-permute-start.3 = (bf16[2,128,128]{2,1,0:T(8,128)(2,1)S(1)}, bf16[2,128,128]{2,1,0:T(8,128)(2,1)S(1)}, u32[]{:S(2)}, u32[]{:S(2)}) collective-permute-start(bf16[2,128,128]{2,1,0:T(8,128)(2,1)S(1)} %get-tuple-element.28.refs_4_), channel_id=1, source_target_pairs={{0,8},{8,0},{16,24},{24,16},{1,9},{9,1},{17,25},{25,17},{2,10},{10... | collective-permute-start | bytes 196616 | tf_op jit(solution)/shard_map/ppermute | solution.py:28
  7.1 0.5 %collective-permute-start.4 = (bf16[2,128,128]{2,1,0:T(8,128)(2,1)S(1)}, bf16[2,128,128]{2,1,0:T(8,128)(2,1)S(1)}, u32[]{:S(2)}, u32[]{:S(2)}) collective-permute-start(bf16[2,128,128]{2,1,0:T(8,128)(2,1)S(1)} %get-tuple-element.29.refs_5_), channel_id=1, source_target_pairs={{0,16},{8,24},{16,0},{24,8},{1,17},{9,25},{17,1},{25,9},{2,18},{10... | collective-permute-start | bytes 196616 | tf_op jit(solution)/shard_map/ppermute | solution.py:28
  7.6 0.0 copy-done
  7.6 0.1 shard_map.46
  7.8 1.8 %collective-permute-done.refs_0_ = bf16[8,128,128]{2,1,0:T(8,128)(2,1)S(1)} collective-permute-done((bf16[8,128,128]{2,1,0:T(8,128)(2,1)}, bf16[8,128,128]{2,1,0:T(8,128)(2,1)S(1)}, u32[]{:S(2)}, u32[]{:S(2)}) %collective-permute-start) | collective-permute-done | bytes 262176 | tf_op jit(solution)/shard_map/ppermute | solution.py:20
  9.6 0.1 shard_map.47
  9.8 0.0 collective-permute-done.1.refs_6_
  9.8 0.0 collective-permute-done.2.refs_7_.refs_6_
  9.8 0.9 %shard_map.49 = (f32[3,32,128]{2,1,0:T(8,128)S(1)}, bf16[3,32,128]{2,1,0:T(8,128)(2,1)S(1)}, bf16[2,1,32,128]{3,2,1,0:T(8,128)(2,1)S(1)}) custom-call(bf16[1024,128]{1,0:T(8,128)(2,1)S(1)} %get-tuple-element.20.refs_0_, bf16[512,128]{1,0:T(8,128)(2,1)S(1)} %get-tuple-element.21.refs_1_, bf16[1024,128]{1,0:T(8,128)(2,1)S(1)} %get-tuple-element.22.refs_2_, ...), custom_call_target="tpu_custom_call" | custom-call | flops 268435456 | bytes 1048576 | tf_op jit(solution)/shard_map/pallas_call | solution.py:198
  10.6 0.3 %collective-permute-done.3.refs_6_.refs_4_ = bf16[2,128,128]{2,1,0:T(8,128)(2,1)S(1)} collective-permute-done((bf16[2,128,128]{2,1,0:T(8,128)(2,1)S(1)}, bf16[2,128,128]{2,1,0:T(8,128)(2,1)S(1)}, u32[]{:S(2)}, u32[]{:S(2)}) %collective-permute-start.3) | collective-permute-done | bytes 65568 | tf_op jit(solution)/shard_map/ppermute | solution.py:28
  10.9 0.4 %collective-permute-done.4.refs_7_.refs_5_ = bf16[2,128,128]{2,1,0:T(8,128)(2,1)S(1)} collective-permute-done((bf16[2,128,128]{2,1,0:T(8,128)(2,1)S(1)}, bf16[2,128,128]{2,1,0:T(8,128)(2,1)S(1)}, u32[]{:S(2)}, u32[]{:S(2)}) %collective-permute-start.4) | collective-permute-done | bytes 65568 | tf_op jit(solution)/shard_map/ppermute | solution.py:28
  11.4 0.6 %shard_map.51 = bf16[2,3,32,128]{3,2,1,0:T(8,128)(2,1)S(1)} custom-call(bf16[1024,128]{1,0:T(8,128)(2,1)S(1)} %get-tuple-element.20.refs_0_, bf16[512,128]{1,0:T(8,128)(2,1)S(1)} %get-tuple-element.21.refs_1_, bf16[1024,128]{1,0:T(8,128)(2,1)S(1)} %get-tuple-element.22.refs_2_, bf16[512,128]{1,0:T(8,128)(2,1)S(1)} %get-tuple-element.23.refs_3_, ...), custom_call_target="tpu_custom_call" | custom-call | flops 134217728 | bytes 1048576 | tf_op jit(solution)/shard_map/pallas_call | solution.py:198
  12.0 0.1 collective-permute-start.5
  12.1 0.6 %shard_map.50 = (f32[2,32,128]{2,1,0:T(8,128)S(1)}, bf16[2,32,128]{2,1,0:T(8,128)(2,1)S(1)}) custom-call(bf16[1024,128]{1,0:T(8,128)(2,1)S(1)} %get-tuple-element.20.refs_0_, bf16[512,128]{1,0:T(8,128)(2,1)S(1)} %get-tuple-element.21.refs_1_, bf16[1024,128]{1,0:T(8,128)(2,1)S(1)} %get-tuple-element.22.refs_2_, ...), custom_call_target="tpu_custom_call" | custom-call | flops 134217728 | bytes 1048576 | tf_op jit(solution)/shard_map/pallas_call | solution.py:198
  12.8 0.6 %collective-permute-done.5.back_ref = bf16[2,3,32,128]{3,2,1,0:T(8,128)(2,1)S(1)} collective-permute-done((bf16[2,3,32,128]{3,2,1,0:T(8,128)(2,1)S(1)}, bf16[2,3,32,128]{3,2,1,0:T(8,128)(2,1)S(1)}, u32[]{:S(2)}, u32[]{:S(2)}) %collective-permute-start.5) | collective-permute-done | bytes 49184 | tf_op jit(solution)/shard_map/ppermute | solution.py:24
  13.3 2.6 %collective-permute-start.6 = (bf16[8,32,128]{2,1,0:T(8,128)(2,1)S(1)}, bf16[8,32,128]{2,1,0:T(8,128)(2,1)S(1)}, u32[]{:S(2)}, u32[]{:S(2)}) collective-permute-start(bf16[8,32,128]{2,1,0:T(8,128)(2,1)S(1)} %shard_map.52), channel_id=1, source_target_pairs={{0,2},{1,3},{2,0},{3,1},{4,6},{5,7},{6,4},{7,5},{8,10},{9,11},{10,... | collective-permute-start | bytes 196616 | tf_op jit(solution)/shard_map/ppermute | solution.py:20
  15.9 3.9 %collective-permute-done.6.got_ref = bf16[8,32,128]{2,1,0:T(8,128)(2,1)S(1)} collective-permute-done((bf16[8,32,128]{2,1,0:T(8,128)(2,1)S(1)}, bf16[8,32,128]{2,1,0:T(8,128)(2,1)S(1)}, u32[]{:S(2)}, u32[]{:S(2)}) %collective-permute-start.6) | collective-permute-done | bytes 65568 | tf_op jit(solution)/shard_map/ppermute | solution.py:20
  19.8 0.6 %shard_map.53 = bf16[2,4,32,128]{3,2,1,0:T(8,128)(2,1)} custom-call(f32[3,32,128]{2,1,0:T(8,128)S(1)} %get-tuple-element.27.first_ref, f32[2,32,128]{2,1,0:T(8,128)S(1)} %get-tuple-element.30.second_ref, bf16[2,3,32,128]{3,2,1,0:T(8,128)(2,1)S(1)} %collective-permute-done.5.back_ref, bf16[8,32,128]{2,1,0:T(8,128)(2,1)S(1)} %collective-permute-done.6.got_ref, ...), custom_call_target="tpu_custom_call" | custom-call | bytes 1048576 | tf_op jit(solution)/shard_map/pallas_call | solution.py:198
  (1 shorter events, 0.0 us)
Async XLA Ops:
  0.0 7.6 %copy-start = (bf16[8,128,128]{2,1,0:T(8,128)(2,1)S(1)}, bf16[8,128,128]{2,1,0:T(8,128)(2,1)}, u32[]{:S(2)}) copy-start(bf16[8,128,128]{2,1,0:T(8,128)(2,1)} %refs_0_.1) | copy-start | bytes 786436
  0.0 9.6 %collective-permute-start = (bf16[8,128,128]{2,1,0:T(8,128)(2,1)}, bf16[8,128,128]{2,1,0:T(8,128)(2,1)S(1)}, u32[]{:S(2)}, u32[]{:S(2)}) collective-permute-start(bf16[8,128,128]{2,1,0:T(8,128)(2,1)} %refs_0_.1), channel_id=1, source_target_pairs={{0,1},{1,0},{2,3},{3,2},{4,5},{5,4},{6,7},{7,6},{8,9},{9,8},{10,11... | collective-permute-start | bytes 786440 | tf_op jit(solution)/shard_map/ppermute | solution.py:20
  4.0 5.8 %collective-permute-start.2 = (bf16[4,128,128]{2,1,0:T(8,128)(2,1)S(1)}, bf16[4,128,128]{2,1,0:T(8,128)(2,1)S(1)}, u32[]{:S(2)}, u32[]{:S(2)}) collective-permute-start(bf16[4,128,128]{2,1,0:T(8,128)(2,1)S(1)} %get-tuple-element.26), channel_id=1, source_target_pairs={{0,4},{4,0},{1,5},{5,1},{2,6},{6,2},{3,7},{7,3},{8,12},{12,8},{9,1... | collective-permute-start | bytes 393224 | tf_op jit(solution)/shard_map/ppermute | solution.py:24
  4.1 5.7 %collective-permute-start.1 = (bf16[2,128,128]{2,1,0:T(8,128)(2,1)S(1)}, bf16[2,128,128]{2,1,0:T(8,128)(2,1)S(1)}, u32[]{:S(2)}, u32[]{:S(2)}) collective-permute-start(bf16[2,128,128]{2,1,0:T(8,128)(2,1)S(1)} %get-tuple-element.25.refs_5_), channel_id=1, source_target_pairs={{0,24},{8,16},{16,8},{24,0},{1,25},{9,17},{17,9},{25,1},{2,26},{10... | collective-permute-start | bytes 196616 | tf_op jit(solution)/shard_map/ppermute | solution.py:28
  6.6 4.4 %collective-permute-start.3 = (bf16[2,128,128]{2,1,0:T(8,128)(2,1)S(1)}, bf16[2,128,128]{2,1,0:T(8,128)(2,1)S(1)}, u32[]{:S(2)}, u32[]{:S(2)}) collective-permute-start(bf16[2,128,128]{2,1,0:T(8,128)(2,1)S(1)} %get-tuple-element.28.refs_4_), channel_id=1, source_target_pairs={{0,8},{8,0},{16,24},{24,16},{1,9},{9,1},{17,25},{25,17},{2,10},{10... | collective-permute-start | bytes 196616 | tf_op jit(solution)/shard_map/ppermute | solution.py:28
  7.1 4.3 %collective-permute-start.4 = (bf16[2,128,128]{2,1,0:T(8,128)(2,1)S(1)}, bf16[2,128,128]{2,1,0:T(8,128)(2,1)S(1)}, u32[]{:S(2)}, u32[]{:S(2)}) collective-permute-start(bf16[2,128,128]{2,1,0:T(8,128)(2,1)S(1)} %get-tuple-element.29.refs_5_), channel_id=1, source_target_pairs={{0,16},{8,24},{16,0},{24,8},{1,17},{9,25},{17,1},{25,9},{2,18},{10... | collective-permute-start | bytes 196616 | tf_op jit(solution)/shard_map/ppermute | solution.py:28
  12.0 1.3 %collective-permute-start.5 = (bf16[2,3,32,128]{3,2,1,0:T(8,128)(2,1)S(1)}, bf16[2,3,32,128]{3,2,1,0:T(8,128)(2,1)S(1)}, u32[]{:S(2)}, u32[]{:S(2)}) collective-permute-start(bf16[2,3,32,128]{3,2,1,0:T(8,128)(2,1)S(1)} %shard_map.51), channel_id=1, source_target_pairs={{0,4},{4,0},{1,5},{5,1},{2,6},{6,2},{3,7},{7,3},{8,12},{12,8},{9,1... | collective-permute-start | bytes 147464 | tf_op jit(solution)/shard_map/ppermute | solution.py:24
  13.3 6.5 %collective-permute-start.6 = (bf16[8,32,128]{2,1,0:T(8,128)(2,1)S(1)}, bf16[8,32,128]{2,1,0:T(8,128)(2,1)S(1)}, u32[]{:S(2)}, u32[]{:S(2)}) collective-permute-start(bf16[8,32,128]{2,1,0:T(8,128)(2,1)S(1)} %shard_map.52), channel_id=1, source_target_pairs={{0,2},{1,3},{2,0},{3,1},{4,6},{5,7},{6,4},{7,5},{8,10},{9,11},{10,... | collective-permute-start | bytes 196616 | tf_op jit(solution)/shard_map/ppermute | solution.py:20

commit v11 on v9

--- a/solution.py
+++ b/solution.py
@@ -171,7 +171,7 @@
     lax.fori_loop(0, kept_ref.shape[0] // 2, two, 0)
 
 
-def finish_kernel(first_ref, second_ref, same_ref, cross_ref, lent_ref, gate_ref, out_ref):
+def finish_kernel(first_ref, second_ref, cross_ref, same_ref, lent_ref, gate_ref, out_ref):
     for n, step in enumerate(ORDER):
         own = first_ref[n] if n < 2 else second_ref[n - 2]
         totals = own + same_ref[n].astype(F32), lent_ref[n].astype(F32) + cross_ref[n].astype(F32)
@@ -260,7 +260,7 @@
             scratch=[inner(4)],
             flops=work(4),
         )
-        operands = (own_first, own_second, swap_virt(same, 2), swap_both(crossing, 2), swap_core(lent), gates)
+        operands = (own_first, own_second, swap_both(crossing, 2), swap_virt(same, 2), swap_core(lent), gates)
         (out,) = kernel(finish_kernel, [shaped(BF16, firsts, seconds, rows, slab)], operands)
         return out
     kept, gates = kernel(

time: 20 us -> 19.7 us (0.985)
  starting transfers between devices: 9.75 us -> 9.47 us
    ppermute x1, starting transfers between devices: 0.01 us -> 1.35 us  [swap_both(): return lax.ppermute(array, ('occj', 'virt'), moves)]
    ppermute x2, starting transfers between devices: 5.68 us -> 4.42 us  [swap_virt(): lax.ppermute(array, 'virt', [(d, d ^ step) for d in range(lax.axis_size('...]
    ppermute x1, waiting for transfers between devices: 2.02 us -> 1.59 us  [swap_both(): return lax.ppermute(array, ('occj', 'virt'), moves)]
    ppermute x2, starting transfers between devices: 0.52 us -> 0.15 us  [swap_core(): return lax.ppermute(array, 'occj', [(0, 1), (1, 0)])]
    ppermute x2, waiting for transfers between devices: 3.6 us -> 3.93 us  [swap_virt(): lax.ppermute(array, 'virt', [(d, d ^ step) for d in range(lax.axis_size('...]
where the time goes in v11:
time: 19.7 us; the launch traced here: 19.4 us
  starting transfers between devices  9.47 us (48%)
  waiting for transfers between devices  6.3 us (32%)
  Pallas kernels  3.57 us (18%)
    ppermute x2, starting transfers between devices, swap_virt(): lax.ppermute(array, 'virt', [(d, d ^ step) for d in range(lax.axis_size('...  4.42 us
    ppermute x2, waiting for transfers between devices, swap_virt(): lax.ppermute(array, 'virt', [(d, d ^ step) for d in range(lax.axis_size('...  3.93 us
    pallas_call x6, Pallas kernels, kernel(): pl.pallas_call(body, out_shape=outs, in_specs=[pl.BlockSpec(memory_space=...  3.57 us
    ppermute x3, starting transfers between devices, swap_chip(): lax.ppermute(array, 'occi', [(d, d ^ step) for d in range(lax.axis_size('...  3.55 us
    ppermute x1, waiting for transfers between devices, swap_both(): return lax.ppermute(array, ('occj', 'virt'), moves)  1.59 us
    ppermute x1, starting transfers between devices, swap_both(): return lax.ppermute(array, ('occj', 'virt'), moves)  1.35 us
    ppermute x3, waiting for transfers between devices, swap_chip(): lax.ppermute(array, 'occi', [(d, d ^ step) for d in range(lax.axis_size('...  0.77 us
  transfers between devices with their start and end apart: 8, of which 5 were waited for; matrix products, arithmetic and copies ran while one was open for 0% of the time, Pallas kernels for 11%

profile of v11, /device:TPU:0, one launch (start us, length us, event | category | flops | bytes accessed | tf_op | source)
XLA Modules:
  0.0 19.4 jit_solution(16582063636570962648)
XLA Ops:
  0.0 0.0 copy-start
  0.0 3.0 %collective-permute-start = (bf16[8,128,128]{2,1,0:T(8,128)(2,1)}, bf16[8,128,128]{2,1,0:T(8,128)(2,1)S(1)}, u32[]{:S(2)}, u32[]{:S(2)}) collective-permute-start(bf16[8,128,128]{2,1,0:T(8,128)(2,1)} %vec_ref.1), channel_id=1, source_target_pairs={{0,1},{1,0},{2,3},{3,2},{4,5},{5,4},{6,7},{7,6},{8,9},{9,8},{10,11... | collective-permute-start | bytes 786440 | tf_op jit(solution)/shard_map/ppermute | solution.py:20
  3.0 1.0 %shard_map.48 = (bf16[2,128,128]{2,1,0:T(8,128)(2,1)S(1)}, bf16[2,128,128]{2,1,0:T(8,128)(2,1)S(1)}, bf16[2,128,128]{2,1,0:T(8,128)(2,1)S(1)}, bf16[2,128,128]{2...) custom-call(s32[2,2,2,4]{3,2,1,0:T(2,128)} %bitcast.1, s32[2,4]{1,0:T(2,128)} %pair_hbm.1, ...), custom_call_target="tpu_custom_call" | custom-call | bytes 1048576 | tf_op jit(solution)/shard_map/pallas_call | solution.py:194
  4.0 0.1 collective-permute-start.2
  4.1 2.5 %collective-permute-start.1 = (bf16[2,128,128]{2,1,0:T(8,128)(2,1)S(1)}, bf16[2,128,128]{2,1,0:T(8,128)(2,1)S(1)}, u32[]{:S(2)}, u32[]{:S(2)}) collective-permute-start(bf16[2,128,128]{2,1,0:T(8,128)(2,1)S(1)} %get-tuple-element.27.refs_5_), channel_id=1, source_target_pairs={{0,24},{8,16},{16,8},{24,0},{1,25},{9,17},{17,9},{25,1},{2,26},{10... | collective-permute-start | bytes 196616 | tf_op jit(solution)/shard_map/ppermute | solution.py:34
  6.6 0.5 %collective-permute-start.3 = (bf16[2,128,128]{2,1,0:T(8,128)(2,1)S(1)}, bf16[2,128,128]{2,1,0:T(8,128)(2,1)S(1)}, u32[]{:S(2)}, u32[]{:S(2)}) collective-permute-start(bf16[2,128,128]{2,1,0:T(8,128)(2,1)S(1)} %get-tuple-element.30.refs_4_), channel_id=1, source_target_pairs={{0,8},{8,0},{16,24},{24,16},{1,9},{9,1},{17,25},{25,17},{2,10},{10... | collective-permute-start | bytes 196616 | tf_op jit(solution)/shard_map/ppermute | solution.py:34
  7.1 0.5 %collective-permute-start.4 = (bf16[2,128,128]{2,1,0:T(8,128)(2,1)S(1)}, bf16[2,128,128]{2,1,0:T(8,128)(2,1)S(1)}, u32[]{:S(2)}, u32[]{:S(2)}) collective-permute-start(bf16[2,128,128]{2,1,0:T(8,128)(2,1)S(1)} %get-tuple-element.31.refs_5_), channel_id=1, source_target_pairs={{0,16},{8,24},{16,0},{24,8},{1,17},{9,25},{17,1},{25,9},{2,18},{10... | collective-permute-start | bytes 196616 | tf_op jit(solution)/shard_map/ppermute | solution.py:34
  7.6 0.0 copy-done
  7.6 0.1 shard_map.46
  7.8 1.8 %collective-permute-done.vec_ref = bf16[8,128,128]{2,1,0:T(8,128)(2,1)S(1)} collective-permute-done((bf16[8,128,128]{2,1,0:T(8,128)(2,1)}, bf16[8,128,128]{2,1,0:T(8,128)(2,1)S(1)}, u32[]{:S(2)}, u32[]{:S(2)}) %collective-permute-start) | collective-permute-done | bytes 262176 | tf_op jit(solution)/shard_map/ppermute | solution.py:20
  9.6 0.1 shard_map.47
  9.8 0.0 collective-permute-done.1.refs_6_
  9.8 0.0 collective-permute-done.2.refs_7_.refs_8_
  9.8 0.8 %shard_map.49 = (f32[2,32,128]{2,1,0:T(8,128)S(1)}, bf16[2,32,128]{2,1,0:T(8,128)(2,1)S(1)}, bf16[4,32,128]{2,1,0:T(8,128)(2,1)S(1)}) custom-call(bf16[1024,128]{1,0:T(8,128)(2,1)S(1)} %get-tuple-element.22.refs_0_, bf16[512,128]{1,0:T(8,128)(2,1)S(1)} %get-tuple-element.23.refs_1_, bf16[1024,128]{1,0:T(8,128)(2,1)S(1)} %get-tuple-element.24.refs_2_, ...), custom_call_target="tpu_custom_call" | custom-call | flops 268435456 | bytes 1048576 | tf_op jit(solution)/shard_map/pallas_call | solution.py:194
  10.6 0.3 %collective-permute-done.3.refs_6_ = bf16[2,128,128]{2,1,0:T(8,128)(2,1)S(1)} collective-permute-done((bf16[2,128,128]{2,1,0:T(8,128)(2,1)S(1)}, bf16[2,128,128]{2,1,0:T(8,128)(2,1)S(1)}, u32[]{:S(2)}, u32[]{:S(2)}) %collective-permute-start.3) | collective-permute-done | bytes 65568 | tf_op jit(solution)/shard_map/ppermute | solution.py:34
  10.9 0.4 %collective-permute-done.4.refs_7_ = bf16[2,128,128]{2,1,0:T(8,128)(2,1)S(1)} collective-permute-done((bf16[2,128,128]{2,1,0:T(8,128)(2,1)S(1)}, bf16[2,128,128]{2,1,0:T(8,128)(2,1)S(1)}, u32[]{:S(2)}, u32[]{:S(2)}) %collective-permute-start.4) | collective-permute-done | bytes 65568 | tf_op jit(solution)/shard_map/ppermute | solution.py:34
  11.4 0.8 %shard_map.50 = (f32[2,32,128]{2,1,0:T(8,128)S(1)}, bf16[4,32,128]{2,1,0:T(8,128)(2,1)S(1)}, bf16[4,32,128]{2,1,0:T(8,128)(2,1)S(1)}, bf16[4,32,128]{2,1,0:T(8,128)(2,1)S(1)}) custom-call(bf16[1024,128]{1,0:T(8,128)(2,1)S(1)} %get-tuple-element.22.refs_0_, bf16[512,128]{1,0:T(8,128)(2,1)S(1)} %get-tuple-element.23.refs_1_, ...), custom_call_target="tpu_custom_call" | custom-call | flops 268435456 | bytes 1048576 | tf_op jit(solution)/shard_map/pallas_call | solution.py:194
  12.2 1.4 %collective-permute-start.5 = (bf16[4,32,128]{2,1,0:T(8,128)(2,1)S(1)}, bf16[4,32,128]{2,1,0:T(8,128)(2,1)S(1)}, u32[]{:S(2)}, u32[]{:S(2)}) collective-permute-start(bf16[4,32,128]{2,1,0:T(8,128)(2,1)S(1)} %get-tuple-element.35), channel_id=1, source_target_pairs={{0,6},{1,7},{2,4},{3,5},{4,2},{5,3},{6,0},{7,1},{8,14},{9,15},{10,... | collective-permute-start | bytes 98312 | tf_op jit(solution)/shard_map/ppermute | solution.py:26
  13.6 1.4 %collective-permute-start.6 = (bf16[4,32,128]{2,1,0:T(8,128)(2,1)S(1)}, bf16[4,32,128]{2,1,0:T(8,128)(2,1)S(1)}, u32[]{:S(2)}, u32[]{:S(2)}) collective-permute-start(bf16[4,32,128]{2,1,0:T(8,128)(2,1)S(1)} %get-tuple-element.36), channel_id=1, source_target_pairs={{0,2},{1,3},{2,0},{3,1},{4,6},{5,7},{6,4},{7,5},{8,10},{9,11},{10,... | collective-permute-start | bytes 98312 | tf_op jit(solution)/shard_map/ppermute | solution.py:20
  15.0 0.1 collective-permute-start.7
  15.1 1.6 %collective-permute-done.5.cross_ref = bf16[4,32,128]{2,1,0:T(8,128)(2,1)S(1)} collective-permute-done((bf16[4,32,128]{2,1,0:T(8,128)(2,1)S(1)}, bf16[4,32,128]{2,1,0:T(8,128)(2,1)S(1)}, u32[]{:S(2)}, u32[]{:S(2)}) %collective-permute-start.5) | collective-permute-done | bytes 32800 | tf_op jit(solution)/shard_map/ppermute | solution.py:26
  16.7 2.1 %collective-permute-done.6.same_ref = bf16[4,32,128]{2,1,0:T(8,128)(2,1)S(1)} collective-permute-done((bf16[4,32,128]{2,1,0:T(8,128)(2,1)S(1)}, bf16[4,32,128]{2,1,0:T(8,128)(2,1)S(1)}, u32[]{:S(2)}, u32[]{:S(2)}) %collective-permute-start.6) | collective-permute-done | bytes 32800 | tf_op jit(solution)/shard_map/ppermute | solution.py:20
  18.8 0.0 collective-permute-done.7.lent_ref
  18.8 0.7 %shard_map.51 = bf16[2,4,32,128]{3,2,1,0:T(8,128)(2,1)} custom-call(f32[2,32,128]{2,1,0:T(8,128)S(1)} %get-tuple-element.29.first_ref, f32[2,32,128]{2,1,0:T(8,128)S(1)} %get-tuple-element.34.second_ref, bf16[4,32,128]{2,1,0:T(8,128)(2,1)S(1)} %collective-permute-done.5.cross_ref, bf16[4,32,128]{2,1,0:T(8,128)(2,1)S(1)} %collective-permute-done.6.same_ref, ...), custom_call_target="tpu_custom_call" | custom-call | bytes 1048576 | tf_op jit(solution)/shard_map/pallas_call | solution.py:194
Async XLA Ops:
  0.0 7.6 %copy-start = (bf16[8,128,128]{2,1,0:T(8,128)(2,1)S(1)}, bf16[8,128,128]{2,1,0:T(8,128)(2,1)}, u32[]{:S(2)}) copy-start(bf16[8,128,128]{2,1,0:T(8,128)(2,1)} %vec_ref.1) | copy-start | bytes 786436
  0.0 9.6 %collective-permute-start = (bf16[8,128,128]{2,1,0:T(8,128)(2,1)}, bf16[8,128,128]{2,1,0:T(8,128)(2,1)S(1)}, u32[]{:S(2)}, u32[]{:S(2)}) collective-permute-start(bf16[8,128,128]{2,1,0:T(8,128)(2,1)} %vec_ref.1), channel_id=1, source_target_pairs={{0,1},{1,0},{2,3},{3,2},{4,5},{5,4},{6,7},{7,6},{8,9},{9,8},{10,11... | collective-permute-start | bytes 786440 | tf_op jit(solution)/shard_map/ppermute | solution.py:20
  4.0 5.8 %collective-permute-start.2 = (bf16[4,128,128]{2,1,0:T(8,128)(2,1)S(1)}, bf16[4,128,128]{2,1,0:T(8,128)(2,1)S(1)}, u32[]{:S(2)}, u32[]{:S(2)}) collective-permute-start(bf16[4,128,128]{2,1,0:T(8,128)(2,1)S(1)} %get-tuple-element.28), channel_id=1, source_target_pairs={{0,4},{4,0},{1,5},{5,1},{2,6},{6,2},{3,7},{7,3},{8,12},{12,8},{9,1... | collective-permute-start | bytes 393224 | tf_op jit(solution)/shard_map/ppermute | solution.py:30
  4.1 5.7 %collective-permute-start.1 = (bf16[2,128,128]{2,1,0:T(8,128)(2,1)S(1)}, bf16[2,128,128]{2,1,0:T(8,128)(2,1)S(1)}, u32[]{:S(2)}, u32[]{:S(2)}) collective-permute-start(bf16[2,128,128]{2,1,0:T(8,128)(2,1)S(1)} %get-tuple-element.27.refs_5_), channel_id=1, source_target_pairs={{0,24},{8,16},{16,8},{24,0},{1,25},{9,17},{17,9},{25,1},{2,26},{10... | collective-permute-start | bytes 196616 | tf_op jit(solution)/shard_map/ppermute | solution.py:34
  6.6 4.4 %collective-permute-start.3 = (bf16[2,128,128]{2,1,0:T(8,128)(2,1)S(1)}, bf16[2,128,128]{2,1,0:T(8,128)(2,1)S(1)}, u32[]{:S(2)}, u32[]{:S(2)}) collective-permute-start(bf16[2,128,128]{2,1,0:T(8,128)(2,1)S(1)} %get-tuple-element.30.refs_4_), channel_id=1, source_target_pairs={{0,8},{8,0},{16,24},{24,16},{1,9},{9,1},{17,25},{25,17},{2,10},{10... | collective-permute-start | bytes 196616 | tf_op jit(solution)/shard_map/ppermute | solution.py:34
  7.1 4.3 %collective-permute-start.4 = (bf16[2,128,128]{2,1,0:T(8,128)(2,1)S(1)}, bf16[2,128,128]{2,1,0:T(8,128)(2,1)S(1)}, u32[]{:S(2)}, u32[]{:S(2)}) collective-permute-start(bf16[2,128,128]{2,1,0:T(8,128)(2,1)S(1)} %get-tuple-element.31.refs_5_), channel_id=1, source_target_pairs={{0,16},{8,24},{16,0},{24,8},{1,17},{9,25},{17,1},{25,9},{2,18},{10... | collective-permute-start | bytes 196616 | tf_op jit(solution)/shard_map/ppermute | solution.py:34
  12.2 4.4 %collective-permute-start.5 = (bf16[4,32,128]{2,1,0:T(8,128)(2,1)S(1)}, bf16[4,32,128]{2,1,0:T(8,128)(2,1)S(1)}, u32[]{:S(2)}, u32[]{:S(2)}) collective-permute-start(bf16[4,32,128]{2,1,0:T(8,128)(2,1)S(1)} %get-tuple-element.35), channel_id=1, source_target_pairs={{0,6},{1,7},{2,4},{3,5},{4,2},{5,3},{6,0},{7,1},{8,14},{9,15},{10,... | collective-permute-start | bytes 98312 | tf_op jit(solution)/shard_map/ppermute | solution.py:26
  13.6 5.2 %collective-permute-start.6 = (bf16[4,32,128]{2,1,0:T(8,128)(2,1)S(1)}, bf16[4,32,128]{2,1,0:T(8,128)(2,1)S(1)}, u32[]{:S(2)}, u32[]{:S(2)}) collective-permute-start(bf16[4,32,128]{2,1,0:T(8,128)(2,1)S(1)} %get-tuple-element.36), channel_id=1, source_target_pairs={{0,2},{1,3},{2,0},{3,1},{4,6},{5,7},{6,4},{7,5},{8,10},{9,11},{10,... | collective-permute-start | bytes 98312 | tf_op jit(solution)/shard_map/ppermute | solution.py:20
  15.0 3.8 %collective-permute-start.7 = (bf16[4,32,128]{2,1,0:T(8,128)(2,1)S(1)}, bf16[4,32,128]{2,1,0:T(8,128)(2,1)S(1)}, u32[]{:S(2)}, u32[]{:S(2)}) collective-permute-start(bf16[4,32,128]{2,1,0:T(8,128)(2,1)S(1)} %get-tuple-element.37), channel_id=1, source_target_pairs={{0,4},{4,0},{1,5},{5,1},{2,6},{6,2},{3,7},{7,3},{8,12},{12,8},{9,1... | collective-permute-start | bytes 98312 | tf_op jit(solution)/shard_map/ppermute | solution.py:30

commit v12 on v11

--- a/solution.py
+++ b/solution.py
@@ -102,6 +102,17 @@
             left_ref[low : low + rows] = vec_ref[q, pl.ds(start, rows), :]
 
 
+def near_kernel(chunks, both_hbm, turned_ref, left_ref, vec_ref, sems):
+    count = vec_ref.shape[0]
+    base = (1 - lax.axis_index("virt") % 2) * count
+    copies = [pltpu.make_async_copy(both_hbm.at[base + q], vec_ref.at[q], sems.at[q]) for q in range(count)]
+    for copy in copies:
+        copy.start()
+    for copy in copies:
+        copy.wait()
+    turn_kernel(chunks, vec_ref, turned_ref, left_ref)
+
+
 def products(ready, inner_ref, sources, outs):
     turned_refs, left_refs = ready[::2], ready[1::2]
     slab = turned_refs[0].shape[1]
@@ -226,7 +237,15 @@
     def work(count):
         return 2 * count * depth * slab * slab
 
-    near = swap_virt(vectors, 1)
+    groups = [[d, d + 1] for d in range(0, virt, 2)]
+    both = lax.all_gather(vectors, "virt", axis_index_groups=groups, tiled=True)
+    near = kernel(
+        functools.partial(near_kernel, chunks),
+        arranged,
+        [pltpu.with_memory_space_constraint(both, pltpu.HBM)],
+        spaces=[pltpu.HBM],
+        scratch=[pltpu.VMEM(vectors.shape, vectors.dtype), pltpu.SemaphoreType.DMA((vectors.shape[0],))],
+    )
     if (firsts, seconds, chips, cores, virt) == (2, CHIPS, CHIPS, 2, 4):
         *kept, cross, gates = kernel(
             mask_split_kernel,
@@ -244,7 +263,7 @@
         )
         got = {step: swap_chip(kept[step], step) for step in STEPS}
         beside = swap_core(cross)
-        ready = kernel(turn, arranged, (vectors,)) + kernel(turn, arranged, (near,))
+        ready = kernel(turn, arranged, (vectors,)) + near
         _, far, *rest = ORDER
         own_first, lent, sending = kernel(
             first_kernel,
@@ -270,7 +289,7 @@
         spaces=[pltpu.SMEM] * 2,
     )
     partner = lax.all_to_all(kept, ("occj", "occi"), split_axis=0, concat_axis=0, tiled=True)
-    ready = kernel(turn, arranged, (vectors,)) + kernel(turn, arranged, (near,))
+    ready = kernel(turn, arranged, (vectors,)) + near
     part = sent(
         kernel(whole_kernel, parts(pairs), (*ready, kept, partner), scratch=[inner(2)], flops=work(pairs))
     )

time: 19.7 us -> 25.1 us (1.27)
  blocking collectives: 0 us -> 9.06 us
  waiting for transfers between devices: 6.3 us -> 3.41 us
  starting transfers between devices: 9.47 us -> 7.64 us
  Pallas kernels: 3.57 us -> 4.66 us
    all_gather x0 -> x1, blocking collectives: none -> 9.06 us  [shards(): both = lax.all_gather(vectors, 'virt', axis_index_groups=groups, tiled=True)]
    ppermute x2 -> x1, starting transfers between devices: 4.42 us -> 1.38 us  [swap_virt(): lax.ppermute(array, 'virt', [(d, d ^ step) for d in range(lax.axis_size('...]
    ppermute x2 -> x1, waiting for transfers between devices: 3.93 us -> 2.05 us  [swap_virt(): lax.ppermute(array, 'virt', [(d, d ^ step) for d in range(lax.axis_size('...]
    ppermute x3, starting transfers between devices: 3.55 us -> 4.68 us  [swap_chip(): lax.ppermute(array, 'occi', [(d, d ^ step) for d in range(lax.axis_size('...]
    pallas_call x6, Pallas kernels: 3.57 us -> 4.66 us  [kernel(): pl.pallas_call(body, out_shape=outs, in_specs=[pl.BlockSpec(memory_space=...]
    ppermute x3, waiting for transfers between devices: 0.77 us -> 0.01 us  [swap_chip(): lax.ppermute(array, 'occi', [(d, d ^ step) for d in range(lax.axis_size('...]
  transfers between devices with their start and end apart: 8 -> 7, of which waited for: 5 -> 2; matrix products, arithmetic and copies ran while one was open for 0% -> 0% of each run, Pallas kernels for 11% -> 8%
where the time goes in v12:
time: 25.1 us; the launch traced here: 24.9 us
  blocking collectives  9.06 us (36%)
  starting transfers between devices  7.64 us (30%)
  Pallas kernels  4.66 us (19%)
  waiting for transfers between devices  3.41 us (14%)
    all_gather x1, blocking collectives, shards(): both = lax.all_gather(vectors, 'virt', axis_index_groups=groups, tiled=True)  9.06 us
    ppermute x3, starting transfers between devices, swap_chip(): lax.ppermute(array, 'occi', [(d, d ^ step) for d in range(lax.axis_size('...  4.68 us
    pallas_call x6, Pallas kernels, kernel(): pl.pallas_call(body, out_shape=outs, in_specs=[pl.BlockSpec(memory_space=...  4.66 us
    ppermute x1, waiting for transfers between devices, swap_virt(): lax.ppermute(array, 'virt', [(d, d ^ step) for d in range(lax.axis_size('...  2.05 us
    ppermute x1, starting transfers between devices, swap_both(): return lax.ppermute(array, ('occj', 'virt'), moves)  1.54 us
    ppermute x1, starting transfers between devices, swap_virt(): lax.ppermute(array, 'virt', [(d, d ^ step) for d in range(lax.axis_size('...  1.38 us
    ppermute x1, waiting for transfers between devices, swap_both(): return lax.ppermute(array, ('occj', 'virt'), moves)  1.34 us
  transfers between devices with their start and end apart: 7, of which 2 were waited for; matrix products, arithmetic and copies ran while one was open for 0% of the time, Pallas kernels for 8%

profile of v12, /device:TPU:0, one launch (start us, length us, event | category | flops | bytes accessed | tf_op | source)
XLA Modules:
  0.0 24.9 jit_solution(1961716293113627291)
XLA Ops:
  0.0 0.0 copy-start
  0.0 1.1 %shard_map.48 = (bf16[2,128,128]{2,1,0:T(8,128)(2,1)S(1)}, bf16[2,128,128]{2,1,0:T(8,128)(2,1)S(1)}, bf16[2,128,128]{2,1,0:T(8,128)(2,1)S(1)}, bf16[2,128,128]{2...) custom-call(s32[2,2,2,4]{3,2,1,0:T(2,128)} %bitcast.1, s32[2,4]{1,0:T(2,128)} %pair_hbm.1, ...), custom_call_target="tpu_custom_call" | custom-call | bytes 1048576 | tf_op jit(solution)/shard_map/pallas_call | solution.py:205
  1.1 4.0 %collective-permute-start = (bf16[2,128,128]{2,1,0:T(8,128)(2,1)S(1)}, bf16[2,128,128]{2,1,0:T(8,128)(2,1)S(1)}, u32[]{:S(2)}, u32[]{:S(2)}) collective-permute-start(bf16[2,128,128]{2,1,0:T(8,128)(2,1)S(1)} %get-tuple-element.27.refs_5_), channel_id=1, source_target_pairs={{0,24},{8,16},{16,8},{24,0},{1,25},{9,17},{17,9},{25,1},{2,26},{10... | collective-permute-start | bytes 196616 | tf_op jit(solution)/shard_map/ppermute | solution.py:34
  5.1 0.0 collective-permute-start.1
  5.1 0.5 %collective-permute-start.2 = (bf16[2,128,128]{2,1,0:T(8,128)(2,1)S(1)}, bf16[2,128,128]{2,1,0:T(8,128)(2,1)S(1)}, u32[]{:S(2)}, u32[]{:S(2)}) collective-permute-start(bf16[2,128,128]{2,1,0:T(8,128)(2,1)S(1)} %get-tuple-element.30.refs_4_), channel_id=1, source_target_pairs={{0,8},{8,0},{16,24},{24,16},{1,9},{9,1},{17,25},{25,17},{2,10},{10... | collective-permute-start | bytes 196616 | tf_op jit(solution)/shard_map/ppermute | solution.py:34
  5.6 0.2 collective-permute-start.3
  5.8 0.0 copy-done
  5.8 9.1 %all_gather.3.both_hbm = bf16[16,128,128]{2,1,0:T(8,128)(2,1)} all-gather(bf16[8,128,128]{2,1,0:T(8,128)(2,1)S(1)} %copy-done), channel_id=1, replica_groups={{0,1},{2,3},{4,5},{6,7},{8,9},{10,11},{12,13},{14,15},{16,17},{18,19},{..., dimensions={0}, use_global_device_ids=true | all-gather | bytes 786432 | tf_op jit(solution)/shard_map/all_gather | solution.py:241
  14.8 0.1 shard_map.46
  15.0 1.1 %shard_map.47 = (bf16[1024,128]{1,0:T(8,128)(2,1)S(1)}, bf16[512,128]{1,0:T(8,128)(2,1)S(1)}) custom-call(bf16[16,128,128]{2,1,0:T(8,128)(2,1)} %all_gather.3.both_hbm), custom_call_target="tpu_custom_call" | custom-call | bytes 1048576 | tf_op jit(solution)/shard_map/pallas_call | solution.py:205
  16.1 0.0 collective-permute-done.refs_6_
  16.1 0.0 collective-permute-done.1.refs_7_.refs_8_
  16.1 0.8 %shard_map.49 = (f32[2,32,128]{2,1,0:T(8,128)S(1)}, bf16[2,32,128]{2,1,0:T(8,128)(2,1)S(1)}, bf16[4,32,128]{2,1,0:T(8,128)(2,1)S(1)}) custom-call(bf16[1024,128]{1,0:T(8,128)(2,1)S(1)} %get-tuple-element.22.refs_0_, bf16[512,128]{1,0:T(8,128)(2,1)S(1)} %get-tuple-element.23.refs_1_, bf16[1024,128]{1,0:T(8,128)(2,1)S(1)} %get-tuple-element.24.refs_2_, ...), custom_call_target="tpu_custom_call" | custom-call | flops 268435456 | bytes 1048576 | tf_op jit(solution)/shard_map/pallas_call | solution.py:205
  17.0 0.0 collective-permute-done.2.refs_6_
  17.0 0.0 collective-permute-done.3.refs_7_
  17.0 0.8 %shard_map.50 = (f32[2,32,128]{2,1,0:T(8,128)S(1)}, bf16[4,32,128]{2,1,0:T(8,128)(2,1)S(1)}, bf16[4,32,128]{2,1,0:T(8,128)(2,1)S(1)}, bf16[4,32,128]{2,1,0:T(8,128)(2,1)S(1)}) custom-call(bf16[1024,128]{1,0:T(8,128)(2,1)S(1)} %get-tuple-element.22.refs_0_, bf16[512,128]{1,0:T(8,128)(2,1)S(1)} %get-tuple-element.23.refs_1_, ...), custom_call_target="tpu_custom_call" | custom-call | flops 268435456 | bytes 1048576 | tf_op jit(solution)/shard_map/pallas_call | solution.py:205
  17.8 1.5 %collective-permute-start.4 = (bf16[4,32,128]{2,1,0:T(8,128)(2,1)S(1)}, bf16[4,32,128]{2,1,0:T(8,128)(2,1)S(1)}, u32[]{:S(2)}, u32[]{:S(2)}) collective-permute-start(bf16[4,32,128]{2,1,0:T(8,128)(2,1)S(1)} %get-tuple-element.35), channel_id=1, source_target_pairs={{0,6},{1,7},{2,4},{3,5},{4,2},{5,3},{6,0},{7,1},{8,14},{9,15},{10,... | collective-permute-start | bytes 98312 | tf_op jit(solution)/shard_map/ppermute | solution.py:26
  19.4 1.4 %collective-permute-start.5 = (bf16[4,32,128]{2,1,0:T(8,128)(2,1)S(1)}, bf16[4,32,128]{2,1,0:T(8,128)(2,1)S(1)}, u32[]{:S(2)}, u32[]{:S(2)}) collective-permute-start(bf16[4,32,128]{2,1,0:T(8,128)(2,1)S(1)} %get-tuple-element.36), channel_id=1, source_target_pairs={{0,2},{1,3},{2,0},{3,1},{4,6},{5,7},{6,4},{7,5},{8,10},{9,11},{10,... | collective-permute-start | bytes 98312 | tf_op jit(solution)/shard_map/ppermute | solution.py:20
  20.8 0.0 collective-permute-start.6
  20.8 1.3 %collective-permute-done.4.cross_ref = bf16[4,32,128]{2,1,0:T(8,128)(2,1)S(1)} collective-permute-done((bf16[4,32,128]{2,1,0:T(8,128)(2,1)S(1)}, bf16[4,32,128]{2,1,0:T(8,128)(2,1)S(1)}, u32[]{:S(2)}, u32[]{:S(2)}) %collective-permute-start.4) | collective-permute-done | bytes 32800 | tf_op jit(solution)/shard_map/ppermute | solution.py:26
  22.1 2.1 %collective-permute-done.5.same_ref = bf16[4,32,128]{2,1,0:T(8,128)(2,1)S(1)} collective-permute-done((bf16[4,32,128]{2,1,0:T(8,128)(2,1)S(1)}, bf16[4,32,128]{2,1,0:T(8,128)(2,1)S(1)}, u32[]{:S(2)}, u32[]{:S(2)}) %collective-permute-start.5) | collective-permute-done | bytes 32800 | tf_op jit(solution)/shard_map/ppermute | solution.py:20
  24.2 0.0 collective-permute-done.6.lent_ref
  24.2 0.7 %shard_map.51 = bf16[2,4,32,128]{3,2,1,0:T(8,128)(2,1)} custom-call(f32[2,32,128]{2,1,0:T(8,128)S(1)} %get-tuple-element.29.first_ref, f32[2,32,128]{2,1,0:T(8,128)S(1)} %get-tuple-element.34.second_ref, bf16[4,32,128]{2,1,0:T(8,128)(2,1)S(1)} %collective-permute-done.4.cross_ref, bf16[4,32,128]{2,1,0:T(8,128)(2,1)S(1)} %collective-permute-done.5.same_ref, ...), custom_call_target="tpu_custom_call" | custom-call | bytes 1048576 | tf_op jit(solution)/shard_map/pallas_call | solution.py:205
Async XLA Ops:
  0.0 5.8 %copy-start = (bf16[8,128,128]{2,1,0:T(8,128)(2,1)S(1)}, bf16[8,128,128]{2,1,0:T(8,128)(2,1)}, u32[]{:S(2)}) copy-start(bf16[8,128,128]{2,1,0:T(8,128)(2,1)} %vec_ref.1) | copy-start | bytes 786436
  1.1 15.0 %collective-permute-start = (bf16[2,128,128]{2,1,0:T(8,128)(2,1)S(1)}, bf16[2,128,128]{2,1,0:T(8,128)(2,1)S(1)}, u32[]{:S(2)}, u32[]{:S(2)}) collective-permute-start(bf16[2,128,128]{2,1,0:T(8,128)(2,1)S(1)} %get-tuple-element.27.refs_5_), channel_id=1, source_target_pairs={{0,24},{8,16},{16,8},{24,0},{1,25},{9,17},{17,9},{25,1},{2,26},{10... | collective-permute-start | bytes 196616 | tf_op jit(solution)/shard_map/ppermute | solution.py:34
  5.1 11.0 %collective-permute-start.1 = (bf16[4,128,128]{2,1,0:T(8,128)(2,1)S(1)}, bf16[4,128,128]{2,1,0:T(8,128)(2,1)S(1)}, u32[]{:S(2)}, u32[]{:S(2)}) collective-permute-start(bf16[4,128,128]{2,1,0:T(8,128)(2,1)S(1)} %get-tuple-element.28), channel_id=1, source_target_pairs={{0,4},{4,0},{1,5},{5,1},{2,6},{6,2},{3,7},{7,3},{8,12},{12,8},{9,1... | collective-permute-start | bytes 393224 | tf_op jit(solution)/shard_map/ppermute | solution.py:30
  5.1 11.9 %collective-permute-start.2 = (bf16[2,128,128]{2,1,0:T(8,128)(2,1)S(1)}, bf16[2,128,128]{2,1,0:T(8,128)(2,1)S(1)}, u32[]{:S(2)}, u32[]{:S(2)}) collective-permute-start(bf16[2,128,128]{2,1,0:T(8,128)(2,1)S(1)} %get-tuple-element.30.refs_4_), channel_id=1, source_target_pairs={{0,8},{8,0},{16,24},{24,16},{1,9},{9,1},{17,25},{25,17},{2,10},{10... | collective-permute-start | bytes 196616 | tf_op jit(solution)/shard_map/ppermute | solution.py:34
  5.6 11.4 %collective-permute-start.3 = (bf16[2,128,128]{2,1,0:T(8,128)(2,1)S(1)}, bf16[2,128,128]{2,1,0:T(8,128)(2,1)S(1)}, u32[]{:S(2)}, u32[]{:S(2)}) collective-permute-start(bf16[2,128,128]{2,1,0:T(8,128)(2,1)S(1)} %get-tuple-element.31.refs_5_), channel_id=1, source_target_pairs={{0,16},{8,24},{16,0},{24,8},{1,17},{9,25},{17,1},{25,9},{2,18},{10... | collective-permute-start | bytes 196616 | tf_op jit(solution)/shard_map/ppermute | solution.py:34
  17.8 4.3 %collective-permute-start.4 = (bf16[4,32,128]{2,1,0:T(8,128)(2,1)S(1)}, bf16[4,32,128]{2,1,0:T(8,128)(2,1)S(1)}, u32[]{:S(2)}, u32[]{:S(2)}) collective-permute-start(bf16[4,32,128]{2,1,0:T(8,128)(2,1)S(1)} %get-tuple-element.35), channel_id=1, source_target_pairs={{0,6},{1,7},{2,4},{3,5},{4,2},{5,3},{6,0},{7,1},{8,14},{9,15},{10,... | collective-permute-start | bytes 98312 | tf_op jit(solution)/shard_map/ppermute | solution.py:26
  19.4 4.8 %collective-permute-start.5 = (bf16[4,32,128]{2,1,0:T(8,128)(2,1)S(1)}, bf16[4,32,128]{2,1,0:T(8,128)(2,1)S(1)}, u32[]{:S(2)}, u32[]{:S(2)}) collective-permute-start(bf16[4,32,128]{2,1,0:T(8,128)(2,1)S(1)} %get-tuple-element.36), channel_id=1, source_target_pairs={{0,2},{1,3},{2,0},{3,1},{4,6},{5,7},{6,4},{7,5},{8,10},{9,11},{10,... | collective-permute-start | bytes 98312 | tf_op jit(solution)/shard_map/ppermute | solution.py:20
  20.8 3.4 %collective-permute-start.6 = (bf16[4,32,128]{2,1,0:T(8,128)(2,1)S(1)}, bf16[4,32,128]{2,1,0:T(8,128)(2,1)S(1)}, u32[]{:S(2)}, u32[]{:S(2)}) collective-permute-start(bf16[4,32,128]{2,1,0:T(8,128)(2,1)S(1)} %get-tuple-element.37), channel_id=1, source_target_pairs={{0,4},{4,0},{1,5},{5,1},{2,6},{6,2},{3,7},{7,3},{8,12},{12,8},{9,1... | collective-permute-start | bytes 98312 | tf_op jit(solution)/shard_map/ppermute | solution.py:30

commit v13 on v11

--- a/solution.py
+++ b/solution.py
@@ -10,8 +10,8 @@
 TILE = 64
 SLAB_TILES = 2
 CHIPS = 4
-STEPS = (3, 1, 2)
-ORDER = (0, 3, 1, 2)
+STEPS = (1, 3, 2)
+ORDER = (0, 1, 3, 2)
 BF16 = jnp.bfloat16
 F32 = jnp.float32
 

time: 19.7 us -> 21.5 us (1.091)
  waiting for transfers between devices: 6.3 us -> 8.17 us
    ppermute x3, waiting for transfers between devices: 0.77 us -> 1.61 us  [swap_chip(): lax.ppermute(array, 'occi', [(d, d ^ step) for d in range(lax.axis_size('...]
    ppermute x1, starting transfers between devices: 1.35 us -> 2.16 us  [swap_both(): return lax.ppermute(array, ('occj', 'virt'), moves)]
    ppermute x2, starting transfers between devices: 4.42 us -> 3.62 us  [swap_virt(): lax.ppermute(array, 'virt', [(d, d ^ step) for d in range(lax.axis_size('...]
    ppermute x1, waiting for transfers between devices: 1.59 us -> 2.39 us  [swap_both(): return lax.ppermute(array, ('occj', 'virt'), moves)]
    ppermute x2, waiting for transfers between devices: 3.93 us -> 4.17 us  [swap_virt(): lax.ppermute(array, 'virt', [(d, d ^ step) for d in range(lax.axis_size('...]
  transfers between devices with their start and end apart: 8 -> 8, of which waited for: 5 -> 5; matrix products, arithmetic and copies ran while one was open for 0% -> 0% of each run, Pallas kernels for 11% -> 10%
where the time goes in v13:
time: 21.5 us; the launch traced here: 21.3 us
  starting transfers between devices  9.47 us (44%)
  waiting for transfers between devices  8.17 us (38%)
  Pallas kernels  3.58 us (17%)
    ppermute x2, waiting for transfers between devices, swap_virt(): lax.ppermute(array, 'virt', [(d, d ^ step) for d in range(lax.axis_size('...  4.17 us
    ppermute x2, starting transfers between devices, swap_virt(): lax.ppermute(array, 'virt', [(d, d ^ step) for d in range(lax.axis_size('...  3.62 us
    pallas_call x6, Pallas kernels, kernel(): pl.pallas_call(body, out_shape=outs, in_specs=[pl.BlockSpec(memory_space=...  3.58 us
    ppermute x3, starting transfers between devices, swap_chip(): lax.ppermute(array, 'occi', [(d, d ^ step) for d in range(lax.axis_size('...  3.55 us
    ppermute x1, waiting for transfers between devices, swap_both(): return lax.ppermute(array, ('occj', 'virt'), moves)  2.39 us
    ppermute x1, starting transfers between devices, swap_both(): return lax.ppermute(array, ('occj', 'virt'), moves)  2.16 us
    ppermute x3, waiting for transfers between devices, swap_chip(): lax.ppermute(array, 'occi', [(d, d ^ step) for d in range(lax.axis_size('...  1.61 us
  transfers between devices with their start and end apart: 8, of which 5 were waited for; matrix products, arithmetic and copies ran while one was open for 0% of the time, Pallas kernels for 10%

profile of v13, /device:TPU:0, one launch (start us, length us, event | category | flops | bytes accessed | tf_op | source)
XLA Modules:
  0.0 21.3 jit_solution(11100655420881345354)
XLA Ops:
  0.0 0.0 copy-start
  0.0 3.0 %collective-permute-start = (bf16[8,128,128]{2,1,0:T(8,128)(2,1)}, bf16[8,128,128]{2,1,0:T(8,128)(2,1)S(1)}, u32[]{:S(2)}, u32[]{:S(2)}) collective-permute-start(bf16[8,128,128]{2,1,0:T(8,128)(2,1)} %vec_ref.1), channel_id=1, source_target_pairs={{0,1},{1,0},{2,3},{3,2},{4,5},{5,4},{6,7},{7,6},{8,9},{9,8},{10,11... | collective-permute-start | bytes 786440 | tf_op jit(solution)/shard_map/ppermute | solution.py:20
  3.0 1.0 %shard_map.48 = (bf16[2,128,128]{2,1,0:T(8,128)(2,1)S(1)}, bf16[2,128,128]{2,1,0:T(8,128)(2,1)S(1)}, bf16[2,128,128]{2,1,0:T(8,128)(2,1)S(1)}, bf16[2,128,128]{2...) custom-call(s32[2,2,2,4]{3,2,1,0:T(2,128)} %bitcast.1, s32[2,4]{1,0:T(2,128)} %pair_hbm.1, ...), custom_call_target="tpu_custom_call" | custom-call | bytes 1048576 | tf_op jit(solution)/shard_map/pallas_call | solution.py:194
  4.0 0.1 collective-permute-start.2
  4.1 1.6 %collective-permute-start.1 = (bf16[2,128,128]{2,1,0:T(8,128)(2,1)S(1)}, bf16[2,128,128]{2,1,0:T(8,128)(2,1)S(1)}, u32[]{:S(2)}, u32[]{:S(2)}) collective-permute-start(bf16[2,128,128]{2,1,0:T(8,128)(2,1)S(1)} %get-tuple-element.27.refs_5_), channel_id=1, source_target_pairs={{0,8},{8,0},{16,24},{24,16},{1,9},{9,1},{17,25},{25,17},{2,10},{10... | collective-permute-start | bytes 196616 | tf_op jit(solution)/shard_map/ppermute | solution.py:34
  5.6 1.5 %collective-permute-start.3 = (bf16[2,128,128]{2,1,0:T(8,128)(2,1)S(1)}, bf16[2,128,128]{2,1,0:T(8,128)(2,1)S(1)}, u32[]{:S(2)}, u32[]{:S(2)}) collective-permute-start(bf16[2,128,128]{2,1,0:T(8,128)(2,1)S(1)} %get-tuple-element.30.refs_4_), channel_id=1, source_target_pairs={{0,24},{8,16},{16,8},{24,0},{1,25},{9,17},{17,9},{25,1},{2,26},{10... | collective-permute-start | bytes 196616 | tf_op jit(solution)/shard_map/ppermute | solution.py:34
  7.1 0.5 %collective-permute-start.4 = (bf16[2,128,128]{2,1,0:T(8,128)(2,1)S(1)}, bf16[2,128,128]{2,1,0:T(8,128)(2,1)S(1)}, u32[]{:S(2)}, u32[]{:S(2)}) collective-permute-start(bf16[2,128,128]{2,1,0:T(8,128)(2,1)S(1)} %get-tuple-element.31.refs_5_), channel_id=1, source_target_pairs={{0,16},{8,24},{16,0},{24,8},{1,17},{9,25},{17,1},{25,9},{2,18},{10... | collective-permute-start | bytes 196616 | tf_op jit(solution)/shard_map/ppermute | solution.py:34
  7.6 0.0 copy-done
  7.6 0.1 shard_map.46
  7.8 1.8 %collective-permute-done.vec_ref = bf16[8,128,128]{2,1,0:T(8,128)(2,1)S(1)} collective-permute-done((bf16[8,128,128]{2,1,0:T(8,128)(2,1)}, bf16[8,128,128]{2,1,0:T(8,128)(2,1)S(1)}, u32[]{:S(2)}, u32[]{:S(2)}) %collective-permute-start) | collective-permute-done | bytes 262176 | tf_op jit(solution)/shard_map/ppermute | solution.py:20
  9.6 0.1 shard_map.47
  9.8 0.0 collective-permute-done.1.refs_6_
  9.8 0.0 collective-permute-done.2.refs_7_.refs_8_
  9.8 0.8 %shard_map.49 = (f32[2,32,128]{2,1,0:T(8,128)S(1)}, bf16[2,32,128]{2,1,0:T(8,128)(2,1)S(1)}, bf16[4,32,128]{2,1,0:T(8,128)(2,1)S(1)}) custom-call(bf16[1024,128]{1,0:T(8,128)(2,1)S(1)} %get-tuple-element.22.refs_0_, bf16[512,128]{1,0:T(8,128)(2,1)S(1)} %get-tuple-element.23.refs_1_, bf16[1024,128]{1,0:T(8,128)(2,1)S(1)} %get-tuple-element.24.refs_2_, ...), custom_call_target="tpu_custom_call" | custom-call | flops 268435456 | bytes 1048576 | tf_op jit(solution)/shard_map/pallas_call | solution.py:194
  10.6 0.4 %collective-permute-done.3.refs_6_ = bf16[2,128,128]{2,1,0:T(8,128)(2,1)S(1)} collective-permute-done((bf16[2,128,128]{2,1,0:T(8,128)(2,1)S(1)}, bf16[2,128,128]{2,1,0:T(8,128)(2,1)S(1)}, u32[]{:S(2)}, u32[]{:S(2)}) %collective-permute-start.3) | collective-permute-done | bytes 65568 | tf_op jit(solution)/shard_map/ppermute | solution.py:34
  11.1 1.2 %collective-permute-done.4.refs_7_ = bf16[2,128,128]{2,1,0:T(8,128)(2,1)S(1)} collective-permute-done((bf16[2,128,128]{2,1,0:T(8,128)(2,1)S(1)}, bf16[2,128,128]{2,1,0:T(8,128)(2,1)S(1)}, u32[]{:S(2)}, u32[]{:S(2)}) %collective-permute-start.4) | collective-permute-done | bytes 65568 | tf_op jit(solution)/shard_map/ppermute | solution.py:34
  12.2 0.8 %shard_map.50 = (f32[2,32,128]{2,1,0:T(8,128)S(1)}, bf16[4,32,128]{2,1,0:T(8,128)(2,1)S(1)}, bf16[4,32,128]{2,1,0:T(8,128)(2,1)S(1)}, bf16[4,32,128]{2,1,0:T(8,128)(2,1)S(1)}) custom-call(bf16[1024,128]{1,0:T(8,128)(2,1)S(1)} %get-tuple-element.22.refs_0_, bf16[512,128]{1,0:T(8,128)(2,1)S(1)} %get-tuple-element.23.refs_1_, ...), custom_call_target="tpu_custom_call" | custom-call | flops 268435456 | bytes 1048576 | tf_op jit(solution)/shard_map/pallas_call | solution.py:194
  13.1 2.2 %collective-permute-start.5 = (bf16[4,32,128]{2,1,0:T(8,128)(2,1)S(1)}, bf16[4,32,128]{2,1,0:T(8,128)(2,1)S(1)}, u32[]{:S(2)}, u32[]{:S(2)}) collective-permute-start(bf16[4,32,128]{2,1,0:T(8,128)(2,1)S(1)} %get-tuple-element.35), channel_id=1, source_target_pairs={{0,6},{1,7},{2,4},{3,5},{4,2},{5,3},{6,0},{7,1},{8,14},{9,15},{10,... | collective-permute-start | bytes 98312 | tf_op jit(solution)/shard_map/ppermute | solution.py:26
  15.2 0.6 %collective-permute-start.6 = (bf16[4,32,128]{2,1,0:T(8,128)(2,1)S(1)}, bf16[4,32,128]{2,1,0:T(8,128)(2,1)S(1)}, u32[]{:S(2)}, u32[]{:S(2)}) collective-permute-start(bf16[4,32,128]{2,1,0:T(8,128)(2,1)S(1)} %get-tuple-element.36), channel_id=1, source_target_pairs={{0,2},{1,3},{2,0},{3,1},{4,6},{5,7},{6,4},{7,5},{8,10},{9,11},{10,... | collective-permute-start | bytes 98312 | tf_op jit(solution)/shard_map/ppermute | solution.py:20
  15.8 0.1 collective-permute-start.7
  15.9 2.4 %collective-permute-done.5.cross_ref = bf16[4,32,128]{2,1,0:T(8,128)(2,1)S(1)} collective-permute-done((bf16[4,32,128]{2,1,0:T(8,128)(2,1)S(1)}, bf16[4,32,128]{2,1,0:T(8,128)(2,1)S(1)}, u32[]{:S(2)}, u32[]{:S(2)}) %collective-permute-start.5) | collective-permute-done | bytes 32800 | tf_op jit(solution)/shard_map/ppermute | solution.py:26
  18.3 2.3 %collective-permute-done.6.same_ref = bf16[4,32,128]{2,1,0:T(8,128)(2,1)S(1)} collective-permute-done((bf16[4,32,128]{2,1,0:T(8,128)(2,1)S(1)}, bf16[4,32,128]{2,1,0:T(8,128)(2,1)S(1)}, u32[]{:S(2)}, u32[]{:S(2)}) %collective-permute-start.6) | collective-permute-done | bytes 32800 | tf_op jit(solution)/shard_map/ppermute | solution.py:20
  20.6 0.0 collective-permute-done.7.lent_ref
  20.6 0.7 %shard_map.51 = bf16[2,4,32,128]{3,2,1,0:T(8,128)(2,1)} custom-call(f32[2,32,128]{2,1,0:T(8,128)S(1)} %get-tuple-element.29.first_ref, f32[2,32,128]{2,1,0:T(8,128)S(1)} %get-tuple-element.34.second_ref, bf16[4,32,128]{2,1,0:T(8,128)(2,1)S(1)} %collective-permute-done.5.cross_ref, bf16[4,32,128]{2,1,0:T(8,128)(2,1)S(1)} %collective-permute-done.6.same_ref, ...), custom_call_target="tpu_custom_call" | custom-call | bytes 1048576 | tf_op jit(solution)/shard_map/pallas_call | solution.py:194
Async XLA Ops:
  0.0 7.6 %copy-start = (bf16[8,128,128]{2,1,0:T(8,128)(2,1)S(1)}, bf16[8,128,128]{2,1,0:T(8,128)(2,1)}, u32[]{:S(2)}) copy-start(bf16[8,128,128]{2,1,0:T(8,128)(2,1)} %vec_ref.1) | copy-start | bytes 786436
  0.0 9.6 %collective-permute-start = (bf16[8,128,128]{2,1,0:T(8,128)(2,1)}, bf16[8,128,128]{2,1,0:T(8,128)(2,1)S(1)}, u32[]{:S(2)}, u32[]{:S(2)}) collective-permute-start(bf16[8,128,128]{2,1,0:T(8,128)(2,1)} %vec_ref.1), channel_id=1, source_target_pairs={{0,1},{1,0},{2,3},{3,2},{4,5},{5,4},{6,7},{7,6},{8,9},{9,8},{10,11... | collective-permute-start | bytes 786440 | tf_op jit(solution)/shard_map/ppermute | solution.py:20
  4.0 5.8 %collective-permute-start.2 = (bf16[4,128,128]{2,1,0:T(8,128)(2,1)S(1)}, bf16[4,128,128]{2,1,0:T(8,128)(2,1)S(1)}, u32[]{:S(2)}, u32[]{:S(2)}) collective-permute-start(bf16[4,128,128]{2,1,0:T(8,128)(2,1)S(1)} %get-tuple-element.28), channel_id=1, source_target_pairs={{0,4},{4,0},{1,5},{5,1},{2,6},{6,2},{3,7},{7,3},{8,12},{12,8},{9,1... | collective-permute-start | bytes 393224 | tf_op jit(solution)/shard_map/ppermute | solution.py:30
  4.1 5.7 %collective-permute-start.1 = (bf16[2,128,128]{2,1,0:T(8,128)(2,1)S(1)}, bf16[2,128,128]{2,1,0:T(8,128)(2,1)S(1)}, u32[]{:S(2)}, u32[]{:S(2)}) collective-permute-start(bf16[2,128,128]{2,1,0:T(8,128)(2,1)S(1)} %get-tuple-element.27.refs_5_), channel_id=1, source_target_pairs={{0,8},{8,0},{16,24},{24,16},{1,9},{9,1},{17,25},{25,17},{2,10},{10... | collective-permute-start | bytes 196616 | tf_op jit(solution)/shard_map/ppermute | solution.py:34
  5.6 5.4 %collective-permute-start.3 = (bf16[2,128,128]{2,1,0:T(8,128)(2,1)S(1)}, bf16[2,128,128]{2,1,0:T(8,128)(2,1)S(1)}, u32[]{:S(2)}, u32[]{:S(2)}) collective-permute-start(bf16[2,128,128]{2,1,0:T(8,128)(2,1)S(1)} %get-tuple-element.30.refs_4_), channel_id=1, source_target_pairs={{0,24},{8,16},{16,8},{24,0},{1,25},{9,17},{17,9},{25,1},{2,26},{10... | collective-permute-start | bytes 196616 | tf_op jit(solution)/shard_map/ppermute | solution.py:34
  7.1 5.1 %collective-permute-start.4 = (bf16[2,128,128]{2,1,0:T(8,128)(2,1)S(1)}, bf16[2,128,128]{2,1,0:T(8,128)(2,1)S(1)}, u32[]{:S(2)}, u32[]{:S(2)}) collective-permute-start(bf16[2,128,128]{2,1,0:T(8,128)(2,1)S(1)} %get-tuple-element.31.refs_5_), channel_id=1, source_target_pairs={{0,16},{8,24},{16,0},{24,8},{1,17},{9,25},{17,1},{25,9},{2,18},{10... | collective-permute-start | bytes 196616 | tf_op jit(solution)/shard_map/ppermute | solution.py:34
  13.1 5.2 %collective-permute-start.5 = (bf16[4,32,128]{2,1,0:T(8,128)(2,1)S(1)}, bf16[4,32,128]{2,1,0:T(8,128)(2,1)S(1)}, u32[]{:S(2)}, u32[]{:S(2)}) collective-permute-start(bf16[4,32,128]{2,1,0:T(8,128)(2,1)S(1)} %get-tuple-element.35), channel_id=1, source_target_pairs={{0,6},{1,7},{2,4},{3,5},{4,2},{5,3},{6,0},{7,1},{8,14},{9,15},{10,... | collective-permute-start | bytes 98312 | tf_op jit(solution)/shard_map/ppermute | solution.py:26
  15.2 5.4 %collective-permute-start.6 = (bf16[4,32,128]{2,1,0:T(8,128)(2,1)S(1)}, bf16[4,32,128]{2,1,0:T(8,128)(2,1)S(1)}, u32[]{:S(2)}, u32[]{:S(2)}) collective-permute-start(bf16[4,32,128]{2,1,0:T(8,128)(2,1)S(1)} %get-tuple-element.36), channel_id=1, source_target_pairs={{0,2},{1,3},{2,0},{3,1},{4,6},{5,7},{6,4},{7,5},{8,10},{9,11},{10,... | collective-permute-start | bytes 98312 | tf_op jit(solution)/shard_map/ppermute | solution.py:20
  15.8 4.8 %collective-permute-start.7 = (bf16[4,32,128]{2,1,0:T(8,128)(2,1)S(1)}, bf16[4,32,128]{2,1,0:T(8,128)(2,1)S(1)}, u32[]{:S(2)}, u32[]{:S(2)}) collective-permute-start(bf16[4,32,128]{2,1,0:T(8,128)(2,1)S(1)} %get-tuple-element.37), channel_id=1, source_target_pairs={{0,4},{4,0},{1,5},{5,1},{2,6},{6,2},{3,7},{7,3},{8,12},{12,8},{9,1... | collective-permute-start | bytes 98312 | tf_op jit(solution)/shard_map/ppermute | solution.py:30

commit v14 on v13

--- a/solution.py
+++ b/solution.py
@@ -10,8 +10,8 @@
 TILE = 64
 SLAB_TILES = 2
 CHIPS = 4
-STEPS = (1, 3, 2)
-ORDER = (0, 1, 3, 2)
+STEPS = (3, 2, 1)
+ORDER = (0, 3, 2, 1)
 BF16 = jnp.bfloat16
 F32 = jnp.float32
 

time: 21.5 us -> 19.6 us (0.912)
  the two profiles are of different devices: /device:TPU:0 before, /device:TPU:1 now
where the time goes in v14:
time: 19.6 us; the launch traced here: 19.4 us
  starting transfers between devices  10 us (51%)
  waiting for transfers between devices  5.73 us (29%)
  Pallas kernels  3.57 us (18%)
    ppermute x1, starting transfers between devices, swap_both(): return lax.ppermute(array, ('occj', 'virt'), moves)  3.75 us
    pallas_call x6, Pallas kernels, kernel(): pl.pallas_call(body, out_shape=outs, in_specs=[pl.BlockSpec(memory_space=...  3.57 us
    ppermute x2, waiting for transfers between devices, swap_virt(): lax.ppermute(array, 'virt', [(d, d ^ step) for d in range(lax.axis_size('...  3.31 us
    ppermute x3, starting transfers between devices, swap_chip(): lax.ppermute(array, 'occi', [(d, d ^ step) for d in range(lax.axis_size('...  2.66 us
    ppermute x2, starting transfers between devices, swap_virt(): lax.ppermute(array, 'virt', [(d, d ^ step) for d in range(lax.axis_size('...  2.18 us
    ppermute x1, waiting for transfers between devices, swap_both(): return lax.ppermute(array, ('occj', 'virt'), moves)  1.92 us
    ppermute x2, starting transfers between devices, swap_core(): return lax.ppermute(array, 'occj', [(0, 1), (1, 0)])  1.46 us
    ppermute x3, waiting for transfers between devices, swap_chip(): lax.ppermute(array, 'occi', [(d, d ^ step) for d in range(lax.axis_size('...  0.51 us
  transfers between devices with their start and end apart: 8, of which 5 were waited for; matrix products, arithmetic and copies ran while one was open for 0% of the time, Pallas kernels for 11%

profile of v14, /device:TPU:1, one launch (start us, length us, event | category | flops | bytes accessed | tf_op | source)
XLA Modules:
  0.0 19.4 jit_solution(1522947026799342342)
XLA Ops:
  0.0 0.0 copy-start
  0.0 2.1 %collective-permute-start = (bf16[8,128,128]{2,1,0:T(8,128)(2,1)}, bf16[8,128,128]{2,1,0:T(8,128)(2,1)S(1)}, u32[]{:S(2)}, u32[]{:S(2)}) collective-permute-start(bf16[8,128,128]{2,1,0:T(8,128)(2,1)} %vec_ref.1), channel_id=1, source_target_pairs={{0,1},{1,0},{2,3},{3,2},{4,5},{5,4},{6,7},{7,6},{8,9},{9,8},{10,11... | collective-permute-start | bytes 786440 | tf_op jit(solution)/shard_map/ppermute | solution.py:20
  2.1 1.0 %shard_map.48 = (bf16[2,128,128]{2,1,0:T(8,128)(2,1)S(1)}, bf16[2,128,128]{2,1,0:T(8,128)(2,1)S(1)}, bf16[2,128,128]{2,1,0:T(8,128)(2,1)S(1)}, bf16[2,128,128]{2...) custom-call(s32[2,2,2,4]{3,2,1,0:T(2,128)} %bitcast.1, s32[2,4]{1,0:T(2,128)} %pair_hbm.1, ...), custom_call_target="tpu_custom_call" | custom-call | bytes 1048576 | tf_op jit(solution)/shard_map/pallas_call | solution.py:194
  3.1 1.0 %collective-permute-start.2 = (bf16[4,128,128]{2,1,0:T(8,128)(2,1)S(1)}, bf16[4,128,128]{2,1,0:T(8,128)(2,1)S(1)}, u32[]{:S(2)}, u32[]{:S(2)}) collective-permute-start(bf16[4,128,128]{2,1,0:T(8,128)(2,1)S(1)} %get-tuple-element.28), channel_id=1, source_target_pairs={{0,4},{4,0},{1,5},{5,1},{2,6},{6,2},{3,7},{7,3},{8,12},{12,8},{9,1... | collective-permute-start | bytes 393224 | tf_op jit(solution)/shard_map/ppermute | solution.py:30
  4.1 2.2 %collective-permute-start.1 = (bf16[2,128,128]{2,1,0:T(8,128)(2,1)S(1)}, bf16[2,128,128]{2,1,0:T(8,128)(2,1)S(1)}, u32[]{:S(2)}, u32[]{:S(2)}) collective-permute-start(bf16[2,128,128]{2,1,0:T(8,128)(2,1)S(1)} %get-tuple-element.27.refs_5_), channel_id=1, source_target_pairs={{0,24},{8,16},{16,8},{24,0},{1,25},{9,17},{17,9},{25,1},{2,26},{10... | collective-permute-start | bytes 196616 | tf_op jit(solution)/shard_map/ppermute | solution.py:34
  6.3 0.2 %collective-permute-start.3 = (bf16[2,128,128]{2,1,0:T(8,128)(2,1)S(1)}, bf16[2,128,128]{2,1,0:T(8,128)(2,1)S(1)}, u32[]{:S(2)}, u32[]{:S(2)}) collective-permute-start(bf16[2,128,128]{2,1,0:T(8,128)(2,1)S(1)} %get-tuple-element.30.refs_4_), channel_id=1, source_target_pairs={{0,16},{8,24},{16,0},{24,8},{1,17},{9,25},{17,1},{25,9},{2,18},{10... | collective-permute-start | bytes 196616 | tf_op jit(solution)/shard_map/ppermute | solution.py:34
  6.5 0.3 %collective-permute-start.4 = (bf16[2,128,128]{2,1,0:T(8,128)(2,1)S(1)}, bf16[2,128,128]{2,1,0:T(8,128)(2,1)S(1)}, u32[]{:S(2)}, u32[]{:S(2)}) collective-permute-start(bf16[2,128,128]{2,1,0:T(8,128)(2,1)S(1)} %get-tuple-element.31.refs_5_), channel_id=1, source_target_pairs={{0,8},{8,0},{16,24},{24,16},{1,9},{9,1},{17,25},{25,17},{2,10},{10... | collective-permute-start | bytes 196616 | tf_op jit(solution)/shard_map/ppermute | solution.py:34
  6.8 0.0 copy-done
  6.8 0.1 shard_map.46
  6.9 1.5 %collective-permute-done.vec_ref = bf16[8,128,128]{2,1,0:T(8,128)(2,1)S(1)} collective-permute-done((bf16[8,128,128]{2,1,0:T(8,128)(2,1)}, bf16[8,128,128]{2,1,0:T(8,128)(2,1)S(1)}, u32[]{:S(2)}, u32[]{:S(2)}) %collective-permute-start) | collective-permute-done | bytes 262176 | tf_op jit(solution)/shard_map/ppermute | solution.py:20
  8.4 0.1 shard_map.47
  8.6 0.1 collective-permute-done.1.refs_6_
  8.7 0.0 collective-permute-done.2.refs_7_.refs_8_
  8.7 0.8 %shard_map.49 = (f32[2,32,128]{2,1,0:T(8,128)S(1)}, bf16[2,32,128]{2,1,0:T(8,128)(2,1)S(1)}, bf16[4,32,128]{2,1,0:T(8,128)(2,1)S(1)}) custom-call(bf16[1024,128]{1,0:T(8,128)(2,1)S(1)} %get-tuple-element.22.refs_0_, bf16[512,128]{1,0:T(8,128)(2,1)S(1)} %get-tuple-element.23.refs_1_, bf16[1024,128]{1,0:T(8,128)(2,1)S(1)} %get-tuple-element.24.refs_2_, ...), custom_call_target="tpu_custom_call" | custom-call | flops 268435456 | bytes 1048576 | tf_op jit(solution)/shard_map/pallas_call | solution.py:194
  9.5 0.4 %collective-permute-done.3.refs_6_ = bf16[2,128,128]{2,1,0:T(8,128)(2,1)S(1)} collective-permute-done((bf16[2,128,128]{2,1,0:T(8,128)(2,1)S(1)}, bf16[2,128,128]{2,1,0:T(8,128)(2,1)S(1)}, u32[]{:S(2)}, u32[]{:S(2)}) %collective-permute-start.3) | collective-permute-done | bytes 65568 | tf_op jit(solution)/shard_map/ppermute | solution.py:34
  9.9 0.0 collective-permute-done.4.refs_7_
  9.9 0.8 %shard_map.50 = (f32[2,32,128]{2,1,0:T(8,128)S(1)}, bf16[4,32,128]{2,1,0:T(8,128)(2,1)S(1)}, bf16[4,32,128]{2,1,0:T(8,128)(2,1)S(1)}, bf16[4,32,128]{2,1,0:T(8,128)(2,1)S(1)}) custom-call(bf16[1024,128]{1,0:T(8,128)(2,1)S(1)} %get-tuple-element.22.refs_0_, bf16[512,128]{1,0:T(8,128)(2,1)S(1)} %get-tuple-element.23.refs_1_, ...), custom_call_target="tpu_custom_call" | custom-call | flops 268435456 | bytes 1048576 | tf_op jit(solution)/shard_map/pallas_call | solution.py:194
  10.8 3.7 %collective-permute-start.5 = (bf16[4,32,128]{2,1,0:T(8,128)(2,1)S(1)}, bf16[4,32,128]{2,1,0:T(8,128)(2,1)S(1)}, u32[]{:S(2)}, u32[]{:S(2)}) collective-permute-start(bf16[4,32,128]{2,1,0:T(8,128)(2,1)S(1)} %get-tuple-element.35), channel_id=1, source_target_pairs={{0,6},{1,7},{2,4},{3,5},{4,2},{5,3},{6,0},{7,1},{8,14},{9,15},{10,... | collective-permute-start | bytes 98312 | tf_op jit(solution)/shard_map/ppermute | solution.py:26
  14.5 0.1 collective-permute-start.6
  14.6 0.4 %collective-permute-start.7 = (bf16[4,32,128]{2,1,0:T(8,128)(2,1)S(1)}, bf16[4,32,128]{2,1,0:T(8,128)(2,1)S(1)}, u32[]{:S(2)}, u32[]{:S(2)}) collective-permute-start(bf16[4,32,128]{2,1,0:T(8,128)(2,1)S(1)} %get-tuple-element.37), channel_id=1, source_target_pairs={{0,4},{4,0},{1,5},{5,1},{2,6},{6,2},{3,7},{7,3},{8,12},{12,8},{9,1... | collective-permute-start | bytes 98312 | tf_op jit(solution)/shard_map/ppermute | solution.py:30
  15.0 1.9 %collective-permute-done.5.cross_ref = bf16[4,32,128]{2,1,0:T(8,128)(2,1)S(1)} collective-permute-done((bf16[4,32,128]{2,1,0:T(8,128)(2,1)S(1)}, bf16[4,32,128]{2,1,0:T(8,128)(2,1)S(1)}, u32[]{:S(2)}, u32[]{:S(2)}) %collective-permute-start.5) | collective-permute-done | bytes 32800 | tf_op jit(solution)/shard_map/ppermute | solution.py:26
  16.9 1.8 %collective-permute-done.6.same_ref = bf16[4,32,128]{2,1,0:T(8,128)(2,1)S(1)} collective-permute-done((bf16[4,32,128]{2,1,0:T(8,128)(2,1)S(1)}, bf16[4,32,128]{2,1,0:T(8,128)(2,1)S(1)}, u32[]{:S(2)}, u32[]{:S(2)}) %collective-permute-start.6) | collective-permute-done | bytes 32800 | tf_op jit(solution)/shard_map/ppermute | solution.py:20
  18.7 0.0 collective-permute-done.7.lent_ref
  18.7 0.7 %shard_map.51 = bf16[2,4,32,128]{3,2,1,0:T(8,128)(2,1)} custom-call(f32[2,32,128]{2,1,0:T(8,128)S(1)} %get-tuple-element.29.first_ref, f32[2,32,128]{2,1,0:T(8,128)S(1)} %get-tuple-element.34.second_ref, bf16[4,32,128]{2,1,0:T(8,128)(2,1)S(1)} %collective-permute-done.5.cross_ref, bf16[4,32,128]{2,1,0:T(8,128)(2,1)S(1)} %collective-permute-done.6.same_ref, ...), custom_call_target="tpu_custom_call" | custom-call | bytes 1048576 | tf_op jit(solution)/shard_map/pallas_call | solution.py:194
Async XLA Ops:
  0.0 6.8 %copy-start = (bf16[8,128,128]{2,1,0:T(8,128)(2,1)S(1)}, bf16[8,128,128]{2,1,0:T(8,128)(2,1)}, u32[]{:S(2)}) copy-start(bf16[8,128,128]{2,1,0:T(8,128)(2,1)} %vec_ref.1) | copy-start | bytes 786436
  0.0 8.4 %collective-permute-start = (bf16[8,128,128]{2,1,0:T(8,128)(2,1)}, bf16[8,128,128]{2,1,0:T(8,128)(2,1)S(1)}, u32[]{:S(2)}, u32[]{:S(2)}) collective-permute-start(bf16[8,128,128]{2,1,0:T(8,128)(2,1)} %vec_ref.1), channel_id=1, source_target_pairs={{0,1},{1,0},{2,3},{3,2},{4,5},{5,4},{6,7},{7,6},{8,9},{9,8},{10,11... | collective-permute-start | bytes 786440 | tf_op jit(solution)/shard_map/ppermute | solution.py:20
  3.1 5.6 %collective-permute-start.2 = (bf16[4,128,128]{2,1,0:T(8,128)(2,1)S(1)}, bf16[4,128,128]{2,1,0:T(8,128)(2,1)S(1)}, u32[]{:S(2)}, u32[]{:S(2)}) collective-permute-start(bf16[4,128,128]{2,1,0:T(8,128)(2,1)S(1)} %get-tuple-element.28), channel_id=1, source_target_pairs={{0,4},{4,0},{1,5},{5,1},{2,6},{6,2},{3,7},{7,3},{8,12},{12,8},{9,1... | collective-permute-start | bytes 393224 | tf_op jit(solution)/shard_map/ppermute | solution.py:30
  4.1 4.6 %collective-permute-start.1 = (bf16[2,128,128]{2,1,0:T(8,128)(2,1)S(1)}, bf16[2,128,128]{2,1,0:T(8,128)(2,1)S(1)}, u32[]{:S(2)}, u32[]{:S(2)}) collective-permute-start(bf16[2,128,128]{2,1,0:T(8,128)(2,1)S(1)} %get-tuple-element.27.refs_5_), channel_id=1, source_target_pairs={{0,24},{8,16},{16,8},{24,0},{1,25},{9,17},{17,9},{25,1},{2,26},{10... | collective-permute-start | bytes 196616 | tf_op jit(solution)/shard_map/ppermute | solution.py:34
  6.3 3.6 %collective-permute-start.3 = (bf16[2,128,128]{2,1,0:T(8,128)(2,1)S(1)}, bf16[2,128,128]{2,1,0:T(8,128)(2,1)S(1)}, u32[]{:S(2)}, u32[]{:S(2)}) collective-permute-start(bf16[2,128,128]{2,1,0:T(8,128)(2,1)S(1)} %get-tuple-element.30.refs_4_), channel_id=1, source_target_pairs={{0,16},{8,24},{16,0},{24,8},{1,17},{9,25},{17,1},{25,9},{2,18},{10... | collective-permute-start | bytes 196616 | tf_op jit(solution)/shard_map/ppermute | solution.py:34
  6.5 3.4 %collective-permute-start.4 = (bf16[2,128,128]{2,1,0:T(8,128)(2,1)S(1)}, bf16[2,128,128]{2,1,0:T(8,128)(2,1)S(1)}, u32[]{:S(2)}, u32[]{:S(2)}) collective-permute-start(bf16[2,128,128]{2,1,0:T(8,128)(2,1)S(1)} %get-tuple-element.31.refs_5_), channel_id=1, source_target_pairs={{0,8},{8,0},{16,24},{24,16},{1,9},{9,1},{17,25},{25,17},{2,10},{10... | collective-permute-start | bytes 196616 | tf_op jit(solution)/shard_map/ppermute | solution.py:34
  10.8 6.2 %collective-permute-start.5 = (bf16[4,32,128]{2,1,0:T(8,128)(2,1)S(1)}, bf16[4,32,128]{2,1,0:T(8,128)(2,1)S(1)}, u32[]{:S(2)}, u32[]{:S(2)}) collective-permute-start(bf16[4,32,128]{2,1,0:T(8,128)(2,1)S(1)} %get-tuple-element.35), channel_id=1, source_target_pairs={{0,6},{1,7},{2,4},{3,5},{4,2},{5,3},{6,0},{7,1},{8,14},{9,15},{10,... | collective-permute-start | bytes 98312 | tf_op jit(solution)/shard_map/ppermute | solution.py:26
  14.5 4.2 %collective-permute-start.6 = (bf16[4,32,128]{2,1,0:T(8,128)(2,1)S(1)}, bf16[4,32,128]{2,1,0:T(8,128)(2,1)S(1)}, u32[]{:S(2)}, u32[]{:S(2)}) collective-permute-start(bf16[4,32,128]{2,1,0:T(8,128)(2,1)S(1)} %get-tuple-element.36), channel_id=1, source_target_pairs={{0,2},{1,3},{2,0},{3,1},{4,6},{5,7},{6,4},{7,5},{8,10},{9,11},{10,... | collective-permute-start | bytes 98312 | tf_op jit(solution)/shard_map/ppermute | solution.py:20
  14.6 4.2 %collective-permute-start.7 = (bf16[4,32,128]{2,1,0:T(8,128)(2,1)S(1)}, bf16[4,32,128]{2,1,0:T(8,128)(2,1)S(1)}, u32[]{:S(2)}, u32[]{:S(2)}) collective-permute-start(bf16[4,32,128]{2,1,0:T(8,128)(2,1)S(1)} %get-tuple-element.37), channel_id=1, source_target_pairs={{0,4},{4,0},{1,5},{5,1},{2,6},{6,2},{3,7},{7,3},{8,12},{12,8},{9,1... | collective-permute-start | bytes 98312 | tf_op jit(solution)/shard_map/ppermute | solution.py:30

commit v15 on v14

--- a/solution.py
+++ b/solution.py
@@ -90,43 +90,40 @@
     lax.fori_loop(0, kept_ref.shape[0], one, 0)
 
 
-def turn_kernel(chunks, vec_ref, turned_ref, left_ref):
-    vectors, slab, _ = vec_ref.shape
-    rows = left_ref.shape[0] // (vectors * chunks)
+def turn_kernel(chunks, *refs):
+    vec_refs, turned_ref, left_ref = refs[:-2], refs[-2], refs[-1]
+    slab = turned_ref.shape[1]
+    rows = slab * left_ref.shape[0] // (turned_ref.shape[0] * chunks)
     me = lax.axis_index("virt")
-    for q in range(vectors):
-        turned_ref[q * slab : (q + 1) * slab] = vec_ref[q].astype(F32).T.astype(BF16)
-        for chunk in range(chunks):
-            start = pl.multiple_of((me ^ (2 * chunk)) * rows, rows)
-            low = (q * chunks + chunk) * rows
-            left_ref[low : low + rows] = vec_ref[q, pl.ds(start, rows), :]
+    at, low = 0, 0
+    for vec_ref in vec_refs:
+        for q in range(vec_ref.shape[0]):
+            turned_ref[at : at + slab] = vec_ref[q].astype(F32).T.astype(BF16)
+            at += slab
+            for chunk in range(chunks):
+                start = pl.multiple_of((me ^ (2 * chunk)) * rows, rows)
+                left_ref[low : low + rows] = vec_ref[q, pl.ds(start, rows), :]
+                low += rows
 
 
 def products(ready, inner_ref, sources, outs):
-    turned_refs, left_refs = ready[::2], ready[1::2]
-    slab = turned_refs[0].shape[1]
-    depth = turned_refs[0].shape[0]
-    vectors = depth // slab
-    height = left_refs[0].shape[0] // vectors
+    turned_ref, left_ref = ready
+    slab = turned_ref.shape[1]
+    vectors = turned_ref.shape[0] // slab
+    height = left_ref.shape[0] // vectors
     rows = height // len(outs[0])
     for base in range(0, len(sources), 2):
         both = [
             (kept.astype(F32) + partner.astype(F32).T).astype(BF16)
             for kept, partner in sources[base : base + 2]
         ]
-        right = jnp.concatenate(both, axis=1)
-        for side, left_ref in enumerate(left_refs):
-            inner = jnp.dot(left_ref[...], right, preferred_element_type=F32).astype(BF16)
-            for n in range(len(both)):
-                for q in range(vectors):
-                    at = side * depth + q * slab
-                    inner_ref[(base + n) * height : (base + n + 1) * height, at : at + slab] = inner[
-                        q * height : (q + 1) * height, n * slab : (n + 1) * slab
-                    ]
-    half = sum(
-        jnp.dot(inner_ref[:, side * depth : (side + 1) * depth], turned_ref[...], preferred_element_type=F32)
-        for side, turned_ref in enumerate(turned_refs)
-    )
+        inner = jnp.dot(left_ref[...], jnp.concatenate(both, axis=1), preferred_element_type=F32).astype(BF16)
+        for n in range(len(both)):
+            for q in range(vectors):
+                inner_ref[(base + n) * height : (base + n + 1) * height, q * slab : (q + 1) * slab] = inner[
+                    q * height : (q + 1) * height, n * slab : (n + 1) * slab
+                ]
+    half = jnp.dot(inner_ref[...], turned_ref[...], preferred_element_type=F32)
     for n, targets in enumerate(outs):
         for chunk, (ref, index) in enumerate(targets):
             start = n * height + chunk * rows
@@ -134,7 +131,7 @@
 
 
 def first_kernel(*refs):
-    ready, (kept_ref, far_ref, got_ref, beside_ref), outs = refs[:4], refs[4:8], refs[8:]
+    ready, (kept_ref, far_ref, got_ref, beside_ref), outs = refs[:2], refs[2:6], refs[6:]
     own_ref, lent_ref, send_ref, inner_ref = outs
     sources = [
         (kept_ref[0], kept_ref[0]),
@@ -147,8 +144,8 @@
 
 
 def second_kernel(*refs):
-    ready, kept_refs, got_refs, (beside_ref, lent_in, send_in) = refs[:4], refs[4:6], refs[6:8], refs[8:11]
-    own_ref, lent_ref, same_ref, cross_ref, inner_ref = refs[11:]
+    ready, kept_refs, got_refs, (beside_ref, lent_in, send_in) = refs[:2], refs[2:4], refs[4:6], refs[6:9]
+    own_ref, lent_ref, same_ref, cross_ref, inner_ref = refs[9:]
     sources = [(kept[0], got[0]) for kept, got in zip(kept_refs, got_refs)]
     sources += [(beside_ref[step], got[1]) for step, got in zip(ORDER[2:], got_refs)]
     targets = [[(own_ref, n), (same_ref, 2 + n)] for n in range(2)]
@@ -160,7 +157,7 @@
 
 
 def whole_kernel(*refs):
-    ready, (kept_ref, partner_ref), part_refs, inner_ref = refs[:4], refs[4:6], refs[6:-1], refs[-1]
+    ready, (kept_ref, partner_ref), part_refs, inner_ref = refs[:2], refs[2:4], refs[4:-1], refs[-1]
 
     def two(g, carry):
         pairs = [2 * g, 2 * g + 1]
@@ -211,7 +208,7 @@
     depth = 2 * vectors.shape[0] * slab
     turned_mask = jnp.transpose(tile_mask, (0, 2, 3, 1))
     gate = shaped(F32, pairs, 8, slab)
-    arranged = [shaped(BF16, depth // 2, slab), shaped(BF16, depth // 4, slab)]
+    arranged = [shaped(BF16, depth, slab), shaped(BF16, depth // slab * chunks * rows, slab)]
     turn = functools.partial(turn_kernel, chunks)
 
     def parts(count):
@@ -244,7 +241,7 @@
         )
         got = {step: swap_chip(kept[step], step) for step in STEPS}
         beside = swap_core(cross)
-        ready = kernel(turn, arranged, (vectors,)) + kernel(turn, arranged, (near,))
+        ready = kernel(turn, arranged, (vectors, near))
         _, far, *rest = ORDER
         own_first, lent, sending = kernel(
             first_kernel,
@@ -270,7 +267,7 @@
         spaces=[pltpu.SMEM] * 2,
     )
     partner = lax.all_to_all(kept, ("occj", "occi"), split_axis=0, concat_axis=0, tiled=True)
-    ready = kernel(turn, arranged, (vectors,)) + kernel(turn, arranged, (near,))
+    ready = kernel(turn, arranged, (vectors, near))
     part = sent(
         kernel(whole_kernel, parts(pairs), (*ready, kept, partner), scratch=[inner(2)], flops=work(pairs))
     )

time: 19.6 us -> 19.6 us (level)
    pallas_call x6 -> x5, Pallas kernels: 3.57 us -> 3.48 us  [kernel(): pl.pallas_call(body, out_shape=outs, in_specs=[pl.BlockSpec(memory_space=...]
  transfers between devices with their start and end apart: 8 -> 8, of which waited for: 5 -> 4; matrix products, arithmetic and copies ran while one was open for 0% -> 0% of each run, Pallas kernels for 11% -> 10%
where the time goes in v15:
time: 19.6 us; the launch traced here: 19.4 us
  starting transfers between devices  10 us (51%)
  waiting for transfers between devices  5.85 us (30%)
  Pallas kernels  3.48 us (18%)
    ppermute x1, starting transfers between devices, swap_both(): return lax.ppermute(array, ('occj', 'virt'), moves)  3.74 us
    ppermute x2, waiting for transfers between devices, swap_virt(): lax.ppermute(array, 'virt', [(d, d ^ step) for d in range(lax.axis_size('...  3.48 us
    pallas_call x5, Pallas kernels, kernel(): pl.pallas_call(body, out_shape=outs, in_specs=[pl.BlockSpec(memory_space=...  3.48 us
    ppermute x3, starting transfers between devices, swap_chip(): lax.ppermute(array, 'occi', [(d, d ^ step) for d in range(lax.axis_size('...  2.66 us
    ppermute x2, starting transfers between devices, swap_virt(): lax.ppermute(array, 'virt', [(d, d ^ step) for d in range(lax.axis_size('...  2.18 us
    ppermute x1, waiting for transfers between devices, swap_both(): return lax.ppermute(array, ('occj', 'virt'), moves)  1.92 us
    ppermute x2, starting transfers between devices, swap_core(): return lax.ppermute(array, 'occj', [(0, 1), (1, 0)])  1.45 us
    ppermute x3, waiting for transfers between devices, swap_chip(): lax.ppermute(array, 'occi', [(d, d ^ step) for d in range(lax.axis_size('...  0.45 us
  transfers between devices with their start and end apart: 8, of which 4 were waited for; matrix products, arithmetic and copies ran while one was open for 0% of the time, Pallas kernels for 10%

profile of v15, /device:TPU:1, one launch (start us, length us, event | category | flops | bytes accessed | tf_op | source)
XLA Modules:
  0.0 19.4 jit_solution(6327979831825070702)
XLA Ops:
  0.0 0.0 copy-start
  0.0 2.1 %collective-permute-start = (bf16[8,128,128]{2,1,0:T(8,128)(2,1)}, bf16[8,128,128]{2,1,0:T(8,128)(2,1)S(1)}, u32[]{:S(2)}, u32[]{:S(2)}) collective-permute-start(bf16[8,128,128]{2,1,0:T(8,128)(2,1)} %refs_0_.1), channel_id=1, source_target_pairs={{0,1},{1,0},{2,3},{3,2},{4,5},{5,4},{6,7},{7,6},{8,9},{9,8},{10,11... | collective-permute-start | bytes 786440 | tf_op jit(solution)/shard_map/ppermute | solution.py:20
  2.1 1.0 %shard_map.47 = (bf16[2,128,128]{2,1,0:T(8,128)(2,1)S(1)}, bf16[2,128,128]{2,1,0:T(8,128)(2,1)S(1)}, bf16[2,128,128]{2,1,0:T(8,128)(2,1)S(1)}, bf16[2,128,128]{2...) custom-call(s32[2,2,2,4]{3,2,1,0:T(2,128)} %bitcast.1, s32[2,4]{1,0:T(2,128)} %pair_hbm.1, ...), custom_call_target="tpu_custom_call" | custom-call | bytes 1048576 | tf_op jit(solution)/shard_map/pallas_call | solution.py:191
  3.1 1.0 %collective-permute-start.2 = (bf16[4,128,128]{2,1,0:T(8,128)(2,1)S(1)}, bf16[4,128,128]{2,1,0:T(8,128)(2,1)S(1)}, u32[]{:S(2)}, u32[]{:S(2)}) collective-permute-start(bf16[4,128,128]{2,1,0:T(8,128)(2,1)S(1)} %get-tuple-element.24), channel_id=1, source_target_pairs={{0,4},{4,0},{1,5},{5,1},{2,6},{6,2},{3,7},{7,3},{8,12},{12,8},{9,1... | collective-permute-start | bytes 393224 | tf_op jit(solution)/shard_map/ppermute | solution.py:30
  4.1 2.2 %collective-permute-start.1 = (bf16[2,128,128]{2,1,0:T(8,128)(2,1)S(1)}, bf16[2,128,128]{2,1,0:T(8,128)(2,1)S(1)}, u32[]{:S(2)}, u32[]{:S(2)}) collective-permute-start(bf16[2,128,128]{2,1,0:T(8,128)(2,1)S(1)} %get-tuple-element.23.refs_3_), channel_id=1, source_target_pairs={{0,24},{8,16},{16,8},{24,0},{1,25},{9,17},{17,9},{25,1},{2,26},{10... | collective-permute-start | bytes 196616 | tf_op jit(solution)/shard_map/ppermute | solution.py:34
  6.3 0.2 %collective-permute-start.3 = (bf16[2,128,128]{2,1,0:T(8,128)(2,1)S(1)}, bf16[2,128,128]{2,1,0:T(8,128)(2,1)S(1)}, u32[]{:S(2)}, u32[]{:S(2)}) collective-permute-start(bf16[2,128,128]{2,1,0:T(8,128)(2,1)S(1)} %get-tuple-element.26.refs_2_), channel_id=1, source_target_pairs={{0,16},{8,24},{16,0},{24,8},{1,17},{9,25},{17,1},{25,9},{2,18},{10... | collective-permute-start | bytes 196616 | tf_op jit(solution)/shard_map/ppermute | solution.py:34
  6.5 0.3 %collective-permute-start.4 = (bf16[2,128,128]{2,1,0:T(8,128)(2,1)S(1)}, bf16[2,128,128]{2,1,0:T(8,128)(2,1)S(1)}, u32[]{:S(2)}, u32[]{:S(2)}) collective-permute-start(bf16[2,128,128]{2,1,0:T(8,128)(2,1)S(1)} %get-tuple-element.27.refs_3_), channel_id=1, source_target_pairs={{0,8},{8,0},{16,24},{24,16},{1,9},{9,1},{17,25},{25,17},{2,10},{10... | collective-permute-start | bytes 196616 | tf_op jit(solution)/shard_map/ppermute | solution.py:34
  6.8 1.7 %collective-permute-done.refs_1_ = bf16[8,128,128]{2,1,0:T(8,128)(2,1)S(1)} collective-permute-done((bf16[8,128,128]{2,1,0:T(8,128)(2,1)}, bf16[8,128,128]{2,1,0:T(8,128)(2,1)S(1)}, u32[]{:S(2)}, u32[]{:S(2)}) %collective-permute-start) | collective-permute-done | bytes 262176 | tf_op jit(solution)/shard_map/ppermute | solution.py:20
  8.4 0.0 copy-done
  8.4 0.2 %shard_map.46 = (bf16[2048,128]{1,0:T(8,128)(2,1)S(1)}, bf16[1024,128]{1,0:T(8,128)(2,1)S(1)}) custom-call(bf16[8,128,128]{2,1,0:T(8,128)(2,1)S(1)} %copy-done, bf16[8,128,128]{2,1,0:T(8,128)(2,1)S(1)} %collective-permute-done.refs_1_), custom_call_target="tpu_custom_call" | custom-call | bytes 1048576 | tf_op jit(solution)/shard_map/pallas_call | solution.py:191
  8.7 0.0 collective-permute-done.1.refs_4_
  8.7 0.0 collective-permute-done.2.refs_5_.refs_6_
  8.7 0.8 %shard_map.48 = (f32[2,32,128]{2,1,0:T(8,128)S(1)}, bf16[2,32,128]{2,1,0:T(8,128)(2,1)S(1)}, bf16[4,32,128]{2,1,0:T(8,128)(2,1)S(1)}) custom-call(bf16[2048,128]{1,0:T(8,128)(2,1)S(1)} %get-tuple-element.20.refs_0_, bf16[1024,128]{1,0:T(8,128)(2,1)S(1)} %get-tuple-element.21.refs_1_, bf16[2,128,128]{2,1,0:T(8,128)(2,1)S(1)} %get-tuple-element.22.refs_2_, ...), custom_call_target="tpu_custom_call" | custom-call | flops 268435456 | bytes 1048576 | tf_op jit(solution)/shard_map/pallas_call | solution.py:191
  9.5 0.4 %collective-permute-done.3.refs_4_ = bf16[2,128,128]{2,1,0:T(8,128)(2,1)S(1)} collective-permute-done((bf16[2,128,128]{2,1,0:T(8,128)(2,1)S(1)}, bf16[2,128,128]{2,1,0:T(8,128)(2,1)S(1)}, u32[]{:S(2)}, u32[]{:S(2)}) %collective-permute-start.3) | collective-permute-done | bytes 65568 | tf_op jit(solution)/shard_map/ppermute | solution.py:34
  9.9 0.0 collective-permute-done.4.refs_5_
  9.9 0.8 %shard_map.49 = (f32[2,32,128]{2,1,0:T(8,128)S(1)}, bf16[4,32,128]{2,1,0:T(8,128)(2,1)S(1)}, bf16[4,32,128]{2,1,0:T(8,128)(2,1)S(1)}, bf16[4,32,128]{2,1,0:T(8,128)(2,1)S(1)}) custom-call(bf16[2048,128]{1,0:T(8,128)(2,1)S(1)} %get-tuple-element.20.refs_0_, bf16[1024,128]{1,0:T(8,128)(2,1)S(1)} %get-tuple-element.21.refs_1_, ...), custom_call_target="tpu_custom_call" | custom-call | flops 268435456 | bytes 1048576 | tf_op jit(solution)/shard_map/pallas_call | solution.py:191
  10.8 3.7 %collective-permute-start.5 = (bf16[4,32,128]{2,1,0:T(8,128)(2,1)S(1)}, bf16[4,32,128]{2,1,0:T(8,128)(2,1)S(1)}, u32[]{:S(2)}, u32[]{:S(2)}) collective-permute-start(bf16[4,32,128]{2,1,0:T(8,128)(2,1)S(1)} %get-tuple-element.31), channel_id=1, source_target_pairs={{0,6},{1,7},{2,4},{3,5},{4,2},{5,3},{6,0},{7,1},{8,14},{9,15},{10,... | collective-permute-start | bytes 98312 | tf_op jit(solution)/shard_map/ppermute | solution.py:26
  14.5 0.1 collective-permute-start.6
  14.6 0.4 %collective-permute-start.7 = (bf16[4,32,128]{2,1,0:T(8,128)(2,1)S(1)}, bf16[4,32,128]{2,1,0:T(8,128)(2,1)S(1)}, u32[]{:S(2)}, u32[]{:S(2)}) collective-permute-start(bf16[4,32,128]{2,1,0:T(8,128)(2,1)S(1)} %get-tuple-element.33), channel_id=1, source_target_pairs={{0,4},{4,0},{1,5},{5,1},{2,6},{6,2},{3,7},{7,3},{8,12},{12,8},{9,1... | collective-permute-start | bytes 98312 | tf_op jit(solution)/shard_map/ppermute | solution.py:30
  15.0 1.9 %collective-permute-done.5.cross_ref = bf16[4,32,128]{2,1,0:T(8,128)(2,1)S(1)} collective-permute-done((bf16[4,32,128]{2,1,0:T(8,128)(2,1)S(1)}, bf16[4,32,128]{2,1,0:T(8,128)(2,1)S(1)}, u32[]{:S(2)}, u32[]{:S(2)}) %collective-permute-start.5) | collective-permute-done | bytes 32800 | tf_op jit(solution)/shard_map/ppermute | solution.py:26
  16.9 1.8 %collective-permute-done.6.same_ref = bf16[4,32,128]{2,1,0:T(8,128)(2,1)S(1)} collective-permute-done((bf16[4,32,128]{2,1,0:T(8,128)(2,1)S(1)}, bf16[4,32,128]{2,1,0:T(8,128)(2,1)S(1)}, u32[]{:S(2)}, u32[]{:S(2)}) %collective-permute-start.6) | collective-permute-done | bytes 32800 | tf_op jit(solution)/shard_map/ppermute | solution.py:20
  18.8 0.0 collective-permute-done.7.lent_ref
  18.8 0.7 %shard_map.50 = bf16[2,4,32,128]{3,2,1,0:T(8,128)(2,1)} custom-call(f32[2,32,128]{2,1,0:T(8,128)S(1)} %get-tuple-element.25.first_ref, f32[2,32,128]{2,1,0:T(8,128)S(1)} %get-tuple-element.30.second_ref, bf16[4,32,128]{2,1,0:T(8,128)(2,1)S(1)} %collective-permute-done.5.cross_ref, bf16[4,32,128]{2,1,0:T(8,128)(2,1)S(1)} %collective-permute-done.6.same_ref, ...), custom_call_target="tpu_custom_call" | custom-call | bytes 1048576 | tf_op jit(solution)/shard_map/pallas_call | solution.py:191
Async XLA Ops:
  0.0 8.4 %copy-start = (bf16[8,128,128]{2,1,0:T(8,128)(2,1)S(1)}, bf16[8,128,128]{2,1,0:T(8,128)(2,1)}, u32[]{:S(2)}) copy-start(bf16[8,128,128]{2,1,0:T(8,128)(2,1)} %refs_0_.1) | copy-start | bytes 786436
  0.0 8.4 %collective-permute-start = (bf16[8,128,128]{2,1,0:T(8,128)(2,1)}, bf16[8,128,128]{2,1,0:T(8,128)(2,1)S(1)}, u32[]{:S(2)}, u32[]{:S(2)}) collective-permute-start(bf16[8,128,128]{2,1,0:T(8,128)(2,1)} %refs_0_.1), channel_id=1, source_target_pairs={{0,1},{1,0},{2,3},{3,2},{4,5},{5,4},{6,7},{7,6},{8,9},{9,8},{10,11... | collective-permute-start | bytes 786440 | tf_op jit(solution)/shard_map/ppermute | solution.py:20
  3.1 5.6 %collective-permute-start.2 = (bf16[4,128,128]{2,1,0:T(8,128)(2,1)S(1)}, bf16[4,128,128]{2,1,0:T(8,128)(2,1)S(1)}, u32[]{:S(2)}, u32[]{:S(2)}) collective-permute-start(bf16[4,128,128]{2,1,0:T(8,128)(2,1)S(1)} %get-tuple-element.24), channel_id=1, source_target_pairs={{0,4},{4,0},{1,5},{5,1},{2,6},{6,2},{3,7},{7,3},{8,12},{12,8},{9,1... | collective-permute-start | bytes 393224 | tf_op jit(solution)/shard_map/ppermute | solution.py:30
  4.1 4.6 %collective-permute-start.1 = (bf16[2,128,128]{2,1,0:T(8,128)(2,1)S(1)}, bf16[2,128,128]{2,1,0:T(8,128)(2,1)S(1)}, u32[]{:S(2)}, u32[]{:S(2)}) collective-permute-start(bf16[2,128,128]{2,1,0:T(8,128)(2,1)S(1)} %get-tuple-element.23.refs_3_), channel_id=1, source_target_pairs={{0,24},{8,16},{16,8},{24,0},{1,25},{9,17},{17,9},{25,1},{2,26},{10... | collective-permute-start | bytes 196616 | tf_op jit(solution)/shard_map/ppermute | solution.py:34
  6.3 3.6 %collective-permute-start.3 = (bf16[2,128,128]{2,1,0:T(8,128)(2,1)S(1)}, bf16[2,128,128]{2,1,0:T(8,128)(2,1)S(1)}, u32[]{:S(2)}, u32[]{:S(2)}) collective-permute-start(bf16[2,128,128]{2,1,0:T(8,128)(2,1)S(1)} %get-tuple-element.26.refs_2_), channel_id=1, source_target_pairs={{0,16},{8,24},{16,0},{24,8},{1,17},{9,25},{17,1},{25,9},{2,18},{10... | collective-permute-start | bytes 196616 | tf_op jit(solution)/shard_map/ppermute | solution.py:34
  6.5 3.4 %collective-permute-start.4 = (bf16[2,128,128]{2,1,0:T(8,128)(2,1)S(1)}, bf16[2,128,128]{2,1,0:T(8,128)(2,1)S(1)}, u32[]{:S(2)}, u32[]{:S(2)}) collective-permute-start(bf16[2,128,128]{2,1,0:T(8,128)(2,1)S(1)} %get-tuple-element.27.refs_3_), channel_id=1, source_target_pairs={{0,8},{8,0},{16,24},{24,16},{1,9},{9,1},{17,25},{25,17},{2,10},{10... | collective-permute-start | bytes 196616 | tf_op jit(solution)/shard_map/ppermute | solution.py:34
  10.8 6.2 %collective-permute-start.5 = (bf16[4,32,128]{2,1,0:T(8,128)(2,1)S(1)}, bf16[4,32,128]{2,1,0:T(8,128)(2,1)S(1)}, u32[]{:S(2)}, u32[]{:S(2)}) collective-permute-start(bf16[4,32,128]{2,1,0:T(8,128)(2,1)S(1)} %get-tuple-element.31), channel_id=1, source_target_pairs={{0,6},{1,7},{2,4},{3,5},{4,2},{5,3},{6,0},{7,1},{8,14},{9,15},{10,... | collective-permute-start | bytes 98312 | tf_op jit(solution)/shard_map/ppermute | solution.py:26
  14.5 4.2 %collective-permute-start.6 = (bf16[4,32,128]{2,1,0:T(8,128)(2,1)S(1)}, bf16[4,32,128]{2,1,0:T(8,128)(2,1)S(1)}, u32[]{:S(2)}, u32[]{:S(2)}) collective-permute-start(bf16[4,32,128]{2,1,0:T(8,128)(2,1)S(1)} %get-tuple-element.32), channel_id=1, source_target_pairs={{0,2},{1,3},{2,0},{3,1},{4,6},{5,7},{6,4},{7,5},{8,10},{9,11},{10,... | collective-permute-start | bytes 98312 | tf_op jit(solution)/shard_map/ppermute | solution.py:20
  14.6 4.2 %collective-permute-start.7 = (bf16[4,32,128]{2,1,0:T(8,128)(2,1)S(1)}, bf16[4,32,128]{2,1,0:T(8,128)(2,1)S(1)}, u32[]{:S(2)}, u32[]{:S(2)}) collective-permute-start(bf16[4,32,128]{2,1,0:T(8,128)(2,1)S(1)} %get-tuple-element.33), channel_id=1, source_target_pairs={{0,4},{4,0},{1,5},{5,1},{2,6},{6,2},{3,7},{7,3},{8,12},{12,8},{9,1... | collective-permute-start | bytes 98312 | tf_op jit(solution)/shard_map/ppermute | solution.py:30

commit v16 on v15

--- a/solution.py
+++ b/solution.py
@@ -48,32 +48,30 @@
 
 
 def mask_split_kernel(mask_hbm, pair_hbm, amp_hbm, *refs):
-    kept_refs, (cross_ref, gate_ref, mask_ref, pair_ref, sems) = refs[:CHIPS], refs[CHIPS:]
+    kept_refs, (cross_ref, gate_ref, mask_ref, pair_ref, amp_ref, sems) = refs[:CHIPS], refs[CHIPS:]
     copies = [
         pltpu.make_async_copy(mask_hbm, mask_ref, sems.at[0]),
         pltpu.make_async_copy(pair_hbm, pair_ref, sems.at[1]),
     ]
-    blocks = []
+    firsts, seconds = amp_ref.shape[:2]
+    for first in range(firsts):
+        for low in range(0, seconds, 2):
+            part = first, pl.ds(low, 2)
+            copies.append(pltpu.make_async_copy(amp_hbm.at[part], amp_ref.at[part], sems.at[len(copies)]))
+    for copy in copies:
+        copy.start()
+    for copy in copies:
+        copy.wait()
     for step in STEPS + (0,):
         for kind in range(2):
             first, second = slot(kind, step)
-            target = kept_refs[step].at[kind]
-            copies.append(pltpu.make_async_copy(amp_hbm.at[first, second], target, sems.at[len(copies)]))
-            blocks.append((first, second, target, kind, step, copies[-1]))
-    for copy in copies:
-        copy.start()
-    copies[0].wait()
-    copies[1].wait()
-    for first, second, target, kind, step, copy in blocks:
-        gate_ref[kind * CHIPS + step] = jnp.full(gate_ref.shape[1:], pair_ref[first, second].astype(F32))
-        keeps = [keep_rows(mask_ref, first, second, half) for half in range(SLAB_TILES)]
-        copy.wait()
-        for half, keep in enumerate(keeps):
-            part = slice(half * TILE, (half + 1) * TILE)
-            kept = target[part] * keep
-            target[part] = kept
-            if kind:
-                cross_ref[step, part] = kept
+            gate_ref[kind * CHIPS + step] = jnp.full(gate_ref.shape[1:], pair_ref[first, second].astype(F32))
+            for half in range(SLAB_TILES):
+                part = slice(half * TILE, (half + 1) * TILE)
+                kept = amp_ref[first, second, part] * keep_rows(mask_ref, first, second, half)
+                kept_refs[step][kind, part] = kept
+                if kind:
+                    cross_ref[step, part] = kept
 
 
 def mask_whole_kernel(mask_ref, pair_ref, amp_ref, kept_ref, gate_ref):
@@ -236,7 +234,8 @@
             scratch=[
                 pltpu.SMEM(turned_mask.shape, jnp.int32),
                 pltpu.SMEM(pair_mask.shape, jnp.int32),
-                pltpu.SemaphoreType.DMA((pairs + 2,)),
+                pltpu.VMEM(amplitudes.shape, BF16),
+                pltpu.SemaphoreType.DMA((pairs // 2 + 2,)),
             ],
         )
         got = {step: swap_chip(kept[step], step) for step in STEPS}

time: 19.6 us -> 19.6 us (level)
  transfers between devices with their start and end apart: 8 -> 8, of which waited for: 4 -> 5; matrix products, arithmetic and copies ran while one was open for 0% -> 0% of each run, Pallas kernels for 10% -> 11%
where the time goes in v16:
time: 19.6 us; the launch traced here: 19.5 us
  starting transfers between devices  10 us (51%)
  waiting for transfers between devices  5.83 us (30%)
  Pallas kernels  3.58 us (18%)
    ppermute x1, starting transfers between devices, swap_both(): return lax.ppermute(array, ('occj', 'virt'), moves)  3.74 us
    pallas_call x5, Pallas kernels, kernel(): pl.pallas_call(body, out_shape=outs, in_specs=[pl.BlockSpec(memory_space=...  3.58 us
    ppermute x2, waiting for transfers between devices, swap_virt(): lax.ppermute(array, 'virt', [(d, d ^ step) for d in range(lax.axis_size('...  3.3 us
    ppermute x3, starting transfers between devices, swap_chip(): lax.ppermute(array, 'occi', [(d, d ^ step) for d in range(lax.axis_size('...  2.66 us
    ppermute x2, starting transfers between devices, swap_virt(): lax.ppermute(array, 'virt', [(d, d ^ step) for d in range(lax.axis_size('...  2.19 us
    ppermute x1, waiting for transfers between devices, swap_both(): return lax.ppermute(array, ('occj', 'virt'), moves)  1.98 us
    ppermute x2, starting transfers between devices, swap_core(): return lax.ppermute(array, 'occj', [(0, 1), (1, 0)])  1.45 us
    ppermute x3, waiting for transfers between devices, swap_chip(): lax.ppermute(array, 'occi', [(d, d ^ step) for d in range(lax.axis_size('...  0.55 us
  transfers between devices with their start and end apart: 8, of which 5 were waited for; matrix products, arithmetic and copies ran while one was open for 0% of the time, Pallas kernels for 11%

profile of v16, /device:TPU:1, one launch (start us, length us, event | category | flops | bytes accessed | tf_op | source)
XLA Modules:
  0.0 19.5 jit_solution(7229562646531946719)
XLA Ops:
  0.0 0.0 copy-start
  0.0 2.1 %collective-permute-start = (bf16[8,128,128]{2,1,0:T(8,128)(2,1)}, bf16[8,128,128]{2,1,0:T(8,128)(2,1)S(1)}, u32[]{:S(2)}, u32[]{:S(2)}) collective-permute-start(bf16[8,128,128]{2,1,0:T(8,128)(2,1)} %refs_0_.1), channel_id=1, source_target_pairs={{0,1},{1,0},{2,3},{3,2},{4,5},{5,4},{6,7},{7,6},{8,9},{9,8},{10,11... | collective-permute-start | bytes 786440 | tf_op jit(solution)/shard_map/ppermute | solution.py:20
  2.1 1.1 %shard_map.47 = (bf16[2,128,128]{2,1,0:T(8,128)(2,1)S(1)}, bf16[2,128,128]{2,1,0:T(8,128)(2,1)S(1)}, bf16[2,128,128]{2,1,0:T(8,128)(2,1)S(1)}, bf16[2,128,128]{2...) custom-call(s32[2,2,2,4]{3,2,1,0:T(2,128)} %bitcast.1, s32[2,4]{1,0:T(2,128)} %pair_hbm.1, ...), custom_call_target="tpu_custom_call" | custom-call | bytes 1048576 | tf_op jit(solution)/shard_map/pallas_call | solution.py:189
  3.2 1.0 %collective-permute-start.2 = (bf16[4,128,128]{2,1,0:T(8,128)(2,1)S(1)}, bf16[4,128,128]{2,1,0:T(8,128)(2,1)S(1)}, u32[]{:S(2)}, u32[]{:S(2)}) collective-permute-start(bf16[4,128,128]{2,1,0:T(8,128)(2,1)S(1)} %get-tuple-element.24), channel_id=1, source_target_pairs={{0,4},{4,0},{1,5},{5,1},{2,6},{6,2},{3,7},{7,3},{8,12},{12,8},{9,1... | collective-permute-start | bytes 393224 | tf_op jit(solution)/shard_map/ppermute | solution.py:30
  4.2 2.2 %collective-permute-start.1 = (bf16[2,128,128]{2,1,0:T(8,128)(2,1)S(1)}, bf16[2,128,128]{2,1,0:T(8,128)(2,1)S(1)}, u32[]{:S(2)}, u32[]{:S(2)}) collective-permute-start(bf16[2,128,128]{2,1,0:T(8,128)(2,1)S(1)} %get-tuple-element.23.refs_3_), channel_id=1, source_target_pairs={{0,24},{8,16},{16,8},{24,0},{1,25},{9,17},{17,9},{25,1},{2,26},{10... | collective-permute-start | bytes 196616 | tf_op jit(solution)/shard_map/ppermute | solution.py:34
  6.4 0.2 %collective-permute-start.3 = (bf16[2,128,128]{2,1,0:T(8,128)(2,1)S(1)}, bf16[2,128,128]{2,1,0:T(8,128)(2,1)S(1)}, u32[]{:S(2)}, u32[]{:S(2)}) collective-permute-start(bf16[2,128,128]{2,1,0:T(8,128)(2,1)S(1)} %get-tuple-element.26.refs_2_), channel_id=1, source_target_pairs={{0,16},{8,24},{16,0},{24,8},{1,17},{9,25},{17,1},{25,9},{2,18},{10... | collective-permute-start | bytes 196616 | tf_op jit(solution)/shard_map/ppermute | solution.py:34
  6.6 0.3 %collective-permute-start.4 = (bf16[2,128,128]{2,1,0:T(8,128)(2,1)S(1)}, bf16[2,128,128]{2,1,0:T(8,128)(2,1)S(1)}, u32[]{:S(2)}, u32[]{:S(2)}) collective-permute-start(bf16[2,128,128]{2,1,0:T(8,128)(2,1)S(1)} %get-tuple-element.27.refs_3_), channel_id=1, source_target_pairs={{0,8},{8,0},{16,24},{24,16},{1,9},{9,1},{17,25},{25,17},{2,10},{10... | collective-permute-start | bytes 196616 | tf_op jit(solution)/shard_map/ppermute | solution.py:34
  6.9 1.6 %collective-permute-done.refs_1_ = bf16[8,128,128]{2,1,0:T(8,128)(2,1)S(1)} collective-permute-done((bf16[8,128,128]{2,1,0:T(8,128)(2,1)}, bf16[8,128,128]{2,1,0:T(8,128)(2,1)S(1)}, u32[]{:S(2)}, u32[]{:S(2)}) %collective-permute-start) | collective-permute-done | bytes 262176 | tf_op jit(solution)/shard_map/ppermute | solution.py:20
  8.4 0.0 copy-done
  8.4 0.2 %shard_map.46 = (bf16[2048,128]{1,0:T(8,128)(2,1)S(1)}, bf16[1024,128]{1,0:T(8,128)(2,1)S(1)}) custom-call(bf16[8,128,128]{2,1,0:T(8,128)(2,1)S(1)} %copy-done, bf16[8,128,128]{2,1,0:T(8,128)(2,1)S(1)} %collective-permute-done.refs_1_), custom_call_target="tpu_custom_call" | custom-call | bytes 1048576 | tf_op jit(solution)/shard_map/pallas_call | solution.py:189
  8.7 0.1 collective-permute-done.1.refs_4_
  8.8 0.0 collective-permute-done.2.refs_5_.refs_6_
  8.8 0.8 %shard_map.48 = (f32[2,32,128]{2,1,0:T(8,128)S(1)}, bf16[2,32,128]{2,1,0:T(8,128)(2,1)S(1)}, bf16[4,32,128]{2,1,0:T(8,128)(2,1)S(1)}) custom-call(bf16[2048,128]{1,0:T(8,128)(2,1)S(1)} %get-tuple-element.20.refs_0_, bf16[1024,128]{1,0:T(8,128)(2,1)S(1)} %get-tuple-element.21.refs_1_, bf16[2,128,128]{2,1,0:T(8,128)(2,1)S(1)} %get-tuple-element.22.refs_2_, ...), custom_call_target="tpu_custom_call" | custom-call | flops 268435456 | bytes 1048576 | tf_op jit(solution)/shard_map/pallas_call | solution.py:189
  9.6 0.4 %collective-permute-done.3.refs_4_ = bf16[2,128,128]{2,1,0:T(8,128)(2,1)S(1)} collective-permute-done((bf16[2,128,128]{2,1,0:T(8,128)(2,1)S(1)}, bf16[2,128,128]{2,1,0:T(8,128)(2,1)S(1)}, u32[]{:S(2)}, u32[]{:S(2)}) %collective-permute-start.3) | collective-permute-done | bytes 65568 | tf_op jit(solution)/shard_map/ppermute | solution.py:34
  10.0 0.0 collective-permute-done.4.refs_5_
  10.0 0.8 %shard_map.49 = (f32[2,32,128]{2,1,0:T(8,128)S(1)}, bf16[4,32,128]{2,1,0:T(8,128)(2,1)S(1)}, bf16[4,32,128]{2,1,0:T(8,128)(2,1)S(1)}, bf16[4,32,128]{2,1,0:T(8,128)(2,1)S(1)}) custom-call(bf16[2048,128]{1,0:T(8,128)(2,1)S(1)} %get-tuple-element.20.refs_0_, bf16[1024,128]{1,0:T(8,128)(2,1)S(1)} %get-tuple-element.21.refs_1_, ...), custom_call_target="tpu_custom_call" | custom-call | flops 268435456 | bytes 1048576 | tf_op jit(solution)/shard_map/pallas_call | solution.py:189
  10.9 3.7 %collective-permute-start.5 = (bf16[4,32,128]{2,1,0:T(8,128)(2,1)S(1)}, bf16[4,32,128]{2,1,0:T(8,128)(2,1)S(1)}, u32[]{:S(2)}, u32[]{:S(2)}) collective-permute-start(bf16[4,32,128]{2,1,0:T(8,128)(2,1)S(1)} %get-tuple-element.31), channel_id=1, source_target_pairs={{0,6},{1,7},{2,4},{3,5},{4,2},{5,3},{6,0},{7,1},{8,14},{9,15},{10,... | collective-permute-start | bytes 98312 | tf_op jit(solution)/shard_map/ppermute | solution.py:26
  14.6 0.1 collective-permute-start.6
  14.7 0.4 %collective-permute-start.7 = (bf16[4,32,128]{2,1,0:T(8,128)(2,1)S(1)}, bf16[4,32,128]{2,1,0:T(8,128)(2,1)S(1)}, u32[]{:S(2)}, u32[]{:S(2)}) collective-permute-start(bf16[4,32,128]{2,1,0:T(8,128)(2,1)S(1)} %get-tuple-element.33), channel_id=1, source_target_pairs={{0,4},{4,0},{1,5},{5,1},{2,6},{6,2},{3,7},{7,3},{8,12},{12,8},{9,1... | collective-permute-start | bytes 98312 | tf_op jit(solution)/shard_map/ppermute | solution.py:30
  15.1 2.0 %collective-permute-done.5.cross_ref = bf16[4,32,128]{2,1,0:T(8,128)(2,1)S(1)} collective-permute-done((bf16[4,32,128]{2,1,0:T(8,128)(2,1)S(1)}, bf16[4,32,128]{2,1,0:T(8,128)(2,1)S(1)}, u32[]{:S(2)}, u32[]{:S(2)}) %collective-permute-start.5) | collective-permute-done | bytes 32800 | tf_op jit(solution)/shard_map/ppermute | solution.py:26
  17.1 1.7 %collective-permute-done.6.same_ref = bf16[4,32,128]{2,1,0:T(8,128)(2,1)S(1)} collective-permute-done((bf16[4,32,128]{2,1,0:T(8,128)(2,1)S(1)}, bf16[4,32,128]{2,1,0:T(8,128)(2,1)S(1)}, u32[]{:S(2)}, u32[]{:S(2)}) %collective-permute-start.6) | collective-permute-done | bytes 32800 | tf_op jit(solution)/shard_map/ppermute | solution.py:20
  18.8 0.0 collective-permute-done.7.lent_ref
  18.8 0.7 %shard_map.50 = bf16[2,4,32,128]{3,2,1,0:T(8,128)(2,1)} custom-call(f32[2,32,128]{2,1,0:T(8,128)S(1)} %get-tuple-element.25.first_ref, f32[2,32,128]{2,1,0:T(8,128)S(1)} %get-tuple-element.30.second_ref, bf16[4,32,128]{2,1,0:T(8,128)(2,1)S(1)} %collective-permute-done.5.cross_ref, bf16[4,32,128]{2,1,0:T(8,128)(2,1)S(1)} %collective-permute-done.6.same_ref, ...), custom_call_target="tpu_custom_call" | custom-call | bytes 1048576 | tf_op jit(solution)/shard_map/pallas_call | solution.py:189
Async XLA Ops:
  0.0 8.4 %copy-start = (bf16[8,128,128]{2,1,0:T(8,128)(2,1)S(1)}, bf16[8,128,128]{2,1,0:T(8,128)(2,1)}, u32[]{:S(2)}) copy-start(bf16[8,128,128]{2,1,0:T(8,128)(2,1)} %refs_0_.1) | copy-start | bytes 786436
  0.0 8.4 %collective-permute-start = (bf16[8,128,128]{2,1,0:T(8,128)(2,1)}, bf16[8,128,128]{2,1,0:T(8,128)(2,1)S(1)}, u32[]{:S(2)}, u32[]{:S(2)}) collective-permute-start(bf16[8,128,128]{2,1,0:T(8,128)(2,1)} %refs_0_.1), channel_id=1, source_target_pairs={{0,1},{1,0},{2,3},{3,2},{4,5},{5,4},{6,7},{7,6},{8,9},{9,8},{10,11... | collective-permute-start | bytes 786440 | tf_op jit(solution)/shard_map/ppermute | solution.py:20
  3.2 5.6 %collective-permute-start.2 = (bf16[4,128,128]{2,1,0:T(8,128)(2,1)S(1)}, bf16[4,128,128]{2,1,0:T(8,128)(2,1)S(1)}, u32[]{:S(2)}, u32[]{:S(2)}) collective-permute-start(bf16[4,128,128]{2,1,0:T(8,128)(2,1)S(1)} %get-tuple-element.24), channel_id=1, source_target_pairs={{0,4},{4,0},{1,5},{5,1},{2,6},{6,2},{3,7},{7,3},{8,12},{12,8},{9,1... | collective-permute-start | bytes 393224 | tf_op jit(solution)/shard_map/ppermute | solution.py:30
  4.2 4.6 %collective-permute-start.1 = (bf16[2,128,128]{2,1,0:T(8,128)(2,1)S(1)}, bf16[2,128,128]{2,1,0:T(8,128)(2,1)S(1)}, u32[]{:S(2)}, u32[]{:S(2)}) collective-permute-start(bf16[2,128,128]{2,1,0:T(8,128)(2,1)S(1)} %get-tuple-element.23.refs_3_), channel_id=1, source_target_pairs={{0,24},{8,16},{16,8},{24,0},{1,25},{9,17},{17,9},{25,1},{2,26},{10... | collective-permute-start | bytes 196616 | tf_op jit(solution)/shard_map/ppermute | solution.py:34
  6.4 3.6 %collective-permute-start.3 = (bf16[2,128,128]{2,1,0:T(8,128)(2,1)S(1)}, bf16[2,128,128]{2,1,0:T(8,128)(2,1)S(1)}, u32[]{:S(2)}, u32[]{:S(2)}) collective-permute-start(bf16[2,128,128]{2,1,0:T(8,128)(2,1)S(1)} %get-tuple-element.26.refs_2_), channel_id=1, source_target_pairs={{0,16},{8,24},{16,0},{24,8},{1,17},{9,25},{17,1},{25,9},{2,18},{10... | collective-permute-start | bytes 196616 | tf_op jit(solution)/shard_map/ppermute | solution.py:34
  6.6 3.4 %collective-permute-start.4 = (bf16[2,128,128]{2,1,0:T(8,128)(2,1)S(1)}, bf16[2,128,128]{2,1,0:T(8,128)(2,1)S(1)}, u32[]{:S(2)}, u32[]{:S(2)}) collective-permute-start(bf16[2,128,128]{2,1,0:T(8,128)(2,1)S(1)} %get-tuple-element.27.refs_3_), channel_id=1, source_target_pairs={{0,8},{8,0},{16,24},{24,16},{1,9},{9,1},{17,25},{25,17},{2,10},{10... | collective-permute-start | bytes 196616 | tf_op jit(solution)/shard_map/ppermute | solution.py:34
  10.9 6.2 %collective-permute-start.5 = (bf16[4,32,128]{2,1,0:T(8,128)(2,1)S(1)}, bf16[4,32,128]{2,1,0:T(8,128)(2,1)S(1)}, u32[]{:S(2)}, u32[]{:S(2)}) collective-permute-start(bf16[4,32,128]{2,1,0:T(8,128)(2,1)S(1)} %get-tuple-element.31), channel_id=1, source_target_pairs={{0,6},{1,7},{2,4},{3,5},{4,2},{5,3},{6,0},{7,1},{8,14},{9,15},{10,... | collective-permute-start | bytes 98312 | tf_op jit(solution)/shard_map/ppermute | solution.py:26
  14.6 4.2 %collective-permute-start.6 = (bf16[4,32,128]{2,1,0:T(8,128)(2,1)S(1)}, bf16[4,32,128]{2,1,0:T(8,128)(2,1)S(1)}, u32[]{:S(2)}, u32[]{:S(2)}) collective-permute-start(bf16[4,32,128]{2,1,0:T(8,128)(2,1)S(1)} %get-tuple-element.32), channel_id=1, source_target_pairs={{0,2},{1,3},{2,0},{3,1},{4,6},{5,7},{6,4},{7,5},{8,10},{9,11},{10,... | collective-permute-start | bytes 98312 | tf_op jit(solution)/shard_map/ppermute | solution.py:20
  14.7 4.2 %collective-permute-start.7 = (bf16[4,32,128]{2,1,0:T(8,128)(2,1)S(1)}, bf16[4,32,128]{2,1,0:T(8,128)(2,1)S(1)}, u32[]{:S(2)}, u32[]{:S(2)}) collective-permute-start(bf16[4,32,128]{2,1,0:T(8,128)(2,1)S(1)} %get-tuple-element.33), channel_id=1, source_target_pairs={{0,4},{4,0},{1,5},{5,1},{2,6},{6,2},{3,7},{7,3},{8,12},{12,8},{9,1... | collective-permute-start | bytes 98312 | tf_op jit(solution)/shard_map/ppermute | solution.py:30

commit v17 on v15

--- a/solution.py
+++ b/solution.py
@@ -74,6 +74,8 @@
             target[part] = kept
             if kind:
                 cross_ref[step, part] = kept
+            elif step == 0:
+                cross_ref[CHIPS, part] = kept
 
 
 def mask_whole_kernel(mask_ref, pair_ref, amp_ref, kept_ref, gate_ref):
@@ -134,25 +136,25 @@
     ready, (kept_ref, far_ref, got_ref, beside_ref), outs = refs[:2], refs[2:6], refs[6:]
     own_ref, lent_ref, send_ref, inner_ref = outs
     sources = [
-        (kept_ref[0], kept_ref[0]),
         (far_ref[0], got_ref[0]),
+        (beside_ref[CHIPS], beside_ref[CHIPS]),
         (beside_ref[0], kept_ref[1]),
         (beside_ref[ORDER[1]], got_ref[1]),
     ]
-    targets = [[(ref, n), (send_ref, at + n)] for at, ref in ((0, own_ref), (2, lent_ref)) for n in range(2)]
+    targets = [[(own_ref, 0), (send_ref, 0)]] + [[(lent_ref, n), (send_ref, 1 + n)] for n in range(3)]
     products(ready, inner_ref, sources, targets)
 
 
 def second_kernel(*refs):
     ready, kept_refs, got_refs, (beside_ref, lent_in, send_in) = refs[:2], refs[2:4], refs[4:6], refs[6:9]
-    own_ref, lent_ref, same_ref, cross_ref, inner_ref = refs[9:]
+    own_ref, lent_ref, more_ref, same_ref, cross_ref, inner_ref = refs[9:]
     sources = [(kept[0], got[0]) for kept, got in zip(kept_refs, got_refs)]
     sources += [(beside_ref[step], got[1]) for step, got in zip(ORDER[2:], got_refs)]
-    targets = [[(own_ref, n), (same_ref, 2 + n)] for n in range(2)]
-    targets += [[(lent_ref, 2 + n), (cross_ref, 2 + n)] for n in range(2)]
-    lent_ref[:2] = lent_in[...]
-    same_ref[:2] = send_in[:2]
-    cross_ref[:2] = send_in[2:]
+    targets = [[(own_ref, n), (same_ref, 1 + n)] for n in range(2)]
+    targets += [[(more_ref, n), (cross_ref, 3 + n)] for n in range(2)]
+    lent_ref[...] = lent_in[...]
+    same_ref[:1] = send_in[:1]
+    cross_ref[:3] = send_in[1:]
     products(ready, inner_ref, sources, targets)
 
 
@@ -168,14 +170,17 @@
     lax.fori_loop(0, kept_ref.shape[0] // 2, two, 0)
 
 
-def finish_kernel(first_ref, second_ref, cross_ref, same_ref, lent_ref, gate_ref, out_ref):
-    for n, step in enumerate(ORDER):
-        own = first_ref[n] if n < 2 else second_ref[n - 2]
-        totals = own + same_ref[n].astype(F32), lent_ref[n].astype(F32) + cross_ref[n].astype(F32)
-        for kind, total in enumerate(totals):
-            first, second = slot(kind, step)
-            gate = gate_ref[kind * CHIPS + step, :1]
-            out_ref[first, second] = (total * gate).astype(BF16)
+def finish_kernel(first_ref, second_ref, cross_ref, same_ref, lent_ref, more_ref, gate_ref, out_ref):
+    def put(kind, step, total):
+        first, second = slot(kind, step)
+        out_ref[first, second] = (total * gate_ref[kind * CHIPS + step, :1]).astype(BF16)
+
+    for n, (kind, step) in enumerate([(0, 0)] + [(1, step) for step in ORDER]):
+        lent = lent_ref[n] if n < 3 else more_ref[n - 3]
+        put(kind, step, lent.astype(F32) + cross_ref[n].astype(F32))
+    for n, step in enumerate(ORDER[1:]):
+        own = first_ref[0] if n == 0 else second_ref[n - 1]
+        put(0, step, own + same_ref[n].astype(F32))
 
 
 def vmem_specs(count):
@@ -227,7 +232,7 @@
     if (firsts, seconds, chips, cores, virt) == (2, CHIPS, CHIPS, 2, 4):
         *kept, cross, gates = kernel(
             mask_split_kernel,
-            [shaped(BF16, 2, slab, slab)] * CHIPS + [shaped(BF16, CHIPS, slab, slab), gate],
+            [shaped(BF16, 2, slab, slab)] * CHIPS + [shaped(BF16, CHIPS + 1, slab, slab), gate],
             [
                 pltpu.with_memory_space_constraint(array, pltpu.HBM)
                 for array in (turned_mask, pair_mask, amplitudes)
@@ -245,19 +250,19 @@
         _, far, *rest = ORDER
         own_first, lent, sending = kernel(
             first_kernel,
-            [shaped(F32, 2, rows, slab), shaped(BF16, 2, rows, slab), shaped(BF16, 4, rows, slab)],
+            [shaped(F32, 1, rows, slab), shaped(BF16, 3, rows, slab), shaped(BF16, 4, rows, slab)],
             (*ready, kept[0], kept[far], got[far], beside),
             scratch=[inner(4)],
             flops=work(4),
         )
-        own_second, lent, same, crossing = kernel(
+        own_second, lent, more, same, crossing = kernel(
             second_kernel,
-            [shaped(F32, 2, rows, slab)] + [shaped(BF16, 4, rows, slab)] * 3,
+            [shaped(F32, 2, rows, slab)] + [shaped(BF16, count, rows, slab) for count in (3, 2, 3, 5)],
             (*ready, *[kept[step] for step in rest], *[got[step] for step in rest], beside, lent, sending),
             scratch=[inner(4)],
             flops=work(4),
         )
-        operands = (own_first, own_second, swap_both(crossing, 2), swap_virt(same, 2), swap_core(lent), gates)
+        operands = (own_first, own_second, swap_both(crossing, 2), swap_virt(same, 2), swap_core(lent), swap_core(more), gates)
         (out,) = kernel(finish_kernel, [shaped(BF16, firsts, seconds, rows, slab)], operands)
         return out
     kept, gates = kernel(

time: 19.6 us -> 19.1 us (0.974)
  the two profiles are of different devices: /device:TPU:1 before, /device:TPU:0 now
where the time goes in v17:
time: 19.1 us; the launch traced here: 18.9 us
  starting transfers between devices  9.91 us (52%)
  waiting for transfers between devices  5.42 us (28%)
  Pallas kernels  3.49 us (18%)
    ppermute x2, starting transfers between devices, swap_virt(): lax.ppermute(array, 'virt', [(d, d ^ step) for d in range(lax.axis_size('...  4.48 us
    ppermute x2, waiting for transfers between devices, swap_virt(): lax.ppermute(array, 'virt', [(d, d ^ step) for d in range(lax.axis_size('...  3.89 us
    ppermute x3, starting transfers between devices, swap_chip(): lax.ppermute(array, 'occi', [(d, d ^ step) for d in range(lax.axis_size('...  3.55 us
    pallas_call x5, Pallas kernels, kernel(): pl.pallas_call(body, out_shape=outs, in_specs=[pl.BlockSpec(memory_space=...  3.49 us
    ppermute x1, starting transfers between devices, swap_both(): return lax.ppermute(array, ('occj', 'virt'), moves)  1.29 us
    ppermute x3, waiting for transfers between devices, swap_core(): return lax.ppermute(array, 'occj', [(0, 1), (1, 0)])  0.84 us
    ppermute x3, waiting for transfers between devices, swap_chip(): lax.ppermute(array, 'occi', [(d, d ^ step) for d in range(lax.axis_size('...  0.68 us
    ppermute x3, starting transfers between devices, swap_core(): return lax.ppermute(array, 'occj', [(0, 1), (1, 0)])  0.58 us
  transfers between devices with their start and end apart: 9, of which 5 were waited for; matrix products, arithmetic and copies ran while one was open for 0% of the time, Pallas kernels for 11%

profile of v17, /device:TPU:0, one launch (start us, length us, event | category | flops | bytes accessed | tf_op | source)
XLA Modules:
  0.0 18.9 jit_solution(15433967836405102832)
XLA Ops:
  0.0 3.0 %collective-permute-start = (bf16[8,128,128]{2,1,0:T(8,128)(2,1)}, bf16[8,128,128]{2,1,0:T(8,128)(2,1)S(1)}, u32[]{:S(2)}, u32[]{:S(2)}) collective-permute-start(bf16[8,128,128]{2,1,0:T(8,128)(2,1)} %refs_0_.1), channel_id=1, source_target_pairs={{0,1},{1,0},{2,3},{3,2},{4,5},{5,4},{6,7},{7,6},{8,9},{9,8},{10,11... | collective-permute-start | bytes 786440 | tf_op jit(solution)/shard_map/ppermute | solution.py:20
  3.0 1.0 %shard_map.47 = (bf16[2,128,128]{2,1,0:T(8,128)(2,1)S(1)}, bf16[2,128,128]{2,1,0:T(8,128)(2,1)S(1)}, bf16[2,128,128]{2,1,0:T(8,128)(2,1)S(1)}, bf16[2,128,128]{2...) custom-call(s32[2,2,2,4]{3,2,1,0:T(2,128)} %bitcast.1, s32[2,4]{1,0:T(2,128)} %pair_hbm.1, ...), custom_call_target="tpu_custom_call" | custom-call | bytes 1048576 | tf_op jit(solution)/shard_map/pallas_call | solution.py:196
  4.0 0.1 collective-permute-start.2
  4.1 2.5 %collective-permute-start.1 = (bf16[2,128,128]{2,1,0:T(8,128)(2,1)S(1)}, bf16[2,128,128]{2,1,0:T(8,128)(2,1)S(1)}, u32[]{:S(2)}, u32[]{:S(2)}) collective-permute-start(bf16[2,128,128]{2,1,0:T(8,128)(2,1)S(1)} %get-tuple-element.24.refs_3_), channel_id=1, source_target_pairs={{0,24},{8,16},{16,8},{24,0},{1,25},{9,17},{17,9},{25,1},{2,26},{10... | collective-permute-start | bytes 196616 | tf_op jit(solution)/shard_map/ppermute | solution.py:34
  6.6 0.5 %collective-permute-start.3 = (bf16[2,128,128]{2,1,0:T(8,128)(2,1)S(1)}, bf16[2,128,128]{2,1,0:T(8,128)(2,1)S(1)}, u32[]{:S(2)}, u32[]{:S(2)}) collective-permute-start(bf16[2,128,128]{2,1,0:T(8,128)(2,1)S(1)} %get-tuple-element.27.refs_2_), channel_id=1, source_target_pairs={{0,16},{8,24},{16,0},{24,8},{1,17},{9,25},{17,1},{25,9},{2,18},{10... | collective-permute-start | bytes 196616 | tf_op jit(solution)/shard_map/ppermute | solution.py:34
  7.1 0.5 %collective-permute-start.4 = (bf16[2,128,128]{2,1,0:T(8,128)(2,1)S(1)}, bf16[2,128,128]{2,1,0:T(8,128)(2,1)S(1)}, u32[]{:S(2)}, u32[]{:S(2)}) collective-permute-start(bf16[2,128,128]{2,1,0:T(8,128)(2,1)S(1)} %get-tuple-element.28.refs_3_), channel_id=1, source_target_pairs={{0,8},{8,0},{16,24},{24,16},{1,9},{9,1},{17,25},{25,17},{2,10},{10... | collective-permute-start | bytes 196616 | tf_op jit(solution)/shard_map/ppermute | solution.py:34
  7.6 2.0 %collective-permute-done.refs_1_ = bf16[8,128,128]{2,1,0:T(8,128)(2,1)S(1)} collective-permute-done((bf16[8,128,128]{2,1,0:T(8,128)(2,1)}, bf16[8,128,128]{2,1,0:T(8,128)(2,1)S(1)}, u32[]{:S(2)}, u32[]{:S(2)}) %collective-permute-start) | collective-permute-done | bytes 262176 | tf_op jit(solution)/shard_map/ppermute | solution.py:20
  9.6 0.0 copy-done
  9.6 0.2 %shard_map.46 = (bf16[2048,128]{1,0:T(8,128)(2,1)S(1)}, bf16[1024,128]{1,0:T(8,128)(2,1)S(1)}) custom-call(bf16[8,128,128]{2,1,0:T(8,128)(2,1)S(1)} %copy-done, bf16[8,128,128]{2,1,0:T(8,128)(2,1)S(1)} %collective-permute-done.refs_1_), custom_call_target="tpu_custom_call" | custom-call | bytes 1048576 | tf_op jit(solution)/shard_map/pallas_call | solution.py:196
  9.8 0.0 collective-permute-done.1.refs_4_
  9.8 0.0 collective-permute-done.2.refs_5_.refs_6_
  9.8 0.8 %shard_map.48 = (f32[1,32,128]{2,1,0:T(8,128)S(1)}, bf16[3,32,128]{2,1,0:T(8,128)(2,1)S(1)}, bf16[4,32,128]{2,1,0:T(8,128)(2,1)S(1)}) custom-call(bf16[2048,128]{1,0:T(8,128)(2,1)S(1)} %get-tuple-element.21.refs_0_, bf16[1024,128]{1,0:T(8,128)(2,1)S(1)} %get-tuple-element.22.refs_1_, bf16[2,128,128]{2,1,0:T(8,128)(2,1)S(1)} %get-tuple-element.23.refs_2_, ...), custom_call_target="tpu_custom_call" | custom-call | flops 268435456 | bytes 1048576 | tf_op jit(solution)/shard_map/pallas_call | solution.py:196
  10.7 0.2 %collective-permute-done.3.refs_4_ = bf16[2,128,128]{2,1,0:T(8,128)(2,1)S(1)} collective-permute-done((bf16[2,128,128]{2,1,0:T(8,128)(2,1)S(1)}, bf16[2,128,128]{2,1,0:T(8,128)(2,1)S(1)}, u32[]{:S(2)}, u32[]{:S(2)}) %collective-permute-start.3) | collective-permute-done | bytes 65568 | tf_op jit(solution)/shard_map/ppermute | solution.py:34
  10.9 0.5 %collective-permute-done.4.refs_5_ = bf16[2,128,128]{2,1,0:T(8,128)(2,1)S(1)} collective-permute-done((bf16[2,128,128]{2,1,0:T(8,128)(2,1)S(1)}, bf16[2,128,128]{2,1,0:T(8,128)(2,1)S(1)}, u32[]{:S(2)}, u32[]{:S(2)}) %collective-permute-start.4) | collective-permute-done | bytes 65568 | tf_op jit(solution)/shard_map/ppermute | solution.py:34
  11.4 0.8 %shard_map.49 = (f32[2,32,128]{2,1,0:T(8,128)S(1)}, bf16[3,32,128]{2,1,0:T(8,128)(2,1)S(1)}, bf16[2,32,128]{2,1,0:T(8,128)(2,1)S(1)}, bf16[3,32,128]{2,1,0:T(8,128)(2,1)S(1)}, bf16[5,32,128]{2,1,0:T(8,128)(2,1)S(1)}) custom-call(bf16[2048,128]{1,0:T(8,128)(2,1)S(1)} %get-tuple-element.21.refs_0_, bf16[1024,128]{1,0:T(8,128)(2,1)S(1)} %get-tuple-element.22.refs_1_, ...), custom_call_target="tpu_custom_call" | custom-call | flops 268435456 | bytes 1048576 | tf_op jit(solution)/shard_map/pallas_call | solution.py:196
  12.2 1.3 %collective-permute-start.5 = (bf16[5,32,128]{2,1,0:T(8,128)(2,1)S(1)}, bf16[5,32,128]{2,1,0:T(8,128)(2,1)S(1)}, u32[]{:S(2)}, u32[]{:S(2)}) collective-permute-start(bf16[5,32,128]{2,1,0:T(8,128)(2,1)S(1)} %get-tuple-element.32), channel_id=1, source_target_pairs={{0,6},{1,7},{2,4},{3,5},{4,2},{5,3},{6,0},{7,1},{8,14},{9,15},{10,... | collective-permute-start | bytes 122888 | tf_op jit(solution)/shard_map/ppermute | solution.py:26
  13.5 1.5 %collective-permute-start.6 = (bf16[3,32,128]{2,1,0:T(8,128)(2,1)S(1)}, bf16[3,32,128]{2,1,0:T(8,128)(2,1)S(1)}, u32[]{:S(2)}, u32[]{:S(2)}) collective-permute-start(bf16[3,32,128]{2,1,0:T(8,128)(2,1)S(1)} %get-tuple-element.33), channel_id=1, source_target_pairs={{0,2},{1,3},{2,0},{3,1},{4,6},{5,7},{6,4},{7,5},{8,10},{9,11},{10,... | collective-permute-start | bytes 73736 | tf_op jit(solution)/shard_map/ppermute | solution.py:20
  15.0 0.1 collective-permute-start.7
  15.0 0.4 %collective-permute-start.8 = (bf16[2,32,128]{2,1,0:T(8,128)(2,1)S(1)}, bf16[2,32,128]{2,1,0:T(8,128)(2,1)S(1)}, u32[]{:S(2)}, u32[]{:S(2)}) collective-permute-start(bf16[2,32,128]{2,1,0:T(8,128)(2,1)S(1)} %get-tuple-element.35), channel_id=1, source_target_pairs={{0,4},{4,0},{1,5},{5,1},{2,6},{6,2},{3,7},{7,3},{8,12},{12,8},{9,1... | collective-permute-start | bytes 49160 | tf_op jit(solution)/shard_map/ppermute | solution.py:30
  15.5 0.8 %collective-permute-done.8.more_ref = bf16[2,32,128]{2,1,0:T(8,128)(2,1)S(1)} collective-permute-done((bf16[2,32,128]{2,1,0:T(8,128)(2,1)S(1)}, bf16[2,32,128]{2,1,0:T(8,128)(2,1)S(1)}, u32[]{:S(2)}, u32[]{:S(2)}) %collective-permute-start.8) | collective-permute-done | bytes 16416 | tf_op jit(solution)/shard_map/ppermute | solution.py:30
  16.3 1.9 %collective-permute-done.6.same_ref = bf16[3,32,128]{2,1,0:T(8,128)(2,1)S(1)} collective-permute-done((bf16[3,32,128]{2,1,0:T(8,128)(2,1)S(1)}, bf16[3,32,128]{2,1,0:T(8,128)(2,1)S(1)}, u32[]{:S(2)}, u32[]{:S(2)}) %collective-permute-start.6) | collective-permute-done | bytes 24608 | tf_op jit(solution)/shard_map/ppermute | solution.py:20
  18.2 0.0 collective-permute-done.7.lent_ref
  18.2 0.0 collective-permute-done.5.cross_ref
  18.2 0.7 %shard_map.50 = bf16[2,4,32,128]{3,2,1,0:T(8,128)(2,1)} custom-call(f32[1,32,128]{2,1,0:T(8,128)S(1)} %get-tuple-element.26.first_ref, f32[2,32,128]{2,1,0:T(8,128)S(1)} %get-tuple-element.31.second_ref, bf16[5,32,128]{2,1,0:T(8,128)(2,1)S(1)} %collective-permute-done.5.cross_ref, bf16[3,32,128]{2,1,0:T(8,128)(2,1)S(1)} %collective-permute-done.6.same_ref, ...), custom_call_target="tpu_custom_call" | custom-call | bytes 1048576 | tf_op jit(solution)/shard_map/pallas_call | solution.py:196
  (1 shorter events, 0.0 us)
Async XLA Ops:
  0.0 9.6 %copy-start = (bf16[8,128,128]{2,1,0:T(8,128)(2,1)S(1)}, bf16[8,128,128]{2,1,0:T(8,128)(2,1)}, u32[]{:S(2)}) copy-start(bf16[8,128,128]{2,1,0:T(8,128)(2,1)} %refs_0_.1) | copy-start | bytes 786436
  0.0 9.6 %collective-permute-start = (bf16[8,128,128]{2,1,0:T(8,128)(2,1)}, bf16[8,128,128]{2,1,0:T(8,128)(2,1)S(1)}, u32[]{:S(2)}, u32[]{:S(2)}) collective-permute-start(bf16[8,128,128]{2,1,0:T(8,128)(2,1)} %refs_0_.1), channel_id=1, source_target_pairs={{0,1},{1,0},{2,3},{3,2},{4,5},{5,4},{6,7},{7,6},{8,9},{9,8},{10,11... | collective-permute-start | bytes 786440 | tf_op jit(solution)/shard_map/ppermute | solution.py:20
  4.0 5.8 %collective-permute-start.2 = (bf16[5,128,128]{2,1,0:T(8,128)(2,1)S(1)}, bf16[5,128,128]{2,1,0:T(8,128)(2,1)S(1)}, u32[]{:S(2)}, u32[]{:S(2)}) collective-permute-start(bf16[5,128,128]{2,1,0:T(8,128)(2,1)S(1)} %get-tuple-element.25), channel_id=1, source_target_pairs={{0,4},{4,0},{1,5},{5,1},{2,6},{6,2},{3,7},{7,3},{8,12},{12,8},{9,1... | collective-permute-start | bytes 491528 | tf_op jit(solution)/shard_map/ppermute | solution.py:30
  4.1 5.7 %collective-permute-start.1 = (bf16[2,128,128]{2,1,0:T(8,128)(2,1)S(1)}, bf16[2,128,128]{2,1,0:T(8,128)(2,1)S(1)}, u32[]{:S(2)}, u32[]{:S(2)}) collective-permute-start(bf16[2,128,128]{2,1,0:T(8,128)(2,1)S(1)} %get-tuple-element.24.refs_3_), channel_id=1, source_target_pairs={{0,24},{8,16},{16,8},{24,0},{1,25},{9,17},{17,9},{25,1},{2,26},{10... | collective-permute-start | bytes 196616 | tf_op jit(solution)/shard_map/ppermute | solution.py:34
  6.6 4.3 %collective-permute-start.3 = (bf16[2,128,128]{2,1,0:T(8,128)(2,1)S(1)}, bf16[2,128,128]{2,1,0:T(8,128)(2,1)S(1)}, u32[]{:S(2)}, u32[]{:S(2)}) collective-permute-start(bf16[2,128,128]{2,1,0:T(8,128)(2,1)S(1)} %get-tuple-element.27.refs_2_), channel_id=1, source_target_pairs={{0,16},{8,24},{16,0},{24,8},{1,17},{9,25},{17,1},{25,9},{2,18},{10... | collective-permute-start | bytes 196616 | tf_op jit(solution)/shard_map/ppermute | solution.py:34
  7.1 4.3 %collective-permute-start.4 = (bf16[2,128,128]{2,1,0:T(8,128)(2,1)S(1)}, bf16[2,128,128]{2,1,0:T(8,128)(2,1)S(1)}, u32[]{:S(2)}, u32[]{:S(2)}) collective-permute-start(bf16[2,128,128]{2,1,0:T(8,128)(2,1)S(1)} %get-tuple-element.28.refs_3_), channel_id=1, source_target_pairs={{0,8},{8,0},{16,24},{24,16},{1,9},{9,1},{17,25},{25,17},{2,10},{10... | collective-permute-start | bytes 196616 | tf_op jit(solution)/shard_map/ppermute | solution.py:34
  12.2 6.0 %collective-permute-start.5 = (bf16[5,32,128]{2,1,0:T(8,128)(2,1)S(1)}, bf16[5,32,128]{2,1,0:T(8,128)(2,1)S(1)}, u32[]{:S(2)}, u32[]{:S(2)}) collective-permute-start(bf16[5,32,128]{2,1,0:T(8,128)(2,1)S(1)} %get-tuple-element.32), channel_id=1, source_target_pairs={{0,6},{1,7},{2,4},{3,5},{4,2},{5,3},{6,0},{7,1},{8,14},{9,15},{10,... | collective-permute-start | bytes 122888 | tf_op jit(solution)/shard_map/ppermute | solution.py:26
  13.5 4.7 %collective-permute-start.6 = (bf16[3,32,128]{2,1,0:T(8,128)(2,1)S(1)}, bf16[3,32,128]{2,1,0:T(8,128)(2,1)S(1)}, u32[]{:S(2)}, u32[]{:S(2)}) collective-permute-start(bf16[3,32,128]{2,1,0:T(8,128)(2,1)S(1)} %get-tuple-element.33), channel_id=1, source_target_pairs={{0,2},{1,3},{2,0},{3,1},{4,6},{5,7},{6,4},{7,5},{8,10},{9,11},{10,... | collective-permute-start | bytes 73736 | tf_op jit(solution)/shard_map/ppermute | solution.py:20
  15.0 3.3 %collective-permute-start.7 = (bf16[3,32,128]{2,1,0:T(8,128)(2,1)S(1)}, bf16[3,32,128]{2,1,0:T(8,128)(2,1)S(1)}, u32[]{:S(2)}, u32[]{:S(2)}) collective-permute-start(bf16[3,32,128]{2,1,0:T(8,128)(2,1)S(1)} %get-tuple-element.34), channel_id=1, source_target_pairs={{0,4},{4,0},{1,5},{5,1},{2,6},{6,2},{3,7},{7,3},{8,12},{12,8},{9,1... | collective-permute-start | bytes 73736 | tf_op jit(solution)/shard_map/ppermute | solution.py:30
  15.0 1.3 %collective-permute-start.8 = (bf16[2,32,128]{2,1,0:T(8,128)(2,1)S(1)}, bf16[2,32,128]{2,1,0:T(8,128)(2,1)S(1)}, u32[]{:S(2)}, u32[]{:S(2)}) collective-permute-start(bf16[2,32,128]{2,1,0:T(8,128)(2,1)S(1)} %get-tuple-element.35), channel_id=1, source_target_pairs={{0,4},{4,0},{1,5},{5,1},{2,6},{6,2},{3,7},{7,3},{8,12},{12,8},{9,1... | collective-permute-start | bytes 49160 | tf_op jit(solution)/shard_map/ppermute | solution.py:30

commit v18 on v17

--- a/solution.py
+++ b/solution.py
@@ -57,25 +57,27 @@
     for step in STEPS + (0,):
         for kind in range(2):
             first, second = slot(kind, step)
-            target = kept_refs[step].at[kind]
-            copies.append(pltpu.make_async_copy(amp_hbm.at[first, second], target, sems.at[len(copies)]))
-            blocks.append((first, second, target, kind, step, copies[-1]))
+            for half in range(SLAB_TILES):
+                part = pl.ds(half * TILE, TILE)
+                source, target = amp_hbm.at[first, second, part], kept_refs[step].at[kind, part]
+                copies.append(pltpu.make_async_copy(source, target, sems.at[len(copies)]))
+                blocks.append((first, second, target, kind, step, half, copies[-1]))
     for copy in copies:
         copy.start()
     copies[0].wait()
     copies[1].wait()
-    for first, second, target, kind, step, copy in blocks:
-        gate_ref[kind * CHIPS + step] = jnp.full(gate_ref.shape[1:], pair_ref[first, second].astype(F32))
-        keeps = [keep_rows(mask_ref, first, second, half) for half in range(SLAB_TILES)]
+    for first, second, target, kind, step, half, copy in blocks:
+        if half == 0:
+            gate_ref[kind * CHIPS + step] = jnp.full(gate_ref.shape[1:], pair_ref[first, second].astype(F32))
+        keep = keep_rows(mask_ref, first, second, half)
         copy.wait()
-        for half, keep in enumerate(keeps):
-            part = slice(half * TILE, (half + 1) * TILE)
-            kept = target[part] * keep
-            target[part] = kept
-            if kind:
-                cross_ref[step, part] = kept
-            elif step == 0:
-                cross_ref[CHIPS, part] = kept
+        kept = target[...] * keep
+        target[...] = kept
+        part = slice(half * TILE, (half + 1) * TILE)
+        if kind:
+            cross_ref[step, part] = kept
+        elif step == 0:
+            cross_ref[CHIPS, part] = kept
 
 
 def mask_whole_kernel(mask_ref, pair_ref, amp_ref, kept_ref, gate_ref):
@@ -241,7 +243,7 @@
             scratch=[
                 pltpu.SMEM(turned_mask.shape, jnp.int32),
                 pltpu.SMEM(pair_mask.shape, jnp.int32),
-                pltpu.SemaphoreType.DMA((pairs + 2,)),
+                pltpu.SemaphoreType.DMA((SLAB_TILES * pairs + 2,)),
             ],
         )
         got = {step: swap_chip(kept[step], step) for step in STEPS}

time: 19.1 us -> 19.2 us (level)
  no operation moved by 1% of the time
where the time goes in v18:
time: 19.2 us; the launch traced here: 19 us
  starting transfers between devices  9.91 us (52%)
  waiting for transfers between devices  5.42 us (28%)
  Pallas kernels  3.6 us (19%)
    ppermute x2, starting transfers between devices, swap_virt(): lax.ppermute(array, 'virt', [(d, d ^ step) for d in range(lax.axis_size('...  4.48 us
    ppermute x2, waiting for transfers between devices, swap_virt(): lax.ppermute(array, 'virt', [(d, d ^ step) for d in range(lax.axis_size('...  3.78 us
    pallas_call x5, Pallas kernels, kernel(): pl.pallas_call(body, out_shape=outs, in_specs=[pl.BlockSpec(memory_space=...  3.6 us
    ppermute x3, starting transfers between devices, swap_chip(): lax.ppermute(array, 'occi', [(d, d ^ step) for d in range(lax.axis_size('...  3.55 us
    ppermute x1, starting transfers between devices, swap_both(): return lax.ppermute(array, ('occj', 'virt'), moves)  1.29 us
    ppermute x3, waiting for transfers between devices, swap_core(): return lax.ppermute(array, 'occj', [(0, 1), (1, 0)])  0.84 us
    ppermute x3, waiting for transfers between devices, swap_chip(): lax.ppermute(array, 'occi', [(d, d ^ step) for d in range(lax.axis_size('...  0.79 us
    ppermute x3, starting transfers between devices, swap_core(): return lax.ppermute(array, 'occj', [(0, 1), (1, 0)])  0.58 us
  transfers between devices with their start and end apart: 9, of which 5 were waited for; matrix products, arithmetic and copies ran while one was open for 0% of the time, Pallas kernels for 11%

profile of v18, /device:TPU:0, one launch (start us, length us, event | category | flops | bytes accessed | tf_op | source)
XLA Modules:
  0.0 19.0 jit_solution(8403002377337213304)
XLA Ops:
  0.0 3.0 %collective-permute-start = (bf16[8,128,128]{2,1,0:T(8,128)(2,1)}, bf16[8,128,128]{2,1,0:T(8,128)(2,1)S(1)}, u32[]{:S(2)}, u32[]{:S(2)}) collective-permute-start(bf16[8,128,128]{2,1,0:T(8,128)(2,1)} %refs_0_.1), channel_id=1, source_target_pairs={{0,1},{1,0},{2,3},{3,2},{4,5},{5,4},{6,7},{7,6},{8,9},{9,8},{10,11... | collective-permute-start | bytes 786440 | tf_op jit(solution)/shard_map/ppermute | solution.py:20
  3.0 1.1 %shard_map.47 = (bf16[2,128,128]{2,1,0:T(8,128)(2,1)S(1)}, bf16[2,128,128]{2,1,0:T(8,128)(2,1)S(1)}, bf16[2,128,128]{2,1,0:T(8,128)(2,1)S(1)}, bf16[2,128,128]{2...) custom-call(s32[2,2,2,4]{3,2,1,0:T(2,128)} %bitcast.1, s32[2,4]{1,0:T(2,128)} %pair_hbm.1, ...), custom_call_target="tpu_custom_call" | custom-call | bytes 1048576 | tf_op jit(solution)/shard_map/pallas_call | solution.py:198
  4.1 0.1 collective-permute-start.2
  4.2 2.5 %collective-permute-start.1 = (bf16[2,128,128]{2,1,0:T(8,128)(2,1)S(1)}, bf16[2,128,128]{2,1,0:T(8,128)(2,1)S(1)}, u32[]{:S(2)}, u32[]{:S(2)}) collective-permute-start(bf16[2,128,128]{2,1,0:T(8,128)(2,1)S(1)} %get-tuple-element.24.refs_3_), channel_id=1, source_target_pairs={{0,24},{8,16},{16,8},{24,0},{1,25},{9,17},{17,9},{25,1},{2,26},{10... | collective-permute-start | bytes 196616 | tf_op jit(solution)/shard_map/ppermute | solution.py:34
  6.7 0.5 %collective-permute-start.3 = (bf16[2,128,128]{2,1,0:T(8,128)(2,1)S(1)}, bf16[2,128,128]{2,1,0:T(8,128)(2,1)S(1)}, u32[]{:S(2)}, u32[]{:S(2)}) collective-permute-start(bf16[2,128,128]{2,1,0:T(8,128)(2,1)S(1)} %get-tuple-element.27.refs_2_), channel_id=1, source_target_pairs={{0,16},{8,24},{16,0},{24,8},{1,17},{9,25},{17,1},{25,9},{2,18},{10... | collective-permute-start | bytes 196616 | tf_op jit(solution)/shard_map/ppermute | solution.py:34
  7.2 0.5 %collective-permute-start.4 = (bf16[2,128,128]{2,1,0:T(8,128)(2,1)S(1)}, bf16[2,128,128]{2,1,0:T(8,128)(2,1)S(1)}, u32[]{:S(2)}, u32[]{:S(2)}) collective-permute-start(bf16[2,128,128]{2,1,0:T(8,128)(2,1)S(1)} %get-tuple-element.28.refs_3_), channel_id=1, source_target_pairs={{0,8},{8,0},{16,24},{24,16},{1,9},{9,1},{17,25},{25,17},{2,10},{10... | collective-permute-start | bytes 196616 | tf_op jit(solution)/shard_map/ppermute | solution.py:34
  7.7 1.9 %collective-permute-done.refs_1_ = bf16[8,128,128]{2,1,0:T(8,128)(2,1)S(1)} collective-permute-done((bf16[8,128,128]{2,1,0:T(8,128)(2,1)}, bf16[8,128,128]{2,1,0:T(8,128)(2,1)S(1)}, u32[]{:S(2)}, u32[]{:S(2)}) %collective-permute-start) | collective-permute-done | bytes 262176 | tf_op jit(solution)/shard_map/ppermute | solution.py:20
  9.6 0.0 copy-done
  9.6 0.2 %shard_map.46 = (bf16[2048,128]{1,0:T(8,128)(2,1)S(1)}, bf16[1024,128]{1,0:T(8,128)(2,1)S(1)}) custom-call(bf16[8,128,128]{2,1,0:T(8,128)(2,1)S(1)} %copy-done, bf16[8,128,128]{2,1,0:T(8,128)(2,1)S(1)} %collective-permute-done.refs_1_), custom_call_target="tpu_custom_call" | custom-call | bytes 1048576 | tf_op jit(solution)/shard_map/pallas_call | solution.py:198
  9.8 0.0 collective-permute-done.1.refs_4_
  9.8 0.0 collective-permute-done.2.refs_5_.refs_6_
  9.8 0.8 %shard_map.48 = (f32[1,32,128]{2,1,0:T(8,128)S(1)}, bf16[3,32,128]{2,1,0:T(8,128)(2,1)S(1)}, bf16[4,32,128]{2,1,0:T(8,128)(2,1)S(1)}) custom-call(bf16[2048,128]{1,0:T(8,128)(2,1)S(1)} %get-tuple-element.21.refs_0_, bf16[1024,128]{1,0:T(8,128)(2,1)S(1)} %get-tuple-element.22.refs_1_, bf16[2,128,128]{2,1,0:T(8,128)(2,1)S(1)} %get-tuple-element.23.refs_2_, ...), custom_call_target="tpu_custom_call" | custom-call | flops 268435456 | bytes 1048576 | tf_op jit(solution)/shard_map/pallas_call | solution.py:198
  10.7 0.3 %collective-permute-done.3.refs_4_ = bf16[2,128,128]{2,1,0:T(8,128)(2,1)S(1)} collective-permute-done((bf16[2,128,128]{2,1,0:T(8,128)(2,1)S(1)}, bf16[2,128,128]{2,1,0:T(8,128)(2,1)S(1)}, u32[]{:S(2)}, u32[]{:S(2)}) %collective-permute-start.3) | collective-permute-done | bytes 65568 | tf_op jit(solution)/shard_map/ppermute | solution.py:34
  11.0 0.5 %collective-permute-done.4.refs_5_ = bf16[2,128,128]{2,1,0:T(8,128)(2,1)S(1)} collective-permute-done((bf16[2,128,128]{2,1,0:T(8,128)(2,1)S(1)}, bf16[2,128,128]{2,1,0:T(8,128)(2,1)S(1)}, u32[]{:S(2)}, u32[]{:S(2)}) %collective-permute-start.4) | collective-permute-done | bytes 65568 | tf_op jit(solution)/shard_map/ppermute | solution.py:34
  11.5 0.8 %shard_map.49 = (f32[2,32,128]{2,1,0:T(8,128)S(1)}, bf16[3,32,128]{2,1,0:T(8,128)(2,1)S(1)}, bf16[2,32,128]{2,1,0:T(8,128)(2,1)S(1)}, bf16[3,32,128]{2,1,0:T(8,128)(2,1)S(1)}, bf16[5,32,128]{2,1,0:T(8,128)(2,1)S(1)}) custom-call(bf16[2048,128]{1,0:T(8,128)(2,1)S(1)} %get-tuple-element.21.refs_0_, bf16[1024,128]{1,0:T(8,128)(2,1)S(1)} %get-tuple-element.22.refs_1_, ...), custom_call_target="tpu_custom_call" | custom-call | flops 268435456 | bytes 1048576 | tf_op jit(solution)/shard_map/pallas_call | solution.py:198
  12.3 1.3 %collective-permute-start.5 = (bf16[5,32,128]{2,1,0:T(8,128)(2,1)S(1)}, bf16[5,32,128]{2,1,0:T(8,128)(2,1)S(1)}, u32[]{:S(2)}, u32[]{:S(2)}) collective-permute-start(bf16[5,32,128]{2,1,0:T(8,128)(2,1)S(1)} %get-tuple-element.32), channel_id=1, source_target_pairs={{0,6},{1,7},{2,4},{3,5},{4,2},{5,3},{6,0},{7,1},{8,14},{9,15},{10,... | collective-permute-start | bytes 122888 | tf_op jit(solution)/shard_map/ppermute | solution.py:26
  13.6 1.5 %collective-permute-start.6 = (bf16[3,32,128]{2,1,0:T(8,128)(2,1)S(1)}, bf16[3,32,128]{2,1,0:T(8,128)(2,1)S(1)}, u32[]{:S(2)}, u32[]{:S(2)}) collective-permute-start(bf16[3,32,128]{2,1,0:T(8,128)(2,1)S(1)} %get-tuple-element.33), channel_id=1, source_target_pairs={{0,2},{1,3},{2,0},{3,1},{4,6},{5,7},{6,4},{7,5},{8,10},{9,11},{10,... | collective-permute-start | bytes 73736 | tf_op jit(solution)/shard_map/ppermute | solution.py:20
  15.1 0.1 collective-permute-start.7
  15.1 0.4 %collective-permute-start.8 = (bf16[2,32,128]{2,1,0:T(8,128)(2,1)S(1)}, bf16[2,32,128]{2,1,0:T(8,128)(2,1)S(1)}, u32[]{:S(2)}, u32[]{:S(2)}) collective-permute-start(bf16[2,32,128]{2,1,0:T(8,128)(2,1)S(1)} %get-tuple-element.35), channel_id=1, source_target_pairs={{0,4},{4,0},{1,5},{5,1},{2,6},{6,2},{3,7},{7,3},{8,12},{12,8},{9,1... | collective-permute-start | bytes 49160 | tf_op jit(solution)/shard_map/ppermute | solution.py:30
  15.6 0.8 %collective-permute-done.8.more_ref = bf16[2,32,128]{2,1,0:T(8,128)(2,1)S(1)} collective-permute-done((bf16[2,32,128]{2,1,0:T(8,128)(2,1)S(1)}, bf16[2,32,128]{2,1,0:T(8,128)(2,1)S(1)}, u32[]{:S(2)}, u32[]{:S(2)}) %collective-permute-start.8) | collective-permute-done | bytes 16416 | tf_op jit(solution)/shard_map/ppermute | solution.py:30
  16.4 1.9 %collective-permute-done.6.same_ref = bf16[3,32,128]{2,1,0:T(8,128)(2,1)S(1)} collective-permute-done((bf16[3,32,128]{2,1,0:T(8,128)(2,1)S(1)}, bf16[3,32,128]{2,1,0:T(8,128)(2,1)S(1)}, u32[]{:S(2)}, u32[]{:S(2)}) %collective-permute-start.6) | collective-permute-done | bytes 24608 | tf_op jit(solution)/shard_map/ppermute | solution.py:20
  18.3 0.0 collective-permute-done.7.lent_ref
  18.3 0.0 collective-permute-done.5.cross_ref
  18.3 0.7 %shard_map.50 = bf16[2,4,32,128]{3,2,1,0:T(8,128)(2,1)} custom-call(f32[1,32,128]{2,1,0:T(8,128)S(1)} %get-tuple-element.26.first_ref, f32[2,32,128]{2,1,0:T(8,128)S(1)} %get-tuple-element.31.second_ref, bf16[5,32,128]{2,1,0:T(8,128)(2,1)S(1)} %collective-permute-done.5.cross_ref, bf16[3,32,128]{2,1,0:T(8,128)(2,1)S(1)} %collective-permute-done.6.same_ref, ...), custom_call_target="tpu_custom_call" | custom-call | bytes 1048576 | tf_op jit(solution)/shard_map/pallas_call | solution.py:198
  (1 shorter events, 0.0 us)
Async XLA Ops:
  0.0 9.6 %copy-start = (bf16[8,128,128]{2,1,0:T(8,128)(2,1)S(1)}, bf16[8,128,128]{2,1,0:T(8,128)(2,1)}, u32[]{:S(2)}) copy-start(bf16[8,128,128]{2,1,0:T(8,128)(2,1)} %refs_0_.1) | copy-start | bytes 786436
  0.0 9.6 %collective-permute-start = (bf16[8,128,128]{2,1,0:T(8,128)(2,1)}, bf16[8,128,128]{2,1,0:T(8,128)(2,1)S(1)}, u32[]{:S(2)}, u32[]{:S(2)}) collective-permute-start(bf16[8,128,128]{2,1,0:T(8,128)(2,1)} %refs_0_.1), channel_id=1, source_target_pairs={{0,1},{1,0},{2,3},{3,2},{4,5},{5,4},{6,7},{7,6},{8,9},{9,8},{10,11... | collective-permute-start | bytes 786440 | tf_op jit(solution)/shard_map/ppermute | solution.py:20
  4.1 5.7 %collective-permute-start.2 = (bf16[5,128,128]{2,1,0:T(8,128)(2,1)S(1)}, bf16[5,128,128]{2,1,0:T(8,128)(2,1)S(1)}, u32[]{:S(2)}, u32[]{:S(2)}) collective-permute-start(bf16[5,128,128]{2,1,0:T(8,128)(2,1)S(1)} %get-tuple-element.25), channel_id=1, source_target_pairs={{0,4},{4,0},{1,5},{5,1},{2,6},{6,2},{3,7},{7,3},{8,12},{12,8},{9,1... | collective-permute-start | bytes 491528 | tf_op jit(solution)/shard_map/ppermute | solution.py:30
  4.2 5.6 %collective-permute-start.1 = (bf16[2,128,128]{2,1,0:T(8,128)(2,1)S(1)}, bf16[2,128,128]{2,1,0:T(8,128)(2,1)S(1)}, u32[]{:S(2)}, u32[]{:S(2)}) collective-permute-start(bf16[2,128,128]{2,1,0:T(8,128)(2,1)S(1)} %get-tuple-element.24.refs_3_), channel_id=1, source_target_pairs={{0,24},{8,16},{16,8},{24,0},{1,25},{9,17},{17,9},{25,1},{2,26},{10... | collective-permute-start | bytes 196616 | tf_op jit(solution)/shard_map/ppermute | solution.py:34
  6.7 4.3 %collective-permute-start.3 = (bf16[2,128,128]{2,1,0:T(8,128)(2,1)S(1)}, bf16[2,128,128]{2,1,0:T(8,128)(2,1)S(1)}, u32[]{:S(2)}, u32[]{:S(2)}) collective-permute-start(bf16[2,128,128]{2,1,0:T(8,128)(2,1)S(1)} %get-tuple-element.27.refs_2_), channel_id=1, source_target_pairs={{0,16},{8,24},{16,0},{24,8},{1,17},{9,25},{17,1},{25,9},{2,18},{10... | collective-permute-start | bytes 196616 | tf_op jit(solution)/shard_map/ppermute | solution.py:34
  7.2 4.3 %collective-permute-start.4 = (bf16[2,128,128]{2,1,0:T(8,128)(2,1)S(1)}, bf16[2,128,128]{2,1,0:T(8,128)(2,1)S(1)}, u32[]{:S(2)}, u32[]{:S(2)}) collective-permute-start(bf16[2,128,128]{2,1,0:T(8,128)(2,1)S(1)} %get-tuple-element.28.refs_3_), channel_id=1, source_target_pairs={{0,8},{8,0},{16,24},{24,16},{1,9},{9,1},{17,25},{25,17},{2,10},{10... | collective-permute-start | bytes 196616 | tf_op jit(solution)/shard_map/ppermute | solution.py:34
  12.3 6.0 %collective-permute-start.5 = (bf16[5,32,128]{2,1,0:T(8,128)(2,1)S(1)}, bf16[5,32,128]{2,1,0:T(8,128)(2,1)S(1)}, u32[]{:S(2)}, u32[]{:S(2)}) collective-permute-start(bf16[5,32,128]{2,1,0:T(8,128)(2,1)S(1)} %get-tuple-element.32), channel_id=1, source_target_pairs={{0,6},{1,7},{2,4},{3,5},{4,2},{5,3},{6,0},{7,1},{8,14},{9,15},{10,... | collective-permute-start | bytes 122888 | tf_op jit(solution)/shard_map/ppermute | solution.py:26
  13.6 4.7 %collective-permute-start.6 = (bf16[3,32,128]{2,1,0:T(8,128)(2,1)S(1)}, bf16[3,32,128]{2,1,0:T(8,128)(2,1)S(1)}, u32[]{:S(2)}, u32[]{:S(2)}) collective-permute-start(bf16[3,32,128]{2,1,0:T(8,128)(2,1)S(1)} %get-tuple-element.33), channel_id=1, source_target_pairs={{0,2},{1,3},{2,0},{3,1},{4,6},{5,7},{6,4},{7,5},{8,10},{9,11},{10,... | collective-permute-start | bytes 73736 | tf_op jit(solution)/shard_map/ppermute | solution.py:20
  15.1 3.3 %collective-permute-start.7 = (bf16[3,32,128]{2,1,0:T(8,128)(2,1)S(1)}, bf16[3,32,128]{2,1,0:T(8,128)(2,1)S(1)}, u32[]{:S(2)}, u32[]{:S(2)}) collective-permute-start(bf16[3,32,128]{2,1,0:T(8,128)(2,1)S(1)} %get-tuple-element.34), channel_id=1, source_target_pairs={{0,4},{4,0},{1,5},{5,1},{2,6},{6,2},{3,7},{7,3},{8,12},{12,8},{9,1... | collective-permute-start | bytes 73736 | tf_op jit(solution)/shard_map/ppermute | solution.py:30
  15.1 1.3 %collective-permute-start.8 = (bf16[2,32,128]{2,1,0:T(8,128)(2,1)S(1)}, bf16[2,32,128]{2,1,0:T(8,128)(2,1)S(1)}, u32[]{:S(2)}, u32[]{:S(2)}) collective-permute-start(bf16[2,32,128]{2,1,0:T(8,128)(2,1)S(1)} %get-tuple-element.35), channel_id=1, source_target_pairs={{0,4},{4,0},{1,5},{5,1},{2,6},{6,2},{3,7},{7,3},{8,12},{12,8},{9,1... | collective-permute-start | bytes 49160 | tf_op jit(solution)/shard_map/ppermute | solution.py:30

commit v19 on v17

--- a/solution.py
+++ b/solution.py
@@ -44,7 +44,11 @@
     keep = jnp.zeros(lane.shape, F32)
     for tile in range(SLAB_TILES):
         keep = jnp.where(lane == tile, mask_ref[first, half, tile, second].astype(F32), keep)
-    return jnp.broadcast_to(keep, (TILE, SLAB_TILES * TILE)).astype(BF16)
+    return jnp.broadcast_to(keep, (16, SLAB_TILES * TILE)).astype(BF16)
+
+
+def masked_rows(block, keep):
+    return (block.reshape(TILE // 16, 16, block.shape[1]) * keep[None]).reshape(block.shape)
 
 
 def mask_split_kernel(mask_hbm, pair_hbm, amp_hbm, *refs):
@@ -70,7 +74,7 @@
         copy.wait()
         for half, keep in enumerate(keeps):
             part = slice(half * TILE, (half + 1) * TILE)
-            kept = target[part] * keep
+            kept = masked_rows(target[part], keep)
             target[part] = kept
             if kind:
                 cross_ref[step, part] = kept
@@ -85,7 +89,7 @@
         first, second = block // seconds, block % seconds
         for half in range(SLAB_TILES):
             part = slice(half * TILE, (half + 1) * TILE)
-            kept_ref[block, part] = amp_ref[first, second, part] * keep_rows(mask_ref, first, second, half)
+            kept_ref[block, part] = masked_rows(amp_ref[first, second, part], keep_rows(mask_ref, first, second, half))
         gate_ref[block] = jnp.full(gate_ref.shape[1:], pair_ref[first, second].astype(F32))
         return carry
 

time: 19.1 us -> 19.1 us (level)
  no operation moved by 1% of the time
where the time goes in v19:
time: 19.1 us; the launch traced here: 18.9 us
  starting transfers between devices  9.91 us (52%)
  waiting for transfers between devices  5.42 us (28%)
  Pallas kernels  3.49 us (18%)
    ppermute x2, starting transfers between devices, swap_virt(): lax.ppermute(array, 'virt', [(d, d ^ step) for d in range(lax.axis_size('...  4.48 us
    ppermute x2, waiting for transfers between devices, swap_virt(): lax.ppermute(array, 'virt', [(d, d ^ step) for d in range(lax.axis_size('...  3.89 us
    ppermute x3, starting transfers between devices, swap_chip(): lax.ppermute(array, 'occi', [(d, d ^ step) for d in range(lax.axis_size('...  3.55 us
    pallas_call x5, Pallas kernels, kernel(): pl.pallas_call(body, out_shape=outs, in_specs=[pl.BlockSpec(memory_space=...  3.49 us
    ppermute x1, starting transfers between devices, swap_both(): return lax.ppermute(array, ('occj', 'virt'), moves)  1.29 us
    ppermute x3, waiting for transfers between devices, swap_core(): return lax.ppermute(array, 'occj', [(0, 1), (1, 0)])  0.84 us
    ppermute x3, waiting for transfers between devices, swap_chip(): lax.ppermute(array, 'occi', [(d, d ^ step) for d in range(lax.axis_size('...  0.68 us
    ppermute x3, starting transfers between devices, swap_core(): return lax.ppermute(array, 'occj', [(0, 1), (1, 0)])  0.58 us
  transfers between devices with their start and end apart: 9, of which 5 were waited for; matrix products, arithmetic and copies ran while one was open for 0% of the time, Pallas kernels for 11%

profile of v19, /device:TPU:0, one launch (start us, length us, event | category | flops | bytes accessed | tf_op | source)
XLA Modules:
  0.0 18.9 jit_solution(15433967836405102832)
XLA Ops:
  0.0 3.0 %collective-permute-start = (bf16[8,128,128]{2,1,0:T(8,128)(2,1)}, bf16[8,128,128]{2,1,0:T(8,128)(2,1)S(1)}, u32[]{:S(2)}, u32[]{:S(2)}) collective-permute-start(bf16[8,128,128]{2,1,0:T(8,128)(2,1)} %refs_0_.1), channel_id=1, source_target_pairs={{0,1},{1,0},{2,3},{3,2},{4,5},{5,4},{6,7},{7,6},{8,9},{9,8},{10,11... | collective-permute-start | bytes 786440 | tf_op jit(solution)/shard_map/ppermute | solution.py:20
  3.0 1.0 %shard_map.47 = (bf16[2,128,128]{2,1,0:T(8,128)(2,1)S(1)}, bf16[2,128,128]{2,1,0:T(8,128)(2,1)S(1)}, bf16[2,128,128]{2,1,0:T(8,128)(2,1)S(1)}, bf16[2,128,128]{2...) custom-call(s32[2,2,2,4]{3,2,1,0:T(2,128)} %bitcast.1, s32[2,4]{1,0:T(2,128)} %pair_hbm.1, ...), custom_call_target="tpu_custom_call" | custom-call | bytes 1048576 | tf_op jit(solution)/shard_map/pallas_call | solution.py:200
  4.0 0.1 collective-permute-start.2
  4.1 2.5 %collective-permute-start.1 = (bf16[2,128,128]{2,1,0:T(8,128)(2,1)S(1)}, bf16[2,128,128]{2,1,0:T(8,128)(2,1)S(1)}, u32[]{:S(2)}, u32[]{:S(2)}) collective-permute-start(bf16[2,128,128]{2,1,0:T(8,128)(2,1)S(1)} %get-tuple-element.24.refs_3_), channel_id=1, source_target_pairs={{0,24},{8,16},{16,8},{24,0},{1,25},{9,17},{17,9},{25,1},{2,26},{10... | collective-permute-start | bytes 196616 | tf_op jit(solution)/shard_map/ppermute | solution.py:34
  6.6 0.5 %collective-permute-start.3 = (bf16[2,128,128]{2,1,0:T(8,128)(2,1)S(1)}, bf16[2,128,128]{2,1,0:T(8,128)(2,1)S(1)}, u32[]{:S(2)}, u32[]{:S(2)}) collective-permute-start(bf16[2,128,128]{2,1,0:T(8,128)(2,1)S(1)} %get-tuple-element.27.refs_2_), channel_id=1, source_target_pairs={{0,16},{8,24},{16,0},{24,8},{1,17},{9,25},{17,1},{25,9},{2,18},{10... | collective-permute-start | bytes 196616 | tf_op jit(solution)/shard_map/ppermute | solution.py:34
  7.1 0.5 %collective-permute-start.4 = (bf16[2,128,128]{2,1,0:T(8,128)(2,1)S(1)}, bf16[2,128,128]{2,1,0:T(8,128)(2,1)S(1)}, u32[]{:S(2)}, u32[]{:S(2)}) collective-permute-start(bf16[2,128,128]{2,1,0:T(8,128)(2,1)S(1)} %get-tuple-element.28.refs_3_), channel_id=1, source_target_pairs={{0,8},{8,0},{16,24},{24,16},{1,9},{9,1},{17,25},{25,17},{2,10},{10... | collective-permute-start | bytes 196616 | tf_op jit(solution)/shard_map/ppermute | solution.py:34
  7.6 2.0 %collective-permute-done.refs_1_ = bf16[8,128,128]{2,1,0:T(8,128)(2,1)S(1)} collective-permute-done((bf16[8,128,128]{2,1,0:T(8,128)(2,1)}, bf16[8,128,128]{2,1,0:T(8,128)(2,1)S(1)}, u32[]{:S(2)}, u32[]{:S(2)}) %collective-permute-start) | collective-permute-done | bytes 262176 | tf_op jit(solution)/shard_map/ppermute | solution.py:20
  9.6 0.0 copy-done
  9.6 0.2 %shard_map.46 = (bf16[2048,128]{1,0:T(8,128)(2,1)S(1)}, bf16[1024,128]{1,0:T(8,128)(2,1)S(1)}) custom-call(bf16[8,128,128]{2,1,0:T(8,128)(2,1)S(1)} %copy-done, bf16[8,128,128]{2,1,0:T(8,128)(2,1)S(1)} %collective-permute-done.refs_1_), custom_call_target="tpu_custom_call" | custom-call | bytes 1048576 | tf_op jit(solution)/shard_map/pallas_call | solution.py:200
  9.8 0.0 collective-permute-done.1.refs_4_
  9.8 0.0 collective-permute-done.2.refs_5_.refs_6_
  9.8 0.8 %shard_map.48 = (f32[1,32,128]{2,1,0:T(8,128)S(1)}, bf16[3,32,128]{2,1,0:T(8,128)(2,1)S(1)}, bf16[4,32,128]{2,1,0:T(8,128)(2,1)S(1)}) custom-call(bf16[2048,128]{1,0:T(8,128)(2,1)S(1)} %get-tuple-element.21.refs_0_, bf16[1024,128]{1,0:T(8,128)(2,1)S(1)} %get-tuple-element.22.refs_1_, bf16[2,128,128]{2,1,0:T(8,128)(2,1)S(1)} %get-tuple-element.23.refs_2_, ...), custom_call_target="tpu_custom_call" | custom-call | flops 268435456 | bytes 1048576 | tf_op jit(solution)/shard_map/pallas_call | solution.py:200
  10.7 0.2 %collective-permute-done.3.refs_4_ = bf16[2,128,128]{2,1,0:T(8,128)(2,1)S(1)} collective-permute-done((bf16[2,128,128]{2,1,0:T(8,128)(2,1)S(1)}, bf16[2,128,128]{2,1,0:T(8,128)(2,1)S(1)}, u32[]{:S(2)}, u32[]{:S(2)}) %collective-permute-start.3) | collective-permute-done | bytes 65568 | tf_op jit(solution)/shard_map/ppermute | solution.py:34
  10.9 0.5 %collective-permute-done.4.refs_5_ = bf16[2,128,128]{2,1,0:T(8,128)(2,1)S(1)} collective-permute-done((bf16[2,128,128]{2,1,0:T(8,128)(2,1)S(1)}, bf16[2,128,128]{2,1,0:T(8,128)(2,1)S(1)}, u32[]{:S(2)}, u32[]{:S(2)}) %collective-permute-start.4) | collective-permute-done | bytes 65568 | tf_op jit(solution)/shard_map/ppermute | solution.py:34
  11.4 0.8 %shard_map.49 = (f32[2,32,128]{2,1,0:T(8,128)S(1)}, bf16[3,32,128]{2,1,0:T(8,128)(2,1)S(1)}, bf16[2,32,128]{2,1,0:T(8,128)(2,1)S(1)}, bf16[3,32,128]{2,1,0:T(8,128)(2,1)S(1)}, bf16[5,32,128]{2,1,0:T(8,128)(2,1)S(1)}) custom-call(bf16[2048,128]{1,0:T(8,128)(2,1)S(1)} %get-tuple-element.21.refs_0_, bf16[1024,128]{1,0:T(8,128)(2,1)S(1)} %get-tuple-element.22.refs_1_, ...), custom_call_target="tpu_custom_call" | custom-call | flops 268435456 | bytes 1048576 | tf_op jit(solution)/shard_map/pallas_call | solution.py:200
  12.2 1.3 %collective-permute-start.5 = (bf16[5,32,128]{2,1,0:T(8,128)(2,1)S(1)}, bf16[5,32,128]{2,1,0:T(8,128)(2,1)S(1)}, u32[]{:S(2)}, u32[]{:S(2)}) collective-permute-start(bf16[5,32,128]{2,1,0:T(8,128)(2,1)S(1)} %get-tuple-element.32), channel_id=1, source_target_pairs={{0,6},{1,7},{2,4},{3,5},{4,2},{5,3},{6,0},{7,1},{8,14},{9,15},{10,... | collective-permute-start | bytes 122888 | tf_op jit(solution)/shard_map/ppermute | solution.py:26
  13.5 1.5 %collective-permute-start.6 = (bf16[3,32,128]{2,1,0:T(8,128)(2,1)S(1)}, bf16[3,32,128]{2,1,0:T(8,128)(2,1)S(1)}, u32[]{:S(2)}, u32[]{:S(2)}) collective-permute-start(bf16[3,32,128]{2,1,0:T(8,128)(2,1)S(1)} %get-tuple-element.33), channel_id=1, source_target_pairs={{0,2},{1,3},{2,0},{3,1},{4,6},{5,7},{6,4},{7,5},{8,10},{9,11},{10,... | collective-permute-start | bytes 73736 | tf_op jit(solution)/shard_map/ppermute | solution.py:20
  15.0 0.1 collective-permute-start.7
  15.0 0.4 %collective-permute-start.8 = (bf16[2,32,128]{2,1,0:T(8,128)(2,1)S(1)}, bf16[2,32,128]{2,1,0:T(8,128)(2,1)S(1)}, u32[]{:S(2)}, u32[]{:S(2)}) collective-permute-start(bf16[2,32,128]{2,1,0:T(8,128)(2,1)S(1)} %get-tuple-element.35), channel_id=1, source_target_pairs={{0,4},{4,0},{1,5},{5,1},{2,6},{6,2},{3,7},{7,3},{8,12},{12,8},{9,1... | collective-permute-start | bytes 49160 | tf_op jit(solution)/shard_map/ppermute | solution.py:30
  15.5 0.8 %collective-permute-done.8.more_ref = bf16[2,32,128]{2,1,0:T(8,128)(2,1)S(1)} collective-permute-done((bf16[2,32,128]{2,1,0:T(8,128)(2,1)S(1)}, bf16[2,32,128]{2,1,0:T(8,128)(2,1)S(1)}, u32[]{:S(2)}, u32[]{:S(2)}) %collective-permute-start.8) | collective-permute-done | bytes 16416 | tf_op jit(solution)/shard_map/ppermute | solution.py:30
  16.3 1.9 %collective-permute-done.6.same_ref = bf16[3,32,128]{2,1,0:T(8,128)(2,1)S(1)} collective-permute-done((bf16[3,32,128]{2,1,0:T(8,128)(2,1)S(1)}, bf16[3,32,128]{2,1,0:T(8,128)(2,1)S(1)}, u32[]{:S(2)}, u32[]{:S(2)}) %collective-permute-start.6) | collective-permute-done | bytes 24608 | tf_op jit(solution)/shard_map/ppermute | solution.py:20
  18.2 0.0 collective-permute-done.7.lent_ref
  18.2 0.0 collective-permute-done.5.cross_ref
  18.2 0.7 %shard_map.50 = bf16[2,4,32,128]{3,2,1,0:T(8,128)(2,1)} custom-call(f32[1,32,128]{2,1,0:T(8,128)S(1)} %get-tuple-element.26.first_ref, f32[2,32,128]{2,1,0:T(8,128)S(1)} %get-tuple-element.31.second_ref, bf16[5,32,128]{2,1,0:T(8,128)(2,1)S(1)} %collective-permute-done.5.cross_ref, bf16[3,32,128]{2,1,0:T(8,128)(2,1)S(1)} %collective-permute-done.6.same_ref, ...), custom_call_target="tpu_custom_call" | custom-call | bytes 1048576 | tf_op jit(solution)/shard_map/pallas_call | solution.py:200
  (1 shorter events, 0.0 us)
Async XLA Ops:
  0.0 9.6 %copy-start = (bf16[8,128,128]{2,1,0:T(8,128)(2,1)S(1)}, bf16[8,128,128]{2,1,0:T(8,128)(2,1)}, u32[]{:S(2)}) copy-start(bf16[8,128,128]{2,1,0:T(8,128)(2,1)} %refs_0_.1) | copy-start | bytes 786436
  0.0 9.6 %collective-permute-start = (bf16[8,128,128]{2,1,0:T(8,128)(2,1)}, bf16[8,128,128]{2,1,0:T(8,128)(2,1)S(1)}, u32[]{:S(2)}, u32[]{:S(2)}) collective-permute-start(bf16[8,128,128]{2,1,0:T(8,128)(2,1)} %refs_0_.1), channel_id=1, source_target_pairs={{0,1},{1,0},{2,3},{3,2},{4,5},{5,4},{6,7},{7,6},{8,9},{9,8},{10,11... | collective-permute-start | bytes 786440 | tf_op jit(solution)/shard_map/ppermute | solution.py:20
  4.0 5.8 %collective-permute-start.2 = (bf16[5,128,128]{2,1,0:T(8,128)(2,1)S(1)}, bf16[5,128,128]{2,1,0:T(8,128)(2,1)S(1)}, u32[]{:S(2)}, u32[]{:S(2)}) collective-permute-start(bf16[5,128,128]{2,1,0:T(8,128)(2,1)S(1)} %get-tuple-element.25), channel_id=1, source_target_pairs={{0,4},{4,0},{1,5},{5,1},{2,6},{6,2},{3,7},{7,3},{8,12},{12,8},{9,1... | collective-permute-start | bytes 491528 | tf_op jit(solution)/shard_map/ppermute | solution.py:30
  4.1 5.7 %collective-permute-start.1 = (bf16[2,128,128]{2,1,0:T(8,128)(2,1)S(1)}, bf16[2,128,128]{2,1,0:T(8,128)(2,1)S(1)}, u32[]{:S(2)}, u32[]{:S(2)}) collective-permute-start(bf16[2,128,128]{2,1,0:T(8,128)(2,1)S(1)} %get-tuple-element.24.refs_3_), channel_id=1, source_target_pairs={{0,24},{8,16},{16,8},{24,0},{1,25},{9,17},{17,9},{25,1},{2,26},{10... | collective-permute-start | bytes 196616 | tf_op jit(solution)/shard_map/ppermute | solution.py:34
  6.6 4.3 %collective-permute-start.3 = (bf16[2,128,128]{2,1,0:T(8,128)(2,1)S(1)}, bf16[2,128,128]{2,1,0:T(8,128)(2,1)S(1)}, u32[]{:S(2)}, u32[]{:S(2)}) collective-permute-start(bf16[2,128,128]{2,1,0:T(8,128)(2,1)S(1)} %get-tuple-element.27.refs_2_), channel_id=1, source_target_pairs={{0,16},{8,24},{16,0},{24,8},{1,17},{9,25},{17,1},{25,9},{2,18},{10... | collective-permute-start | bytes 196616 | tf_op jit(solution)/shard_map/ppermute | solution.py:34
  7.1 4.3 %collective-permute-start.4 = (bf16[2,128,128]{2,1,0:T(8,128)(2,1)S(1)}, bf16[2,128,128]{2,1,0:T(8,128)(2,1)S(1)}, u32[]{:S(2)}, u32[]{:S(2)}) collective-permute-start(bf16[2,128,128]{2,1,0:T(8,128)(2,1)S(1)} %get-tuple-element.28.refs_3_), channel_id=1, source_target_pairs={{0,8},{8,0},{16,24},{24,16},{1,9},{9,1},{17,25},{25,17},{2,10},{10... | collective-permute-start | bytes 196616 | tf_op jit(solution)/shard_map/ppermute | solution.py:34
  12.2 6.0 %collective-permute-start.5 = (bf16[5,32,128]{2,1,0:T(8,128)(2,1)S(1)}, bf16[5,32,128]{2,1,0:T(8,128)(2,1)S(1)}, u32[]{:S(2)}, u32[]{:S(2)}) collective-permute-start(bf16[5,32,128]{2,1,0:T(8,128)(2,1)S(1)} %get-tuple-element.32), channel_id=1, source_target_pairs={{0,6},{1,7},{2,4},{3,5},{4,2},{5,3},{6,0},{7,1},{8,14},{9,15},{10,... | collective-permute-start | bytes 122888 | tf_op jit(solution)/shard_map/ppermute | solution.py:26
  13.5 4.7 %collective-permute-start.6 = (bf16[3,32,128]{2,1,0:T(8,128)(2,1)S(1)}, bf16[3,32,128]{2,1,0:T(8,128)(2,1)S(1)}, u32[]{:S(2)}, u32[]{:S(2)}) collective-permute-start(bf16[3,32,128]{2,1,0:T(8,128)(2,1)S(1)} %get-tuple-element.33), channel_id=1, source_target_pairs={{0,2},{1,3},{2,0},{3,1},{4,6},{5,7},{6,4},{7,5},{8,10},{9,11},{10,... | collective-permute-start | bytes 73736 | tf_op jit(solution)/shard_map/ppermute | solution.py:20
  15.0 3.3 %collective-permute-start.7 = (bf16[3,32,128]{2,1,0:T(8,128)(2,1)S(1)}, bf16[3,32,128]{2,1,0:T(8,128)(2,1)S(1)}, u32[]{:S(2)}, u32[]{:S(2)}) collective-permute-start(bf16[3,32,128]{2,1,0:T(8,128)(2,1)S(1)} %get-tuple-element.34), channel_id=1, source_target_pairs={{0,4},{4,0},{1,5},{5,1},{2,6},{6,2},{3,7},{7,3},{8,12},{12,8},{9,1... | collective-permute-start | bytes 73736 | tf_op jit(solution)/shard_map/ppermute | solution.py:30
  15.0 1.3 %collective-permute-start.8 = (bf16[2,32,128]{2,1,0:T(8,128)(2,1)S(1)}, bf16[2,32,128]{2,1,0:T(8,128)(2,1)S(1)}, u32[]{:S(2)}, u32[]{:S(2)}) collective-permute-start(bf16[2,32,128]{2,1,0:T(8,128)(2,1)S(1)} %get-tuple-element.35), channel_id=1, source_target_pairs={{0,4},{4,0},{1,5},{5,1},{2,6},{6,2},{3,7},{7,3},{8,12},{12,8},{9,1... | collective-permute-start | bytes 49160 | tf_op jit(solution)/shard_map/ppermute | solution.py:30

commit v20 on v19

--- a/solution.py
+++ b/solution.py
@@ -10,8 +10,8 @@
 TILE = 64
 SLAB_TILES = 2
 CHIPS = 4
-STEPS = (3, 2, 1)
-ORDER = (0, 3, 2, 1)
+STEPS = (3, 1, 2)
+ORDER = (0, 3, 1, 2)
 BF16 = jnp.bfloat16
 F32 = jnp.float32
 

time: 19.1 us -> 19.2 us (level)
  no operation moved by 1% of the time
where the time goes in v20:
time: 19.2 us; the launch traced here: 19 us
  starting transfers between devices  9.91 us (52%)
  waiting for transfers between devices  5.52 us (29%)
  Pallas kernels  3.48 us (18%)
    ppermute x2, starting transfers between devices, swap_virt(): lax.ppermute(array, 'virt', [(d, d ^ step) for d in range(lax.axis_size('...  4.42 us
    ppermute x2, waiting for transfers between devices, swap_virt(): lax.ppermute(array, 'virt', [(d, d ^ step) for d in range(lax.axis_size('...  3.96 us
    ppermute x3, starting transfers between devices, swap_chip(): lax.ppermute(array, 'occi', [(d, d ^ step) for d in range(lax.axis_size('...  3.55 us
    pallas_call x5, Pallas kernels, kernel(): pl.pallas_call(body, out_shape=outs, in_specs=[pl.BlockSpec(memory_space=...  3.48 us
    ppermute x1, starting transfers between devices, swap_both(): return lax.ppermute(array, ('occj', 'virt'), moves)  1.36 us
    ppermute x3, waiting for transfers between devices, swap_core(): return lax.ppermute(array, 'occj', [(0, 1), (1, 0)])  0.84 us
    ppermute x3, waiting for transfers between devices, swap_chip(): lax.ppermute(array, 'occi', [(d, d ^ step) for d in range(lax.axis_size('...  0.71 us
    ppermute x3, starting transfers between devices, swap_core(): return lax.ppermute(array, 'occj', [(0, 1), (1, 0)])  0.58 us
  transfers between devices with their start and end apart: 9, of which 5 were waited for; matrix products, arithmetic and copies ran while one was open for 0% of the time, Pallas kernels for 11%

profile of v20, /device:TPU:0, one launch (start us, length us, event | category | flops | bytes accessed | tf_op | source)
XLA Modules:
  0.0 19.0 jit_solution(10023672942530589152)
XLA Ops:
  0.0 3.0 %collective-permute-start = (bf16[8,128,128]{2,1,0:T(8,128)(2,1)}, bf16[8,128,128]{2,1,0:T(8,128)(2,1)S(1)}, u32[]{:S(2)}, u32[]{:S(2)}) collective-permute-start(bf16[8,128,128]{2,1,0:T(8,128)(2,1)} %refs_0_.1), channel_id=1, source_target_pairs={{0,1},{1,0},{2,3},{3,2},{4,5},{5,4},{6,7},{7,6},{8,9},{9,8},{10,11... | collective-permute-start | bytes 786440 | tf_op jit(solution)/shard_map/ppermute | solution.py:20
  3.0 1.0 %shard_map.47 = (bf16[2,128,128]{2,1,0:T(8,128)(2,1)S(1)}, bf16[2,128,128]{2,1,0:T(8,128)(2,1)S(1)}, bf16[2,128,128]{2,1,0:T(8,128)(2,1)S(1)}, bf16[2,128,128]{2...) custom-call(s32[2,2,2,4]{3,2,1,0:T(2,128)} %bitcast.1, s32[2,4]{1,0:T(2,128)} %pair_hbm.1, ...), custom_call_target="tpu_custom_call" | custom-call | bytes 1048576 | tf_op jit(solution)/shard_map/pallas_call | solution.py:200
  4.0 0.1 collective-permute-start.2
  4.1 2.5 %collective-permute-start.1 = (bf16[2,128,128]{2,1,0:T(8,128)(2,1)S(1)}, bf16[2,128,128]{2,1,0:T(8,128)(2,1)S(1)}, u32[]{:S(2)}, u32[]{:S(2)}) collective-permute-start(bf16[2,128,128]{2,1,0:T(8,128)(2,1)S(1)} %get-tuple-element.24.refs_3_), channel_id=1, source_target_pairs={{0,24},{8,16},{16,8},{24,0},{1,25},{9,17},{17,9},{25,1},{2,26},{10... | collective-permute-start | bytes 196616 | tf_op jit(solution)/shard_map/ppermute | solution.py:34
  6.6 0.5 %collective-permute-start.3 = (bf16[2,128,128]{2,1,0:T(8,128)(2,1)S(1)}, bf16[2,128,128]{2,1,0:T(8,128)(2,1)S(1)}, u32[]{:S(2)}, u32[]{:S(2)}) collective-permute-start(bf16[2,128,128]{2,1,0:T(8,128)(2,1)S(1)} %get-tuple-element.27.refs_2_), channel_id=1, source_target_pairs={{0,8},{8,0},{16,24},{24,16},{1,9},{9,1},{17,25},{25,17},{2,10},{10... | collective-permute-start | bytes 196616 | tf_op jit(solution)/shard_map/ppermute | solution.py:34
  7.1 0.5 %collective-permute-start.4 = (bf16[2,128,128]{2,1,0:T(8,128)(2,1)S(1)}, bf16[2,128,128]{2,1,0:T(8,128)(2,1)S(1)}, u32[]{:S(2)}, u32[]{:S(2)}) collective-permute-start(bf16[2,128,128]{2,1,0:T(8,128)(2,1)S(1)} %get-tuple-element.28.refs_3_), channel_id=1, source_target_pairs={{0,16},{8,24},{16,0},{24,8},{1,17},{9,25},{17,1},{25,9},{2,18},{10... | collective-permute-start | bytes 196616 | tf_op jit(solution)/shard_map/ppermute | solution.py:34
  7.6 2.0 %collective-permute-done.refs_1_ = bf16[8,128,128]{2,1,0:T(8,128)(2,1)S(1)} collective-permute-done((bf16[8,128,128]{2,1,0:T(8,128)(2,1)}, bf16[8,128,128]{2,1,0:T(8,128)(2,1)S(1)}, u32[]{:S(2)}, u32[]{:S(2)}) %collective-permute-start) | collective-permute-done | bytes 262176 | tf_op jit(solution)/shard_map/ppermute | solution.py:20
  9.6 0.0 copy-done
  9.6 0.2 %shard_map.46 = (bf16[2048,128]{1,0:T(8,128)(2,1)S(1)}, bf16[1024,128]{1,0:T(8,128)(2,1)S(1)}) custom-call(bf16[8,128,128]{2,1,0:T(8,128)(2,1)S(1)} %copy-done, bf16[8,128,128]{2,1,0:T(8,128)(2,1)S(1)} %collective-permute-done.refs_1_), custom_call_target="tpu_custom_call" | custom-call | bytes 1048576 | tf_op jit(solution)/shard_map/pallas_call | solution.py:200
  9.8 0.0 collective-permute-done.1.refs_4_
  9.8 0.0 collective-permute-done.2.refs_5_.refs_6_
  9.8 0.8 %shard_map.48 = (f32[1,32,128]{2,1,0:T(8,128)S(1)}, bf16[3,32,128]{2,1,0:T(8,128)(2,1)S(1)}, bf16[4,32,128]{2,1,0:T(8,128)(2,1)S(1)}) custom-call(bf16[2048,128]{1,0:T(8,128)(2,1)S(1)} %get-tuple-element.21.refs_0_, bf16[1024,128]{1,0:T(8,128)(2,1)S(1)} %get-tuple-element.22.refs_1_, bf16[2,128,128]{2,1,0:T(8,128)(2,1)S(1)} %get-tuple-element.23.refs_2_, ...), custom_call_target="tpu_custom_call" | custom-call | flops 268435456 | bytes 1048576 | tf_op jit(solution)/shard_map/pallas_call | solution.py:200
  10.7 0.3 %collective-permute-done.3.refs_4_ = bf16[2,128,128]{2,1,0:T(8,128)(2,1)S(1)} collective-permute-done((bf16[2,128,128]{2,1,0:T(8,128)(2,1)S(1)}, bf16[2,128,128]{2,1,0:T(8,128)(2,1)S(1)}, u32[]{:S(2)}, u32[]{:S(2)}) %collective-permute-start.3) | collective-permute-done | bytes 65568 | tf_op jit(solution)/shard_map/ppermute | solution.py:34
  10.9 0.4 %collective-permute-done.4.refs_5_ = bf16[2,128,128]{2,1,0:T(8,128)(2,1)S(1)} collective-permute-done((bf16[2,128,128]{2,1,0:T(8,128)(2,1)S(1)}, bf16[2,128,128]{2,1,0:T(8,128)(2,1)S(1)}, u32[]{:S(2)}, u32[]{:S(2)}) %collective-permute-start.4) | collective-permute-done | bytes 65568 | tf_op jit(solution)/shard_map/ppermute | solution.py:34
  11.4 0.8 %shard_map.49 = (f32[2,32,128]{2,1,0:T(8,128)S(1)}, bf16[3,32,128]{2,1,0:T(8,128)(2,1)S(1)}, bf16[2,32,128]{2,1,0:T(8,128)(2,1)S(1)}, bf16[3,32,128]{2,1,0:T(8,128)(2,1)S(1)}, bf16[5,32,128]{2,1,0:T(8,128)(2,1)S(1)}) custom-call(bf16[2048,128]{1,0:T(8,128)(2,1)S(1)} %get-tuple-element.21.refs_0_, bf16[1024,128]{1,0:T(8,128)(2,1)S(1)} %get-tuple-element.22.refs_1_, ...), custom_call_target="tpu_custom_call" | custom-call | flops 268435456 | bytes 1048576 | tf_op jit(solution)/shard_map/pallas_call | solution.py:200
  12.2 1.4 %collective-permute-start.5 = (bf16[5,32,128]{2,1,0:T(8,128)(2,1)S(1)}, bf16[5,32,128]{2,1,0:T(8,128)(2,1)S(1)}, u32[]{:S(2)}, u32[]{:S(2)}) collective-permute-start(bf16[5,32,128]{2,1,0:T(8,128)(2,1)S(1)} %get-tuple-element.32), channel_id=1, source_target_pairs={{0,6},{1,7},{2,4},{3,5},{4,2},{5,3},{6,0},{7,1},{8,14},{9,15},{10,... | collective-permute-start | bytes 122888 | tf_op jit(solution)/shard_map/ppermute | solution.py:26
  13.6 1.4 %collective-permute-start.6 = (bf16[3,32,128]{2,1,0:T(8,128)(2,1)S(1)}, bf16[3,32,128]{2,1,0:T(8,128)(2,1)S(1)}, u32[]{:S(2)}, u32[]{:S(2)}) collective-permute-start(bf16[3,32,128]{2,1,0:T(8,128)(2,1)S(1)} %get-tuple-element.33), channel_id=1, source_target_pairs={{0,2},{1,3},{2,0},{3,1},{4,6},{5,7},{6,4},{7,5},{8,10},{9,11},{10,... | collective-permute-start | bytes 73736 | tf_op jit(solution)/shard_map/ppermute | solution.py:20
  15.0 0.1 collective-permute-start.7
  15.1 0.4 %collective-permute-start.8 = (bf16[2,32,128]{2,1,0:T(8,128)(2,1)S(1)}, bf16[2,32,128]{2,1,0:T(8,128)(2,1)S(1)}, u32[]{:S(2)}, u32[]{:S(2)}) collective-permute-start(bf16[2,32,128]{2,1,0:T(8,128)(2,1)S(1)} %get-tuple-element.35), channel_id=1, source_target_pairs={{0,4},{4,0},{1,5},{5,1},{2,6},{6,2},{3,7},{7,3},{8,12},{12,8},{9,1... | collective-permute-start | bytes 49160 | tf_op jit(solution)/shard_map/ppermute | solution.py:30
  15.5 0.8 %collective-permute-done.8.more_ref = bf16[2,32,128]{2,1,0:T(8,128)(2,1)S(1)} collective-permute-done((bf16[2,32,128]{2,1,0:T(8,128)(2,1)S(1)}, bf16[2,32,128]{2,1,0:T(8,128)(2,1)S(1)}, u32[]{:S(2)}, u32[]{:S(2)}) %collective-permute-start.8) | collective-permute-done | bytes 16416 | tf_op jit(solution)/shard_map/ppermute | solution.py:30
  16.3 2.0 %collective-permute-done.6.same_ref = bf16[3,32,128]{2,1,0:T(8,128)(2,1)S(1)} collective-permute-done((bf16[3,32,128]{2,1,0:T(8,128)(2,1)S(1)}, bf16[3,32,128]{2,1,0:T(8,128)(2,1)S(1)}, u32[]{:S(2)}, u32[]{:S(2)}) %collective-permute-start.6) | collective-permute-done | bytes 24608 | tf_op jit(solution)/shard_map/ppermute | solution.py:20
  18.3 0.0 collective-permute-done.7.lent_ref
  18.3 0.0 collective-permute-done.5.cross_ref
  18.3 0.7 %shard_map.50 = bf16[2,4,32,128]{3,2,1,0:T(8,128)(2,1)} custom-call(f32[1,32,128]{2,1,0:T(8,128)S(1)} %get-tuple-element.26.first_ref, f32[2,32,128]{2,1,0:T(8,128)S(1)} %get-tuple-element.31.second_ref, bf16[5,32,128]{2,1,0:T(8,128)(2,1)S(1)} %collective-permute-done.5.cross_ref, bf16[3,32,128]{2,1,0:T(8,128)(2,1)S(1)} %collective-permute-done.6.same_ref, ...), custom_call_target="tpu_custom_call" | custom-call | bytes 1048576 | tf_op jit(solution)/shard_map/pallas_call | solution.py:200
  (1 shorter events, 0.0 us)
Async XLA Ops:
  0.0 9.6 %copy-start = (bf16[8,128,128]{2,1,0:T(8,128)(2,1)S(1)}, bf16[8,128,128]{2,1,0:T(8,128)(2,1)}, u32[]{:S(2)}) copy-start(bf16[8,128,128]{2,1,0:T(8,128)(2,1)} %refs_0_.1) | copy-start | bytes 786436
  0.0 9.6 %collective-permute-start = (bf16[8,128,128]{2,1,0:T(8,128)(2,1)}, bf16[8,128,128]{2,1,0:T(8,128)(2,1)S(1)}, u32[]{:S(2)}, u32[]{:S(2)}) collective-permute-start(bf16[8,128,128]{2,1,0:T(8,128)(2,1)} %refs_0_.1), channel_id=1, source_target_pairs={{0,1},{1,0},{2,3},{3,2},{4,5},{5,4},{6,7},{7,6},{8,9},{9,8},{10,11... | collective-permute-start | bytes 786440 | tf_op jit(solution)/shard_map/ppermute | solution.py:20
  4.0 5.8 %collective-permute-start.2 = (bf16[5,128,128]{2,1,0:T(8,128)(2,1)S(1)}, bf16[5,128,128]{2,1,0:T(8,128)(2,1)S(1)}, u32[]{:S(2)}, u32[]{:S(2)}) collective-permute-start(bf16[5,128,128]{2,1,0:T(8,128)(2,1)S(1)} %get-tuple-element.25), channel_id=1, source_target_pairs={{0,4},{4,0},{1,5},{5,1},{2,6},{6,2},{3,7},{7,3},{8,12},{12,8},{9,1... | collective-permute-start | bytes 491528 | tf_op jit(solution)/shard_map/ppermute | solution.py:30
  4.1 5.7 %collective-permute-start.1 = (bf16[2,128,128]{2,1,0:T(8,128)(2,1)S(1)}, bf16[2,128,128]{2,1,0:T(8,128)(2,1)S(1)}, u32[]{:S(2)}, u32[]{:S(2)}) collective-permute-start(bf16[2,128,128]{2,1,0:T(8,128)(2,1)S(1)} %get-tuple-element.24.refs_3_), channel_id=1, source_target_pairs={{0,24},{8,16},{16,8},{24,0},{1,25},{9,17},{17,9},{25,1},{2,26},{10... | collective-permute-start | bytes 196616 | tf_op jit(solution)/shard_map/ppermute | solution.py:34
  6.6 4.4 %collective-permute-start.3 = (bf16[2,128,128]{2,1,0:T(8,128)(2,1)S(1)}, bf16[2,128,128]{2,1,0:T(8,128)(2,1)S(1)}, u32[]{:S(2)}, u32[]{:S(2)}) collective-permute-start(bf16[2,128,128]{2,1,0:T(8,128)(2,1)S(1)} %get-tuple-element.27.refs_2_), channel_id=1, source_target_pairs={{0,8},{8,0},{16,24},{24,16},{1,9},{9,1},{17,25},{25,17},{2,10},{10... | collective-permute-start | bytes 196616 | tf_op jit(solution)/shard_map/ppermute | solution.py:34
  7.1 4.3 %collective-permute-start.4 = (bf16[2,128,128]{2,1,0:T(8,128)(2,1)S(1)}, bf16[2,128,128]{2,1,0:T(8,128)(2,1)S(1)}, u32[]{:S(2)}, u32[]{:S(2)}) collective-permute-start(bf16[2,128,128]{2,1,0:T(8,128)(2,1)S(1)} %get-tuple-element.28.refs_3_), channel_id=1, source_target_pairs={{0,16},{8,24},{16,0},{24,8},{1,17},{9,25},{17,1},{25,9},{2,18},{10... | collective-permute-start | bytes 196616 | tf_op jit(solution)/shard_map/ppermute | solution.py:34
  12.2 6.1 %collective-permute-start.5 = (bf16[5,32,128]{2,1,0:T(8,128)(2,1)S(1)}, bf16[5,32,128]{2,1,0:T(8,128)(2,1)S(1)}, u32[]{:S(2)}, u32[]{:S(2)}) collective-permute-start(bf16[5,32,128]{2,1,0:T(8,128)(2,1)S(1)} %get-tuple-element.32), channel_id=1, source_target_pairs={{0,6},{1,7},{2,4},{3,5},{4,2},{5,3},{6,0},{7,1},{8,14},{9,15},{10,... | collective-permute-start | bytes 122888 | tf_op jit(solution)/shard_map/ppermute | solution.py:26
  13.6 4.7 %collective-permute-start.6 = (bf16[3,32,128]{2,1,0:T(8,128)(2,1)S(1)}, bf16[3,32,128]{2,1,0:T(8,128)(2,1)S(1)}, u32[]{:S(2)}, u32[]{:S(2)}) collective-permute-start(bf16[3,32,128]{2,1,0:T(8,128)(2,1)S(1)} %get-tuple-element.33), channel_id=1, source_target_pairs={{0,2},{1,3},{2,0},{3,1},{4,6},{5,7},{6,4},{7,5},{8,10},{9,11},{10,... | collective-permute-start | bytes 73736 | tf_op jit(solution)/shard_map/ppermute | solution.py:20
  15.0 3.3 %collective-permute-start.7 = (bf16[3,32,128]{2,1,0:T(8,128)(2,1)S(1)}, bf16[3,32,128]{2,1,0:T(8,128)(2,1)S(1)}, u32[]{:S(2)}, u32[]{:S(2)}) collective-permute-start(bf16[3,32,128]{2,1,0:T(8,128)(2,1)S(1)} %get-tuple-element.34), channel_id=1, source_target_pairs={{0,4},{4,0},{1,5},{5,1},{2,6},{6,2},{3,7},{7,3},{8,12},{12,8},{9,1... | collective-permute-start | bytes 73736 | tf_op jit(solution)/shard_map/ppermute | solution.py:30
  15.1 1.3 %collective-permute-start.8 = (bf16[2,32,128]{2,1,0:T(8,128)(2,1)S(1)}, bf16[2,32,128]{2,1,0:T(8,128)(2,1)S(1)}, u32[]{:S(2)}, u32[]{:S(2)}) collective-permute-start(bf16[2,32,128]{2,1,0:T(8,128)(2,1)S(1)} %get-tuple-element.35), channel_id=1, source_target_pairs={{0,4},{4,0},{1,5},{5,1},{2,6},{6,2},{3,7},{7,3},{8,12},{12,8},{9,1... | collective-permute-start | bytes 49160 | tf_op jit(solution)/shard_map/ppermute | solution.py:30
